TPU v7x, 32 devices: a whole 2x2x4 slice. The times are simulated.
32 devices in a mesh: sample: 16 (over z, y, core), spatial: 2 (over x).
Axes of the slice: x: 2, y: 2, z: 4, core: 2. Of those that a mesh axis runs over, the one named last changes fastest.
Arguments:
- volume: bfloat16 [16, 32, 16, 1024], P('sample', 'spatial'), may hold values from -6 to 6
- w_first: bfloat16 [1728, 128], replicated, may hold values from -0.15625 to 0.15625
- w_second: bfloat16 [3456, 256], replicated, may hold values from -0.109375 to 0.109375
- cotangent: bfloat16 [16, 8, 4, 1024], P('sample', 'spatial'), may hold values from -0.13183594 to 0.13183594
Outputs:
- grad_first: float32 [1728, 128], replicated
- grad_second: float32 [3456, 256], replicated
All inputs are finite; a program needn't handle non-finite values.
Results may differ from a plain program's by a relative error of at most 0.0052.
Values may be sent and summed in bfloat16 or wider, within the bound.
No kernel may reach another device: no remote copies, remote signals or barrier semaphores. Data moves between devices by JAX's collectives and lax.ppermute only.
A program may use at most 64 MiB of HBM per device.

v0:
```python
import jax
import jax.numpy as jnp
from jax import lax
from jax.sharding import PartitionSpec as P

tap_offsets = [
    (first, second, third) for first in range(3) for second in range(3) for third in range(3)
]


def from_behind(shard, axis, by):
    peers = lax.axis_size(axis)
    pairs = [(i, i + by) for i in range(peers) if 0 <= i + by < peers]
    return lax.ppermute(shard, axis, pairs)


def silu_slope(value):
    sigmoid_value = jax.nn.sigmoid(value)
    return sigmoid_value * (1.0 + value * (1.0 - sigmoid_value))


def pad_cells(cells_in):
    return jnp.pad(cells_in, ((0, 0), (1, 1), (1, 1), (1, 1), (0, 0)))


def pad_sides(cells_in):
    return jnp.pad(cells_in, ((0, 0), (0, 0), (1, 1), (1, 1), (0, 0)))


def tap_slices(padded):
    batch_size, len_z, len_y, len_x, channels = padded.shape
    halves = padded.reshape(batch_size, len_z // 2, 2, len_y // 2, 2, len_x // 2, 2, channels)
    out_z, out_y, out_x = (len_z // 2 - 1, len_y // 2 - 1, len_x // 2 - 1)
    result = []
    for offset_z, offset_y, offset_x in tap_offsets:
        result.append(
            halves[
                :,
                offset_z // 2 : offset_z // 2 + out_z,
                offset_z % 2,
                offset_y // 2 : offset_y // 2 + out_y,
                offset_y % 2,
                offset_x // 2 : offset_x // 2 + out_x,
                offset_x % 2,
                :,
            ]
        )
    return result


def conv_taps(padded, weights):
    channels = padded.shape[-1]
    stacked = weights.reshape(27, channels, weights.shape[1])
    summed = None
    for tap_index, sliced in enumerate(tap_slices(padded)):
        product = jnp.dot(sliced, stacked[tap_index], preferred_element_type=jnp.float32)
        summed = product if summed is None else summed + product
    return summed


def weight_grads(padded, delta_cells):
    flat_grad = delta_cells.reshape(-1, delta_cells.shape[-1])
    blocks = []
    for sliced in tap_slices(padded):
        flat_in = sliced.reshape(-1, sliced.shape[-1])
        blocks.append(jnp.dot(flat_in.T, flat_grad, preferred_element_type=jnp.float32))
    return jnp.concatenate(blocks, axis=0)


def input_grads(delta_cells, weights):
    batch_size, out_z, out_y, out_x, outputs = delta_cells.shape
    channels = weights.shape[0] // 27
    stacked = weights.reshape(27, channels, outputs)
    parity_sums = {}
    for tap_index, (offset_z, offset_y, offset_x) in enumerate(tap_offsets):
        product = jnp.dot(delta_cells, stacked[tap_index].T, preferred_element_type=jnp.float32)
        placed = jnp.pad(
            product,
            (
                (0, 0),
                (offset_z // 2, 1 - offset_z // 2),
                (offset_y // 2, 1 - offset_y // 2),
                (offset_x // 2, 1 - offset_x // 2),
                (0, 0),
            ),
        )
        parity = (offset_z % 2, offset_y % 2, offset_x % 2)
        parity_sums[parity] = placed if parity not in parity_sums else parity_sums[parity] + placed
    planes = []
    for parity_z in range(2):
        rows_list = []
        for parity_y in range(2):
            rows_list.append(
                jnp.stack(
                    [parity_sums[parity_z, parity_y, 0], parity_sums[parity_z, parity_y, 1]], axis=4
                )
            )
        planes.append(jnp.stack(rows_list, axis=3))
    joined = jnp.stack(planes, axis=2)
    return joined.reshape(batch_size, 2 * out_z + 2, 2 * out_y + 2, 2 * out_x + 2, channels)


def body(volume, w_first, w_second, cotangent):
    first_in = w_first.shape[0] // 27
    first_out = w_first.shape[1]
    groups, slab_z, side_cells, merged = volume.shape
    cells_in = volume.reshape(groups, slab_z, side_cells, side_cells, first_in)
    lower_face = from_behind(volume[:, -1], "spatial", 1)
    empty_face = jnp.zeros_like(cells_in[:, :1])
    padded_in = pad_sides(
        jnp.concatenate(
            [lower_face.reshape(groups, 1, side_cells, side_cells, first_in), cells_in, empty_face],
            axis=1,
        )
    )
    first_pre = conv_taps(padded_in, w_first)
    hidden = jax.nn.silu(first_pre).astype(jnp.bfloat16)
    half_z, half_side = (slab_z // 2, side_cells // 2)
    hidden_flat = hidden.reshape(groups, half_z, half_side, half_side * first_out)
    index_here = lax.axis_index("spatial")
    spatial_count = lax.axis_size("spatial")
    outputs = w_second.shape[1]
    column_share = outputs // spatial_count
    whole_flat = lax.all_gather(hidden_flat, "spatial", axis=1, tiled=True)
    full_z = whole_flat.shape[1]
    padded_hidden = pad_cells(whole_flat.reshape(groups, full_z, half_side, half_side, first_out))
    quarter_z, quarter_side = (cotangent.shape[1], cotangent.shape[2])
    split_cot = cotangent.reshape(
        groups, quarter_z, quarter_side, quarter_side, spatial_count, column_share
    )
    split_cot = jnp.moveaxis(split_cot, 4, 1).reshape(
        groups, spatial_count, quarter_z, quarter_side, quarter_side * column_share
    )
    owned_cot = lax.all_to_all(split_cot, "spatial", split_axis=1, concat_axis=2, tiled=True)
    owned_cot = owned_cot.reshape(
        groups, spatial_count * quarter_z, quarter_side, quarter_side, column_share
    )
    w_columns = lax.dynamic_slice_in_dim(w_second, index_here * column_share, column_share, 1)
    second_pre = conv_taps(padded_hidden, w_columns)
    second_delta = (owned_cot.astype(jnp.float32) * silu_slope(second_pre)).astype(jnp.bfloat16)
    column_grad = weight_grads(padded_hidden, second_delta)
    grad_second = lax.dynamic_update_slice_in_dim(
        jnp.zeros((w_second.shape[0], outputs), jnp.float32),
        column_grad,
        index_here * column_share,
        1,
    )
    partial_grad = input_grads(second_delta, w_columns)[:, 1:-1, 1:-1, 1:-1, :]
    summed_grad = lax.psum_scatter(
        partial_grad.reshape(groups, full_z, half_side, half_side * first_out),
        "spatial",
        scatter_dimension=1,
        tiled=True,
    )
    hidden_grad = summed_grad.reshape(groups, half_z, half_side, half_side, first_out).astype(
        jnp.bfloat16
    )
    hidden_grad = lax.optimization_barrier(hidden_grad)
    first_delta = (hidden_grad.astype(jnp.float32) * silu_slope(first_pre)).astype(jnp.bfloat16)
    local_first = weight_grads(padded_in, first_delta)
    grad_first, grad_second = lax.psum((local_first, grad_second), ("sample", "spatial"))
    return (grad_first, grad_second)


def solution(mesh):
    return jax.shard_map(
        body,
        mesh=mesh,
        in_specs=(P("sample", "spatial", None, None), P(), P(), P("sample", "spatial", None, None)),
        out_specs=(P(), P()),
        check_vma=False,
    )
```

profile of v0, /device:TPU:0, one launch (start us, length us, event | category | flops | bytes accessed | tf_op | source)
XLA Modules:
  0.0 273.5 jit_solution(14134160546126813618)
XLA Ops:
  7.2 0.9 slice_bitcast_fusion
  8.1 4.8 %collective-permute-start = (bf16[1,16,1024]{2,1,0:T(8,128)(2,1)S(1)}, bf16[1,16,1024]{2,1,0:T(8,128)(2,1)S(1)}, u32[]{:S(2)}, u32[]{:S(2)}) collective-permute-start(bf16[1,16,1024]{2,1,0:T(8,128)(2,1)S(1)} %slice_bitcast_fusion), channel_id=1, source_target_pairs={{0,1},{2,3},{4,5},{6,7},{8,9},{10,11},{12,13},{14,15},{16,17},{18,... | collective-permute-start | bytes 98312 | tf_op jit(solution)/shard_map/ppermute | solution.py:14
  12.9 0.8 reshape.604
  13.7 0.6 reshape.605
  14.3 3.3 %all-to-all-start = ((bf16[1,2,4,4,512]{4,3,2,0,1:T(4,128)(2,1)}), bf16[1,2,4,4,512]{4,3,2,0,1:T(4,128)(2,1)S(1)}, u32[]{:S(2)}, u32[]{:S(2)}) async-start(bf16[1,2,4,4,512]{4,3,2,0,1:T(4,128)(2,1)} %bitcast.3), calls=%async_computation | async-start | bytes 65536 | tf_op jit(solution)/shard_map/all_to_all | solution.py:134
  17.7 1.8 reshape.602
  19.5 2.0 all-to-all-done
  21.5 0.7 reshape.667
  22.6 1.9 pad.97
  24.5 3.7 %reshape.603 = bf16[1,9,2,9,2,9,2,64]{7,6,5,4,3,2,1,0:T(2,128)(2,1)S(1)} reshape(bf16[1,18,18,18,64]{4,3,2,1,0:T(8,128)(2,1)} %pad.97) | data formatting | bytes 1492992 | tf_op jit(solution)/shard_map/reshape | solution.py:32
  28.1 2.3 fusion.88
  30.4 5.6 %fusion.87 = (bf16[1,8,1,8,1,8,1,64]{7,6,5,4,3,2,1,0:T(2,128)(2,1)S(1)}, bf16[1,8,1,8,1,8,1,64]{7,6,5,4,3,2,1,0:T(2,128)(2,1)S(1)}, bf16[1,8,1,8,1,8,1,64]{7,6,5...) fusion(bf16[1,9,2,9,2,9,2,64]{7,6,5,4,3,2,1,0:T(2,128)(2,1)S(1), ...), kind=kLoop, calls=%fused_computation.301 | loop fusion | bytes 2490368 | tf_op jit(solution)/shard_map/slice | solution.py:37
  37.0 1.0 copy-done.47
  42.7 0.9 multiply_convert_fusion
  43.6 5.8 %all_gather.3 = bf16[1,16,8,1024]{3,2,0,1:T(8,128)(2,1)S(1)} all-gather(bf16[1,8,8,1024]{3,2,0,1:T(8,128)(2,1)S(1)} %bitcast.857), channel_id=1, replica_groups=mesh['sample'=16,'spatial'=2] {'spatial'}, dimensions={1}, use_global_device_ids=true | all-gather | bytes 393216 | tf_op jit(solution)/shard_map/all_gather | solution.py:124
  50.3 1.2 fusion.89
  51.6 0.6 copy.245
  52.2 0.6 copy.244
  53.4 0.6 copy.242
  54.0 0.6 copy.241
  55.3 0.6 copy.239
  55.9 0.6 copy.237
  57.1 0.6 copy.247
  60.8 0.6 copy.253
  74.7 0.9 copy.236
  75.7 1.3 slice_reduce_fusion
  77.2 0.9 reshape.664
  78.3 0.9 convolution_dynamic-update-slice_fusion.26
  79.3 0.9 convolution_dynamic-update-slice_fusion.25
  80.2 0.9 convolution_dynamic-update-slice_fusion.24
  85.9 2.0 broadcast_in_dim.7
  87.9 1.3 constant_dynamic-update-slice_fusion
  89.2 4.0 %reduce-scatter.2.cloned.1.call-done = f32[1,8,8,1024]{3,2,1,0:T(8,128)} async-done(((f32[1,16,8,1024]{3,2,1,0:T(8,128)}), f32[1,8,8,1024]{3,2,1,0:T(8,128)}) %reduce-scatter.2.cloned.1.call-update) | async-done | bytes 262160 | tf_op jit(solution)/shard_map/reduce_scatter | solution.py:149
  93.2 1.0 convert_bitcast_fusion
  94.4 0.8 convolution_dynamic-update-slice_fusion.53
  95.2 0.8 convolution_dynamic-update-slice_fusion.52
  96.1 0.8 convolution_dynamic-update-slice_fusion.51
  96.9 0.8 convolution_dynamic-update-slice_fusion.50
  97.7 0.8 convolution_dynamic-update-slice_fusion.49
  98.5 0.8 convolution_dynamic-update-slice_fusion.48
  99.4 0.8 convolution_dynamic-update-slice_fusion.47
  100.2 0.8 convolution_dynamic-update-slice_fusion.46
  101.0 0.8 convolution_dynamic-update-slice_fusion.45
  101.9 0.8 convolution_dynamic-update-slice_fusion.44
  102.7 0.8 convolution_dynamic-update-slice_fusion.43
  103.5 0.8 convolution_dynamic-update-slice_fusion.42
  104.3 0.8 convolution_dynamic-update-slice_fusion.41
  105.2 0.8 convolution_dynamic-update-slice_fusion.40
  106.0 0.8 convolution_dynamic-update-slice_fusion.39
  106.8 0.8 convolution_dynamic-update-slice_fusion.38
  107.6 0.8 convolution_dynamic-update-slice_fusion.37
  108.5 0.8 convolution_dynamic-update-slice_fusion.36
  109.3 0.8 convolution_dynamic-update-slice_fusion.35
  110.1 0.8 convolution_dynamic-update-slice_fusion.34
  110.9 0.8 convolution_dynamic-update-slice_fusion.33
  111.8 0.8 convolution_dynamic-update-slice_fusion.32
  112.6 0.8 convolution_dynamic-update-slice_fusion.31
  113.4 0.8 convolution_dynamic-update-slice_fusion.30
  114.2 0.8 convolution_dynamic-update-slice_fusion.29
  115.0 0.8 convolution_dynamic-update-slice_fusion.28
  115.9 0.8 convolution_dynamic-update-slice_fusion.27
  116.7 143.8 %all-reduce.32.cloned.1.call-done = (f32[1728,128]{1,0:T(8,128)}, f32[3456,256]{1,0:T(8,128)}) async-done(((f32[1728,128]{1,0:T(8,128)}, f32[3456,256]{1,0:T(8,128)}), (f32[1728,128]{1,0:T(8,128)}, f32[3456,256]{1,0:T(8,128)})) %all-reduce.32.cloned.1.call-update) | async-done | bytes 4423696 | tf_op jit(solution)/shard_map/psum | solution.py:161
  260.5 2.1 copy.548
  262.6 4.0 %copy.549 = f32[3456,256]{1,0:T(8,128)} copy(f32[3456,256]{1,0:T(8,128)} %get-tuple-element.69) | data formatting | bytes 7077888
  (321 shorter events, 29.4 us)
Async XLA Ops:
  7.2 58.6 %copy-start = (bf16[3456,256]{1,0:T(8,128)(2,1)S(1)}, bf16[3456,256]{1,0:T(8,128)(2,1)}, u32[]{:S(2)}) copy-start(bf16[3456,256]{1,0:T(8,128)(2,1)} %param.6) | copy-start | bytes 5308420
  8.1 14.1 %collective-permute-start = (bf16[1,16,1024]{2,1,0:T(8,128)(2,1)S(1)}, bf16[1,16,1024]{2,1,0:T(8,128)(2,1)S(1)}, u32[]{:S(2)}, u32[]{:S(2)}) collective-permute-start(bf16[1,16,1024]{2,1,0:T(8,128)(2,1)S(1)} %slice_bitcast_fusion), channel_id=1, source_target_pairs={{0,1},{2,3},{4,5},{6,7},{8,9},{10,11},{12,13},{14,15},{16,17},{18,... | collective-permute-start | bytes 98312 | tf_op jit(solution)/shard_map/ppermute | solution.py:14
  14.3 7.2 %all-to-all-start = ((bf16[1,2,4,4,512]{4,3,2,0,1:T(4,128)(2,1)}), bf16[1,2,4,4,512]{4,3,2,0,1:T(4,128)(2,1)S(1)}, u32[]{:S(2)}, u32[]{:S(2)}) async-start(bf16[1,2,4,4,512]{4,3,2,0,1:T(4,128)(2,1)} %bitcast.3), calls=%async_computation | async-start | bytes 65536 | tf_op jit(solution)/shard_map/all_to_all | solution.py:134
  17.6 75.6 %reduce-scatter.2.cloned.1.call-start = ((), (), s32[]{:S(2)}) async-start(), calls=%async_computation.2 | async-start | bytes 786432 | tf_op jit(solution)/shard_map/reduce_scatter | solution.py:149
  36.0 3.2 %copy-start.9 = (bf16[1,8,1,8,1,8,1,64]{7,5,3,1,6,4,2,0:T(8,128)(2,1)}, bf16[1,8,1,8,1,8,1,64]{7,5,3,1,6,4,2,0:T(8,128)(2,1)S(1)}, u32[]{:S(2)}) copy-start(bf16[1,8,1,8,1,8,1,64]{7,5,3,1,6,4,2,0:T(8,128)(2,1)S(1)} %copy.354) | copy-start | bytes 196612
  36.3 6.3 %copy-start.45 = (bf16[1,8,1,8,1,8,1,64]{7,5,3,1,6,4,2,0:T(8,128)(2,1)}, bf16[1,8,1,8,1,8,1,64]{7,5,3,1,6,4,2,0:T(8,128)(2,1)S(1)}, u32[]{:S(2)}) copy-start(bf16[1,8,1,8,1,8,1,64]{7,5,3,1,6,4,2,0:T(8,128)(2,1)S(1)} %copy.373) | copy-start | bytes 196612
  36.5 5.5 %copy-start.1 = (bf16[1,8,1,8,1,8,1,64]{7,5,3,1,6,4,2,0:T(8,128)(2,1)}, bf16[1,8,1,8,1,8,1,64]{7,5,3,1,6,4,2,0:T(8,128)(2,1)S(1)}, u32[]{:S(2)}) copy-start(bf16[1,8,1,8,1,8,1,64]{7,5,3,1,6,4,2,0:T(8,128)(2,1)S(1)} %copy.369) | copy-start | bytes 196612
  36.5 5.3 %copy-start.3 = (bf16[1,8,1,8,1,8,1,64]{7,5,3,1,6,4,2,0:T(8,128)(2,1)}, bf16[1,8,1,8,1,8,1,64]{7,5,3,1,6,4,2,0:T(8,128)(2,1)S(1)}, u32[]{:S(2)}) copy-start(bf16[1,8,1,8,1,8,1,64]{7,5,3,1,6,4,2,0:T(8,128)(2,1)S(1)} %copy.368) | copy-start | bytes 196612
  36.5 5.1 %copy-start.5 = (bf16[1,8,1,8,1,8,1,64]{7,5,3,1,6,4,2,0:T(8,128)(2,1)}, bf16[1,8,1,8,1,8,1,64]{7,5,3,1,6,4,2,0:T(8,128)(2,1)S(1)}, u32[]{:S(2)}) copy-start(bf16[1,8,1,8,1,8,1,64]{7,5,3,1,6,4,2,0:T(8,128)(2,1)S(1)} %copy.367) | copy-start | bytes 196612
  36.6 4.9 %copy-start.7 = (bf16[1,8,1,8,1,8,1,64]{7,5,3,1,6,4,2,0:T(8,128)(2,1)}, bf16[1,8,1,8,1,8,1,64]{7,5,3,1,6,4,2,0:T(8,128)(2,1)S(1)}, u32[]{:S(2)}) copy-start(bf16[1,8,1,8,1,8,1,64]{7,5,3,1,6,4,2,0:T(8,128)(2,1)S(1)} %copy.366) | copy-start | bytes 196612
  36.6 4.6 %copy-start.11 = (bf16[1,8,1,8,1,8,1,64]{7,5,3,1,6,4,2,0:T(8,128)(2,1)}, bf16[1,8,1,8,1,8,1,64]{7,5,3,1,6,4,2,0:T(8,128)(2,1)S(1)}, u32[]{:S(2)}) copy-start(bf16[1,8,1,8,1,8,1,64]{7,5,3,1,6,4,2,0:T(8,128)(2,1)S(1)} %copy.365) | copy-start | bytes 196612
  36.6 4.4 %copy-start.15 = (bf16[1,8,1,8,1,8,1,64]{7,5,3,1,6,4,2,0:T(8,128)(2,1)}, bf16[1,8,1,8,1,8,1,64]{7,5,3,1,6,4,2,0:T(8,128)(2,1)S(1)}, u32[]{:S(2)}) copy-start(bf16[1,8,1,8,1,8,1,64]{7,5,3,1,6,4,2,0:T(8,128)(2,1)S(1)} %copy.364) | copy-start | bytes 196612
  36.7 4.2 %copy-start.19 = (bf16[1,8,1,8,1,8,1,64]{7,5,3,1,6,4,2,0:T(8,128)(2,1)}, bf16[1,8,1,8,1,8,1,64]{7,5,3,1,6,4,2,0:T(8,128)(2,1)S(1)}, u32[]{:S(2)}) copy-start(bf16[1,8,1,8,1,8,1,64]{7,5,3,1,6,4,2,0:T(8,128)(2,1)S(1)} %copy.363) | copy-start | bytes 196612
  36.7 4.0 %copy-start.23 = (bf16[1,8,1,8,1,8,1,64]{7,5,3,1,6,4,2,0:T(8,128)(2,1)}, bf16[1,8,1,8,1,8,1,64]{7,5,3,1,6,4,2,0:T(8,128)(2,1)S(1)}, u32[]{:S(2)}) copy-start(bf16[1,8,1,8,1,8,1,64]{7,5,3,1,6,4,2,0:T(8,128)(2,1)S(1)} %copy.362) | copy-start | bytes 196612
  36.8 3.8 %copy-start.27 = (bf16[1,8,1,8,1,8,1,64]{7,5,3,1,6,4,2,0:T(8,128)(2,1)}, bf16[1,8,1,8,1,8,1,64]{7,5,3,1,6,4,2,0:T(8,128)(2,1)S(1)}, u32[]{:S(2)}) copy-start(bf16[1,8,1,8,1,8,1,64]{7,5,3,1,6,4,2,0:T(8,128)(2,1)S(1)} %copy.361) | copy-start | bytes 196612
  36.8 3.5 %copy-start.31 = (bf16[1,8,1,8,1,8,1,64]{7,5,3,1,6,4,2,0:T(8,128)(2,1)}, bf16[1,8,1,8,1,8,1,64]{7,5,3,1,6,4,2,0:T(8,128)(2,1)S(1)}, u32[]{:S(2)}) copy-start(bf16[1,8,1,8,1,8,1,64]{7,5,3,1,6,4,2,0:T(8,128)(2,1)S(1)} %copy.360) | copy-start | bytes 196612
  36.9 3.3 %copy-start.35 = (bf16[1,8,1,8,1,8,1,64]{7,5,3,1,6,4,2,0:T(8,128)(2,1)}, bf16[1,8,1,8,1,8,1,64]{7,5,3,1,6,4,2,0:T(8,128)(2,1)S(1)}, u32[]{:S(2)}) copy-start(bf16[1,8,1,8,1,8,1,64]{7,5,3,1,6,4,2,0:T(8,128)(2,1)S(1)} %copy.359) | copy-start | bytes 196612
  51.5 18.0 %copy-start.48 = (bf16[1,8,1,4,1,4,1,128]{7,6,5,4,3,2,1,0:T(2,128)(2,1)}, bf16[1,8,1,4,1,4,1,128]{7,6,5,4,3,2,1,0:T(2,128)(2,1)S(1)}, u32[]{:S(2)}) copy-start(bf16[1,8,1,4,1,4,1,128]{7,6,5,4,3,2,1,0:T(2,128)(2,1)S(1)} %get-tuple-element.31) | copy-start | bytes 98308
  75.7 5.5 %copy-start.70 = (bf16[1,8,1,4,1,4,1,128]{7,5,3,1,6,4,2,0:T(4,128)(2,1)S(1)}, bf16[1,8,1,4,1,4,1,128]{7,5,3,1,6,4,2,0:T(4,128)(2,1)}, u32[]{:S(2)}) copy-start(bf16[1,8,1,4,1,4,1,128]{7,5,3,1,6,4,2,0:T(4,128)(2,1)} %copy.241) | copy-start | bytes 98308
  75.7 5.7 %copy-start.69 = (bf16[1,8,1,4,1,4,1,128]{7,5,3,1,6,4,2,0:T(4,128)(2,1)S(1)}, bf16[1,8,1,4,1,4,1,128]{7,5,3,1,6,4,2,0:T(4,128)(2,1)}, u32[]{:S(2)}) copy-start(bf16[1,8,1,4,1,4,1,128]{7,5,3,1,6,4,2,0:T(4,128)(2,1)} %copy.242) | copy-start | bytes 98308
  75.7 5.9 %copy-start.68 = (bf16[1,8,1,4,1,4,1,128]{7,5,3,1,6,4,2,0:T(4,128)(2,1)S(1)}, bf16[1,8,1,4,1,4,1,128]{7,5,3,1,6,4,2,0:T(4,128)(2,1)}, u32[]{:S(2)}) copy-start(bf16[1,8,1,4,1,4,1,128]{7,5,3,1,6,4,2,0:T(4,128)(2,1)} %copy.243) | copy-start | bytes 98308
  75.7 6.1 %copy-start.65 = (bf16[1,8,1,4,1,4,1,128]{7,5,3,1,6,4,2,0:T(4,128)(2,1)S(1)}, bf16[1,8,1,4,1,4,1,128]{7,5,3,1,6,4,2,0:T(4,128)(2,1)}, u32[]{:S(2)}) copy-start(bf16[1,8,1,4,1,4,1,128]{7,5,3,1,6,4,2,0:T(4,128)(2,1)} %copy.244) | copy-start | bytes 98308
  75.7 6.2 %copy-start.62 = (bf16[1,8,1,4,1,4,1,128]{7,5,3,1,6,4,2,0:T(4,128)(2,1)S(1)}, bf16[1,8,1,4,1,4,1,128]{7,5,3,1,6,4,2,0:T(4,128)(2,1)}, u32[]{:S(2)}) copy-start(bf16[1,8,1,4,1,4,1,128]{7,5,3,1,6,4,2,0:T(4,128)(2,1)} %copy.245) | copy-start | bytes 98308
  75.7 6.4 %copy-start.67 = (bf16[1,8,1,4,1,4,1,128]{7,5,3,1,6,4,2,0:T(4,128)(2,1)S(1)}, bf16[1,8,1,4,1,4,1,128]{7,5,3,1,6,4,2,0:T(4,128)(2,1)}, u32[]{:S(2)}) copy-start(bf16[1,8,1,4,1,4,1,128]{7,5,3,1,6,4,2,0:T(4,128)(2,1)} %copy.246) | copy-start | bytes 98308
  75.7 6.6 %copy-start.66 = (bf16[1,8,1,4,1,4,1,128]{7,5,3,1,6,4,2,0:T(4,128)(2,1)S(1)}, bf16[1,8,1,4,1,4,1,128]{7,5,3,1,6,4,2,0:T(4,128)(2,1)}, u32[]{:S(2)}) copy-start(bf16[1,8,1,4,1,4,1,128]{7,5,3,1,6,4,2,0:T(4,128)(2,1)} %copy.247) | copy-start | bytes 98308
  75.7 6.8 %copy-start.64 = (bf16[1,8,1,4,1,4,1,128]{7,5,3,1,6,4,2,0:T(4,128)(2,1)S(1)}, bf16[1,8,1,4,1,4,1,128]{7,5,3,1,6,4,2,0:T(4,128)(2,1)}, u32[]{:S(2)}) copy-start(bf16[1,8,1,4,1,4,1,128]{7,5,3,1,6,4,2,0:T(4,128)(2,1)} %copy.248) | copy-start | bytes 98308
  77.1 5.7 %copy-start.63 = (bf16[1,8,1,4,1,4,1,128]{7,5,3,1,6,4,2,0:T(4,128)(2,1)S(1)}, bf16[1,8,1,4,1,4,1,128]{7,5,3,1,6,4,2,0:T(4,128)(2,1)}, u32[]{:S(2)}) copy-start(bf16[1,8,1,4,1,4,1,128]{7,5,3,1,6,4,2,0:T(4,128)(2,1)} %copy.249) | copy-start | bytes 98308
  77.1 5.8 %copy-start.61 = (bf16[1,8,1,4,1,4,1,128]{7,5,3,1,6,4,2,0:T(4,128)(2,1)S(1)}, bf16[1,8,1,4,1,4,1,128]{7,5,3,1,6,4,2,0:T(4,128)(2,1)}, u32[]{:S(2)}) copy-start(bf16[1,8,1,4,1,4,1,128]{7,5,3,1,6,4,2,0:T(4,128)(2,1)} %copy.250) | copy-start | bytes 98308
  77.1 6.0 %copy-start.60 = (bf16[1,8,1,4,1,4,1,128]{7,5,3,1,6,4,2,0:T(4,128)(2,1)S(1)}, bf16[1,8,1,4,1,4,1,128]{7,5,3,1,6,4,2,0:T(4,128)(2,1)}, u32[]{:S(2)}) copy-start(bf16[1,8,1,4,1,4,1,128]{7,5,3,1,6,4,2,0:T(4,128)(2,1)} %copy.251) | copy-start | bytes 98308
  77.1 6.2 %copy-start.59 = (bf16[1,8,1,4,1,4,1,128]{7,5,3,1,6,4,2,0:T(4,128)(2,1)S(1)}, bf16[1,8,1,4,1,4,1,128]{7,5,3,1,6,4,2,0:T(4,128)(2,1)}, u32[]{:S(2)}) copy-start(bf16[1,8,1,4,1,4,1,128]{7,5,3,1,6,4,2,0:T(4,128)(2,1)} %copy.252) | copy-start | bytes 98308
  77.1 6.4 %copy-start.58 = (bf16[1,8,1,4,1,4,1,128]{7,5,3,1,6,4,2,0:T(4,128)(2,1)S(1)}, bf16[1,8,1,4,1,4,1,128]{7,5,3,1,6,4,2,0:T(4,128)(2,1)}, u32[]{:S(2)}) copy-start(bf16[1,8,1,4,1,4,1,128]{7,5,3,1,6,4,2,0:T(4,128)(2,1)} %copy.253) | copy-start | bytes 98308
  77.1 6.6 %copy-start.57 = (bf16[1,8,1,4,1,4,1,128]{7,5,3,1,6,4,2,0:T(4,128)(2,1)S(1)}, bf16[1,8,1,4,1,4,1,128]{7,5,3,1,6,4,2,0:T(4,128)(2,1)}, u32[]{:S(2)}) copy-start(bf16[1,8,1,4,1,4,1,128]{7,5,3,1,6,4,2,0:T(4,128)(2,1)} %copy.254) | copy-start | bytes 98308
  77.1 6.8 %copy-start.56 = (bf16[1,8,1,4,1,4,1,128]{7,5,3,1,6,4,2,0:T(4,128)(2,1)S(1)}, bf16[1,8,1,4,1,4,1,128]{7,5,3,1,6,4,2,0:T(4,128)(2,1)}, u32[]{:S(2)}) copy-start(bf16[1,8,1,4,1,4,1,128]{7,5,3,1,6,4,2,0:T(4,128)(2,1)} %copy.255) | copy-start | bytes 98308
  77.1 6.9 %copy-start.55 = (bf16[1,8,1,4,1,4,1,128]{7,5,3,1,6,4,2,0:T(4,128)(2,1)S(1)}, bf16[1,8,1,4,1,4,1,128]{7,5,3,1,6,4,2,0:T(4,128)(2,1)}, u32[]{:S(2)}) copy-start(bf16[1,8,1,4,1,4,1,128]{7,5,3,1,6,4,2,0:T(4,128)(2,1)} %copy.256) | copy-start | bytes 98308
  78.0 6.3 %copy-start.54 = (bf16[1,8,1,4,1,4,1,128]{7,5,3,1,6,4,2,0:T(4,128)(2,1)S(1)}, bf16[1,8,1,4,1,4,1,128]{7,5,3,1,6,4,2,0:T(4,128)(2,1)}, u32[]{:S(2)}) copy-start(bf16[1,8,1,4,1,4,1,128]{7,5,3,1,6,4,2,0:T(4,128)(2,1)} %copy.257) | copy-start | bytes 98308
  78.0 6.4 %copy-start.53 = (bf16[1,8,1,4,1,4,1,128]{7,5,3,1,6,4,2,0:T(4,128)(2,1)S(1)}, bf16[1,8,1,4,1,4,1,128]{7,5,3,1,6,4,2,0:T(4,128)(2,1)}, u32[]{:S(2)}) copy-start(bf16[1,8,1,4,1,4,1,128]{7,5,3,1,6,4,2,0:T(4,128)(2,1)} %copy.258) | copy-start | bytes 98308
  78.0 6.6 %copy-start.52 = (bf16[1,8,1,4,1,4,1,128]{7,5,3,1,6,4,2,0:T(4,128)(2,1)S(1)}, bf16[1,8,1,4,1,4,1,128]{7,5,3,1,6,4,2,0:T(4,128)(2,1)}, u32[]{:S(2)}) copy-start(bf16[1,8,1,4,1,4,1,128]{7,5,3,1,6,4,2,0:T(4,128)(2,1)} %copy.259) | copy-start | bytes 98308
  78.0 6.8 %copy-start.51 = (bf16[1,8,1,4,1,4,1,128]{7,5,3,1,6,4,2,0:T(4,128)(2,1)S(1)}, bf16[1,8,1,4,1,4,1,128]{7,5,3,1,6,4,2,0:T(4,128)(2,1)}, u32[]{:S(2)}) copy-start(bf16[1,8,1,4,1,4,1,128]{7,5,3,1,6,4,2,0:T(4,128)(2,1)} %copy.260) | copy-start | bytes 98308
  78.1 7.4 %copy-start.49 = (bf16[1,8,1,4,1,4,1,128]{7,6,5,4,3,2,1,0:T(2,128)(2,1)S(1)}, bf16[1,8,1,4,1,4,1,128]{7,6,5,4,3,2,1,0:T(2,128)(2,1)}, u32[]{:S(2)}) copy-start(bf16[1,8,1,4,1,4,1,128]{7,6,5,4,3,2,1,0:T(2,128)(2,1)} %copy-done.48) | copy-start | bytes 98308
  78.1 182.4 %all-reduce.32.cloned.1.call-start = ((), (), s32[]{:S(2)}) async-start(), calls=%async_computation.3 | async-start | bytes 8847360 | tf_op jit(solution)/shard_map/psum | solution.py:161
  87.9 6.4 %copy-start.50 = (f32[8,8,8,128]{3,2,1,0:T(8,128)S(1)}, f32[8,8,8,128]{3,2,1,0:T(8,128)}, u32[]{:S(2)}) copy-start(f32[8,8,8,128]{3,2,1,0:T(8,128)} %get-tuple-element.59) | copy-start | bytes 786436
  87.9 7.4 %copy-start.34 = (bf16[1,8,1,8,1,8,1,64]{7,5,3,1,6,4,2,0:T(8,128)(2,1)S(1)}, bf16[1,8,1,8,1,8,1,64]{7,5,3,1,6,4,2,0:T(8,128)(2,1)}, u32[]{:S(2)}) copy-start(bf16[1,8,1,8,1,8,1,64]{7,5,3,1,6,4,2,0:T(8,128)(2,1)} %copy-done.33) | copy-start | bytes 196612
  89.2 6.9 %copy-start.30 = (bf16[1,8,1,8,1,8,1,64]{7,5,3,1,6,4,2,0:T(8,128)(2,1)S(1)}, bf16[1,8,1,8,1,8,1,64]{7,5,3,1,6,4,2,0:T(8,128)(2,1)}, u32[]{:S(2)}) copy-start(bf16[1,8,1,8,1,8,1,64]{7,5,3,1,6,4,2,0:T(8,128)(2,1)} %copy-done.29) | copy-start | bytes 196612
  89.2 7.7 %copy-start.26 = (bf16[1,8,1,8,1,8,1,64]{7,5,3,1,6,4,2,0:T(8,128)(2,1)S(1)}, bf16[1,8,1,8,1,8,1,64]{7,5,3,1,6,4,2,0:T(8,128)(2,1)}, u32[]{:S(2)}) copy-start(bf16[1,8,1,8,1,8,1,64]{7,5,3,1,6,4,2,0:T(8,128)(2,1)} %copy-done.25) | copy-start | bytes 196612
  89.2 8.5 %copy-start.22 = (bf16[1,8,1,8,1,8,1,64]{7,5,3,1,6,4,2,0:T(8,128)(2,1)S(1)}, bf16[1,8,1,8,1,8,1,64]{7,5,3,1,6,4,2,0:T(8,128)(2,1)}, u32[]{:S(2)}) copy-start(bf16[1,8,1,8,1,8,1,64]{7,5,3,1,6,4,2,0:T(8,128)(2,1)} %copy-done.21) | copy-start | bytes 196612
  89.2 9.3 %copy-start.18 = (bf16[1,8,1,8,1,8,1,64]{7,5,3,1,6,4,2,0:T(8,128)(2,1)S(1)}, bf16[1,8,1,8,1,8,1,64]{7,5,3,1,6,4,2,0:T(8,128)(2,1)}, u32[]{:S(2)}) copy-start(bf16[1,8,1,8,1,8,1,64]{7,5,3,1,6,4,2,0:T(8,128)(2,1)} %copy-done.17) | copy-start | bytes 196612
  89.2 10.2 %copy-start.14 = (bf16[1,8,1,8,1,8,1,64]{7,5,3,1,6,4,2,0:T(8,128)(2,1)S(1)}, bf16[1,8,1,8,1,8,1,64]{7,5,3,1,6,4,2,0:T(8,128)(2,1)}, u32[]{:S(2)}) copy-start(bf16[1,8,1,8,1,8,1,64]{7,5,3,1,6,4,2,0:T(8,128)(2,1)} %copy-done.13) | copy-start | bytes 196612
  89.2 11.0 %copy-start.10 = (bf16[1,8,1,8,1,8,1,64]{7,5,3,1,6,4,2,0:T(8,128)(2,1)S(1)}, bf16[1,8,1,8,1,8,1,64]{7,5,3,1,6,4,2,0:T(8,128)(2,1)}, u32[]{:S(2)}) copy-start(bf16[1,8,1,8,1,8,1,64]{7,5,3,1,6,4,2,0:T(8,128)(2,1)} %copy-done.9) | copy-start | bytes 196612
  93.2 7.8 %copy-start.44 = (bf16[1,8,1,8,1,8,1,64]{7,5,3,1,6,4,2,0:T(8,128)(2,1)S(1)}, bf16[1,8,1,8,1,8,1,64]{7,5,3,1,6,4,2,0:T(8,128)(2,1)}, u32[]{:S(2)}) copy-start(bf16[1,8,1,8,1,8,1,64]{7,5,3,1,6,4,2,0:T(8,128)(2,1)} %copy-done.43) | copy-start | bytes 196612
  94.2 7.6 %copy-start.42 = (bf16[1,8,1,8,1,8,1,64]{7,5,3,1,6,4,2,0:T(8,128)(2,1)S(1)}, bf16[1,8,1,8,1,8,1,64]{7,5,3,1,6,4,2,0:T(8,128)(2,1)}, u32[]{:S(2)}) copy-start(bf16[1,8,1,8,1,8,1,64]{7,5,3,1,6,4,2,0:T(8,128)(2,1)} %copy-done.41) | copy-start | bytes 196612
  94.2 8.4 %copy-start.40 = (bf16[1,8,1,8,1,8,1,64]{7,5,3,1,6,4,2,0:T(8,128)(2,1)S(1)}, bf16[1,8,1,8,1,8,1,64]{7,5,3,1,6,4,2,0:T(8,128)(2,1)}, u32[]{:S(2)}) copy-start(bf16[1,8,1,8,1,8,1,64]{7,5,3,1,6,4,2,0:T(8,128)(2,1)} %copy-done.39) | copy-start | bytes 196612
  94.3 9.2 %copy-start.38 = (bf16[1,8,1,8,1,8,1,64]{7,5,3,1,6,4,2,0:T(8,128)(2,1)S(1)}, bf16[1,8,1,8,1,8,1,64]{7,5,3,1,6,4,2,0:T(8,128)(2,1)}, u32[]{:S(2)}) copy-start(bf16[1,8,1,8,1,8,1,64]{7,5,3,1,6,4,2,0:T(8,128)(2,1)} %copy-done.37) | copy-start | bytes 196612
  94.4 9.9 %copy-start.36 = (bf16[1,8,1,8,1,8,1,64]{7,5,3,1,6,4,2,0:T(8,128)(2,1)S(1)}, bf16[1,8,1,8,1,8,1,64]{7,5,3,1,6,4,2,0:T(8,128)(2,1)}, u32[]{:S(2)}) copy-start(bf16[1,8,1,8,1,8,1,64]{7,5,3,1,6,4,2,0:T(8,128)(2,1)} %copy-done.35) | copy-start | bytes 196612
  95.2 9.9 %copy-start.32 = (bf16[1,8,1,8,1,8,1,64]{7,5,3,1,6,4,2,0:T(8,128)(2,1)S(1)}, bf16[1,8,1,8,1,8,1,64]{7,5,3,1,6,4,2,0:T(8,128)(2,1)}, u32[]{:S(2)}) copy-start(bf16[1,8,1,8,1,8,1,64]{7,5,3,1,6,4,2,0:T(8,128)(2,1)} %copy-done.31) | copy-start | bytes 196612
  96.1 9.9 %copy-start.28 = (bf16[1,8,1,8,1,8,1,64]{7,5,3,1,6,4,2,0:T(8,128)(2,1)S(1)}, bf16[1,8,1,8,1,8,1,64]{7,5,3,1,6,4,2,0:T(8,128)(2,1)}, u32[]{:S(2)}) copy-start(bf16[1,8,1,8,1,8,1,64]{7,5,3,1,6,4,2,0:T(8,128)(2,1)} %copy-done.27) | copy-start | bytes 196612
  96.9 9.9 %copy-start.24 = (bf16[1,8,1,8,1,8,1,64]{7,5,3,1,6,4,2,0:T(8,128)(2,1)S(1)}, bf16[1,8,1,8,1,8,1,64]{7,5,3,1,6,4,2,0:T(8,128)(2,1)}, u32[]{:S(2)}) copy-start(bf16[1,8,1,8,1,8,1,64]{7,5,3,1,6,4,2,0:T(8,128)(2,1)} %copy-done.23) | copy-start | bytes 196612
  97.7 9.9 %copy-start.20 = (bf16[1,8,1,8,1,8,1,64]{7,5,3,1,6,4,2,0:T(8,128)(2,1)S(1)}, bf16[1,8,1,8,1,8,1,64]{7,5,3,1,6,4,2,0:T(8,128)(2,1)}, u32[]{:S(2)}) copy-start(bf16[1,8,1,8,1,8,1,64]{7,5,3,1,6,4,2,0:T(8,128)(2,1)} %copy-done.19) | copy-start | bytes 196612
  98.5 9.9 %copy-start.16 = (bf16[1,8,1,8,1,8,1,64]{7,5,3,1,6,4,2,0:T(8,128)(2,1)S(1)}, bf16[1,8,1,8,1,8,1,64]{7,5,3,1,6,4,2,0:T(8,128)(2,1)}, u32[]{:S(2)}) copy-start(bf16[1,8,1,8,1,8,1,64]{7,5,3,1,6,4,2,0:T(8,128)(2,1)} %copy-done.15) | copy-start | bytes 196612
  99.4 9.9 %copy-start.12 = (bf16[1,8,1,8,1,8,1,64]{7,5,3,1,6,4,2,0:T(8,128)(2,1)S(1)}, bf16[1,8,1,8,1,8,1,64]{7,5,3,1,6,4,2,0:T(8,128)(2,1)}, u32[]{:S(2)}) copy-start(bf16[1,8,1,8,1,8,1,64]{7,5,3,1,6,4,2,0:T(8,128)(2,1)} %copy-done.11) | copy-start | bytes 196612
  100.2 9.9 %copy-start.8 = (bf16[1,8,1,8,1,8,1,64]{7,5,3,1,6,4,2,0:T(8,128)(2,1)S(1)}, bf16[1,8,1,8,1,8,1,64]{7,5,3,1,6,4,2,0:T(8,128)(2,1)}, u32[]{:S(2)}) copy-start(bf16[1,8,1,8,1,8,1,64]{7,5,3,1,6,4,2,0:T(8,128)(2,1)} %copy-done.7) | copy-start | bytes 196612
  101.0 9.9 %copy-start.6 = (bf16[1,8,1,8,1,8,1,64]{7,5,3,1,6,4,2,0:T(8,128)(2,1)S(1)}, bf16[1,8,1,8,1,8,1,64]{7,5,3,1,6,4,2,0:T(8,128)(2,1)}, u32[]{:S(2)}) copy-start(bf16[1,8,1,8,1,8,1,64]{7,5,3,1,6,4,2,0:T(8,128)(2,1)} %copy-done.5) | copy-start | bytes 196612
  101.9 9.9 %copy-start.4 = (bf16[1,8,1,8,1,8,1,64]{7,5,3,1,6,4,2,0:T(8,128)(2,1)S(1)}, bf16[1,8,1,8,1,8,1,64]{7,5,3,1,6,4,2,0:T(8,128)(2,1)}, u32[]{:S(2)}) copy-start(bf16[1,8,1,8,1,8,1,64]{7,5,3,1,6,4,2,0:T(8,128)(2,1)} %copy-done.3) | copy-start | bytes 196612
  102.7 9.9 %copy-start.2 = (bf16[1,8,1,8,1,8,1,64]{7,5,3,1,6,4,2,0:T(8,128)(2,1)S(1)}, bf16[1,8,1,8,1,8,1,64]{7,5,3,1,6,4,2,0:T(8,128)(2,1)}, u32[]{:S(2)}) copy-start(bf16[1,8,1,8,1,8,1,64]{7,5,3,1,6,4,2,0:T(8,128)(2,1)} %copy-done.1) | copy-start | bytes 196612
  106.0 9.9 %copy-start.46 = (bf16[1,8,1,8,1,8,1,64]{7,5,3,1,6,4,2,0:T(8,128)(2,1)S(1)}, bf16[1,8,1,8,1,8,1,64]{7,5,3,1,6,4,2,0:T(8,128)(2,1)}, u32[]{:S(2)}) copy-start(bf16[1,8,1,8,1,8,1,64]{7,5,3,1,6,4,2,0:T(8,128)(2,1)} %copy-done.45) | copy-start | bytes 196612
  (12 other events, 28.8 us)
Sparse Core Ops, SparseCore 0:
  78.2 14.9 reduce-scatter.1
  116.8 143.5 all-reduce.31
where the time goes:
time: 274 us; the launch traced here: 273 us
  waiting for transfers between devices  150 us (55%)
  local copies, waits for them, and re-layouts  49.1 us (18%)
  matrix products  42.7 us (16%)
  between operations  15.6 us (6%)
  starting transfers between devices  8.39 us (3%)
  blocking collectives  5.83 us (2%)
    psum x1, waiting for transfers between devices, body(): lax.psum((local_first, grad_second), ('sample', 'spatial'))  144 us
    dot_general x54, matrix products, weight_grads(): jnp.dot(flat_in.T, flat_grad, preferred_element_type=jnp.float32)  29.4 us
    slice x31, local copies, waits for them, and re-layouts, tap_slices(): halves[:, offset_z // 2:offset_z // 2 + out_z, offset_z % 2, offset_y //...  23.6 us
    dot_general x54, matrix products, conv_taps(): jnp.dot(sliced, stacked[tap_index], preferred_element_type=jnp.float32)  9.14 us
    unnamed x175, local copies, waits for them, and re-layouts  8.06 us
    all_gather x1, blocking collectives, body(): whole_flat = lax.all_gather(hidden_flat, 'spatial', axis=1, tiled=True)  5.83 us
  transfers between devices with their start and end apart: 4, of which 3 were waited for; matrix products, arithmetic and copies ran while one was open for 5% of the time, Pallas kernels for 0%

commit v1 on v0

v1 whole, which is shorter than its diff:
```python
import functools

import jax
import jax.numpy as jnp
from jax import lax
from jax.experimental import pallas as pl
from jax.experimental.pallas import tpu as pltpu
from jax.sharding import PartitionSpec as P

BOTH = ("sample", "spatial")
LANES = 128
VMEM_BYTES = 48 * 1024 * 1024
f32, bf16 = jnp.float32, jnp.bfloat16


def full(shape):
    return pl.BlockSpec(memory_space=pltpu.VMEM)


def params():
    return pltpu.CompilerParams(vmem_limit_bytes=VMEM_BYTES)


def call(kernel, outs, *args, scratch=(), cost=None):
    shapes = [jax.ShapeDtypeStruct(s, d) for s, d in outs]
    return pl.pallas_call(
        kernel,
        out_shape=shapes,
        in_specs=[full(a.shape) for a in args],
        out_specs=[full(s.shape) for s in shapes],
        scratch_shapes=scratch,
        compiler_params=params(),
        cost_estimate=cost,
    )(*args)


def flat_index(spatial_count):
    return lax.axis_index("sample") * spatial_count + lax.axis_index("spatial")


def bit_of(value, bit):
    return lax.rem(lax.div(value, jnp.int32(1 << bit)), jnp.int32(2))


def sigmoid(value):
    return 1.0 / (1.0 + jnp.exp(-value))


def slope_of(value, sig):
    return sig * (1.0 + value * (1.0 - sig))


def dot(a, b, dims=((1,), (0,))):
    return lax.dot_general(a, b, (dims, ((), ())), preferred_element_type=f32)


def selection():
    row = lax.broadcasted_iota(jnp.int32, (144, 64), 0)
    col = lax.broadcasted_iota(jnp.int32, (144, 64), 1)
    pair, cell = lax.div(row, 16), lax.rem(row, 16)
    b, c = lax.div(pair, 3), lax.rem(pair, 3)
    k, j = lax.div(cell, 4), lax.rem(cell, 4)
    x, y = lax.div(col, 8), lax.rem(col, 8)
    hit = (x == 2 * k + c - 1) & (y == 2 * j + b - 1)
    return hit.astype(f32).astype(bf16)


def main_kernel(
    core_bit, spatial_count, halo, vol, w1, w2, cot, keep, send, vpad, x1, w1p, x2, g1
):
    planes = vol.shape[0] + 3
    hidden_planes = (planes - 1) // 2
    out_planes = (hidden_planes - 1) // 2
    core = bit_of(flat_index(spatial_count), core_bit)
    vpad[:, :, 0:8, :] = jnp.zeros((planes, 8, 8, LANES), f32)
    for e in range(planes):
        plane = halo[e] if e < 3 else vol[e - 3]
        for kt in range(8):
            vpad[e, kt, 8:24, :] = plane[:, kt * LANES : (kt + 1) * LANES].astype(f32)
    for ab in range(9):
        w1p[ab * 256 : ab * 256 + 64, :] = jnp.zeros((64, 128), bf16)
        w1p[ab * 256 + 64 : (ab + 1) * 256, :] = w1[ab * 192 : (ab + 1) * 192, :]
    for e in range(planes):
        for b in range(3):
            tiles = [jnp.zeros((8, LANES), f32)]
            for kt in range(8):
                tiles.append(vpad[e, kt, pl.ds(7 + b, 8, stride=2), :])
            for kk in range(4):
                left = jnp.concatenate([tiles[2 * kk], tiles[2 * kk + 1]], 0).astype(bf16)
                right = jnp.concatenate([tiles[2 * kk + 1], tiles[2 * kk + 2]], 0).astype(bf16)
                for a in range(e % 2, 3, 2):
                    h = (e - a) // 2
                    if 0 <= h < hidden_planes:
                        rows = slice(h * 64 + kk * 16, h * 64 + kk * 16 + 16)
                        col = (a * 3 + b) * 256
                        x1[rows, col : col + LANES] = left
                        x1[rows, col + LANES : col + 2 * LANES] = right
    first_pre = dot(x1[...], w1p[...])
    sig = sigmoid(first_pre)
    hidden = (first_pre * sig).astype(bf16)
    slope1 = slope_of(first_pre, sig)
    select = selection()
    for h in range(hidden_planes):
        picked = dot(select, hidden[h * 64 : (h + 1) * 64]).astype(bf16)
        for a in range(h % 2, 3, 2):
            o = (h - a) // 2
            if 0 <= o < out_planes:
                for pair in range(9):
                    tap = a * 9 + pair
                    x2[o * 16 : (o + 1) * 16, tap * LANES : (tap + 1) * LANES] = picked[
                        pair * 16 : (pair + 1) * 16
                    ]
    second_pre = dot(x2[...], w2[...])
    sig2 = sigmoid(second_pre)
    delta2 = cot[...].astype(f32) * slope_of(second_pre, sig2)
    d2 = delta2.astype(bf16)
    lo, hi = delta2[:, :LANES], delta2[:, LANES:]
    own_first = jnp.concatenate(
        [jnp.where(core == 0, lo, hi), jnp.where(core == 0, hi, lo)], 1
    ).astype(bf16)
    taps = 9 * LANES
    for a in range(3):
        grad = dot(x2[:, a * taps : (a + 1) * taps], own_first, ((0,), (0,)))
        keep[a, 0:taps, :] = grad[:, :LANES]
        send[a, 0:taps, :] = grad[:, LANES:].astype(bf16)
    spread = dot(d2, w2[...], ((1,), (1,)))
    coarse = spread.astype(bf16)
    fine = (spread - coarse.astype(f32)).astype(bf16)
    deltas = []
    for h in range(hidden_planes):
        total = None
        for a in range(h % 2, 3, 2):
            o = (h - a) // 2
            if 0 <= o < out_planes:
                for piece in (coarse, fine):
                    stack = jnp.concatenate(
                        [
                            piece[o * 16 : (o + 1) * 16, tap * LANES : (tap + 1) * LANES]
                            for tap in range(a * 9, a * 9 + 9)
                        ],
                        0,
                    )
                    part = dot(select, stack, ((0,), (0,)))
                    total = part if total is None else total + part
        rounded = total.astype(bf16).astype(f32)
        deltas.append((rounded * slope1[h * 64 : (h + 1) * 64]).astype(bf16))
    d1 = jnp.concatenate(deltas, 0)
    half = 288
    for a in range(3):
        grad = dot(x1[:, a * 768 : (a + 1) * 768], d1, ((0,), (0,)))
        for b in range(3):
            g1[b * 192 : (b + 1) * 192, :] = grad[b * 256 + 64 : (b + 1) * 256]
        keep[a, taps : taps + half, :] = g1[pl.ds(core * half, half), :]
        send[a, taps : taps + half, :] = g1[pl.ds((1 - core) * half, half), :].astype(bf16)
        rest = keep.shape[1] - taps - half
        keep[a, taps + half :, :] = jnp.zeros((rest, LANES), f32)
        send[a, taps + half :, :] = jnp.zeros((rest, LANES), bf16)


def reduce_kernel(orders, step, spatial_count, merged_in, merged_out, keep, *refs):
    lanes = len(orders)
    recv = refs[:1] if merged_in else refs[:lanes]
    outs = refs[len(recv) :]
    half = keep.shape[1] // 2
    flat = flat_index(spatial_count)
    for t in range(lanes):
        bit = bit_of(flat, orders[t][step])
        mine, other = pl.ds(bit * half, half), pl.ds((1 - bit) * half, half)
        if merged_in:
            got_mine, got_other = recv[0][t, mine, :], recv[0][t, other, :]
        else:
            got_mine, got_other = recv[t][mine, :], recv[t][other, :]
        outs[0][t] = keep[t, mine, :] + got_mine.astype(f32)
        gone = (keep[t, other, :] + got_other.astype(f32)).astype(bf16)
        if merged_out:
            outs[1][t] = gone
        else:
            outs[1 + t][...] = gone


def last_sum_kernel(merged_in, keep, *refs):
    out = refs[-1]
    for t in range(keep.shape[0]):
        got = refs[0][t] if merged_in else refs[t][...]
        out[t] = (keep[t] + got.astype(f32)).astype(bf16)


def final_kernel(core_bit, orders, chunk, spatial_count, *refs):
    lanes = len(orders)
    own, got, (grad_first, grad_second) = refs[:lanes], refs[lanes : 2 * lanes], refs[2 * lanes :]
    flat = flat_index(spatial_count)
    core = bit_of(flat, core_bit)
    taps, half = 9 * LANES, 288
    for t in range(lanes):
        steps = len(orders[t])
        bits = [bit_of(flat, orders[t][s]) for s in range(steps)]
        for place in range((taps + half) // chunk):
            position = jnp.int32(0)
            for s in range(steps):
                want = (place >> (steps - 1 - s)) & 1
                differs = (1 - bits[s]) if want else bits[s]
                position = position + differs * (1 << (steps - 1 - s))
            rows = pl.ds(position * chunk, chunk)
            a_half, b_half = own[t][rows, :].astype(f32), got[t][rows, :].astype(f32)
            low = jnp.where(core == 0, a_half, b_half)
            high = jnp.where(core == 0, b_half, a_half)
            at = place * chunk
            if at < taps:
                grad_second[t * taps + at : t * taps + at + chunk, :LANES] = low
                grad_second[t * taps + at : t * taps + at + chunk, LANES:] = high
            else:
                at = t * 2 * half + at - taps
                grad_first[at : at + chunk, :] = low
                grad_first[at + half : at + half + chunk, :] = high


def body(spatial_count, sample_count, volume, w_first, w_second, cotangent):
    count = spatial_count * sample_count
    bits = count.bit_length() - 1
    core_bit = spatial_count.bit_length() - 1
    others = [bit for bit in range(bits) if bit != core_bit]
    turn, rest = others[:3], others[3:]
    orders = [tuple(turn[t:] + turn[:t] + rest) for t in range(3)]
    steps = len(others)
    same = [len({order[s] for order in orders}) == 1 for s in range(steps)]
    chunk = -(-1440 // (16 << steps)) * 16
    rows = chunk << steps

    def swap(array, bit):
        return lax.ppermute(array, BOTH, [(i, i ^ (1 << bit)) for i in range(count)])

    slab = volume[0]
    planes = slab.shape[0] + 3
    hidden_planes = (planes - 1) // 2
    out_planes = (hidden_planes - 1) // 2
    halo = lax.ppermute(slab[-3:], "spatial", [(i, i + 1) for i in range(spatial_count - 1)])
    cot = cotangent[0].reshape(out_planes, 4, 4, 256).transpose(0, 2, 1, 3)
    cot = cot.reshape(out_planes * 16, 256)
    keep, send = call(
        functools.partial(main_kernel, core_bit, spatial_count),
        [((3, rows, LANES), f32), ((3, rows, LANES), bf16)],
        halo,
        slab,
        w_first,
        w_second,
        cot,
        scratch=[
            pltpu.VMEM((planes, 8, 24, LANES), f32),
            pltpu.VMEM((hidden_planes * 64, 9 * 256), bf16),
            pltpu.VMEM((9 * 256, 128), bf16),
            pltpu.VMEM((out_planes * 16, 27 * LANES), bf16),
            pltpu.VMEM((576, LANES), f32),
        ],
    )
    recv = [swap(send, core_bit)]
    merged = True
    for step in range(steps):
        half = keep.shape[1] // 2
        outs = [((3, half, LANES), f32)]
        outs += [((3, half, LANES), bf16)] if same[step] else [((half, LANES), bf16)] * 3
        keep, *send = call(
            functools.partial(reduce_kernel, orders, step, spatial_count, merged, same[step]),
            outs,
            keep,
            *recv,
        )
        merged = same[step]
        if merged:
            recv = [swap(send[0], orders[0][step])]
        else:
            recv = [swap(send[t], orders[t][step]) for t in range(3)]
    own = call(
        functools.partial(last_sum_kernel, merged), [((3, chunk, LANES), bf16)], keep, *recv
    )[0]
    for step in reversed(range(steps)):
        if same[step]:
            got = swap(own, orders[0][step])
            own = jnp.concatenate([own, got], 1)
        else:
            got = [swap(own[t], orders[t][step]) for t in range(3)]
            own = [jnp.concatenate([own[t], got[t]], 0) for t in range(3)]
    got = [swap(own[t], core_bit) for t in range(3)]
    return call(
        functools.partial(final_kernel, core_bit, orders, chunk, spatial_count),
        [((1728, 128), f32), ((3456, 256), f32)],
        *[own[t] for t in range(3)],
        *got,
    )


def solution(mesh):
    sizes = dict(mesh.shape)

    def run(*args):
        return tuple(body(sizes["spatial"], sizes["sample"], *args))

    return jax.shard_map(
        run,
        mesh=mesh,
        in_specs=(P("sample", "spatial", None, None), P(), P(), P("sample", "spatial", None, None)),
        out_specs=(P(), P()),
        check_vma=False,
    )
```

time: 274 us -> 82.6 us (0.30)
  waiting for transfers between devices: 150 us -> 29.7 us
  matrix products: 42.7 us -> 0 us
  local copies, waits for them, and re-layouts: 49.1 us -> 6.87 us
  starting transfers between devices: 8.39 us -> 35.5 us
  between operations: 15.6 us -> 0.77 us
  Pallas kernels: 0 us -> 9.24 us
  blocking collectives: 5.83 us -> 0 us
    psum x1 -> x0, waiting for transfers between devices: 144 us -> none  [body(): lax.psum((local_first, grad_second), ('sample', 'spatial'))]
    dot_general x135 -> x0, matrix products: 42.7 us -> none  [the longest x54 29.4 us: weight_grads(): jnp.dot(flat_in.T, flat_grad, preferred_element_type=jnp.float32)]
    ppermute x1 -> x25, starting transfers between devices: 4.83 us -> 35.5 us  [the longest x24 30.6 us: swap(): return lax.ppermute(array, BOTH, [(i, i ^ 1 << bit) for i in range(count)])]
    ppermute x1 -> x25, waiting for transfers between devices: 0.01 us -> 29.7 us  [the longest x24 28.3 us: swap(): return lax.ppermute(array, BOTH, [(i, i ^ 1 << bit) for i in range(count)])]
    slice x32 -> x1, local copies, waits for them, and re-layouts: 25 us -> 0.9 us  [body(): slab[-3:]]
    pallas_call x0 -> x7, Pallas kernels: none -> 9.24 us  [call(): pl.pallas_call(kernel, out_shape=shapes, in_specs=[full(a.shape) for a in...]
    reshape x9 -> x1, local copies, waits for them, and re-layouts: 8.13 us -> 0.77 us  [body(): cot = cot.reshape(out_planes * 16, 256)]
    all_gather x1 -> x0, blocking collectives: 5.83 us -> none  [body(): whole_flat = lax.all_gather(hidden_flat, 'spatial', axis=1, tiled=True)]
  transfers between devices with their start and end apart: 4 -> 25, of which waited for: 3 -> 19; matrix products, arithmetic and copies ran while one was open for 5% -> 1% of each run, Pallas kernels for 0% -> 0%
where the time goes in v1:
time: 82.6 us; the launch traced here: 82.2 us
  starting transfers between devices  35.5 us (43%)
  waiting for transfers between devices  29.7 us (36%)
  Pallas kernels  9.24 us (11%)
  local copies, waits for them, and re-layouts  6.87 us (8%)
    ppermute x24, starting transfers between devices, swap(): return lax.ppermute(array, BOTH, [(i, i ^ 1 << bit) for i in range(count)])  30.6 us
    ppermute x24, waiting for transfers between devices, swap(): return lax.ppermute(array, BOTH, [(i, i ^ 1 << bit) for i in range(count)])  28.3 us
    pallas_call x7, Pallas kernels, call(): pl.pallas_call(kernel, out_shape=shapes, in_specs=[full(a.shape) for a in...  9.24 us
    unnamed x8, local copies, waits for them, and re-layouts  5.19 us
    ppermute x1, starting transfers between devices, body(): lax.ppermute(slab[-3:], 'spatial', [(i, i + 1) for i in range(spatial_cou...  4.84 us
  transfers between devices with their start and end apart: 25, of which 19 were waited for; matrix products, arithmetic and copies ran while one was open for 1% of the time, Pallas kernels for 0%

profile of v1, /device:TPU:0, one launch (start us, length us, event | category | flops | bytes accessed | tf_op | source)
XLA Modules:
  0.0 82.2 jit_solution(18114438289835388190)
XLA Ops:
  0.6 0.9 %slice_bitcast_fusion = bf16[3,16,1024]{2,1,0:T(8,128)(2,1)S(1)} fusion(bf16[1,16,16,1024]{3,2,1,0:T(8,128)(2,1)} %param.4), kind=kLoop, calls=%fused_computation.13 | loop fusion | bytes 196608 | tf_op jit(solution)/shard_map/slice | solution.py:236
  1.5 4.8 %collective-permute-start = (bf16[3,16,1024]{2,1,0:T(8,128)(2,1)S(1)}, bf16[3,16,1024]{2,1,0:T(8,128)(2,1)S(1)}, u32[]{:S(2)}, u32[]{:S(2)}) collective-permute-start(bf16[3,16,1024]{2,1,0:T(8,128)(2,1)S(1)} %slice_bitcast_fusion), channel_id=1, source_target_pairs={{0,1},{2,3},{4,5},{6,7},{8,9},{10,11},{12,13},{14,15},{16,17},{18,... | collective-permute-start | bytes 294920 | tf_op jit(solution)/shard_map/ppermute | solution.py:236
  6.4 0.8 reshape.8.cot
  7.2 1.4 %collective-permute-done.halo = bf16[3,16,1024]{2,1,0:T(8,128)(2,1)S(1)} collective-permute-done((bf16[3,16,1024]{2,1,0:T(8,128)(2,1)S(1)}, bf16[3,16,1024]{2,1,0:T(8,128)(2,1)S(1)}, u32[]{:S(2)}, u32[]{:S(2)}) %collective-permute-start) | collective-permute-done | bytes 98336 | tf_op jit(solution)/shard_map/ppermute | solution.py:236
  8.6 0.0 copy-start.1
  8.6 1.5 %copy-done.1 = bf16[3456,256]{1,0:T(8,128)(2,1)S(1)} copy-done((bf16[3456,256]{1,0:T(8,128)(2,1)S(1)}, bf16[3456,256]{1,0:T(8,128)(2,1)}, u32[]{:S(2)}) %copy-start.1) | copy-done | bytes 1769496
  10.0 0.0 copy-start.2
  10.0 1.0 %copy-done.2 = bf16[1,16,16,1024]{3,2,1,0:T(8,128)(2,1)S(1)} copy-done((bf16[1,16,16,1024]{3,2,1,0:T(8,128)(2,1)S(1)}, bf16[1,16,16,1024]{3,2,1,0:T(8,128)(2,1)}, u32[]{:S(2)}) %copy-start.2) | copy-done | bytes 524312
  11.1 0.0 copy-start.3
  11.1 1.0 %copy-done.3 = bf16[1728,128]{1,0:T(8,128)(2,1)S(1)} copy-done((bf16[1728,128]{1,0:T(8,128)(2,1)S(1)}, bf16[1728,128]{1,0:T(8,128)(2,1)}, u32[]{:S(2)}) %copy-start.3) | copy-done | bytes 442392
  12.1 6.5 %shard_map.59 = (f32[3,1536,128]{2,1,0:T(8,128)}, bf16[3,1536,128]{2,1,0:T(8,128)(2,1)S(1)}) custom-call(bf16[3,16,1024]{2,1,0:T(8,128)(2,1)S(1)} %collective-permute-done.halo, bf16[16,16,1024]{2,1,0:T(8,128)(2,1)S(1)} %bitcast.12, bf16[1728,128]{1,0:T(8,128)(2,1)S(1)} %copy-done.3, bf16[3456,256]{1,0:T(8,128)(2,1)S(1)} %copy-done.1, ...), custom_call_target="tpu_custom_call" | custom-call | tf_op jit(solution)/shard_map/pallas_call | solution.py:26
  18.6 0.0 collective-permute-start.1
  18.6 2.8 %collective-permute-done.1.refs_0_ = bf16[3,1536,128]{2,1,0:T(8,128)(2,1)S(1)} collective-permute-done((bf16[3,1536,128]{2,1,0:T(8,128)(2,1)S(1)}, bf16[3,1536,128]{2,1,0:T(8,128)(2,1)S(1)}, u32[]{:S(2)}, u32[]{:S(2)}) %collective-permute-start.1) | collective-permute-done | bytes 1179680 | tf_op jit(solution)/shard_map/ppermute | solution.py:230
  21.5 0.0 copy-start
  21.5 1.7 %copy-done = f32[3,1536,128]{2,1,0:T(8,128)S(1)} copy-done((f32[3,1536,128]{2,1,0:T(8,128)S(1)}, f32[3,1536,128]{2,1,0:T(8,128)}, u32[]{:S(2)}) %copy-start) | copy-done | bytes 2359320
  23.1 0.2 shard_map.60
  23.3 2.5 %collective-permute-start.2 = (bf16[768,128]{1,0:T(8,128)(2,1)S(1)}, bf16[768,128]{1,0:T(8,128)(2,1)S(1)}, u32[]{:S(2)}, u32[]{:S(2)}) collective-permute-start(bf16[768,128]{1,0:T(8,128)(2,1)S(1)} %get-tuple-element.21), channel_id=1, source_target_pairs={{0,1},{1,0},{2,3},{3,2},{4,5},{5,4},{6,7},{7,6},{8,9},{9,8},{10,11... | collective-permute-start | bytes 589832 | tf_op jit(solution)/shard_map/ppermute | solution.py:230
  25.8 1.5 %collective-permute-start.3 = (bf16[768,128]{1,0:T(8,128)(2,1)S(1)}, bf16[768,128]{1,0:T(8,128)(2,1)S(1)}, u32[]{:S(2)}, u32[]{:S(2)}) collective-permute-start(bf16[768,128]{1,0:T(8,128)(2,1)S(1)} %get-tuple-element.22), channel_id=1, source_target_pairs={{0,4},{1,5},{2,6},{3,7},{4,0},{5,1},{6,2},{7,3},{8,12},{9,13},{10,... | collective-permute-start | bytes 589832 | tf_op jit(solution)/shard_map/ppermute | solution.py:230
  27.3 1.6 %collective-permute-start.4 = (bf16[768,128]{1,0:T(8,128)(2,1)S(1)}, bf16[768,128]{1,0:T(8,128)(2,1)S(1)}, u32[]{:S(2)}, u32[]{:S(2)}) collective-permute-start(bf16[768,128]{1,0:T(8,128)(2,1)S(1)} %get-tuple-element.23), channel_id=1, source_target_pairs={{0,8},{1,9},{2,10},{3,11},{4,12},{5,13},{6,14},{7,15},{8,0},{9,1},... | collective-permute-start | bytes 589832 | tf_op jit(solution)/shard_map/ppermute | solution.py:230
  28.9 2.1 %collective-permute-done.2.refs_0_ = bf16[768,128]{1,0:T(8,128)(2,1)S(1)} collective-permute-done((bf16[768,128]{1,0:T(8,128)(2,1)S(1)}, bf16[768,128]{1,0:T(8,128)(2,1)S(1)}, u32[]{:S(2)}, u32[]{:S(2)}) %collective-permute-start.2) | collective-permute-done | bytes 196640 | tf_op jit(solution)/shard_map/ppermute | solution.py:230
  31.0 1.5 %collective-permute-done.3.refs_1_ = bf16[768,128]{1,0:T(8,128)(2,1)S(1)} collective-permute-done((bf16[768,128]{1,0:T(8,128)(2,1)S(1)}, bf16[768,128]{1,0:T(8,128)(2,1)S(1)}, u32[]{:S(2)}, u32[]{:S(2)}) %collective-permute-start.3) | collective-permute-done | bytes 196640 | tf_op jit(solution)/shard_map/ppermute | solution.py:230
  32.5 1.2 %collective-permute-done.4.refs_2_ = bf16[768,128]{1,0:T(8,128)(2,1)S(1)} collective-permute-done((bf16[768,128]{1,0:T(8,128)(2,1)S(1)}, bf16[768,128]{1,0:T(8,128)(2,1)S(1)}, u32[]{:S(2)}, u32[]{:S(2)}) %collective-permute-start.4) | collective-permute-done | bytes 196640 | tf_op jit(solution)/shard_map/ppermute | solution.py:230
  33.7 0.1 shard_map.61
  33.8 0.6 collective-permute-start.5
  34.4 1.6 %collective-permute-start.6 = (bf16[384,128]{1,0:T(8,128)(2,1)S(1)}, bf16[384,128]{1,0:T(8,128)(2,1)S(1)}, u32[]{:S(2)}, u32[]{:S(2)}) collective-permute-start(bf16[384,128]{1,0:T(8,128)(2,1)S(1)} %get-tuple-element.26), channel_id=1, source_target_pairs={{0,8},{1,9},{2,10},{3,11},{4,12},{5,13},{6,14},{7,15},{8,0},{9,1},... | collective-permute-start | bytes 294920 | tf_op jit(solution)/shard_map/ppermute | solution.py:230
  35.9 0.4 collective-permute-start.7
  36.3 2.2 %collective-permute-done.5.refs_0_ = bf16[384,128]{1,0:T(8,128)(2,1)S(1)} collective-permute-done((bf16[384,128]{1,0:T(8,128)(2,1)S(1)}, bf16[384,128]{1,0:T(8,128)(2,1)S(1)}, u32[]{:S(2)}, u32[]{:S(2)}) %collective-permute-start.5) | collective-permute-done | bytes 98336 | tf_op jit(solution)/shard_map/ppermute | solution.py:230
  38.5 0.5 collective-permute-done.6.refs_1_
  39.0 1.6 %collective-permute-done.7.refs_2_ = bf16[384,128]{1,0:T(8,128)(2,1)S(1)} collective-permute-done((bf16[384,128]{1,0:T(8,128)(2,1)S(1)}, bf16[384,128]{1,0:T(8,128)(2,1)S(1)}, u32[]{:S(2)}, u32[]{:S(2)}) %collective-permute-start.7) | collective-permute-done | bytes 98336 | tf_op jit(solution)/shard_map/ppermute | solution.py:230
  40.6 0.5 collective-permute-start.8
  41.1 0.4 collective-permute-start.9
  41.5 1.5 %collective-permute-start.10 = (bf16[192,128]{1,0:T(8,128)(2,1)S(1)}, bf16[192,128]{1,0:T(8,128)(2,1)S(1)}, u32[]{:S(2)}, u32[]{:S(2)}) collective-permute-start(bf16[192,128]{1,0:T(8,128)(2,1)S(1)} %get-tuple-element.31), channel_id=1, source_target_pairs={{0,4},{1,5},{2,6},{3,7},{4,0},{5,1},{6,2},{7,3},{8,12},{9,13},{10,... | collective-permute-start | bytes 147464 | tf_op jit(solution)/shard_map/ppermute | solution.py:230
  43.0 1.8 %collective-permute-done.8.refs_0_ = bf16[192,128]{1,0:T(8,128)(2,1)S(1)} collective-permute-done((bf16[192,128]{1,0:T(8,128)(2,1)S(1)}, bf16[192,128]{1,0:T(8,128)(2,1)S(1)}, u32[]{:S(2)}, u32[]{:S(2)}) %collective-permute-start.8) | collective-permute-done | bytes 49184 | tf_op jit(solution)/shard_map/ppermute | solution.py:230
  44.8 0.5 collective-permute-done.9.refs_1_
  45.2 0.4 collective-permute-done.10.refs_2_
  45.6 2.6 %collective-permute-start.11 = (bf16[3,96,128]{2,1,0:T(8,128)(2,1)S(1)}, bf16[3,96,128]{2,1,0:T(8,128)(2,1)S(1)}, u32[]{:S(2)}, u32[]{:S(2)}) collective-permute-start(bf16[3,96,128]{2,1,0:T(8,128)(2,1)S(1)} %get-tuple-element.33), channel_id=1, source_target_pairs={{0,16},{1,17},{2,18},{3,19},{4,20},{5,21},{6,22},{7,23},{8,24},{9,... | collective-permute-start | bytes 221192 | tf_op jit(solution)/shard_map/ppermute | solution.py:230
  48.3 2.7 %collective-permute-done.11.refs_0_ = bf16[3,96,128]{2,1,0:T(8,128)(2,1)S(1)} collective-permute-done((bf16[3,96,128]{2,1,0:T(8,128)(2,1)S(1)}, bf16[3,96,128]{2,1,0:T(8,128)(2,1)S(1)}, u32[]{:S(2)}, u32[]{:S(2)}) %collective-permute-start.11) | collective-permute-done | bytes 73760 | tf_op jit(solution)/shard_map/ppermute | solution.py:230
  51.0 2.7 %collective-permute-start.12 = (bf16[3,96,128]{2,1,0:T(8,128)(2,1)S(1)}, bf16[3,96,128]{2,1,0:T(8,128)(2,1)S(1)}, u32[]{:S(2)}, u32[]{:S(2)}) collective-permute-start(bf16[3,96,128]{2,1,0:T(8,128)(2,1)S(1)} %shard_map.64), channel_id=1, source_target_pairs={{0,16},{1,17},{2,18},{3,19},{4,20},{5,21},{6,22},{7,23},{8,24},{9,... | collective-permute-start | bytes 221192 | tf_op jit(solution)/shard_map/ppermute | solution.py:230
  53.6 2.7 %collective-permute-done.12 = bf16[3,96,128]{2,1,0:T(8,128)(2,1)S(1)} collective-permute-done((bf16[3,96,128]{2,1,0:T(8,128)(2,1)S(1)}, bf16[3,96,128]{2,1,0:T(8,128)(2,1)S(1)}, u32[]{:S(2)}, u32[]{:S(2)}) %collective-permute-start.12) | collective-permute-done | bytes 73760 | tf_op jit(solution)/shard_map/ppermute | solution.py:230
  56.4 1.5 %collective-permute-start.19 = (bf16[192,128]{1,0:T(8,128)(2,1)S(1)}, bf16[192,128]{1,0:T(8,128)(2,1)S(1)}, u32[]{:S(2)}, u32[]{:S(2)}) collective-permute-start(bf16[192,128]{1,0:T(8,128)(2,1)S(1)} %get-tuple-element.34), channel_id=1, source_target_pairs={{0,4},{1,5},{2,6},{3,7},{4,0},{5,1},{6,2},{7,3},{8,12},{9,13},{10,... | collective-permute-start | bytes 147464 | tf_op jit(solution)/shard_map/ppermute | solution.py:230
  57.9 2.7 %collective-permute-start.13 = (bf16[192,128]{1,0:T(8,128)(2,1)S(1)}, bf16[192,128]{1,0:T(8,128)(2,1)S(1)}, u32[]{:S(2)}, u32[]{:S(2)}) collective-permute-start(bf16[192,128]{1,0:T(8,128)(2,1)S(1)} %get-tuple-element.35), channel_id=1, source_target_pairs={{0,8},{1,9},{2,10},{3,11},{4,12},{5,13},{6,14},{7,15},{8,0},{9,1},... | collective-permute-start | bytes 147464 | tf_op jit(solution)/shard_map/ppermute | solution.py:230
  60.6 1.4 %collective-permute-start.16 = (bf16[192,128]{1,0:T(8,128)(2,1)S(1)}, bf16[192,128]{1,0:T(8,128)(2,1)S(1)}, u32[]{:S(2)}, u32[]{:S(2)}) collective-permute-start(bf16[192,128]{1,0:T(8,128)(2,1)S(1)} %get-tuple-element.36), channel_id=1, source_target_pairs={{0,1},{1,0},{2,3},{3,2},{4,5},{5,4},{6,7},{7,6},{8,9},{9,8},{10,11... | collective-permute-start | bytes 147464 | tf_op jit(solution)/shard_map/ppermute | solution.py:230
  62.0 0.0 collective-permute-done.19
  62.0 2.5 %collective-permute-start.20 = (bf16[384,128]{1,0:T(8,128)(2,1)S(1)}, bf16[384,128]{1,0:T(8,128)(2,1)S(1)}, u32[]{:S(2)}, u32[]{:S(2)}) collective-permute-start(bf16[384,128]{1,0:T(8,128)(2,1)S(1)} %pad_maximum_fusion.8), channel_id=1, source_target_pairs={{0,1},{1,0},{2,3},{3,2},{4,5},{5,4},{6,7},{7,6},{8,9},{9,8},{10,11... | collective-permute-start | bytes 294920 | tf_op jit(solution)/shard_map/ppermute | solution.py:230
  64.5 0.4 collective-permute-done.16
  64.9 1.2 %collective-permute-start.17 = (bf16[384,128]{1,0:T(8,128)(2,1)S(1)}, bf16[384,128]{1,0:T(8,128)(2,1)S(1)}, u32[]{:S(2)}, u32[]{:S(2)}) collective-permute-start(bf16[384,128]{1,0:T(8,128)(2,1)S(1)} %pad_maximum_fusion.7), channel_id=1, source_target_pairs={{0,8},{1,9},{2,10},{3,11},{4,12},{5,13},{6,14},{7,15},{8,0},{9,1},... | collective-permute-start | bytes 294920 | tf_op jit(solution)/shard_map/ppermute | solution.py:230
  66.1 0.0 collective-permute-done.13
  66.1 0.7 collective-permute-start.14
  66.8 2.8 %collective-permute-done.17 = bf16[384,128]{1,0:T(8,128)(2,1)S(1)} collective-permute-done((bf16[384,128]{1,0:T(8,128)(2,1)S(1)}, bf16[384,128]{1,0:T(8,128)(2,1)S(1)}, u32[]{:S(2)}, u32[]{:S(2)}) %collective-permute-start.17) | collective-permute-done | bytes 98336 | tf_op jit(solution)/shard_map/ppermute | solution.py:230
  69.6 1.8 %collective-permute-start.18 = (bf16[768,128]{1,0:T(8,128)(2,1)S(1)}, bf16[768,128]{1,0:T(8,128)(2,1)S(1)}, u32[]{:S(2)}, u32[]{:S(2)}) collective-permute-start(bf16[768,128]{1,0:T(8,128)(2,1)S(1)} %pad_maximum_fusion.4), channel_id=1, source_target_pairs={{0,4},{1,5},{2,6},{3,7},{4,0},{5,1},{6,2},{7,3},{8,12},{9,13},{10,... | collective-permute-start | bytes 589832 | tf_op jit(solution)/shard_map/ppermute | solution.py:230
  71.4 0.0 collective-permute-done.20
  71.4 0.1 collective-permute-start.21
  71.5 0.0 collective-permute-done.14
  71.5 2.3 %collective-permute-start.15 = (bf16[768,128]{1,0:T(8,128)(2,1)S(1)}, bf16[768,128]{1,0:T(8,128)(2,1)S(1)}, u32[]{:S(2)}, u32[]{:S(2)}) collective-permute-start(bf16[768,128]{1,0:T(8,128)(2,1)S(1)} %pad_maximum_fusion.3), channel_id=1, source_target_pairs={{0,1},{1,0},{2,3},{3,2},{4,5},{5,4},{6,7},{7,6},{8,9},{9,8},{10,11... | collective-permute-start | bytes 589832 | tf_op jit(solution)/shard_map/ppermute | solution.py:230
  73.8 1.5 %collective-permute-done.18 = bf16[768,128]{1,0:T(8,128)(2,1)S(1)} collective-permute-done((bf16[768,128]{1,0:T(8,128)(2,1)S(1)}, bf16[768,128]{1,0:T(8,128)(2,1)S(1)}, u32[]{:S(2)}, u32[]{:S(2)}) %collective-permute-start.18) | collective-permute-done | bytes 196640 | tf_op jit(solution)/shard_map/ppermute | solution.py:230
  75.4 0.1 collective-permute-start.23
  75.5 2.0 %collective-permute-done.15 = bf16[768,128]{1,0:T(8,128)(2,1)S(1)} collective-permute-done((bf16[768,128]{1,0:T(8,128)(2,1)S(1)}, bf16[768,128]{1,0:T(8,128)(2,1)S(1)}, u32[]{:S(2)}, u32[]{:S(2)}) %collective-permute-start.15) | collective-permute-done | bytes 196640 | tf_op jit(solution)/shard_map/ppermute | solution.py:230
  77.5 0.1 collective-permute-start.22
  77.6 0.0 collective-permute-done.21
  77.6 0.5 collective-permute-start.24
  78.2 0.0 collective-permute-done.23.refs_4_
  78.2 1.1 %collective-permute-done.22.refs_3_ = bf16[1536,128]{1,0:T(8,128)(2,1)S(1)} collective-permute-done((bf16[1536,128]{1,0:T(8,128)(2,1)S(1)}, bf16[1536,128]{1,0:T(8,128)(2,1)S(1)}, u32[]{:S(2)}, u32[]{:S(2)}) %collective-permute-start.22) | collective-permute-done | bytes 393248 | tf_op jit(solution)/shard_map/ppermute | solution.py:230
  79.3 0.6 collective-permute-done.24.refs_5_
  79.9 2.3 %shard_map.65 = (f32[1728,128]{1,0:T(8,128)}, f32[3456,256]{1,0:T(8,128)}) custom-call(bf16[1536,128]{1,0:T(8,128)(2,1)S(1)} %pad_maximum_fusion.refs_0_, bf16[1536,128]{1,0:T(8,128)(2,1)S(1)} %pad_maximum_fusion.1.refs_1_, bf16[1536,128]{1,0:T(8,128)(2,1)S(1)} %pad_maximum_fusion.2.refs_2_, bf16[1536,128]{1,0:T(8,128)(2,1)S(1)} %collective-permute-done.22.refs_3_, ...), custom_call_target="tpu_custom_call" | custom-call | tf_op jit(solution)/shard_map/pallas_call | solution.py:26
  (13 shorter events, 0.3 us)
Async XLA Ops:
  1.5 7.0 %collective-permute-start = (bf16[3,16,1024]{2,1,0:T(8,128)(2,1)S(1)}, bf16[3,16,1024]{2,1,0:T(8,128)(2,1)S(1)}, u32[]{:S(2)}, u32[]{:S(2)}) collective-permute-start(bf16[3,16,1024]{2,1,0:T(8,128)(2,1)S(1)} %slice_bitcast_fusion), channel_id=1, source_target_pairs={{0,1},{2,3},{4,5},{6,7},{8,9},{10,11},{12,13},{14,15},{16,17},{18,... | collective-permute-start | bytes 294920 | tf_op jit(solution)/shard_map/ppermute | solution.py:236
  8.6 1.5 %copy-start.1 = (bf16[3456,256]{1,0:T(8,128)(2,1)S(1)}, bf16[3456,256]{1,0:T(8,128)(2,1)}, u32[]{:S(2)}) copy-start(bf16[3456,256]{1,0:T(8,128)(2,1)} %w2.1) | copy-start | bytes 5308420
  10.0 1.0 %copy-start.2 = (bf16[1,16,16,1024]{3,2,1,0:T(8,128)(2,1)S(1)}, bf16[1,16,16,1024]{3,2,1,0:T(8,128)(2,1)}, u32[]{:S(2)}) copy-start(bf16[1,16,16,1024]{3,2,1,0:T(8,128)(2,1)} %param.4) | copy-start | bytes 1572868
  11.1 1.0 %copy-start.3 = (bf16[1728,128]{1,0:T(8,128)(2,1)S(1)}, bf16[1728,128]{1,0:T(8,128)(2,1)}, u32[]{:S(2)}) copy-start(bf16[1728,128]{1,0:T(8,128)(2,1)} %w1.1) | copy-start | bytes 1327108
  18.6 2.8 %collective-permute-start.1 = (bf16[3,1536,128]{2,1,0:T(8,128)(2,1)S(1)}, bf16[3,1536,128]{2,1,0:T(8,128)(2,1)S(1)}, u32[]{:S(2)}, u32[]{:S(2)}) collective-permute-start(bf16[3,1536,128]{2,1,0:T(8,128)(2,1)S(1)} %get-tuple-element.19), channel_id=1, source_target_pairs={{0,2},{1,3},{2,0},{3,1},{4,6},{5,7},{6,4},{7,5},{8,10},{9,11},{10,... | collective-permute-start | bytes 3538952 | tf_op jit(solution)/shard_map/ppermute | solution.py:230
  21.5 1.7 %copy-start = (f32[3,1536,128]{2,1,0:T(8,128)S(1)}, f32[3,1536,128]{2,1,0:T(8,128)}, u32[]{:S(2)}) copy-start(f32[3,1536,128]{2,1,0:T(8,128)} %get-tuple-element.18.keep) | copy-start | bytes 7077892
  23.3 7.7 %collective-permute-start.2 = (bf16[768,128]{1,0:T(8,128)(2,1)S(1)}, bf16[768,128]{1,0:T(8,128)(2,1)S(1)}, u32[]{:S(2)}, u32[]{:S(2)}) collective-permute-start(bf16[768,128]{1,0:T(8,128)(2,1)S(1)} %get-tuple-element.21), channel_id=1, source_target_pairs={{0,1},{1,0},{2,3},{3,2},{4,5},{5,4},{6,7},{7,6},{8,9},{9,8},{10,11... | collective-permute-start | bytes 589832 | tf_op jit(solution)/shard_map/ppermute | solution.py:230
  25.8 6.7 %collective-permute-start.3 = (bf16[768,128]{1,0:T(8,128)(2,1)S(1)}, bf16[768,128]{1,0:T(8,128)(2,1)S(1)}, u32[]{:S(2)}, u32[]{:S(2)}) collective-permute-start(bf16[768,128]{1,0:T(8,128)(2,1)S(1)} %get-tuple-element.22), channel_id=1, source_target_pairs={{0,4},{1,5},{2,6},{3,7},{4,0},{5,1},{6,2},{7,3},{8,12},{9,13},{10,... | collective-permute-start | bytes 589832 | tf_op jit(solution)/shard_map/ppermute | solution.py:230
  27.3 6.4 %collective-permute-start.4 = (bf16[768,128]{1,0:T(8,128)(2,1)S(1)}, bf16[768,128]{1,0:T(8,128)(2,1)S(1)}, u32[]{:S(2)}, u32[]{:S(2)}) collective-permute-start(bf16[768,128]{1,0:T(8,128)(2,1)S(1)} %get-tuple-element.23), channel_id=1, source_target_pairs={{0,8},{1,9},{2,10},{3,11},{4,12},{5,13},{6,14},{7,15},{8,0},{9,1},... | collective-permute-start | bytes 589832 | tf_op jit(solution)/shard_map/ppermute | solution.py:230
  33.8 4.7 %collective-permute-start.5 = (bf16[384,128]{1,0:T(8,128)(2,1)S(1)}, bf16[384,128]{1,0:T(8,128)(2,1)S(1)}, u32[]{:S(2)}, u32[]{:S(2)}) collective-permute-start(bf16[384,128]{1,0:T(8,128)(2,1)S(1)} %get-tuple-element.25), channel_id=1, source_target_pairs={{0,4},{1,5},{2,6},{3,7},{4,0},{5,1},{6,2},{7,3},{8,12},{9,13},{10,... | collective-permute-start | bytes 294920 | tf_op jit(solution)/shard_map/ppermute | solution.py:230
  34.4 4.6 %collective-permute-start.6 = (bf16[384,128]{1,0:T(8,128)(2,1)S(1)}, bf16[384,128]{1,0:T(8,128)(2,1)S(1)}, u32[]{:S(2)}, u32[]{:S(2)}) collective-permute-start(bf16[384,128]{1,0:T(8,128)(2,1)S(1)} %get-tuple-element.26), channel_id=1, source_target_pairs={{0,8},{1,9},{2,10},{3,11},{4,12},{5,13},{6,14},{7,15},{8,0},{9,1},... | collective-permute-start | bytes 294920 | tf_op jit(solution)/shard_map/ppermute | solution.py:230
  35.9 4.6 %collective-permute-start.7 = (bf16[384,128]{1,0:T(8,128)(2,1)S(1)}, bf16[384,128]{1,0:T(8,128)(2,1)S(1)}, u32[]{:S(2)}, u32[]{:S(2)}) collective-permute-start(bf16[384,128]{1,0:T(8,128)(2,1)S(1)} %get-tuple-element.27), channel_id=1, source_target_pairs={{0,1},{1,0},{2,3},{3,2},{4,5},{5,4},{6,7},{7,6},{8,9},{9,8},{10,11... | collective-permute-start | bytes 294920 | tf_op jit(solution)/shard_map/ppermute | solution.py:230
  40.6 4.2 %collective-permute-start.8 = (bf16[192,128]{1,0:T(8,128)(2,1)S(1)}, bf16[192,128]{1,0:T(8,128)(2,1)S(1)}, u32[]{:S(2)}, u32[]{:S(2)}) collective-permute-start(bf16[192,128]{1,0:T(8,128)(2,1)S(1)} %get-tuple-element.29), channel_id=1, source_target_pairs={{0,8},{1,9},{2,10},{3,11},{4,12},{5,13},{6,14},{7,15},{8,0},{9,1},... | collective-permute-start | bytes 147464 | tf_op jit(solution)/shard_map/ppermute | solution.py:230
  41.1 4.1 %collective-permute-start.9 = (bf16[192,128]{1,0:T(8,128)(2,1)S(1)}, bf16[192,128]{1,0:T(8,128)(2,1)S(1)}, u32[]{:S(2)}, u32[]{:S(2)}) collective-permute-start(bf16[192,128]{1,0:T(8,128)(2,1)S(1)} %get-tuple-element.30), channel_id=1, source_target_pairs={{0,1},{1,0},{2,3},{3,2},{4,5},{5,4},{6,7},{7,6},{8,9},{9,8},{10,11... | collective-permute-start | bytes 147464 | tf_op jit(solution)/shard_map/ppermute | solution.py:230
  41.5 4.1 %collective-permute-start.10 = (bf16[192,128]{1,0:T(8,128)(2,1)S(1)}, bf16[192,128]{1,0:T(8,128)(2,1)S(1)}, u32[]{:S(2)}, u32[]{:S(2)}) collective-permute-start(bf16[192,128]{1,0:T(8,128)(2,1)S(1)} %get-tuple-element.31), channel_id=1, source_target_pairs={{0,4},{1,5},{2,6},{3,7},{4,0},{5,1},{6,2},{7,3},{8,12},{9,13},{10,... | collective-permute-start | bytes 147464 | tf_op jit(solution)/shard_map/ppermute | solution.py:230
  45.6 5.3 %collective-permute-start.11 = (bf16[3,96,128]{2,1,0:T(8,128)(2,1)S(1)}, bf16[3,96,128]{2,1,0:T(8,128)(2,1)S(1)}, u32[]{:S(2)}, u32[]{:S(2)}) collective-permute-start(bf16[3,96,128]{2,1,0:T(8,128)(2,1)S(1)} %get-tuple-element.33), channel_id=1, source_target_pairs={{0,16},{1,17},{2,18},{3,19},{4,20},{5,21},{6,22},{7,23},{8,24},{9,... | collective-permute-start | bytes 221192 | tf_op jit(solution)/shard_map/ppermute | solution.py:230
  51.0 5.4 %collective-permute-start.12 = (bf16[3,96,128]{2,1,0:T(8,128)(2,1)S(1)}, bf16[3,96,128]{2,1,0:T(8,128)(2,1)S(1)}, u32[]{:S(2)}, u32[]{:S(2)}) collective-permute-start(bf16[3,96,128]{2,1,0:T(8,128)(2,1)S(1)} %shard_map.64), channel_id=1, source_target_pairs={{0,16},{1,17},{2,18},{3,19},{4,20},{5,21},{6,22},{7,23},{8,24},{9,... | collective-permute-start | bytes 221192 | tf_op jit(solution)/shard_map/ppermute | solution.py:230
  56.4 5.6 %collective-permute-start.19 = (bf16[192,128]{1,0:T(8,128)(2,1)S(1)}, bf16[192,128]{1,0:T(8,128)(2,1)S(1)}, u32[]{:S(2)}, u32[]{:S(2)}) collective-permute-start(bf16[192,128]{1,0:T(8,128)(2,1)S(1)} %get-tuple-element.34), channel_id=1, source_target_pairs={{0,4},{1,5},{2,6},{3,7},{4,0},{5,1},{6,2},{7,3},{8,12},{9,13},{10,... | collective-permute-start | bytes 147464 | tf_op jit(solution)/shard_map/ppermute | solution.py:230
  57.9 8.2 %collective-permute-start.13 = (bf16[192,128]{1,0:T(8,128)(2,1)S(1)}, bf16[192,128]{1,0:T(8,128)(2,1)S(1)}, u32[]{:S(2)}, u32[]{:S(2)}) collective-permute-start(bf16[192,128]{1,0:T(8,128)(2,1)S(1)} %get-tuple-element.35), channel_id=1, source_target_pairs={{0,8},{1,9},{2,10},{3,11},{4,12},{5,13},{6,14},{7,15},{8,0},{9,1},... | collective-permute-start | bytes 147464 | tf_op jit(solution)/shard_map/ppermute | solution.py:230
  60.6 4.3 %collective-permute-start.16 = (bf16[192,128]{1,0:T(8,128)(2,1)S(1)}, bf16[192,128]{1,0:T(8,128)(2,1)S(1)}, u32[]{:S(2)}, u32[]{:S(2)}) collective-permute-start(bf16[192,128]{1,0:T(8,128)(2,1)S(1)} %get-tuple-element.36), channel_id=1, source_target_pairs={{0,1},{1,0},{2,3},{3,2},{4,5},{5,4},{6,7},{7,6},{8,9},{9,8},{10,11... | collective-permute-start | bytes 147464 | tf_op jit(solution)/shard_map/ppermute | solution.py:230
  62.0 9.4 %collective-permute-start.20 = (bf16[384,128]{1,0:T(8,128)(2,1)S(1)}, bf16[384,128]{1,0:T(8,128)(2,1)S(1)}, u32[]{:S(2)}, u32[]{:S(2)}) collective-permute-start(bf16[384,128]{1,0:T(8,128)(2,1)S(1)} %pad_maximum_fusion.8), channel_id=1, source_target_pairs={{0,1},{1,0},{2,3},{3,2},{4,5},{5,4},{6,7},{7,6},{8,9},{9,8},{10,11... | collective-permute-start | bytes 294920 | tf_op jit(solution)/shard_map/ppermute | solution.py:230
  64.9 4.7 %collective-permute-start.17 = (bf16[384,128]{1,0:T(8,128)(2,1)S(1)}, bf16[384,128]{1,0:T(8,128)(2,1)S(1)}, u32[]{:S(2)}, u32[]{:S(2)}) collective-permute-start(bf16[384,128]{1,0:T(8,128)(2,1)S(1)} %pad_maximum_fusion.7), channel_id=1, source_target_pairs={{0,8},{1,9},{2,10},{3,11},{4,12},{5,13},{6,14},{7,15},{8,0},{9,1},... | collective-permute-start | bytes 294920 | tf_op jit(solution)/shard_map/ppermute | solution.py:230
  66.1 5.4 %collective-permute-start.14 = (bf16[384,128]{1,0:T(8,128)(2,1)S(1)}, bf16[384,128]{1,0:T(8,128)(2,1)S(1)}, u32[]{:S(2)}, u32[]{:S(2)}) collective-permute-start(bf16[384,128]{1,0:T(8,128)(2,1)S(1)} %pad_maximum_fusion.6), channel_id=1, source_target_pairs={{0,4},{1,5},{2,6},{3,7},{4,0},{5,1},{6,2},{7,3},{8,12},{9,13},{10,... | collective-permute-start | bytes 294920 | tf_op jit(solution)/shard_map/ppermute | solution.py:230
  69.6 5.7 %collective-permute-start.18 = (bf16[768,128]{1,0:T(8,128)(2,1)S(1)}, bf16[768,128]{1,0:T(8,128)(2,1)S(1)}, u32[]{:S(2)}, u32[]{:S(2)}) collective-permute-start(bf16[768,128]{1,0:T(8,128)(2,1)S(1)} %pad_maximum_fusion.4), channel_id=1, source_target_pairs={{0,4},{1,5},{2,6},{3,7},{4,0},{5,1},{6,2},{7,3},{8,12},{9,13},{10,... | collective-permute-start | bytes 589832 | tf_op jit(solution)/shard_map/ppermute | solution.py:230
  71.4 6.2 %collective-permute-start.21 = (bf16[768,128]{1,0:T(8,128)(2,1)S(1)}, bf16[768,128]{1,0:T(8,128)(2,1)S(1)}, u32[]{:S(2)}, u32[]{:S(2)}) collective-permute-start(bf16[768,128]{1,0:T(8,128)(2,1)S(1)} %pad_maximum_fusion.5), channel_id=1, source_target_pairs={{0,8},{1,9},{2,10},{3,11},{4,12},{5,13},{6,14},{7,15},{8,0},{9,1},... | collective-permute-start | bytes 589832 | tf_op jit(solution)/shard_map/ppermute | solution.py:230
  71.5 5.9 %collective-permute-start.15 = (bf16[768,128]{1,0:T(8,128)(2,1)S(1)}, bf16[768,128]{1,0:T(8,128)(2,1)S(1)}, u32[]{:S(2)}, u32[]{:S(2)}) collective-permute-start(bf16[768,128]{1,0:T(8,128)(2,1)S(1)} %pad_maximum_fusion.3), channel_id=1, source_target_pairs={{0,1},{1,0},{2,3},{3,2},{4,5},{5,4},{6,7},{7,6},{8,9},{9,8},{10,11... | collective-permute-start | bytes 589832 | tf_op jit(solution)/shard_map/ppermute | solution.py:230
  75.4 2.8 %collective-permute-start.23 = (bf16[1536,128]{1,0:T(8,128)(2,1)S(1)}, bf16[1536,128]{1,0:T(8,128)(2,1)S(1)}, u32[]{:S(2)}, u32[]{:S(2)}) collective-permute-start(bf16[1536,128]{1,0:T(8,128)(2,1)S(1)} %pad_maximum_fusion.1.refs_1_), channel_id=1, source_target_pairs={{0,2},{1,3},{2,0},{3,1},{4,6},{5,7},{6,4},{7,5},{8,10},{9,11},{10,... | collective-permute-start | bytes 1179656 | tf_op jit(solution)/shard_map/ppermute | solution.py:230
  77.5 1.8 %collective-permute-start.22 = (bf16[1536,128]{1,0:T(8,128)(2,1)S(1)}, bf16[1536,128]{1,0:T(8,128)(2,1)S(1)}, u32[]{:S(2)}, u32[]{:S(2)}) collective-permute-start(bf16[1536,128]{1,0:T(8,128)(2,1)S(1)} %pad_maximum_fusion.refs_0_), channel_id=1, source_target_pairs={{0,2},{1,3},{2,0},{3,1},{4,6},{5,7},{6,4},{7,5},{8,10},{9,11},{10,... | collective-permute-start | bytes 1179656 | tf_op jit(solution)/shard_map/ppermute | solution.py:230
  77.6 2.2 %collective-permute-start.24 = (bf16[1536,128]{1,0:T(8,128)(2,1)S(1)}, bf16[1536,128]{1,0:T(8,128)(2,1)S(1)}, u32[]{:S(2)}, u32[]{:S(2)}) collective-permute-start(bf16[1536,128]{1,0:T(8,128)(2,1)S(1)} %pad_maximum_fusion.2.refs_2_), channel_id=1, source_target_pairs={{0,2},{1,3},{2,0},{3,1},{4,6},{5,7},{6,4},{7,5},{8,10},{9,11},{10,... | collective-permute-start | bytes 1179656 | tf_op jit(solution)/shard_map/ppermute | solution.py:230

commit v2 on v1

v2 whole, which is shorter than its diff:
```python
import functools

import jax
import jax.numpy as jnp
from jax import lax
from jax.experimental import pallas as pl
from jax.experimental.pallas import tpu as pltpu
from jax.sharding import PartitionSpec as P

BOTH = ("sample", "spatial")
LANES = 128
SECOND, FIRST = 3456, 864
VMEM_BYTES = 32 * 1024 * 1024
SPLIT = 17
LANE_TURNS = (((0, 1, 2), (1, 2, 0)), ((2, 0, 1), (1, 0, 2)))
f32, bf16 = jnp.float32, jnp.bfloat16


def full(shape):
    return pl.BlockSpec(memory_space=pltpu.VMEM)


def params():
    return pltpu.CompilerParams(vmem_limit_bytes=VMEM_BYTES)


def call(kernel, outs, *args, specs=None, scratch=(), cost=None):
    shapes = [jax.ShapeDtypeStruct(s, d) for s, d in outs]
    return pl.pallas_call(
        kernel,
        out_shape=shapes,
        in_specs=specs or [full(a.shape) for a in args],
        out_specs=[full(s.shape) for s in shapes],
        scratch_shapes=scratch,
        compiler_params=params(),
        cost_estimate=cost,
    )(*args)


def flat_index(spatial_count):
    return lax.axis_index("sample") * spatial_count + lax.axis_index("spatial")


def bit_of(value, bit):
    return lax.rem(lax.div(value, jnp.int32(1 << bit)), jnp.int32(2))


def sigmoid(value):
    return 1.0 / (1.0 + jnp.exp(-value))


def slope_of(value, sig):
    return sig * (1.0 + value * (1.0 - sig))


def dot(a, b, dims=((1,), (0,))):
    return lax.dot_general(a, b, (dims, ((), ())), preferred_element_type=f32)


def selection():
    row = lax.broadcasted_iota(jnp.int32, (144, 64), 0)
    col = lax.broadcasted_iota(jnp.int32, (144, 64), 1)
    pair, cell = lax.div(row, 16), lax.rem(row, 16)
    b, c = lax.div(pair, 3), lax.rem(pair, 3)
    k, j = lax.div(cell, 4), lax.rem(cell, 4)
    x, y = lax.div(col, 8), lax.rem(col, 8)
    hit = (x == 2 * k + c - 1) & (y == 2 * j + b - 1)
    return hit.astype(f32).astype(bf16)


def fill(vpad, x1, planes, first_hidden, count):
    for index, (e, plane) in enumerate(planes):
        vpad[index, :, 0:8, :] = jnp.zeros((8, 8, LANES), f32)
        for kt in range(8):
            vpad[index, kt, 8:24, :] = plane[:, kt * LANES : (kt + 1) * LANES].astype(f32)
    for index, (e, plane) in enumerate(planes):
        for b in range(3):
            tiles = [jnp.zeros((8, LANES), f32)]
            for kt in range(8):
                tiles.append(vpad[index, kt, pl.ds(7 + b, 8, stride=2), :])
            for kk in range(4):
                left = jnp.concatenate([tiles[2 * kk], tiles[2 * kk + 1]], 0).astype(bf16)
                right = jnp.concatenate([tiles[2 * kk + 1], tiles[2 * kk + 2]], 0).astype(bf16)
                for a in range(e % 2, 3, 2):
                    h = (e - a) // 2 - first_hidden
                    if 0 <= h < count:
                        rows = slice(h * 64 + kk * 16, h * 64 + kk * 16 + 16)
                        col = (a * 3 + b) * 256
                        x1[rows, col : col + LANES] = left
                        x1[rows, col + LANES : col + 2 * LANES] = right


def load_kernel(vol_hbm, w1_hbm, face, low, x1, w1p, vol, w1, vpad, sems):
    loads = [
        pltpu.make_async_copy(vol_hbm, vol, sems.at[0]),
        pltpu.make_async_copy(w1_hbm, w1, sems.at[1]),
    ]
    for load in loads:
        load.start()
    loads[0].wait()
    depth = vol.shape[0]
    face[...] = vol[depth - 3 : depth]
    low[...] = vol[0:2]
    planes = [(e, vol[e - 3]) for e in range(4, depth + 3)]
    fill(vpad, x1, planes, 2, x1.shape[0] // 64)
    loads[1].wait()
    for ab in range(9):
        w1p[ab * 256 : ab * 256 + 64, :] = jnp.zeros((64, 128), bf16)
        w1p[ab * 256 + 64 : (ab + 1) * 256, :] = w1[ab * 192 : (ab + 1) * 192, :]


def hidden_of(x1, w1p, slope, picked):
    first_pre = dot(x1[...], w1p[...])
    sig = sigmoid(first_pre)
    hidden = (first_pre * sig).astype(bf16)
    slope[...] = slope_of(first_pre, sig)
    select = selection()
    for h in range(hidden.shape[0] // 64):
        picked[h * 144 : (h + 1) * 144, :] = dot(
            select, hidden[h * 64 : (h + 1) * 64]
        ).astype(bf16)


def upper_kernel(x1, w1p, w2_hbm, slope, picked, w2, sem):
    load = pltpu.make_async_copy(w2_hbm, w2, sem)
    load.start()
    hidden_of(x1, w1p, slope, picked)
    load.wait()


def second_taps(x2, own_first, keep, send, first_tap, last_tap):
    columns = slice(first_tap * LANES, last_tap * LANES)
    rows = (last_tap - first_tap) * LANES
    grad = dot(x2[:, columns], own_first, ((0,), (0,)))
    keep[0:rows, :] = grad[:, :LANES]
    send[0:rows, :] = grad[:, LANES:].astype(bf16)


def clear(keep, send, start):
    if start < keep.shape[0]:
        keep[start:, :] = jnp.zeros((keep.shape[0] - start, LANES), f32)
        send[start:, :] = jnp.zeros((keep.shape[0] - start, LANES), bf16)


def lower_kernel(
    core_bit, spatial_count, halo, low, w1p, picked_up, w2, cot,
    keep, send, x1, slope, x2, d2, own_first, vpad, picked,
):
    planes = [(e, halo[e]) for e in range(3)] + [(e, low[e - 3]) for e in (3, 4)]
    fill(vpad, x1, planes, 0, 2)
    hidden_of(x1, w1p, slope, picked)
    out_planes = x2.shape[0] // 16
    for o in range(out_planes):
        for tap in range(27):
            h, pair = 2 * o + tap // 9, tap % 9
            if h < 2:
                cells = picked[h * 144 + pair * 16 : h * 144 + (pair + 1) * 16, :]
            else:
                at = (h - 2) * 144 + pair * 16
                cells = picked_up[at : at + 16, :]
            x2[o * 16 : (o + 1) * 16, tap * LANES : (tap + 1) * LANES] = cells
    second_pre = dot(x2[...], w2[...])
    sig = sigmoid(second_pre)
    delta = cot[...].astype(f32) * slope_of(second_pre, sig)
    d2[...] = delta.astype(bf16)
    core = bit_of(flat_index(spatial_count), core_bit)
    left, right = delta[:, :LANES], delta[:, LANES:]
    own_first[...] = jnp.concatenate(
        [jnp.where(core == 0, left, right), jnp.where(core == 0, right, left)], 1
    ).astype(bf16)
    second_taps(x2, own_first[...], keep, send, 0, SPLIT)
    clear(keep, send, SPLIT * LANES)


def last_kernel(
    core_bit, spatial_count, x1_up, x1_low, slope_up, slope_low, x2, d2, own_first, w2,
    keep, send, g1,
):
    second_taps(x2, own_first[...], keep, send, SPLIT, 27)
    out_planes = x2.shape[0] // 16
    hidden_planes = 2 * out_planes + 1
    select = selection()
    spread = dot(d2[...], w2[...], ((1,), (1,)))
    coarse = spread.astype(bf16)
    fine = (spread - coarse.astype(f32)).astype(bf16)
    deltas = []
    for h in range(hidden_planes):
        total = None
        for a in range(h % 2, 3, 2):
            o = (h - a) // 2
            if 0 <= o < out_planes:
                for piece in (coarse, fine):
                    stack = jnp.concatenate(
                        [
                            piece[o * 16 : (o + 1) * 16, tap * LANES : (tap + 1) * LANES]
                            for tap in range(a * 9, a * 9 + 9)
                        ],
                        0,
                    )
                    part = dot(select, stack, ((0,), (0,)))
                    total = part if total is None else total + part
        rounded = total.astype(bf16).astype(f32)
        if h < 2:
            slope = slope_low[h * 64 : (h + 1) * 64]
        else:
            slope = slope_up[(h - 2) * 64 : (h - 1) * 64]
        deltas.append((rounded * slope).astype(bf16))
    d1_low, d1_up = jnp.concatenate(deltas[:2], 0), jnp.concatenate(deltas[2:], 0)
    for a in range(3):
        columns = slice(a * 768, (a + 1) * 768)
        grad = dot(x1_up[:, columns], d1_up, ((0,), (0,)))
        grad = grad + dot(x1_low[:, columns], d1_low, ((0,), (0,)))
        for b in range(3):
            at = (a * 3 + b) * 192
            g1[at : at + 192, :] = grad[b * 256 + 64 : (b + 1) * 256]
    core = bit_of(flat_index(spatial_count), core_bit)
    start = (27 - SPLIT) * LANES
    mine = pl.ds(pl.multiple_of(core * FIRST, 8), FIRST)
    other = pl.ds(pl.multiple_of((1 - core) * FIRST, 8), FIRST)
    keep[start : start + FIRST, :] = g1[mine, :]
    send[start : start + FIRST, :] = g1[other, :].astype(bf16)
    clear(keep, send, start + FIRST)


def side_of(flat, orders, core, step):
    first, second = bit_of(flat, orders[0][step]), bit_of(flat, orders[1][step])
    return jnp.where(core == 0, first, second)


def reduce_kernel(orders, core_bit, step, spatial_count, keep, recv, kept, gone):
    half = keep.shape[0] // 2
    flat = flat_index(spatial_count)
    bit = side_of(flat, orders, bit_of(flat, core_bit), step)
    mine = pl.ds(pl.multiple_of(bit * half, 16), half)
    other = pl.ds(pl.multiple_of((1 - bit) * half, 16), half)
    kept[...] = keep[mine, :] + recv[mine, :].astype(f32)
    gone[...] = (keep[other, :] + recv[other, :].astype(f32)).astype(bf16)


def sum_kernel(keep, recv, out):
    out[...] = (keep[...].astype(f32) + recv[...].astype(f32)).astype(bf16)


def final_kernel(core_bit, orders, chunk, spatial_count, own, segments, *refs):
    part, grad_first, grad_second, wide, sems = refs[0], *refs[-4:]
    flat = flat_index(spatial_count)
    core = bit_of(flat, core_bit)
    side = core if own else 1 - core
    steps = len(orders[0]) - 1
    bits = [side_of(flat, orders, side, s) for s in range(steps)]
    columns = pl.ds(pl.multiple_of(side * LANES, LANES), LANES)
    copies = []
    for place in range(1 << steps):
        position = jnp.int32(0)
        for s in range(steps):
            want = (place >> (steps - 1 - s)) & 1
            differs = (1 - bits[s]) if want else bits[s]
            position = position + differs * (1 << (steps - 1 - s))
        rows = pl.ds(pl.multiple_of(position * chunk, 16), chunk)
        at = place * chunk
        wide[at : at + chunk, :] = part[rows, :].astype(f32)
        for start, size, second, base in segments:
            low, high = max(start, at), min(start + size, at + chunk)
            if low >= high:
                continue
            to = base + low - start
            if second:
                target = grad_second.at[to : to + high - low, columns]
            else:
                target = grad_first.at[
                    pl.ds(pl.multiple_of(side * FIRST + to, 16), high - low)
                ]
            copy = pltpu.make_async_copy(wide.at[low:high], target, sems.at[len(copies)])
            copy.start()
            copies.append(copy)
    for copy in copies:
        copy.wait()


def body(spatial_count, sample_count, volume, w_first, w_second, cotangent):
    count = spatial_count * sample_count
    bits = count.bit_length() - 1
    core_bit = spatial_count.bit_length() - 1
    others = [bit for bit in range(bits) if bit != core_bit]
    turn, rest = others[:3], others[3:]
    orders = [
        [tuple(turn[i] for i in turns) + tuple(rest) for turns in lane] for lane in LANE_TURNS
    ]
    steps = len(others) - 1
    unit = 16 << steps
    second_rest = (27 - SPLIT) * LANES
    segments = [
        [(0, SPLIT * LANES, True, 0)],
        [(0, second_rest, True, SPLIT * LANES), (second_rest, FIRST, False, 0)],
    ]
    chunks = [-(-sum(seg[1] for seg in lane) // unit) * 16 for lane in segments]

    def swap_core(array):
        return lax.ppermute(array, BOTH, [(i, i ^ (1 << core_bit)) for i in range(count)])

    def swap(array, lane, step):
        pairs = [(i, i ^ (1 << orders[lane][(i >> core_bit) & 1][step])) for i in range(count)]
        return lax.ppermute(array, BOTH, pairs)

    slab = volume[0]
    depth = slab.shape[0]
    out_planes = depth // 4
    up = 2 * out_planes - 1
    cot = cotangent[0].reshape(out_planes, 4, 4, 256).transpose(0, 2, 1, 3)
    cot = cot.reshape(out_planes * 16, 256)
    outside = pl.BlockSpec(memory_space=pl.ANY)
    face, low, x1_up, w1p = call(
        load_kernel,
        [
            ((3, 16, 1024), bf16),
            ((2, 16, 1024), bf16),
            ((up * 64, 9 * 256), bf16),
            ((9 * 256, 128), bf16),
        ],
        slab,
        w_first,
        specs=[outside, outside],
        scratch=[
            pltpu.VMEM(slab.shape, bf16),
            pltpu.VMEM(w_first.shape, bf16),
            pltpu.VMEM((depth - 1, 8, 24, LANES), f32),
            pltpu.SemaphoreType.DMA((2,)),
        ],
    )
    halo = lax.ppermute(face, "spatial", [(i, i + 1) for i in range(spatial_count - 1)])
    slope_up, picked_up, w2 = call(
        upper_kernel,
        [((up * 64, LANES), f32), ((up * 144, LANES), bf16), (w_second.shape, bf16)],
        x1_up,
        w1p,
        w_second,
        specs=[full(None), full(None), outside],
        scratch=[pltpu.SemaphoreType.DMA],
        cost=pl.CostEstimate(flops=4 * 10**8, bytes_accessed=10**7, transcendentals=0),
    )
    rows = [chunk << steps for chunk in chunks]
    cells = out_planes * 16
    keep0, send0, x1_low, slope_low, x2, d2, own_first = call(
        functools.partial(lower_kernel, core_bit, spatial_count),
        [
            ((rows[0], LANES), f32),
            ((rows[0], LANES), bf16),
            ((128, 9 * 256), bf16),
            ((128, LANES), f32),
            ((cells, 27 * LANES), bf16),
            ((cells, 256), bf16),
            ((cells, 256), bf16),
        ],
        halo,
        low,
        w1p,
        picked_up,
        w2,
        cot,
        scratch=[pltpu.VMEM((5, 8, 24, LANES), f32), pltpu.VMEM((288, LANES), bf16)],
    )
    recv0 = swap_core(send0)
    keep1, send1 = call(
        functools.partial(last_kernel, core_bit, spatial_count),
        [((rows[1], LANES), f32), ((rows[1], LANES), bf16)],
        x1_up,
        x1_low,
        slope_up,
        slope_low,
        x2,
        d2,
        own_first,
        w2,
        scratch=[pltpu.VMEM((2 * FIRST, LANES), f32)],
        cost=pl.CostEstimate(flops=10**9, bytes_accessed=10**7, transcendentals=0),
    )
    recv1 = swap_core(send1)
    keep, recv, own = [keep0, keep1], [recv0, recv1], [None, None]
    for step in range(steps):
        for lane in range(2):
            half = keep[lane].shape[0] // 2
            keep[lane], send = call(
                functools.partial(reduce_kernel, orders[lane], core_bit, step, spatial_count),
                [((half, LANES), f32), ((half, LANES), bf16)],
                keep[lane],
                recv[lane],
            )
            recv[lane] = swap(send, lane, step)
    for lane in range(2):
        shape = [((chunks[lane], LANES), bf16)]
        own[lane] = call(sum_kernel, shape, keep[lane], recv[lane])[0]
        own[lane] = call(sum_kernel, shape, own[lane], swap(own[lane], lane, steps))[0]
    for step in reversed(range(steps)):
        for lane in range(2):
            own[lane] = jnp.concatenate([own[lane], swap(own[lane], lane, step)], 0)
    got = [swap_core(own[lane]) for lane in range(2)]
    shapes = [jax.ShapeDtypeStruct((2 * FIRST, LANES), f32)]
    shapes += [jax.ShapeDtypeStruct((SECOND, 2 * LANES), f32)]
    grads = ()
    for lane in range(2):
        for mine in (True, False):
            part = own[lane] if mine else got[lane]
            grads = pl.pallas_call(
                functools.partial(
                    final_kernel, core_bit, orders[lane], chunks[lane], spatial_count, mine,
                    segments[lane],
                ),
                out_shape=shapes,
                in_specs=[full(part.shape)] + [outside] * len(grads),
                out_specs=[outside] * 2,
                scratch_shapes=[
                    pltpu.VMEM((rows[lane], LANES), f32),
                    pltpu.SemaphoreType.DMA(((1 << steps) + 1,)),
                ],
                input_output_aliases={1: 0, 2: 1} if grads else {},
                compiler_params=params(),
            )(part, *grads)
    return grads


def solution(mesh):
    sizes = dict(mesh.shape)

    def run(*args):
        return tuple(body(sizes["spatial"], sizes["sample"], *args))

    return jax.shard_map(
        run,
        mesh=mesh,
        in_specs=(P("sample", "spatial", None, None), P(), P(), P("sample", "spatial", None, None)),
        out_specs=(P(), P()),
        check_vma=False,
    )
```

time: 82.6 us -> 64.5 us (0.78)
  starting transfers between devices: 35.5 us -> 23.5 us
  waiting for transfers between devices: 29.7 us -> 24.7 us
  local copies, waits for them, and re-layouts: 6.87 us -> 4.29 us
  Pallas kernels: 9.24 us -> 10.7 us
    ppermute x25 -> x19, starting transfers between devices: 35.5 us -> 23.5 us  [the longest x14 17.9 us: swap(): return lax.ppermute(array, BOTH, pairs)]
    ppermute x25 -> x19, waiting for transfers between devices: 29.7 us -> 24.7 us  [the longest x14 24.1 us: swap(): return lax.ppermute(array, BOTH, pairs)]
    unnamed x8 -> x6, local copies, waits for them, and re-layouts: 5.19 us -> 3.52 us
    pallas_call x7 -> x18, Pallas kernels: 9.24 us -> 10.7 us  [the longest x14 6.37 us: call(): pl.pallas_call(kernel, out_shape=shapes, in_specs=specs or [full(a.shape)...]
    slice x1 -> x0, local copies, waits for them, and re-layouts: 0.9 us -> none  [body(): slab[-3:]]
  transfers between devices with their start and end apart: 25 -> 19, of which waited for: 19 -> 11; matrix products, arithmetic and copies ran while one was open for 1% -> 1% of each run, Pallas kernels for 0% -> 11%
where the time goes in v2:
time: 64.5 us; the launch traced here: 64.2 us
  waiting for transfers between devices  24.7 us (38%)
  starting transfers between devices  23.5 us (36%)
  Pallas kernels  10.7 us (17%)
  local copies, waits for them, and re-layouts  4.29 us (7%)
  between operations  0.82 us (1%)
    ppermute x14, waiting for transfers between devices, swap(): return lax.ppermute(array, BOTH, pairs)  24.1 us
    ppermute x14, starting transfers between devices, swap(): return lax.ppermute(array, BOTH, pairs)  17.9 us
    pallas_call x14, Pallas kernels, call(): pl.pallas_call(kernel, out_shape=shapes, in_specs=specs or [full(a.shape)...  6.37 us
    ppermute x1, starting transfers between devices, body(): lax.ppermute(face, 'spatial', [(i, i + 1) for i in range(spatial_count -...  4.85 us
    pallas_call x4, Pallas kernels, body(): pl.pallas_call(functools.partial(final_kernel, core_bit, orders[lane], ch...  4.37 us
    unnamed x6, local copies, waits for them, and re-layouts  3.52 us
  transfers between devices with their start and end apart: 19, of which 11 were waited for; matrix products, arithmetic and copies ran while one was open for 1% of the time, Pallas kernels for 11%

profile of v2, /device:TPU:0, one launch (start us, length us, event | category | flops | bytes accessed | tf_op | source)
XLA Modules:
  0.0 64.2 jit_solution(6365127115823518360)
XLA Ops:
  0.6 0.0 copy-start.1
  0.6 1.0 %copy-done.1 = bf16[1,16,16,1024]{3,2,1,0:T(8,128)(2,1)S(1)} copy-done((bf16[1,16,16,1024]{3,2,1,0:T(8,128)(2,1)S(1)}, bf16[1,16,16,1024]{3,2,1,0:T(8,128)(2,1)}, u32[]{:S(2)}) %copy-start.1) | copy-done | bytes 524312
  1.7 0.0 copy-start.2
  1.7 1.0 %copy-done.2 = bf16[1728,128]{1,0:T(8,128)(2,1)S(1)} copy-done((bf16[1728,128]{1,0:T(8,128)(2,1)S(1)}, bf16[1728,128]{1,0:T(8,128)(2,1)}, u32[]{:S(2)}) %copy-start.2) | copy-done | bytes 442392
  2.7 0.6 shard_map.59
  3.3 4.8 %collective-permute-start = (bf16[3,16,1024]{2,1,0:T(8,128)(2,1)S(1)}, bf16[3,16,1024]{2,1,0:T(8,128)(2,1)S(1)}, u32[]{:S(2)}, u32[]{:S(2)}) collective-permute-start(bf16[3,16,1024]{2,1,0:T(8,128)(2,1)S(1)} %get-tuple-element.37), channel_id=1, source_target_pairs={{0,1},{2,3},{4,5},{6,7},{8,9},{10,11},{12,13},{14,15},{16,17},{18,... | collective-permute-start | bytes 294920 | tf_op jit(solution)/shard_map/ppermute | solution.py:330
  8.1 0.8 %reshape.7.cot = bf16[64,256]{1,0:T(8,128)(2,1)S(1)} reshape(bf16[4,4,4,256]{3,2,1,0:T(4,128)(2,1)} %bitcast.5) | data formatting | bytes 65536 | tf_op jit(solution)/shard_map/reshape | solution.py:310
  8.9 0.0 copy-start
  8.9 1.5 %copy-done = bf16[3456,256]{1,0:T(8,128)(2,1)S(1)} copy-done((bf16[3456,256]{1,0:T(8,128)(2,1)S(1)}, bf16[3456,256]{1,0:T(8,128)(2,1)}, u32[]{:S(2)}) %copy-start) | copy-done | bytes 1769496
  10.4 1.5 %shard_map.60 = (f32[448,128]{1,0:T(8,128)S(1)}, bf16[1008,128]{1,0:T(8,128)(2,1)S(1)}, bf16[3456,256]{1,0:T(8,128)(2,1)S(1)}) custom-call(bf16[448,2304]{1,0:T(8,128)(2,1)S(1)} %get-tuple-element.36.x1.x1_up, bf16[2304,128]{1,0:T(8,128)(2,1)S(1)} %get-tuple-element.39.w1p, bf16[3456,256]{1,0:T(8,128)(2,1)S(1)} %copy-done), custom_call_target="tpu_custom_call" | custom-call | flops 400000000 | bytes 10000000 | tf_op jit(solution)/shard_map/pallas_call | solution.py:29
  11.9 0.0 collective-permute-done.halo
  11.9 1.7 %shard_map.61 = (f32[2176,128]{1,0:T(8,128)S(1)}, bf16[2176,128]{1,0:T(8,128)(2,1)S(1)}, bf16[128,2304]{1,0:T(8,128)(2,1)S(1)}, f32[128,128]{1,0:T(8,128)S(1)}, ...) custom-call(bf16[3,16,1024]{2,1,0:T(8,128)(2,1)S(1)} %collective-permute-done.halo, ...), custom_call_target="tpu_custom_call" | custom-call | tf_op jit(solution)/shard_map/pallas_call | solution.py:29
  13.6 0.1 collective-permute-start.10
  13.7 2.1 %shard_map.62 = (f32[2176,128]{1,0:T(8,128)S(1)}, bf16[2176,128]{1,0:T(8,128)(2,1)S(1)}) custom-call(bf16[448,2304]{1,0:T(8,128)(2,1)S(1)} %get-tuple-element.36.x1.x1_up, bf16[128,2304]{1,0:T(8,128)(2,1)S(1)} %get-tuple-element.42.x1_low, f32[448,128]{1,0:T(8,128)S(1)} %get-tuple-element.43.slope_up, f32[128,128]{1,0:T(8,128)S(1)} %get-tuple-element.44.slope_low, ...), custom_call_target="tpu_custom_call" | custom-call | flops 1000000000 | bytes 10000000 | tf_op jit(solution)/shard_map/pallas_call | solution.py:29
  15.8 0.6 collective-permute-start.1
  16.4 0.0 collective-permute-done.10.recv
  16.4 0.1 shard_map.68
  16.5 0.9 %collective-permute-start.11 = (bf16[1088,128]{1,0:T(8,128)(2,1)S(1)}, bf16[1088,128]{1,0:T(8,128)(2,1)S(1)}, u32[]{:S(2)}, u32[]{:S(2)}) collective-permute-start(bf16[1088,128]{1,0:T(8,128)(2,1)S(1)} %get-tuple-element.59), channel_id=1, source_target_pairs={{0,1},{1,0},{2,6},{3,7},{4,5},{5,4},{6,2},{7,3},{8,9},{9,8},{10,14... | collective-permute-start | bytes 835592 | tf_op jit(solution)/shard_map/ppermute | solution.py:303
  17.4 0.6 collective-permute-done.1.recv
  18.0 0.1 shard_map.63
  18.1 1.6 %collective-permute-start.2 = (bf16[1088,128]{1,0:T(8,128)(2,1)S(1)}, bf16[1088,128]{1,0:T(8,128)(2,1)S(1)}, u32[]{:S(2)}, u32[]{:S(2)}) collective-permute-start(bf16[1088,128]{1,0:T(8,128)(2,1)S(1)} %get-tuple-element.51), channel_id=1, source_target_pairs={{0,8},{1,9},{2,6},{3,7},{4,12},{5,13},{6,2},{7,3},{8,0},{9,1},{10,... | collective-permute-start | bytes 835592 | tf_op jit(solution)/shard_map/ppermute | solution.py:303
  19.7 3.4 %collective-permute-done.11.recv = bf16[1088,128]{1,0:T(8,128)(2,1)S(1)} collective-permute-done((bf16[1088,128]{1,0:T(8,128)(2,1)S(1)}, bf16[1088,128]{1,0:T(8,128)(2,1)S(1)}, u32[]{:S(2)}, u32[]{:S(2)}) %collective-permute-start.11) | collective-permute-done | bytes 278560 | tf_op jit(solution)/shard_map/ppermute | solution.py:303
  23.1 0.1 shard_map.69
  23.2 1.6 %collective-permute-start.12 = (bf16[544,128]{1,0:T(8,128)(2,1)S(1)}, bf16[544,128]{1,0:T(8,128)(2,1)S(1)}, u32[]{:S(2)}, u32[]{:S(2)}) collective-permute-start(bf16[544,128]{1,0:T(8,128)(2,1)S(1)} %get-tuple-element.61), channel_id=1, source_target_pairs={{0,4},{1,5},{2,10},{3,11},{4,0},{5,1},{6,14},{7,15},{8,12},{9,13},... | collective-permute-start | bytes 417800 | tf_op jit(solution)/shard_map/ppermute | solution.py:303
  24.7 0.0 collective-permute-done.2.recv
  24.8 0.1 shard_map.64
  24.8 0.9 %collective-permute-start.3 = (bf16[544,128]{1,0:T(8,128)(2,1)S(1)}, bf16[544,128]{1,0:T(8,128)(2,1)S(1)}, u32[]{:S(2)}, u32[]{:S(2)}) collective-permute-start(bf16[544,128]{1,0:T(8,128)(2,1)S(1)} %get-tuple-element.53), channel_id=1, source_target_pairs={{0,1},{1,0},{2,3},{3,2},{4,5},{5,4},{6,7},{7,6},{8,9},{9,8},{10,11... | collective-permute-start | bytes 417800 | tf_op jit(solution)/shard_map/ppermute | solution.py:303
  25.7 2.6 %collective-permute-done.12.recv = bf16[544,128]{1,0:T(8,128)(2,1)S(1)} collective-permute-done((bf16[544,128]{1,0:T(8,128)(2,1)S(1)}, bf16[544,128]{1,0:T(8,128)(2,1)S(1)}, u32[]{:S(2)}, u32[]{:S(2)}) %collective-permute-start.12) | collective-permute-done | bytes 139296 | tf_op jit(solution)/shard_map/ppermute | solution.py:303
  28.3 1.6 %collective-permute-start.13 = (bf16[272,128]{1,0:T(8,128)(2,1)S(1)}, bf16[272,128]{1,0:T(8,128)(2,1)S(1)}, u32[]{:S(2)}, u32[]{:S(2)}) collective-permute-start(bf16[272,128]{1,0:T(8,128)(2,1)S(1)} %get-tuple-element.63), channel_id=1, source_target_pairs={{0,8},{1,9},{2,3},{3,2},{4,12},{5,13},{6,7},{7,6},{8,0},{9,1},{10,... | collective-permute-start | bytes 208904 | tf_op jit(solution)/shard_map/ppermute | solution.py:303
  30.0 1.4 %collective-permute-done.3.recv = bf16[544,128]{1,0:T(8,128)(2,1)S(1)} collective-permute-done((bf16[544,128]{1,0:T(8,128)(2,1)S(1)}, bf16[544,128]{1,0:T(8,128)(2,1)S(1)}, u32[]{:S(2)}, u32[]{:S(2)}) %collective-permute-start.3) | collective-permute-done | bytes 139296 | tf_op jit(solution)/shard_map/ppermute | solution.py:303
  31.4 1.5 %collective-permute-start.4 = (bf16[272,128]{1,0:T(8,128)(2,1)S(1)}, bf16[272,128]{1,0:T(8,128)(2,1)S(1)}, u32[]{:S(2)}, u32[]{:S(2)}) collective-permute-start(bf16[272,128]{1,0:T(8,128)(2,1)S(1)} %get-tuple-element.55), channel_id=1, source_target_pairs={{0,4},{1,5},{2,10},{3,11},{4,0},{5,1},{6,14},{7,15},{8,12},{9,13},... | collective-permute-start | bytes 208904 | tf_op jit(solution)/shard_map/ppermute | solution.py:303
  32.9 0.0 collective-permute-done.13.recv
  33.0 2.7 %collective-permute-start.14 = (bf16[272,128]{1,0:T(8,128)(2,1)S(1)}, bf16[272,128]{1,0:T(8,128)(2,1)S(1)}, u32[]{:S(2)}, u32[]{:S(2)}) collective-permute-start(bf16[272,128]{1,0:T(8,128)(2,1)S(1)} %shard_map.71.keep), channel_id=1, source_target_pairs={{0,16},{1,17},{2,18},{3,19},{4,20},{5,21},{6,22},{7,23},{8,24},{9,... | collective-permute-start | bytes 208904 | tf_op jit(solution)/shard_map/ppermute | solution.py:303
  35.6 0.2 collective-permute-done.4.recv
  35.8 2.7 %collective-permute-start.5 = (bf16[272,128]{1,0:T(8,128)(2,1)S(1)}, bf16[272,128]{1,0:T(8,128)(2,1)S(1)}, u32[]{:S(2)}, u32[]{:S(2)}) collective-permute-start(bf16[272,128]{1,0:T(8,128)(2,1)S(1)} %shard_map.66.keep), channel_id=1, source_target_pairs={{0,16},{1,17},{2,18},{3,19},{4,20},{5,21},{6,22},{7,23},{8,24},{9,... | collective-permute-start | bytes 208904 | tf_op jit(solution)/shard_map/ppermute | solution.py:303
  38.5 2.0 %collective-permute-done.14.recv = bf16[272,128]{1,0:T(8,128)(2,1)S(1)} collective-permute-done((bf16[272,128]{1,0:T(8,128)(2,1)S(1)}, bf16[272,128]{1,0:T(8,128)(2,1)S(1)}, u32[]{:S(2)}, u32[]{:S(2)}) %collective-permute-start.14) | collective-permute-done | bytes 69664 | tf_op jit(solution)/shard_map/ppermute | solution.py:303
  40.5 0.2 collective-permute-start.15
  40.7 0.5 collective-permute-done.5.recv
  41.2 1.4 %collective-permute-start.6 = (bf16[272,128]{1,0:T(8,128)(2,1)S(1)}, bf16[272,128]{1,0:T(8,128)(2,1)S(1)}, u32[]{:S(2)}, u32[]{:S(2)}) collective-permute-start(bf16[272,128]{1,0:T(8,128)(2,1)S(1)} %shard_map.67), channel_id=1, source_target_pairs={{0,4},{1,5},{2,10},{3,11},{4,0},{5,1},{6,14},{7,15},{8,12},{9,13},... | collective-permute-start | bytes 208904 | tf_op jit(solution)/shard_map/ppermute | solution.py:303
  42.6 3.0 %collective-permute-done.15 = bf16[272,128]{1,0:T(8,128)(2,1)S(1)} collective-permute-done((bf16[272,128]{1,0:T(8,128)(2,1)S(1)}, bf16[272,128]{1,0:T(8,128)(2,1)S(1)}, u32[]{:S(2)}, u32[]{:S(2)}) %collective-permute-start.15) | collective-permute-done | bytes 69664 | tf_op jit(solution)/shard_map/ppermute | solution.py:303
  45.6 1.0 %collective-permute-start.16 = (bf16[544,128]{1,0:T(8,128)(2,1)S(1)}, bf16[544,128]{1,0:T(8,128)(2,1)S(1)}, u32[]{:S(2)}, u32[]{:S(2)}) collective-permute-start(bf16[544,128]{1,0:T(8,128)(2,1)S(1)} %pad_maximum_fusion.5), channel_id=1, source_target_pairs={{0,4},{1,5},{2,10},{3,11},{4,0},{5,1},{6,14},{7,15},{8,12},{9,13},... | collective-permute-start | bytes 417800 | tf_op jit(solution)/shard_map/ppermute | solution.py:303
  46.6 0.0 collective-permute-done.6
  46.6 0.9 %collective-permute-start.7 = (bf16[544,128]{1,0:T(8,128)(2,1)S(1)}, bf16[544,128]{1,0:T(8,128)(2,1)S(1)}, u32[]{:S(2)}, u32[]{:S(2)}) collective-permute-start(bf16[544,128]{1,0:T(8,128)(2,1)S(1)} %pad_maximum_fusion.4), channel_id=1, source_target_pairs={{0,1},{1,0},{2,3},{3,2},{4,5},{5,4},{6,7},{7,6},{8,9},{9,8},{10,11... | collective-permute-start | bytes 417800 | tf_op jit(solution)/shard_map/ppermute | solution.py:303
  47.5 4.6 %collective-permute-done.16 = bf16[544,128]{1,0:T(8,128)(2,1)S(1)} collective-permute-done((bf16[544,128]{1,0:T(8,128)(2,1)S(1)}, bf16[544,128]{1,0:T(8,128)(2,1)S(1)}, u32[]{:S(2)}, u32[]{:S(2)}) %collective-permute-start.16) | collective-permute-done | bytes 139296 | tf_op jit(solution)/shard_map/ppermute | solution.py:303
  52.2 0.9 %collective-permute-start.17 = (bf16[1088,128]{1,0:T(8,128)(2,1)S(1)}, bf16[1088,128]{1,0:T(8,128)(2,1)S(1)}, u32[]{:S(2)}, u32[]{:S(2)}) collective-permute-start(bf16[1088,128]{1,0:T(8,128)(2,1)S(1)} %pad_maximum_fusion.3), channel_id=1, source_target_pairs={{0,1},{1,0},{2,6},{3,7},{4,5},{5,4},{6,2},{7,3},{8,9},{9,8},{10,14... | collective-permute-start | bytes 835592 | tf_op jit(solution)/shard_map/ppermute | solution.py:303
  53.0 0.0 collective-permute-done.7
  53.1 0.1 collective-permute-start.8
  53.1 5.6 %collective-permute-done.17 = bf16[1088,128]{1,0:T(8,128)(2,1)S(1)} collective-permute-done((bf16[1088,128]{1,0:T(8,128)(2,1)S(1)}, bf16[1088,128]{1,0:T(8,128)(2,1)S(1)}, u32[]{:S(2)}, u32[]{:S(2)}) %collective-permute-start.17) | collective-permute-done | bytes 278560 | tf_op jit(solution)/shard_map/ppermute | solution.py:303
  58.8 0.1 collective-permute-start.18
  58.9 0.8 %collective-permute-done.8 = bf16[1088,128]{1,0:T(8,128)(2,1)S(1)} collective-permute-done((bf16[1088,128]{1,0:T(8,128)(2,1)S(1)}, bf16[1088,128]{1,0:T(8,128)(2,1)S(1)}, u32[]{:S(2)}, u32[]{:S(2)}) %collective-permute-start.8) | collective-permute-done | bytes 278560 | tf_op jit(solution)/shard_map/ppermute | solution.py:303
  59.7 0.1 collective-permute-start.9
  59.8 1.1 %shard_map.73 = (f32[1728,128]{1,0:T(8,128)}, f32[3456,256]{1,0:T(8,128)}) custom-call(bf16[2176,128]{1,0:T(8,128)(2,1)S(1)} %pad_maximum_fusion.1.refs_0_), custom_call_target="tpu_custom_call" | custom-call | tf_op jit(solution)/shard_map/pallas_call | solution.py:403
  60.9 0.0 collective-permute-done.18.refs_0_
  60.9 1.1 %shard_map.74 = (f32[1728,128]{1,0:T(8,128)}, f32[3456,256]{1,0:T(8,128)}) custom-call(bf16[2176,128]{1,0:T(8,128)(2,1)S(1)} %collective-permute-done.18.refs_0_, f32[1728,128]{1,0:T(8,128)} %get-tuple-element.64.refs_1_, f32[3456,256]{1,0:T(8,128)} %get-tuple-element.65.refs_2_), custom_call_target="tpu_custom_call", output_to_operand_aliasing={{0}: (1, {}), {1}: (2, {})} | custom-call | tf_op jit(solution)/shard_map/pallas_call | solution.py:403
  62.0 1.1 %shard_map.75 = (f32[1728,128]{1,0:T(8,128)}, f32[3456,256]{1,0:T(8,128)}) custom-call(bf16[2176,128]{1,0:T(8,128)(2,1)S(1)} %pad_maximum_fusion.refs_0_, f32[1728,128]{1,0:T(8,128)} %get-tuple-element.66.refs_1_, f32[3456,256]{1,0:T(8,128)} %get-tuple-element.67.refs_2_), custom_call_target="tpu_custom_call", output_to_operand_aliasing={{0}: (1, {}), {1}: (2, {})} | custom-call | tf_op jit(solution)/shard_map/pallas_call | solution.py:403
  63.1 0.0 collective-permute-done.9.refs_0_
  63.1 1.1 %shard_map.76 = (f32[1728,128]{1,0:T(8,128)}, f32[3456,256]{1,0:T(8,128)}) custom-call(bf16[2176,128]{1,0:T(8,128)(2,1)S(1)} %collective-permute-done.9.refs_0_, f32[1728,128]{1,0:T(8,128)} %get-tuple-element.68.refs_1_, f32[3456,256]{1,0:T(8,128)} %get-tuple-element.69.refs_2_), custom_call_target="tpu_custom_call", output_to_operand_aliasing={{0}: (1, {}), {1}: (2, {})} | custom-call | tf_op jit(solution)/shard_map/pallas_call | solution.py:403
  (12 shorter events, 0.3 us)
Async XLA Ops:
  0.6 1.0 %copy-start.1 = (bf16[1,16,16,1024]{3,2,1,0:T(8,128)(2,1)S(1)}, bf16[1,16,16,1024]{3,2,1,0:T(8,128)(2,1)}, u32[]{:S(2)}) copy-start(bf16[1,16,16,1024]{3,2,1,0:T(8,128)(2,1)} %param.4) | copy-start | bytes 1572868
  1.7 1.0 %copy-start.2 = (bf16[1728,128]{1,0:T(8,128)(2,1)S(1)}, bf16[1728,128]{1,0:T(8,128)(2,1)}, u32[]{:S(2)}) copy-start(bf16[1728,128]{1,0:T(8,128)(2,1)} %w1_hbm.1) | copy-start | bytes 1327108
  3.3 8.6 %collective-permute-start = (bf16[3,16,1024]{2,1,0:T(8,128)(2,1)S(1)}, bf16[3,16,1024]{2,1,0:T(8,128)(2,1)S(1)}, u32[]{:S(2)}, u32[]{:S(2)}) collective-permute-start(bf16[3,16,1024]{2,1,0:T(8,128)(2,1)S(1)} %get-tuple-element.37), channel_id=1, source_target_pairs={{0,1},{2,3},{4,5},{6,7},{8,9},{10,11},{12,13},{14,15},{16,17},{18,... | collective-permute-start | bytes 294920 | tf_op jit(solution)/shard_map/ppermute | solution.py:330
  8.9 1.5 %copy-start = (bf16[3456,256]{1,0:T(8,128)(2,1)S(1)}, bf16[3456,256]{1,0:T(8,128)(2,1)}, u32[]{:S(2)}) copy-start(bf16[3456,256]{1,0:T(8,128)(2,1)} %w2_hbm.1) | copy-start | bytes 5308420
  13.6 2.8 %collective-permute-start.10 = (bf16[2176,128]{1,0:T(8,128)(2,1)S(1)}, bf16[2176,128]{1,0:T(8,128)(2,1)S(1)}, u32[]{:S(2)}, u32[]{:S(2)}) collective-permute-start(bf16[2176,128]{1,0:T(8,128)(2,1)S(1)} %get-tuple-element.57), channel_id=1, source_target_pairs={{0,2},{1,3},{2,0},{3,1},{4,6},{5,7},{6,4},{7,5},{8,10},{9,11},{10,... | collective-permute-start | bytes 1671176 | tf_op jit(solution)/shard_map/ppermute | solution.py:299
  15.8 2.2 %collective-permute-start.1 = (bf16[2176,128]{1,0:T(8,128)(2,1)S(1)}, bf16[2176,128]{1,0:T(8,128)(2,1)S(1)}, u32[]{:S(2)}, u32[]{:S(2)}) collective-permute-start(bf16[2176,128]{1,0:T(8,128)(2,1)S(1)} %get-tuple-element.49), channel_id=1, source_target_pairs={{0,2},{1,3},{2,0},{3,1},{4,6},{5,7},{6,4},{7,5},{8,10},{9,11},{10,... | collective-permute-start | bytes 1671176 | tf_op jit(solution)/shard_map/ppermute | solution.py:299
  16.5 6.6 %collective-permute-start.11 = (bf16[1088,128]{1,0:T(8,128)(2,1)S(1)}, bf16[1088,128]{1,0:T(8,128)(2,1)S(1)}, u32[]{:S(2)}, u32[]{:S(2)}) collective-permute-start(bf16[1088,128]{1,0:T(8,128)(2,1)S(1)} %get-tuple-element.59), channel_id=1, source_target_pairs={{0,1},{1,0},{2,6},{3,7},{4,5},{5,4},{6,2},{7,3},{8,9},{9,8},{10,14... | collective-permute-start | bytes 835592 | tf_op jit(solution)/shard_map/ppermute | solution.py:303
  18.1 6.7 %collective-permute-start.2 = (bf16[1088,128]{1,0:T(8,128)(2,1)S(1)}, bf16[1088,128]{1,0:T(8,128)(2,1)S(1)}, u32[]{:S(2)}, u32[]{:S(2)}) collective-permute-start(bf16[1088,128]{1,0:T(8,128)(2,1)S(1)} %get-tuple-element.51), channel_id=1, source_target_pairs={{0,8},{1,9},{2,6},{3,7},{4,12},{5,13},{6,2},{7,3},{8,0},{9,1},{10,... | collective-permute-start | bytes 835592 | tf_op jit(solution)/shard_map/ppermute | solution.py:303
  23.2 5.1 %collective-permute-start.12 = (bf16[544,128]{1,0:T(8,128)(2,1)S(1)}, bf16[544,128]{1,0:T(8,128)(2,1)S(1)}, u32[]{:S(2)}, u32[]{:S(2)}) collective-permute-start(bf16[544,128]{1,0:T(8,128)(2,1)S(1)} %get-tuple-element.61), channel_id=1, source_target_pairs={{0,4},{1,5},{2,10},{3,11},{4,0},{5,1},{6,14},{7,15},{8,12},{9,13},... | collective-permute-start | bytes 417800 | tf_op jit(solution)/shard_map/ppermute | solution.py:303
  24.8 6.6 %collective-permute-start.3 = (bf16[544,128]{1,0:T(8,128)(2,1)S(1)}, bf16[544,128]{1,0:T(8,128)(2,1)S(1)}, u32[]{:S(2)}, u32[]{:S(2)}) collective-permute-start(bf16[544,128]{1,0:T(8,128)(2,1)S(1)} %get-tuple-element.53), channel_id=1, source_target_pairs={{0,1},{1,0},{2,3},{3,2},{4,5},{5,4},{6,7},{7,6},{8,9},{9,8},{10,11... | collective-permute-start | bytes 417800 | tf_op jit(solution)/shard_map/ppermute | solution.py:303
  28.3 4.6 %collective-permute-start.13 = (bf16[272,128]{1,0:T(8,128)(2,1)S(1)}, bf16[272,128]{1,0:T(8,128)(2,1)S(1)}, u32[]{:S(2)}, u32[]{:S(2)}) collective-permute-start(bf16[272,128]{1,0:T(8,128)(2,1)S(1)} %get-tuple-element.63), channel_id=1, source_target_pairs={{0,8},{1,9},{2,3},{3,2},{4,12},{5,13},{6,7},{7,6},{8,0},{9,1},{10,... | collective-permute-start | bytes 208904 | tf_op jit(solution)/shard_map/ppermute | solution.py:303
  31.4 4.4 %collective-permute-start.4 = (bf16[272,128]{1,0:T(8,128)(2,1)S(1)}, bf16[272,128]{1,0:T(8,128)(2,1)S(1)}, u32[]{:S(2)}, u32[]{:S(2)}) collective-permute-start(bf16[272,128]{1,0:T(8,128)(2,1)S(1)} %get-tuple-element.55), channel_id=1, source_target_pairs={{0,4},{1,5},{2,10},{3,11},{4,0},{5,1},{6,14},{7,15},{8,12},{9,13},... | collective-permute-start | bytes 208904 | tf_op jit(solution)/shard_map/ppermute | solution.py:303
  33.0 7.5 %collective-permute-start.14 = (bf16[272,128]{1,0:T(8,128)(2,1)S(1)}, bf16[272,128]{1,0:T(8,128)(2,1)S(1)}, u32[]{:S(2)}, u32[]{:S(2)}) collective-permute-start(bf16[272,128]{1,0:T(8,128)(2,1)S(1)} %shard_map.71.keep), channel_id=1, source_target_pairs={{0,16},{1,17},{2,18},{3,19},{4,20},{5,21},{6,22},{7,23},{8,24},{9,... | collective-permute-start | bytes 208904 | tf_op jit(solution)/shard_map/ppermute | solution.py:303
  35.8 5.4 %collective-permute-start.5 = (bf16[272,128]{1,0:T(8,128)(2,1)S(1)}, bf16[272,128]{1,0:T(8,128)(2,1)S(1)}, u32[]{:S(2)}, u32[]{:S(2)}) collective-permute-start(bf16[272,128]{1,0:T(8,128)(2,1)S(1)} %shard_map.66.keep), channel_id=1, source_target_pairs={{0,16},{1,17},{2,18},{3,19},{4,20},{5,21},{6,22},{7,23},{8,24},{9,... | collective-permute-start | bytes 208904 | tf_op jit(solution)/shard_map/ppermute | solution.py:303
  40.5 5.1 %collective-permute-start.15 = (bf16[272,128]{1,0:T(8,128)(2,1)S(1)}, bf16[272,128]{1,0:T(8,128)(2,1)S(1)}, u32[]{:S(2)}, u32[]{:S(2)}) collective-permute-start(bf16[272,128]{1,0:T(8,128)(2,1)S(1)} %shard_map.72), channel_id=1, source_target_pairs={{0,8},{1,9},{2,3},{3,2},{4,12},{5,13},{6,7},{7,6},{8,0},{9,1},{10,... | collective-permute-start | bytes 208904 | tf_op jit(solution)/shard_map/ppermute | solution.py:303
  41.2 5.4 %collective-permute-start.6 = (bf16[272,128]{1,0:T(8,128)(2,1)S(1)}, bf16[272,128]{1,0:T(8,128)(2,1)S(1)}, u32[]{:S(2)}, u32[]{:S(2)}) collective-permute-start(bf16[272,128]{1,0:T(8,128)(2,1)S(1)} %shard_map.67), channel_id=1, source_target_pairs={{0,4},{1,5},{2,10},{3,11},{4,0},{5,1},{6,14},{7,15},{8,12},{9,13},... | collective-permute-start | bytes 208904 | tf_op jit(solution)/shard_map/ppermute | solution.py:303
  45.6 6.5 %collective-permute-start.16 = (bf16[544,128]{1,0:T(8,128)(2,1)S(1)}, bf16[544,128]{1,0:T(8,128)(2,1)S(1)}, u32[]{:S(2)}, u32[]{:S(2)}) collective-permute-start(bf16[544,128]{1,0:T(8,128)(2,1)S(1)} %pad_maximum_fusion.5), channel_id=1, source_target_pairs={{0,4},{1,5},{2,10},{3,11},{4,0},{5,1},{6,14},{7,15},{8,12},{9,13},... | collective-permute-start | bytes 417800 | tf_op jit(solution)/shard_map/ppermute | solution.py:303
  46.6 6.4 %collective-permute-start.7 = (bf16[544,128]{1,0:T(8,128)(2,1)S(1)}, bf16[544,128]{1,0:T(8,128)(2,1)S(1)}, u32[]{:S(2)}, u32[]{:S(2)}) collective-permute-start(bf16[544,128]{1,0:T(8,128)(2,1)S(1)} %pad_maximum_fusion.4), channel_id=1, source_target_pairs={{0,1},{1,0},{2,3},{3,2},{4,5},{5,4},{6,7},{7,6},{8,9},{9,8},{10,11... | collective-permute-start | bytes 417800 | tf_op jit(solution)/shard_map/ppermute | solution.py:303
  52.2 6.6 %collective-permute-start.17 = (bf16[1088,128]{1,0:T(8,128)(2,1)S(1)}, bf16[1088,128]{1,0:T(8,128)(2,1)S(1)}, u32[]{:S(2)}, u32[]{:S(2)}) collective-permute-start(bf16[1088,128]{1,0:T(8,128)(2,1)S(1)} %pad_maximum_fusion.3), channel_id=1, source_target_pairs={{0,1},{1,0},{2,6},{3,7},{4,5},{5,4},{6,2},{7,3},{8,9},{9,8},{10,14... | collective-permute-start | bytes 835592 | tf_op jit(solution)/shard_map/ppermute | solution.py:303
  53.1 6.6 %collective-permute-start.8 = (bf16[1088,128]{1,0:T(8,128)(2,1)S(1)}, bf16[1088,128]{1,0:T(8,128)(2,1)S(1)}, u32[]{:S(2)}, u32[]{:S(2)}) collective-permute-start(bf16[1088,128]{1,0:T(8,128)(2,1)S(1)} %pad_maximum_fusion.2), channel_id=1, source_target_pairs={{0,8},{1,9},{2,6},{3,7},{4,12},{5,13},{6,2},{7,3},{8,0},{9,1},{10,... | collective-permute-start | bytes 835592 | tf_op jit(solution)/shard_map/ppermute | solution.py:303
  58.8 2.1 %collective-permute-start.18 = (bf16[2176,128]{1,0:T(8,128)(2,1)S(1)}, bf16[2176,128]{1,0:T(8,128)(2,1)S(1)}, u32[]{:S(2)}, u32[]{:S(2)}) collective-permute-start(bf16[2176,128]{1,0:T(8,128)(2,1)S(1)} %pad_maximum_fusion.1.refs_0_), channel_id=1, source_target_pairs={{0,2},{1,3},{2,0},{3,1},{4,6},{5,7},{6,4},{7,5},{8,10},{9,11},{10,... | collective-permute-start | bytes 1671176 | tf_op jit(solution)/shard_map/ppermute | solution.py:299
  59.7 3.4 %collective-permute-start.9 = (bf16[2176,128]{1,0:T(8,128)(2,1)S(1)}, bf16[2176,128]{1,0:T(8,128)(2,1)S(1)}, u32[]{:S(2)}, u32[]{:S(2)}) collective-permute-start(bf16[2176,128]{1,0:T(8,128)(2,1)S(1)} %pad_maximum_fusion.refs_0_), channel_id=1, source_target_pairs={{0,2},{1,3},{2,0},{3,1},{4,6},{5,7},{6,4},{7,5},{8,10},{9,11},{10,... | collective-permute-start | bytes 1671176 | tf_op jit(solution)/shard_map/ppermute | solution.py:299

commit v3 on v2

--- a/solution.py
+++ b/solution.py
@@ -12,8 +12,10 @@
 SECOND, FIRST = 3456, 864
 VMEM_BYTES = 32 * 1024 * 1024
 SPLIT = 17
-LANE_TURNS = (((0, 1, 2), (1, 2, 0)), ((2, 0, 1), (1, 0, 2)))
+LANE_TURNS = (((0, 1, 2), (2, 0, 1)), ((1, 2, 0), (2, 0, 1)))
 f32, bf16 = jnp.float32, jnp.bfloat16
+
+STEP_COST = pl.CostEstimate(flops=4 * 10**9, bytes_accessed=8 * 10**7, transcendentals=0)
 
 
 def full(shape):
@@ -24,17 +26,23 @@
     return pltpu.CompilerParams(vmem_limit_bytes=VMEM_BYTES)
 
 
-def call(kernel, outs, *args, specs=None, scratch=(), cost=None):
+def call(kernel, outs, *args, specs=None, scratch=(), cost=None, after=()):
     shapes = [jax.ShapeDtypeStruct(s, d) for s, d in outs]
+    count = len(args)
+
+    def run(*refs):
+        kernel(*refs[:count], *refs[count + len(after) :])
+
     return pl.pallas_call(
-        kernel,
+        run,
         out_shape=shapes,
-        in_specs=specs or [full(a.shape) for a in args],
+        in_specs=(specs or [full(a.shape) for a in args])
+        + [pl.BlockSpec(memory_space=pl.ANY)] * len(after),
         out_specs=[full(s.shape) for s in shapes],
         scratch_shapes=scratch,
         compiler_params=params(),
         cost_estimate=cost,
-    )(*args)
+    )(*args, *after)
 
 
 def flat_index(spatial_count):
@@ -121,11 +129,25 @@
         ).astype(bf16)
 
 
-def upper_kernel(x1, w1p, w2_hbm, slope, picked, w2, sem):
-    load = pltpu.make_async_copy(w2_hbm, w2, sem)
-    load.start()
+def upper_kernel(x1, w1p, w2_hbm, cot_hbm, slope, picked, w2, cot, cot_in, sems):
+    loads = [
+        pltpu.make_async_copy(cot_hbm, cot_in, sems.at[0]),
+        pltpu.make_async_copy(w2_hbm, w2, sems.at[1]),
+    ]
+    for load in loads:
+        load.start()
     hidden_of(x1, w1p, slope, picked)
-    load.wait()
+    loads[0].wait()
+    row = lax.broadcasted_iota(jnp.int32, (16, 4), 0)
+    col = lax.broadcasted_iota(jnp.int32, (16, 4), 1)
+    for o in range(cot_in.shape[0]):
+        cells = None
+        for k in range(4):
+            place = (row == 4 * k + col).astype(f32).astype(bf16)
+            part = dot(place, cot_in[o, :, k * 256 : (k + 1) * 256])
+            cells = part if cells is None else cells + part
+        cot[o * 16 : (o + 1) * 16, :] = cells
+    loads[1].wait()
 
 
 def second_taps(x2, own_first, keep, send, first_tap, last_tap):
@@ -146,7 +168,9 @@
     core_bit, spatial_count, halo, low, w1p, picked_up, w2, cot,
     keep, send, x1, slope, x2, d2, own_first, vpad, picked,
 ):
-    planes = [(e, halo[e]) for e in range(3)] + [(e, low[e - 3]) for e in (3, 4)]
+    inside = jnp.where(lax.axis_index("spatial") > 0, 1.0, 0.0).astype(f32)
+    planes = [(e, halo[e].astype(f32) * inside) for e in range(3)]
+    planes += [(e, low[e - 3]) for e in (3, 4)]
     fill(vpad, x1, planes, 0, 2)
     hidden_of(x1, w1p, slope, picked)
     out_planes = x2.shape[0] // 16
@@ -161,7 +185,7 @@
             x2[o * 16 : (o + 1) * 16, tap * LANES : (tap + 1) * LANES] = cells
     second_pre = dot(x2[...], w2[...])
     sig = sigmoid(second_pre)
-    delta = cot[...].astype(f32) * slope_of(second_pre, sig)
+    delta = cot[...] * slope_of(second_pre, sig)
     d2[...] = delta.astype(bf16)
     core = bit_of(flat_index(spatial_count), core_bit)
     left, right = delta[:, :LANES], delta[:, LANES:]
@@ -241,11 +265,13 @@
     out[...] = (keep[...].astype(f32) + recv[...].astype(f32)).astype(bf16)
 
 
-def final_kernel(core_bit, orders, chunk, spatial_count, own, segments, *refs):
-    part, grad_first, grad_second, wide, sems = refs[0], *refs[-4:]
-    flat = flat_index(spatial_count)
-    core = bit_of(flat, core_bit)
-    side = core if own else 1 - core
+def join_kernel(own, recv, out):
+    half = own.shape[0]
+    out[0:half, :] = own[...]
+    out[half:, :] = recv[...]
+
+
+def write_half(flat, side, orders, chunk, segments, part, wide, grad_first, grad_second, sems):
     steps = len(orders[0]) - 1
     bits = [side_of(flat, orders, side, s) for s in range(steps)]
     columns = pl.ds(pl.multiple_of(side * LANES, LANES), LANES)
@@ -273,6 +299,22 @@
             copy = pltpu.make_async_copy(wide.at[low:high], target, sems.at[len(copies)])
             copy.start()
             copies.append(copy)
+    return copies
+
+
+def final_kernel(core_bit, spatial_count, jobs, *refs):
+    count = len(jobs)
+    grad_first, grad_second = refs[-2 * count - 2 : -2 * count]
+    wides, sems = refs[-2 * count : -count], refs[-count:]
+    flat = flat_index(spatial_count)
+    core = bit_of(flat, core_bit)
+    copies = []
+    for index, (own, orders, chunk, segments) in enumerate(jobs):
+        side = core if own else 1 - core
+        copies += write_half(
+            flat, side, orders, chunk, segments,
+            refs[index], wides[index], grad_first, grad_second, sems[index],
+        )
     for copy in copies:
         copy.wait()
 
@@ -306,9 +348,9 @@
     depth = slab.shape[0]
     out_planes = depth // 4
     up = 2 * out_planes - 1
-    cot = cotangent[0].reshape(out_planes, 4, 4, 256).transpose(0, 2, 1, 3)
-    cot = cot.reshape(out_planes * 16, 256)
+    slab_cot = cotangent[0]
     outside = pl.BlockSpec(memory_space=pl.ANY)
+    far = pltpu.HBM
     face, low, x1_up, w1p = call(
         load_kernel,
         [
@@ -317,8 +359,8 @@
             ((up * 64, 9 * 256), bf16),
             ((9 * 256, 128), bf16),
         ],
-        slab,
-        w_first,
+        pltpu.with_memory_space_constraint(slab, far),
+        pltpu.with_memory_space_constraint(w_first, far),
         specs=[outside, outside],
         scratch=[
             pltpu.VMEM(slab.shape, bf16),
@@ -327,19 +369,27 @@
             pltpu.SemaphoreType.DMA((2,)),
         ],
     )
-    halo = lax.ppermute(face, "spatial", [(i, i + 1) for i in range(spatial_count - 1)])
-    slope_up, picked_up, w2 = call(
+    halo = lax.ppermute(
+        face, "spatial", [(i, (i + 1) % spatial_count) for i in range(spatial_count)]
+    )
+    cells = out_planes * 16
+    slope_up, picked_up, w2, cot = call(
         upper_kernel,
-        [((up * 64, LANES), f32), ((up * 144, LANES), bf16), (w_second.shape, bf16)],
+        [
+            ((up * 64, LANES), f32),
+            ((up * 144, LANES), bf16),
+            (w_second.shape, bf16),
+            ((cells, 256), f32),
+        ],
         x1_up,
         w1p,
-        w_second,
-        specs=[full(None), full(None), outside],
-        scratch=[pltpu.SemaphoreType.DMA],
+        pltpu.with_memory_space_constraint(w_second, far),
+        pltpu.with_memory_space_constraint(slab_cot, far),
+        specs=[full(None), full(None), outside, outside],
+        scratch=[pltpu.VMEM(slab_cot.shape, bf16), pltpu.SemaphoreType.DMA((2,))],
         cost=pl.CostEstimate(flops=4 * 10**8, bytes_accessed=10**7, transcendentals=0),
     )
     rows = [chunk << steps for chunk in chunks]
-    cells = out_planes * 16
     keep0, send0, x1_low, slope_low, x2, d2, own_first = call(
         functools.partial(lower_kernel, core_bit, spatial_count),
         [
@@ -376,45 +426,46 @@
     )
     recv1 = swap_core(send1)
     keep, recv, own = [keep0, keep1], [recv0, recv1], [None, None]
+    last = send1
     for step in range(steps):
         for lane in range(2):
             half = keep[lane].shape[0] // 2
-            keep[lane], send = call(
+            keep[lane], last = call(
                 functools.partial(reduce_kernel, orders[lane], core_bit, step, spatial_count),
                 [((half, LANES), f32), ((half, LANES), bf16)],
                 keep[lane],
                 recv[lane],
+                after=(last,),
+                cost=STEP_COST,
             )
-            recv[lane] = swap(send, lane, step)
-    for lane in range(2):
-        shape = [((chunks[lane], LANES), bf16)]
-        own[lane] = call(sum_kernel, shape, keep[lane], recv[lane])[0]
-        own[lane] = call(sum_kernel, shape, own[lane], swap(own[lane], lane, steps))[0]
+            recv[lane] = swap(last, lane, step)
+    for turn in range(2):
+        for lane in range(2):
+            shape = [((chunks[lane], LANES), bf16)]
+            last = call(sum_kernel, shape, keep[lane], recv[lane], after=(last,), cost=STEP_COST)[0]
+            keep[lane], recv[lane] = last, swap(last, lane, steps - turn)
     for step in reversed(range(steps)):
         for lane in range(2):
-            own[lane] = jnp.concatenate([own[lane], swap(own[lane], lane, step)], 0)
-    got = [swap_core(own[lane]) for lane in range(2)]
+            shape = [((2 * keep[lane].shape[0], LANES), bf16)]
+            last = call(join_kernel, shape, keep[lane], recv[lane], after=(last,), cost=STEP_COST)[0]
+            keep[lane] = last
+            recv[lane] = swap(last, lane, step - 1) if step else swap_core(last)
     shapes = [jax.ShapeDtypeStruct((2 * FIRST, LANES), f32)]
     shapes += [jax.ShapeDtypeStruct((SECOND, 2 * LANES), f32)]
     grads = ()
-    for lane in range(2):
-        for mine in (True, False):
-            part = own[lane] if mine else got[lane]
-            grads = pl.pallas_call(
-                functools.partial(
-                    final_kernel, core_bit, orders[lane], chunks[lane], spatial_count, mine,
-                    segments[lane],
-                ),
-                out_shape=shapes,
-                in_specs=[full(part.shape)] + [outside] * len(grads),
-                out_specs=[outside] * 2,
-                scratch_shapes=[
-                    pltpu.VMEM((rows[lane], LANES), f32),
-                    pltpu.SemaphoreType.DMA(((1 << steps) + 1,)),
-                ],
-                input_output_aliases={1: 0, 2: 1} if grads else {},
-                compiler_params=params(),
-            )(part, *grads)
+    for group in (((0, True), (0, False), (1, True)), ((1, False),)):
+        parts = [keep[lane] if mine else recv[lane] for lane, mine in group]
+        jobs = [(mine, orders[lane], chunks[lane], segments[lane]) for lane, mine in group]
+        grads = pl.pallas_call(
+            functools.partial(final_kernel, core_bit, spatial_count, jobs),
+            out_shape=shapes,
+            in_specs=[full(part.shape) for part in parts] + [outside] * len(grads),
+            out_specs=[outside] * 2,
+            scratch_shapes=[pltpu.VMEM((rows[lane], LANES), f32) for lane, _ in group]
+            + [pltpu.SemaphoreType.DMA(((1 << steps) + 1,)) for _ in group],
+            input_output_aliases={len(parts): 0, len(parts) + 1: 1} if grads else {},
+            compiler_params=params(),
+        )(*parts, *grads)
     return grads
 
 

time: 64.5 us -> 58.5 us (0.907)
  waiting for transfers between devices: 24.7 us -> 17.5 us
  starting transfers between devices: 23.5 us -> 29 us
  local copies, waits for them, and re-layouts: 4.29 us -> 0 us
    ppermute x14, starting transfers between devices: 17.9 us -> 25.2 us  [swap(): return lax.ppermute(array, BOTH, pairs)]
    ppermute x14, waiting for transfers between devices: 24.1 us -> 17 us  [swap(): return lax.ppermute(array, BOTH, pairs)]
    unnamed x6 -> x0, local copies, waits for them, and re-layouts: 3.52 us -> none
    ppermute x1, starting transfers between devices: 4.85 us -> 3 us  [body(): lax.ppermute(face, 'spatial', [(i, (i + 1) % spatial_count) for i in rang...]
    reshape x1 -> x0, local copies, waits for them, and re-layouts: 0.77 us -> none  [body(): cot = cot.reshape(out_planes * 16, 256)]
    pallas_call x18 -> x22, Pallas kernels: 10.7 us -> 11.1 us  [the longest x20 8.02 us: call(): pl.pallas_call(run, out_shape=shapes, in_specs=(specs or [full(a.shape) f...]
  transfers between devices with their start and end apart: 19 -> 19, of which waited for: 11 -> 10; matrix products, arithmetic and copies ran while one was open for 1% -> 0% of each run, Pallas kernels for 11% -> 12%
where the time goes in v3:
time: 58.5 us; the launch traced here: 58.3 us
  starting transfers between devices  29 us (50%)
  waiting for transfers between devices  17.5 us (30%)
  Pallas kernels  11.1 us (19%)
  between operations  0.77 us (1%)
    ppermute x14, starting transfers between devices, swap(): return lax.ppermute(array, BOTH, pairs)  25.2 us
    ppermute x14, waiting for transfers between devices, swap(): return lax.ppermute(array, BOTH, pairs)  17 us
    pallas_call x20, Pallas kernels, call(): pl.pallas_call(run, out_shape=shapes, in_specs=(specs or [full(a.shape) f...  8.02 us
    pallas_call x2, Pallas kernels, body(): pl.pallas_call(functools.partial(final_kernel, core_bit, spatial_count, j...  3.07 us
    ppermute x1, starting transfers between devices, body(): lax.ppermute(face, 'spatial', [(i, (i + 1) % spatial_count) for i in rang...  3 us
  transfers between devices with their start and end apart: 19, of which 10 were waited for; matrix products, arithmetic and copies ran while one was open for 0% of the time, Pallas kernels for 12%

profile of v3, /device:TPU:0, one launch (start us, length us, event | category | flops | bytes accessed | tf_op | source)
XLA Modules:
  0.0 58.3 jit_solution(2640777211172561761)
XLA Ops:
  0.6 1.3 %shard_map.59 = (bf16[3,16,1024]{2,1,0:T(8,128)(2,1)S(1)}, bf16[2,16,1024]{2,1,0:T(8,128)(2,1)S(1)}, bf16[448,2304]{1,0:T(8,128)(2,1)S(1)}, bf16[2304,128]{1,0:T(8,128)(2,1)S(1)}) custom-call(bf16[16,16,1024]{2,1,0:T(8,128)(2,1)} %bitcast.2, bf16[1728,128]{1,0:T(8,128)(2,1)} %refs_1_.1), custom_call_target="tpu_custom_call" | custom-call | tf_op jit(solution)/shard_map/pallas_call | solution.py:36
  2.0 3.0 %collective-permute-start = (bf16[3,16,1024]{2,1,0:T(8,128)(2,1)S(1)}, bf16[3,16,1024]{2,1,0:T(8,128)(2,1)S(1)}, u32[]{:S(2)}, u32[]{:S(2)}) collective-permute-start(bf16[3,16,1024]{2,1,0:T(8,128)(2,1)S(1)} %get-tuple-element.34), channel_id=1, source_target_pairs={{0,1},{1,0},{2,3},{3,2},{4,5},{5,4},{6,7},{7,6},{8,9},{9,8},{10,11... | collective-permute-start | bytes 294920 | tf_op jit(solution)/shard_map/ppermute | solution.py:372
  5.0 2.3 %shard_map.60 = (f32[448,128]{1,0:T(8,128)S(1)}, bf16[1008,128]{1,0:T(8,128)(2,1)S(1)}, bf16[3456,256]{1,0:T(8,128)(2,1)S(1)}, f32[64,256]{1,0:T(8,128)S(1)}) custom-call(bf16[448,2304]{1,0:T(8,128)(2,1)S(1)} %get-tuple-element.33.refs_0_, bf16[2304,128]{1,0:T(8,128)(2,1)S(1)} %get-tuple-element.36.refs_1_.refs_2_, bf16[3456,256]{1,0:T(8,128)(2,1)} %refs_2_.1, ...), custom_call_target="tpu_custom_call" | custom-call | flops 400000000 | bytes 10000000 | tf_op jit(solution)/shard_map/pallas_call | solution.py:36
  7.3 0.5 collective-permute-done.refs_0_
  7.8 1.7 %shard_map.61 = (f32[2176,128]{1,0:T(8,128)S(1)}, bf16[2176,128]{1,0:T(8,128)(2,1)S(1)}, bf16[128,2304]{1,0:T(8,128)(2,1)S(1)}, f32[128,128]{1,0:T(8,128)S(1)}, ...) custom-call(bf16[3,16,1024]{2,1,0:T(8,128)(2,1)S(1)} %collective-permute-done.refs_0_, ...), custom_call_target="tpu_custom_call" | custom-call | tf_op jit(solution)/shard_map/pallas_call | solution.py:36
  9.5 0.1 collective-permute-start.2
  9.6 2.1 %shard_map.62 = (f32[2176,128]{1,0:T(8,128)S(1)}, bf16[2176,128]{1,0:T(8,128)(2,1)S(1)}) custom-call(bf16[448,2304]{1,0:T(8,128)(2,1)S(1)} %get-tuple-element.33.refs_0_, bf16[128,2304]{1,0:T(8,128)(2,1)S(1)} %get-tuple-element.40.refs_1_, f32[448,128]{1,0:T(8,128)S(1)} %get-tuple-element.41.refs_2_, f32[128,128]{1,0:T(8,128)S(1)} %get-tuple-element.42.refs_3_, ...), custom_call_target="tpu_custom_call" | custom-call | flops 1000000000 | bytes 10000000 | tf_op jit(solution)/shard_map/pallas_call | solution.py:36
  11.7 0.6 collective-permute-start.1
  12.3 0.0 collective-permute-done.2.refs_1_
  12.3 0.1 shard_map.63
  12.4 1.9 %collective-permute-start.4 = (bf16[1088,128]{1,0:T(8,128)(2,1)S(1)}, bf16[1088,128]{1,0:T(8,128)(2,1)S(1)}, u32[]{:S(2)}, u32[]{:S(2)}) collective-permute-start(bf16[1088,128]{1,0:T(8,128)(2,1)S(1)} %get-tuple-element.50.refs_2_), channel_id=1, source_target_pairs={{0,1},{1,0},{2,10},{3,11},{4,5},{5,4},{6,14},{7,15},{8,9},{9,8},{1... | collective-permute-start | bytes 835592 | tf_op jit(solution)/shard_map/ppermute | solution.py:345
  14.3 0.0 collective-permute-done.1.refs_1_
  14.3 0.1 shard_map.64
  14.4 1.6 %collective-permute-start.3 = (bf16[1088,128]{1,0:T(8,128)(2,1)S(1)}, bf16[1088,128]{1,0:T(8,128)(2,1)S(1)}, u32[]{:S(2)}, u32[]{:S(2)}) collective-permute-start(bf16[1088,128]{1,0:T(8,128)(2,1)S(1)} %get-tuple-element.52.refs_2_), channel_id=1, source_target_pairs={{0,4},{1,5},{2,10},{3,11},{4,0},{5,1},{6,14},{7,15},{8,12},{9,13},... | collective-permute-start | bytes 835592 | tf_op jit(solution)/shard_map/ppermute | solution.py:345
  16.0 3.0 %collective-permute-done.4.refs_1_ = bf16[1088,128]{1,0:T(8,128)(2,1)S(1)} collective-permute-done((bf16[1088,128]{1,0:T(8,128)(2,1)S(1)}, bf16[1088,128]{1,0:T(8,128)(2,1)S(1)}, u32[]{:S(2)}, u32[]{:S(2)}) %collective-permute-start.4) | collective-permute-done | bytes 278560 | tf_op jit(solution)/shard_map/ppermute | solution.py:345
  19.0 0.1 shard_map.65
  19.0 1.9 %collective-permute-start.6 = (bf16[544,128]{1,0:T(8,128)(2,1)S(1)}, bf16[544,128]{1,0:T(8,128)(2,1)S(1)}, u32[]{:S(2)}, u32[]{:S(2)}) collective-permute-start(bf16[544,128]{1,0:T(8,128)(2,1)S(1)} %get-tuple-element.54.refs_2_), channel_id=1, source_target_pairs={{0,4},{1,5},{2,3},{3,2},{4,0},{5,1},{6,7},{7,6},{8,12},{9,13},{10,... | collective-permute-start | bytes 417800 | tf_op jit(solution)/shard_map/ppermute | solution.py:345
  21.0 0.0 collective-permute-done.3.refs_1_
  21.0 0.1 shard_map.66
  21.0 1.6 %collective-permute-start.5 = (bf16[544,128]{1,0:T(8,128)(2,1)S(1)}, bf16[544,128]{1,0:T(8,128)(2,1)S(1)}, u32[]{:S(2)}, u32[]{:S(2)}) collective-permute-start(bf16[544,128]{1,0:T(8,128)(2,1)S(1)} %get-tuple-element.56.refs_2_), channel_id=1, source_target_pairs={{0,8},{1,9},{2,3},{3,2},{4,12},{5,13},{6,7},{7,6},{8,0},{9,1},{10,... | collective-permute-start | bytes 417800 | tf_op jit(solution)/shard_map/ppermute | solution.py:345
  22.7 1.5 %collective-permute-done.6.refs_1_ = bf16[544,128]{1,0:T(8,128)(2,1)S(1)} collective-permute-done((bf16[544,128]{1,0:T(8,128)(2,1)S(1)}, bf16[544,128]{1,0:T(8,128)(2,1)S(1)}, u32[]{:S(2)}, u32[]{:S(2)}) %collective-permute-start.6) | collective-permute-done | bytes 139296 | tf_op jit(solution)/shard_map/ppermute | solution.py:345
  24.2 2.0 %collective-permute-start.8 = (bf16[272,128]{1,0:T(8,128)(2,1)S(1)}, bf16[272,128]{1,0:T(8,128)(2,1)S(1)}, u32[]{:S(2)}, u32[]{:S(2)}) collective-permute-start(bf16[272,128]{1,0:T(8,128)(2,1)S(1)} %get-tuple-element.58.refs_2_), channel_id=1, source_target_pairs={{0,8},{1,9},{2,6},{3,7},{4,12},{5,13},{6,2},{7,3},{8,0},{9,1},{10,... | collective-permute-start | bytes 208904 | tf_op jit(solution)/shard_map/ppermute | solution.py:345
  26.2 0.0 collective-permute-done.5.refs_1_
  26.2 1.5 %collective-permute-start.7 = (bf16[272,128]{1,0:T(8,128)(2,1)S(1)}, bf16[272,128]{1,0:T(8,128)(2,1)S(1)}, u32[]{:S(2)}, u32[]{:S(2)}) collective-permute-start(bf16[272,128]{1,0:T(8,128)(2,1)S(1)} %get-tuple-element.60.refs_2_), channel_id=1, source_target_pairs={{0,1},{1,0},{2,6},{3,7},{4,5},{5,4},{6,2},{7,3},{8,9},{9,8},{10,14... | collective-permute-start | bytes 208904 | tf_op jit(solution)/shard_map/ppermute | solution.py:345
  27.8 0.8 %collective-permute-done.8.refs_1_ = bf16[272,128]{1,0:T(8,128)(2,1)S(1)} collective-permute-done((bf16[272,128]{1,0:T(8,128)(2,1)S(1)}, bf16[272,128]{1,0:T(8,128)(2,1)S(1)}, u32[]{:S(2)}, u32[]{:S(2)}) %collective-permute-start.8) | collective-permute-done | bytes 69664 | tf_op jit(solution)/shard_map/ppermute | solution.py:345
  28.6 3.0 %collective-permute-start.10 = (bf16[272,128]{1,0:T(8,128)(2,1)S(1)}, bf16[272,128]{1,0:T(8,128)(2,1)S(1)}, u32[]{:S(2)}, u32[]{:S(2)}) collective-permute-start(bf16[272,128]{1,0:T(8,128)(2,1)S(1)} %shard_map.69.refs_2_.refs_0_), channel_id=1, source_target_pairs={{0,16},{1,17},{2,18},{3,19},{4,20},{5,21},{6,22},{7,23},{8,24},{9,... | collective-permute-start | bytes 208904 | tf_op jit(solution)/shard_map/ppermute | solution.py:345
  31.6 0.0 collective-permute-done.7.refs_1_
  31.6 1.7 %collective-permute-start.9 = (bf16[272,128]{1,0:T(8,128)(2,1)S(1)}, bf16[272,128]{1,0:T(8,128)(2,1)S(1)}, u32[]{:S(2)}, u32[]{:S(2)}) collective-permute-start(bf16[272,128]{1,0:T(8,128)(2,1)S(1)} %shard_map.70.refs_2_.refs_0_), channel_id=1, source_target_pairs={{0,16},{1,17},{2,18},{3,19},{4,20},{5,21},{6,22},{7,23},{8,24},{9,... | collective-permute-start | bytes 208904 | tf_op jit(solution)/shard_map/ppermute | solution.py:345
  33.3 2.6 %collective-permute-done.10.refs_1_ = bf16[272,128]{1,0:T(8,128)(2,1)S(1)} collective-permute-done((bf16[272,128]{1,0:T(8,128)(2,1)S(1)}, bf16[272,128]{1,0:T(8,128)(2,1)S(1)}, u32[]{:S(2)}, u32[]{:S(2)}) %collective-permute-start.10) | collective-permute-done | bytes 69664 | tf_op jit(solution)/shard_map/ppermute | solution.py:345
  35.8 1.3 %collective-permute-start.12 = (bf16[272,128]{1,0:T(8,128)(2,1)S(1)}, bf16[272,128]{1,0:T(8,128)(2,1)S(1)}, u32[]{:S(2)}, u32[]{:S(2)}) collective-permute-start(bf16[272,128]{1,0:T(8,128)(2,1)S(1)} %shard_map.71.refs_2_.refs_0_), channel_id=1, source_target_pairs={{0,8},{1,9},{2,6},{3,7},{4,12},{5,13},{6,2},{7,3},{8,0},{9,1},{10,... | collective-permute-start | bytes 208904 | tf_op jit(solution)/shard_map/ppermute | solution.py:345
  37.1 0.0 collective-permute-done.9.refs_1_
  37.1 1.6 %collective-permute-start.11 = (bf16[272,128]{1,0:T(8,128)(2,1)S(1)}, bf16[272,128]{1,0:T(8,128)(2,1)S(1)}, u32[]{:S(2)}, u32[]{:S(2)}) collective-permute-start(bf16[272,128]{1,0:T(8,128)(2,1)S(1)} %shard_map.72.refs_2_.refs_0_), channel_id=1, source_target_pairs={{0,1},{1,0},{2,6},{3,7},{4,5},{5,4},{6,2},{7,3},{8,9},{9,8},{10,14... | collective-permute-start | bytes 208904 | tf_op jit(solution)/shard_map/ppermute | solution.py:345
  38.7 1.5 %collective-permute-done.12.refs_1_ = bf16[272,128]{1,0:T(8,128)(2,1)S(1)} collective-permute-done((bf16[272,128]{1,0:T(8,128)(2,1)S(1)}, bf16[272,128]{1,0:T(8,128)(2,1)S(1)}, u32[]{:S(2)}, u32[]{:S(2)}) %collective-permute-start.12) | collective-permute-done | bytes 69664 | tf_op jit(solution)/shard_map/ppermute | solution.py:345
  40.2 1.5 %collective-permute-start.14 = (bf16[544,128]{1,0:T(8,128)(2,1)S(1)}, bf16[544,128]{1,0:T(8,128)(2,1)S(1)}, u32[]{:S(2)}, u32[]{:S(2)}) collective-permute-start(bf16[544,128]{1,0:T(8,128)(2,1)S(1)} %shard_map.73.refs_2_.refs_0_), channel_id=1, source_target_pairs={{0,4},{1,5},{2,3},{3,2},{4,0},{5,1},{6,7},{7,6},{8,12},{9,13},{10,... | collective-permute-start | bytes 417800 | tf_op jit(solution)/shard_map/ppermute | solution.py:345
  41.7 0.0 collective-permute-done.11.refs_1_
  41.7 2.0 %collective-permute-start.13 = (bf16[544,128]{1,0:T(8,128)(2,1)S(1)}, bf16[544,128]{1,0:T(8,128)(2,1)S(1)}, u32[]{:S(2)}, u32[]{:S(2)}) collective-permute-start(bf16[544,128]{1,0:T(8,128)(2,1)S(1)} %shard_map.74.refs_2_.refs_0_), channel_id=1, source_target_pairs={{0,8},{1,9},{2,3},{3,2},{4,12},{5,13},{6,7},{7,6},{8,0},{9,1},{10,... | collective-permute-start | bytes 417800 | tf_op jit(solution)/shard_map/ppermute | solution.py:345
  43.7 1.7 %collective-permute-done.14.refs_1_ = bf16[544,128]{1,0:T(8,128)(2,1)S(1)} collective-permute-done((bf16[544,128]{1,0:T(8,128)(2,1)S(1)}, bf16[544,128]{1,0:T(8,128)(2,1)S(1)}, u32[]{:S(2)}, u32[]{:S(2)}) %collective-permute-start.14) | collective-permute-done | bytes 139296 | tf_op jit(solution)/shard_map/ppermute | solution.py:345
  45.4 1.6 %collective-permute-start.16 = (bf16[1088,128]{1,0:T(8,128)(2,1)S(1)}, bf16[1088,128]{1,0:T(8,128)(2,1)S(1)}, u32[]{:S(2)}, u32[]{:S(2)}) collective-permute-start(bf16[1088,128]{1,0:T(8,128)(2,1)S(1)} %shard_map.75.refs_2_.refs_0_), channel_id=1, source_target_pairs={{0,1},{1,0},{2,10},{3,11},{4,5},{5,4},{6,14},{7,15},{8,9},{9,8},{1... | collective-permute-start | bytes 835592 | tf_op jit(solution)/shard_map/ppermute | solution.py:345
  46.9 1.4 %collective-permute-done.13.refs_1_ = bf16[544,128]{1,0:T(8,128)(2,1)S(1)} collective-permute-done((bf16[544,128]{1,0:T(8,128)(2,1)S(1)}, bf16[544,128]{1,0:T(8,128)(2,1)S(1)}, u32[]{:S(2)}, u32[]{:S(2)}) %collective-permute-start.13) | collective-permute-done | bytes 139296 | tf_op jit(solution)/shard_map/ppermute | solution.py:345
  48.4 2.2 %collective-permute-start.15 = (bf16[1088,128]{1,0:T(8,128)(2,1)S(1)}, bf16[1088,128]{1,0:T(8,128)(2,1)S(1)}, u32[]{:S(2)}, u32[]{:S(2)}) collective-permute-start(bf16[1088,128]{1,0:T(8,128)(2,1)S(1)} %shard_map.76.refs_2_.refs_0_), channel_id=1, source_target_pairs={{0,4},{1,5},{2,10},{3,11},{4,0},{5,1},{6,14},{7,15},{8,12},{9,13},... | collective-permute-start | bytes 835592 | tf_op jit(solution)/shard_map/ppermute | solution.py:345
  50.6 1.4 %collective-permute-done.16.refs_1_ = bf16[1088,128]{1,0:T(8,128)(2,1)S(1)} collective-permute-done((bf16[1088,128]{1,0:T(8,128)(2,1)S(1)}, bf16[1088,128]{1,0:T(8,128)(2,1)S(1)}, u32[]{:S(2)}, u32[]{:S(2)}) %collective-permute-start.16) | collective-permute-done | bytes 278560 | tf_op jit(solution)/shard_map/ppermute | solution.py:345
  52.0 0.1 collective-permute-start.18
  52.1 3.0 %collective-permute-done.15.refs_1_ = bf16[1088,128]{1,0:T(8,128)(2,1)S(1)} collective-permute-done((bf16[1088,128]{1,0:T(8,128)(2,1)S(1)}, bf16[1088,128]{1,0:T(8,128)(2,1)S(1)}, u32[]{:S(2)}, u32[]{:S(2)}) %collective-permute-start.15) | collective-permute-done | bytes 278560 | tf_op jit(solution)/shard_map/ppermute | solution.py:345
  55.1 0.1 collective-permute-start.17
  55.2 0.0 collective-permute-done.18.refs_1_
  55.2 2.0 %shard_map.79 = (f32[1728,128]{1,0:T(8,128)}, f32[3456,256]{1,0:T(8,128)}) custom-call(bf16[2176,128]{1,0:T(8,128)(2,1)S(1)} %shard_map.77.refs_2_.refs_0_, bf16[2176,128]{1,0:T(8,128)(2,1)S(1)} %collective-permute-done.18.refs_1_, bf16[2176,128]{1,0:T(8,128)(2,1)S(1)} %shard_map.78.refs_2_), custom_call_target="tpu_custom_call" | custom-call | tf_op jit(solution)/shard_map/pallas_call | solution.py:459
  57.2 0.0 collective-permute-done.17.refs_0_
  57.2 1.1 %shard_map.80 = (f32[1728,128]{1,0:T(8,128)}, f32[3456,256]{1,0:T(8,128)}) custom-call(bf16[2176,128]{1,0:T(8,128)(2,1)S(1)} %collective-permute-done.17.refs_0_, f32[1728,128]{1,0:T(8,128)} %get-tuple-element.62.refs_1_, f32[3456,256]{1,0:T(8,128)} %get-tuple-element.63.refs_2_), custom_call_target="tpu_custom_call", output_to_operand_aliasing={{0}: (1, {}), {1}: (2, {})} | custom-call | tf_op jit(solution)/shard_map/pallas_call | solution.py:459
  (12 shorter events, 0.3 us)
Async XLA Ops:
  2.0 5.8 %collective-permute-start = (bf16[3,16,1024]{2,1,0:T(8,128)(2,1)S(1)}, bf16[3,16,1024]{2,1,0:T(8,128)(2,1)S(1)}, u32[]{:S(2)}, u32[]{:S(2)}) collective-permute-start(bf16[3,16,1024]{2,1,0:T(8,128)(2,1)S(1)} %get-tuple-element.34), channel_id=1, source_target_pairs={{0,1},{1,0},{2,3},{3,2},{4,5},{5,4},{6,7},{7,6},{8,9},{9,8},{10,11... | collective-permute-start | bytes 294920 | tf_op jit(solution)/shard_map/ppermute | solution.py:372
  9.5 2.7 %collective-permute-start.2 = (bf16[2176,128]{1,0:T(8,128)(2,1)S(1)}, bf16[2176,128]{1,0:T(8,128)(2,1)S(1)}, u32[]{:S(2)}, u32[]{:S(2)}) collective-permute-start(bf16[2176,128]{1,0:T(8,128)(2,1)S(1)} %get-tuple-element.49), channel_id=1, source_target_pairs={{0,2},{1,3},{2,0},{3,1},{4,6},{5,7},{6,4},{7,5},{8,10},{9,11},{10,... | collective-permute-start | bytes 1671176 | tf_op jit(solution)/shard_map/ppermute | solution.py:341
  11.7 2.6 %collective-permute-start.1 = (bf16[2176,128]{1,0:T(8,128)(2,1)S(1)}, bf16[2176,128]{1,0:T(8,128)(2,1)S(1)}, u32[]{:S(2)}, u32[]{:S(2)}) collective-permute-start(bf16[2176,128]{1,0:T(8,128)(2,1)S(1)} %get-tuple-element.47.refs_2_), channel_id=1, source_target_pairs={{0,2},{1,3},{2,0},{3,1},{4,6},{5,7},{6,4},{7,5},{8,10},{9,11},{10,... | collective-permute-start | bytes 1671176 | tf_op jit(solution)/shard_map/ppermute | solution.py:341
  12.4 6.6 %collective-permute-start.4 = (bf16[1088,128]{1,0:T(8,128)(2,1)S(1)}, bf16[1088,128]{1,0:T(8,128)(2,1)S(1)}, u32[]{:S(2)}, u32[]{:S(2)}) collective-permute-start(bf16[1088,128]{1,0:T(8,128)(2,1)S(1)} %get-tuple-element.50.refs_2_), channel_id=1, source_target_pairs={{0,1},{1,0},{2,10},{3,11},{4,5},{5,4},{6,14},{7,15},{8,9},{9,8},{1... | collective-permute-start | bytes 835592 | tf_op jit(solution)/shard_map/ppermute | solution.py:345
  14.4 6.6 %collective-permute-start.3 = (bf16[1088,128]{1,0:T(8,128)(2,1)S(1)}, bf16[1088,128]{1,0:T(8,128)(2,1)S(1)}, u32[]{:S(2)}, u32[]{:S(2)}) collective-permute-start(bf16[1088,128]{1,0:T(8,128)(2,1)S(1)} %get-tuple-element.52.refs_2_), channel_id=1, source_target_pairs={{0,4},{1,5},{2,10},{3,11},{4,0},{5,1},{6,14},{7,15},{8,12},{9,13},... | collective-permute-start | bytes 835592 | tf_op jit(solution)/shard_map/ppermute | solution.py:345
  19.0 5.1 %collective-permute-start.6 = (bf16[544,128]{1,0:T(8,128)(2,1)S(1)}, bf16[544,128]{1,0:T(8,128)(2,1)S(1)}, u32[]{:S(2)}, u32[]{:S(2)}) collective-permute-start(bf16[544,128]{1,0:T(8,128)(2,1)S(1)} %get-tuple-element.54.refs_2_), channel_id=1, source_target_pairs={{0,4},{1,5},{2,3},{3,2},{4,0},{5,1},{6,7},{7,6},{8,12},{9,13},{10,... | collective-permute-start | bytes 417800 | tf_op jit(solution)/shard_map/ppermute | solution.py:345
  21.0 5.1 %collective-permute-start.5 = (bf16[544,128]{1,0:T(8,128)(2,1)S(1)}, bf16[544,128]{1,0:T(8,128)(2,1)S(1)}, u32[]{:S(2)}, u32[]{:S(2)}) collective-permute-start(bf16[544,128]{1,0:T(8,128)(2,1)S(1)} %get-tuple-element.56.refs_2_), channel_id=1, source_target_pairs={{0,8},{1,9},{2,3},{3,2},{4,12},{5,13},{6,7},{7,6},{8,0},{9,1},{10,... | collective-permute-start | bytes 417800 | tf_op jit(solution)/shard_map/ppermute | solution.py:345
  24.2 4.4 %collective-permute-start.8 = (bf16[272,128]{1,0:T(8,128)(2,1)S(1)}, bf16[272,128]{1,0:T(8,128)(2,1)S(1)}, u32[]{:S(2)}, u32[]{:S(2)}) collective-permute-start(bf16[272,128]{1,0:T(8,128)(2,1)S(1)} %get-tuple-element.58.refs_2_), channel_id=1, source_target_pairs={{0,8},{1,9},{2,6},{3,7},{4,12},{5,13},{6,2},{7,3},{8,0},{9,1},{10,... | collective-permute-start | bytes 208904 | tf_op jit(solution)/shard_map/ppermute | solution.py:345
  26.2 5.4 %collective-permute-start.7 = (bf16[272,128]{1,0:T(8,128)(2,1)S(1)}, bf16[272,128]{1,0:T(8,128)(2,1)S(1)}, u32[]{:S(2)}, u32[]{:S(2)}) collective-permute-start(bf16[272,128]{1,0:T(8,128)(2,1)S(1)} %get-tuple-element.60.refs_2_), channel_id=1, source_target_pairs={{0,1},{1,0},{2,6},{3,7},{4,5},{5,4},{6,2},{7,3},{8,9},{9,8},{10,14... | collective-permute-start | bytes 208904 | tf_op jit(solution)/shard_map/ppermute | solution.py:345
  28.6 7.2 %collective-permute-start.10 = (bf16[272,128]{1,0:T(8,128)(2,1)S(1)}, bf16[272,128]{1,0:T(8,128)(2,1)S(1)}, u32[]{:S(2)}, u32[]{:S(2)}) collective-permute-start(bf16[272,128]{1,0:T(8,128)(2,1)S(1)} %shard_map.69.refs_2_.refs_0_), channel_id=1, source_target_pairs={{0,16},{1,17},{2,18},{3,19},{4,20},{5,21},{6,22},{7,23},{8,24},{9,... | collective-permute-start | bytes 208904 | tf_op jit(solution)/shard_map/ppermute | solution.py:345
  31.6 5.5 %collective-permute-start.9 = (bf16[272,128]{1,0:T(8,128)(2,1)S(1)}, bf16[272,128]{1,0:T(8,128)(2,1)S(1)}, u32[]{:S(2)}, u32[]{:S(2)}) collective-permute-start(bf16[272,128]{1,0:T(8,128)(2,1)S(1)} %shard_map.70.refs_2_.refs_0_), channel_id=1, source_target_pairs={{0,16},{1,17},{2,18},{3,19},{4,20},{5,21},{6,22},{7,23},{8,24},{9,... | collective-permute-start | bytes 208904 | tf_op jit(solution)/shard_map/ppermute | solution.py:345
  35.8 4.4 %collective-permute-start.12 = (bf16[272,128]{1,0:T(8,128)(2,1)S(1)}, bf16[272,128]{1,0:T(8,128)(2,1)S(1)}, u32[]{:S(2)}, u32[]{:S(2)}) collective-permute-start(bf16[272,128]{1,0:T(8,128)(2,1)S(1)} %shard_map.71.refs_2_.refs_0_), channel_id=1, source_target_pairs={{0,8},{1,9},{2,6},{3,7},{4,12},{5,13},{6,2},{7,3},{8,0},{9,1},{10,... | collective-permute-start | bytes 208904 | tf_op jit(solution)/shard_map/ppermute | solution.py:345
  37.1 4.5 %collective-permute-start.11 = (bf16[272,128]{1,0:T(8,128)(2,1)S(1)}, bf16[272,128]{1,0:T(8,128)(2,1)S(1)}, u32[]{:S(2)}, u32[]{:S(2)}) collective-permute-start(bf16[272,128]{1,0:T(8,128)(2,1)S(1)} %shard_map.72.refs_2_.refs_0_), channel_id=1, source_target_pairs={{0,1},{1,0},{2,6},{3,7},{4,5},{5,4},{6,2},{7,3},{8,9},{9,8},{10,14... | collective-permute-start | bytes 208904 | tf_op jit(solution)/shard_map/ppermute | solution.py:345
  40.2 5.1 %collective-permute-start.14 = (bf16[544,128]{1,0:T(8,128)(2,1)S(1)}, bf16[544,128]{1,0:T(8,128)(2,1)S(1)}, u32[]{:S(2)}, u32[]{:S(2)}) collective-permute-start(bf16[544,128]{1,0:T(8,128)(2,1)S(1)} %shard_map.73.refs_2_.refs_0_), channel_id=1, source_target_pairs={{0,4},{1,5},{2,3},{3,2},{4,0},{5,1},{6,7},{7,6},{8,12},{9,13},{10,... | collective-permute-start | bytes 417800 | tf_op jit(solution)/shard_map/ppermute | solution.py:345
  41.7 6.7 %collective-permute-start.13 = (bf16[544,128]{1,0:T(8,128)(2,1)S(1)}, bf16[544,128]{1,0:T(8,128)(2,1)S(1)}, u32[]{:S(2)}, u32[]{:S(2)}) collective-permute-start(bf16[544,128]{1,0:T(8,128)(2,1)S(1)} %shard_map.74.refs_2_.refs_0_), channel_id=1, source_target_pairs={{0,8},{1,9},{2,3},{3,2},{4,12},{5,13},{6,7},{7,6},{8,0},{9,1},{10,... | collective-permute-start | bytes 417800 | tf_op jit(solution)/shard_map/ppermute | solution.py:345
  45.4 6.6 %collective-permute-start.16 = (bf16[1088,128]{1,0:T(8,128)(2,1)S(1)}, bf16[1088,128]{1,0:T(8,128)(2,1)S(1)}, u32[]{:S(2)}, u32[]{:S(2)}) collective-permute-start(bf16[1088,128]{1,0:T(8,128)(2,1)S(1)} %shard_map.75.refs_2_.refs_0_), channel_id=1, source_target_pairs={{0,1},{1,0},{2,10},{3,11},{4,5},{5,4},{6,14},{7,15},{8,9},{9,8},{1... | collective-permute-start | bytes 835592 | tf_op jit(solution)/shard_map/ppermute | solution.py:345
  48.4 6.7 %collective-permute-start.15 = (bf16[1088,128]{1,0:T(8,128)(2,1)S(1)}, bf16[1088,128]{1,0:T(8,128)(2,1)S(1)}, u32[]{:S(2)}, u32[]{:S(2)}) collective-permute-start(bf16[1088,128]{1,0:T(8,128)(2,1)S(1)} %shard_map.76.refs_2_.refs_0_), channel_id=1, source_target_pairs={{0,4},{1,5},{2,10},{3,11},{4,0},{5,1},{6,14},{7,15},{8,12},{9,13},... | collective-permute-start | bytes 835592 | tf_op jit(solution)/shard_map/ppermute | solution.py:345
  52.0 3.2 %collective-permute-start.18 = (bf16[2176,128]{1,0:T(8,128)(2,1)S(1)}, bf16[2176,128]{1,0:T(8,128)(2,1)S(1)}, u32[]{:S(2)}, u32[]{:S(2)}) collective-permute-start(bf16[2176,128]{1,0:T(8,128)(2,1)S(1)} %shard_map.77.refs_2_.refs_0_), channel_id=1, source_target_pairs={{0,2},{1,3},{2,0},{3,1},{4,6},{5,7},{6,4},{7,5},{8,10},{9,11},{10,... | collective-permute-start | bytes 1671176 | tf_op jit(solution)/shard_map/ppermute | solution.py:341
  55.1 2.1 %collective-permute-start.17 = (bf16[2176,128]{1,0:T(8,128)(2,1)S(1)}, bf16[2176,128]{1,0:T(8,128)(2,1)S(1)}, u32[]{:S(2)}, u32[]{:S(2)}) collective-permute-start(bf16[2176,128]{1,0:T(8,128)(2,1)S(1)} %shard_map.78.refs_2_), channel_id=1, source_target_pairs={{0,2},{1,3},{2,0},{3,1},{4,6},{5,7},{6,4},{7,5},{8,10},{9,11},{10,... | collective-permute-start | bytes 1671176 | tf_op jit(solution)/shard_map/ppermute | solution.py:341

commit v4 on v3

--- a/solution.py
+++ b/solution.py
@@ -15,6 +15,7 @@
 LANE_TURNS = (((0, 1, 2), (2, 0, 1)), ((1, 2, 0), (2, 0, 1)))
 f32, bf16 = jnp.float32, jnp.bfloat16
 
+WRITES = (((0, 0), (0, 2)), ((0, 1), (1, 0), (1, 2)), ((0, 3), (1, 1)), ((1, 3),))
 STEP_COST = pl.CostEstimate(flops=4 * 10**9, bytes_accessed=8 * 10**7, transcendentals=0)
 
 
@@ -51,6 +52,13 @@
 
 def bit_of(value, bit):
     return lax.rem(lax.div(value, jnp.int32(1 << bit)), jnp.int32(2))
+
+
+def half_of(flat, bits):
+    total = jnp.int32(0)
+    for bit in range(bits):
+        total = total + bit_of(flat, bit)
+    return lax.rem(total, jnp.int32(2))
 
 
 def sigmoid(value):
@@ -152,20 +160,25 @@
 
 def second_taps(x2, own_first, keep, send, first_tap, last_tap):
     columns = slice(first_tap * LANES, last_tap * LANES)
-    rows = (last_tap - first_tap) * LANES
+    rows = (last_tap - first_tap) * LANES // 2
+    half = keep.shape[0] // 2
     grad = dot(x2[:, columns], own_first, ((0,), (0,)))
-    keep[0:rows, :] = grad[:, :LANES]
-    send[0:rows, :] = grad[:, LANES:].astype(bf16)
+    for v in range(2):
+        keep[v * half : v * half + rows, :] = grad[v * rows : (v + 1) * rows, :LANES]
+        send[v * half : v * half + rows, :] = grad[v * rows : (v + 1) * rows, LANES:].astype(bf16)
 
 
 def clear(keep, send, start):
-    if start < keep.shape[0]:
-        keep[start:, :] = jnp.zeros((keep.shape[0] - start, LANES), f32)
-        send[start:, :] = jnp.zeros((keep.shape[0] - start, LANES), bf16)
+    half = keep.shape[0] // 2
+    if start < half:
+        for v in range(2):
+            rows = slice(v * half + start, (v + 1) * half)
+            keep[rows, :] = jnp.zeros((half - start, LANES), f32)
+            send[rows, :] = jnp.zeros((half - start, LANES), bf16)
 
 
 def lower_kernel(
-    core_bit, spatial_count, halo, low, w1p, picked_up, w2, cot,
+    bits, spatial_count, halo, low, w1p, picked_up, w2, cot,
     keep, send, x1, slope, x2, d2, own_first, vpad, picked,
 ):
     inside = jnp.where(lax.axis_index("spatial") > 0, 1.0, 0.0).astype(f32)
@@ -187,17 +200,17 @@
     sig = sigmoid(second_pre)
     delta = cot[...] * slope_of(second_pre, sig)
     d2[...] = delta.astype(bf16)
-    core = bit_of(flat_index(spatial_count), core_bit)
+    core = half_of(flat_index(spatial_count), bits)
     left, right = delta[:, :LANES], delta[:, LANES:]
     own_first[...] = jnp.concatenate(
         [jnp.where(core == 0, left, right), jnp.where(core == 0, right, left)], 1
     ).astype(bf16)
     second_taps(x2, own_first[...], keep, send, 0, SPLIT)
-    clear(keep, send, SPLIT * LANES)
+    clear(keep, send, SPLIT * LANES // 2)
 
 
 def last_kernel(
-    core_bit, spatial_count, x1_up, x1_low, slope_up, slope_low, x2, d2, own_first, w2,
+    bits, spatial_count, x1_up, x1_low, slope_up, slope_low, x2, d2, own_first, w2,
     keep, send, g1,
 ):
     second_taps(x2, own_first[...], keep, send, SPLIT, 27)
@@ -237,13 +250,15 @@
         for b in range(3):
             at = (a * 3 + b) * 192
             g1[at : at + 192, :] = grad[b * 256 + 64 : (b + 1) * 256]
-    core = bit_of(flat_index(spatial_count), core_bit)
-    start = (27 - SPLIT) * LANES
-    mine = pl.ds(pl.multiple_of(core * FIRST, 8), FIRST)
-    other = pl.ds(pl.multiple_of((1 - core) * FIRST, 8), FIRST)
-    keep[start : start + FIRST, :] = g1[mine, :]
-    send[start : start + FIRST, :] = g1[other, :].astype(bf16)
-    clear(keep, send, start + FIRST)
+    core = half_of(flat_index(spatial_count), bits)
+    start, quarter = (27 - SPLIT) * LANES // 2, FIRST // 2
+    for v in range(2):
+        rows = slice(v * (keep.shape[0] // 2) + start, v * (keep.shape[0] // 2) + start + quarter)
+        mine = pl.ds(pl.multiple_of(core * FIRST + v * quarter, 8), quarter)
+        other = pl.ds(pl.multiple_of((1 - core) * FIRST + v * quarter, 8), quarter)
+        keep[rows, :] = g1[mine, :]
+        send[rows, :] = g1[other, :].astype(bf16)
+    clear(keep, send, start + quarter)
 
 
 def side_of(flat, orders, core, step):
@@ -251,10 +266,10 @@
     return jnp.where(core == 0, first, second)
 
 
-def reduce_kernel(orders, core_bit, step, spatial_count, keep, recv, kept, gone):
+def reduce_kernel(orders, bits, step, spatial_count, keep, recv, kept, gone):
     half = keep.shape[0] // 2
     flat = flat_index(spatial_count)
-    bit = side_of(flat, orders, bit_of(flat, core_bit), step)
+    bit = side_of(flat, orders, half_of(flat, bits), step)
     mine = pl.ds(pl.multiple_of(bit * half, 16), half)
     other = pl.ds(pl.multiple_of((1 - bit) * half, 16), half)
     kept[...] = keep[mine, :] + recv[mine, :].astype(f32)
@@ -271,48 +286,54 @@
     out[half:, :] = recv[...]
 
 
-def write_half(flat, side, orders, chunk, segments, part, wide, grad_first, grad_second, sems):
+def copy_kernel(got, out):
+    out[...] = got[...]
+
+
+def start_part(flat, side, orders, chunk, segments, last, part, wide, grad_first, grad_second, sems):
     steps = len(orders[0]) - 1
     bits = [side_of(flat, orders, side, s) for s in range(steps)]
     columns = pl.ds(pl.multiple_of(side * LANES, LANES), LANES)
+    top = 1 - bits[0] if last else bits[0]
     copies = []
-    for place in range(1 << steps):
+    for place in range(1 << (steps - 1)):
         position = jnp.int32(0)
-        for s in range(steps):
+        for s in range(1, steps):
             want = (place >> (steps - 1 - s)) & 1
             differs = (1 - bits[s]) if want else bits[s]
             position = position + differs * (1 << (steps - 1 - s))
+        at = place * chunk
         rows = pl.ds(pl.multiple_of(position * chunk, 16), chunk)
-        at = place * chunk
         wide[at : at + chunk, :] = part[rows, :].astype(f32)
         for start, size, second, base in segments:
             low, high = max(start, at), min(start + size, at + chunk)
             if low >= high:
                 continue
-            to = base + low - start
+            to = top * size + base + low - start
             if second:
-                target = grad_second.at[to : to + high - low, columns]
+                target = grad_second.at[pl.ds(pl.multiple_of(to, 16), high - low), columns]
             else:
-                target = grad_first.at[
-                    pl.ds(pl.multiple_of(side * FIRST + to, 16), high - low)
-                ]
+                to = pl.multiple_of(side * FIRST + to, 16)
+                target = grad_first.at[pl.ds(to, high - low)]
             copy = pltpu.make_async_copy(wide.at[low:high], target, sems.at[len(copies)])
             copy.start()
             copies.append(copy)
     return copies
 
 
-def final_kernel(core_bit, spatial_count, jobs, *refs):
+def final_kernel(bits, spatial_count, jobs, chained, *refs):
     count = len(jobs)
-    grad_first, grad_second = refs[-2 * count - 2 : -2 * count]
+    tokens = refs[count + 2 * chained + 2 : -2 * count]
+    grad_first, grad_second = refs[count + 2 * chained : count + 2 * chained + 2]
     wides, sems = refs[-2 * count : -count], refs[-count:]
     flat = flat_index(spatial_count)
-    core = bit_of(flat, core_bit)
+    core = half_of(flat, bits)
+    for token in tokens:
+        token[...] = jnp.zeros(token.shape, f32)
     copies = []
-    for index, (own, orders, chunk, segments) in enumerate(jobs):
-        side = core if own else 1 - core
-        copies += write_half(
-            flat, side, orders, chunk, segments,
+    for index, (own, orders, chunk, segments, last) in enumerate(jobs):
+        copies += start_part(
+            flat, core if own else 1 - core, orders, chunk, segments, last,
             refs[index], wides[index], grad_first, grad_second, sems[index],
         )
     for copy in copies:
@@ -329,19 +350,23 @@
         [tuple(turn[i] for i in turns) + tuple(rest) for turns in lane] for lane in LANE_TURNS
     ]
     steps = len(others) - 1
+    lanes = len(LANE_TURNS)
     unit = 16 << steps
-    second_rest = (27 - SPLIT) * LANES
+    second_rest = (27 - SPLIT) * LANES // 2
     segments = [
-        [(0, SPLIT * LANES, True, 0)],
-        [(0, second_rest, True, SPLIT * LANES), (second_rest, FIRST, False, 0)],
+        [(0, SPLIT * LANES // 2, True, 0)],
+        [(0, second_rest, True, SPLIT * LANES), (second_rest, FIRST // 2, False, 0)],
     ]
-    chunks = [-(-sum(seg[1] for seg in lane) // unit) * 16 for lane in segments]
+    chunks = [-(-2 * sum(seg[1] for seg in lane) // unit) * 16 for lane in segments]
 
     def swap_core(array):
         return lax.ppermute(array, BOTH, [(i, i ^ (1 << core_bit)) for i in range(count)])
 
     def swap(array, lane, step):
-        pairs = [(i, i ^ (1 << orders[lane][(i >> core_bit) & 1][step])) for i in range(count)]
+        pairs = []
+        for i in range(count):
+            bit = orders[lane][i.bit_count() % 2][step]
+            pairs.append((i, i ^ (1 << bit) ^ (1 << core_bit)))
         return lax.ppermute(array, BOTH, pairs)
 
     slab = volume[0]
@@ -391,7 +416,7 @@
     )
     rows = [chunk << steps for chunk in chunks]
     keep0, send0, x1_low, slope_low, x2, d2, own_first = call(
-        functools.partial(lower_kernel, core_bit, spatial_count),
+        functools.partial(lower_kernel, bits, spatial_count),
         [
             ((rows[0], LANES), f32),
             ((rows[0], LANES), bf16),
@@ -411,7 +436,7 @@
     )
     recv0 = swap_core(send0)
     keep1, send1 = call(
-        functools.partial(last_kernel, core_bit, spatial_count),
+        functools.partial(last_kernel, bits, spatial_count),
         [((rows[1], LANES), f32), ((rows[1], LANES), bf16)],
         x1_up,
         x1_low,
@@ -425,13 +450,13 @@
         cost=pl.CostEstimate(flops=10**9, bytes_accessed=10**7, transcendentals=0),
     )
     recv1 = swap_core(send1)
-    keep, recv, own = [keep0, keep1], [recv0, recv1], [None, None]
+    keep, recv = [keep0, keep1], [recv0, recv1]
     last = send1
     for step in range(steps):
-        for lane in range(2):
+        for lane in range(lanes):
             half = keep[lane].shape[0] // 2
             keep[lane], last = call(
-                functools.partial(reduce_kernel, orders[lane], core_bit, step, spatial_count),
+                functools.partial(reduce_kernel, orders[lane], bits, step, spatial_count),
                 [((half, LANES), f32), ((half, LANES), bf16)],
                 keep[lane],
                 recv[lane],
@@ -440,32 +465,48 @@
             )
             recv[lane] = swap(last, lane, step)
     for turn in range(2):
-        for lane in range(2):
+        for lane in range(lanes):
             shape = [((chunks[lane], LANES), bf16)]
             last = call(sum_kernel, shape, keep[lane], recv[lane], after=(last,), cost=STEP_COST)[0]
             keep[lane], recv[lane] = last, swap(last, lane, steps - turn)
-    for step in reversed(range(steps)):
-        for lane in range(2):
+    for step in reversed(range(1, steps)):
+        for lane in range(lanes):
             shape = [((2 * keep[lane].shape[0], LANES), bf16)]
-            last = call(join_kernel, shape, keep[lane], recv[lane], after=(last,), cost=STEP_COST)[0]
-            keep[lane] = last
-            recv[lane] = swap(last, lane, step - 1) if step else swap_core(last)
+            last = call(
+                join_kernel, shape, keep[lane], recv[lane], after=(last,), cost=STEP_COST
+            )[0]
+            keep[lane], recv[lane] = last, swap(last, lane, step - 1)
+    held = [[keep[lane], None, swap_core(keep[lane]), None] for lane in range(lanes)]
     shapes = [jax.ShapeDtypeStruct((2 * FIRST, LANES), f32)]
     shapes += [jax.ShapeDtypeStruct((SECOND, 2 * LANES), f32)]
-    grads = ()
-    for group in (((0, True), (0, False), (1, True)), ((1, False),)):
-        parts = [keep[lane] if mine else recv[lane] for lane, mine in group]
-        jobs = [(mine, orders[lane], chunks[lane], segments[lane]) for lane, mine in group]
-        grads = pl.pallas_call(
-            functools.partial(final_kernel, core_bit, spatial_count, jobs),
-            out_shape=shapes,
+    token_shape = [jax.ShapeDtypeStruct((8, LANES), f32)]
+    grads = []
+
+    def write(group, grads, token):
+        parts = [held[lane][which] for lane, which in group]
+        jobs = [
+            (which < 2, orders[lane], chunks[lane], segments[lane], which % 2 == 1)
+            for lane, which in group
+        ]
+        return pl.pallas_call(
+            functools.partial(final_kernel, bits, spatial_count, jobs, bool(grads)),
+            out_shape=shapes + token_shape * token,
             in_specs=[full(part.shape) for part in parts] + [outside] * len(grads),
-            out_specs=[outside] * 2,
-            scratch_shapes=[pltpu.VMEM((rows[lane], LANES), f32) for lane, _ in group]
+            out_specs=[outside] * 2 + [full(None)] * token,
+            scratch_shapes=[pltpu.VMEM((rows[lane] // 2, LANES), f32) for lane, _ in group]
             + [pltpu.SemaphoreType.DMA(((1 << steps) + 1,)) for _ in group],
             input_output_aliases={len(parts): 0, len(parts) + 1: 1} if grads else {},
             compiler_params=params(),
+            cost_estimate=STEP_COST,
         )(*parts, *grads)
+
+    for lane, group in enumerate(WRITES[:lanes]):
+        *grads, token = write(group, grads, 1)
+        shape = [(recv[lane].shape, bf16)]
+        last = call(copy_kernel, shape, recv[lane], after=(last, token), cost=STEP_COST)[0]
+        held[lane][1], held[lane][3] = last, swap_core(last)
+    for group in WRITES[lanes:]:
+        grads = write(group, grads, 0)
     return grads
 
 

time: 58.5 us -> 55.8 us (0.954)
  waiting for transfers between devices: 17.5 us -> 11.6 us
  starting transfers between devices: 29 us -> 30.7 us
  Pallas kernels: 11.1 us -> 12.6 us
    ppermute x14, waiting for transfers between devices: 17 us -> 11 us  [swap(): return lax.ppermute(array, BOTH, pairs)]
    ppermute x4 -> x6, starting transfers between devices: 0.77 us -> 3.15 us  [swap_core(): lax.ppermute(array, BOTH, [(i, i ^ 1 << core_bit) for i in range(count)])]
    pallas_call x2 -> x4, Pallas kernels: 3.07 us -> 4.6 us  [write(): pl.pallas_call(functools.partial(final_kernel, bits, spatial_count, jobs,...]
    ppermute x14, starting transfers between devices: 25.2 us -> 24.5 us  [swap(): return lax.ppermute(array, BOTH, pairs)]
  transfers between devices with their start and end apart: 19 -> 21, of which waited for: 10 -> 9; matrix products, arithmetic and copies ran while one was open for 0% -> 0% of each run, Pallas kernels for 12% -> 15%
where the time goes in v4:
time: 55.8 us; the launch traced here: 55.7 us
  starting transfers between devices  30.7 us (55%)
  Pallas kernels  12.6 us (23%)
  waiting for transfers between devices  11.6 us (21%)
  between operations  0.76 us (1%)
    ppermute x14, starting transfers between devices, swap(): return lax.ppermute(array, BOTH, pairs)  24.5 us
    ppermute x14, waiting for transfers between devices, swap(): return lax.ppermute(array, BOTH, pairs)  11 us
    pallas_call x20, Pallas kernels, call(): pl.pallas_call(run, out_shape=shapes, in_specs=(specs or [full(a.shape) f...  7.98 us
    pallas_call x4, Pallas kernels, write(): pl.pallas_call(functools.partial(final_kernel, bits, spatial_count, jobs,...  4.6 us
    ppermute x6, starting transfers between devices, swap_core(): lax.ppermute(array, BOTH, [(i, i ^ 1 << core_bit) for i in range(count)])  3.15 us
    ppermute x1, starting transfers between devices, body(): lax.ppermute(face, 'spatial', [(i, (i + 1) % spatial_count) for i in rang...  3 us
  transfers between devices with their start and end apart: 21, of which 9 were waited for; matrix products, arithmetic and copies ran while one was open for 0% of the time, Pallas kernels for 15%

profile of v4, /device:TPU:0, one launch (start us, length us, event | category | flops | bytes accessed | tf_op | source)
XLA Modules:
  0.0 55.7 jit_solution(9062276036225549265)
XLA Ops:
  0.6 1.3 %shard_map.59 = (bf16[3,16,1024]{2,1,0:T(8,128)(2,1)S(1)}, bf16[2,16,1024]{2,1,0:T(8,128)(2,1)S(1)}, bf16[448,2304]{1,0:T(8,128)(2,1)S(1)}, bf16[2304,128]{1,0:T(8,128)(2,1)S(1)}) custom-call(bf16[16,16,1024]{2,1,0:T(8,128)(2,1)} %bitcast.2, bf16[1728,128]{1,0:T(8,128)(2,1)} %refs_1_.1), custom_call_target="tpu_custom_call" | custom-call | tf_op jit(solution)/shard_map/pallas_call | solution.py:37
  2.0 3.0 %collective-permute-start = (bf16[3,16,1024]{2,1,0:T(8,128)(2,1)S(1)}, bf16[3,16,1024]{2,1,0:T(8,128)(2,1)S(1)}, u32[]{:S(2)}, u32[]{:S(2)}) collective-permute-start(bf16[3,16,1024]{2,1,0:T(8,128)(2,1)S(1)} %get-tuple-element.40), channel_id=1, source_target_pairs={{0,1},{1,0},{2,3},{3,2},{4,5},{5,4},{6,7},{7,6},{8,9},{9,8},{10,11... | collective-permute-start | bytes 294920 | tf_op jit(solution)/shard_map/ppermute | solution.py:397
  5.0 2.3 %shard_map.60 = (f32[448,128]{1,0:T(8,128)S(1)}, bf16[1008,128]{1,0:T(8,128)(2,1)S(1)}, bf16[3456,256]{1,0:T(8,128)(2,1)S(1)}, f32[64,256]{1,0:T(8,128)S(1)}) custom-call(bf16[448,2304]{1,0:T(8,128)(2,1)S(1)} %get-tuple-element.39.refs_0_, bf16[2304,128]{1,0:T(8,128)(2,1)S(1)} %get-tuple-element.42.refs_1_.refs_2_, bf16[3456,256]{1,0:T(8,128)(2,1)} %refs_2_.1, ...), custom_call_target="tpu_custom_call" | custom-call | flops 400000000 | bytes 10000000 | tf_op jit(solution)/shard_map/pallas_call | solution.py:37
  7.3 0.5 collective-permute-done.refs_0_
  7.8 1.7 %shard_map.61 = (f32[2176,128]{1,0:T(8,128)S(1)}, bf16[2176,128]{1,0:T(8,128)(2,1)S(1)}, bf16[128,2304]{1,0:T(8,128)(2,1)S(1)}, f32[128,128]{1,0:T(8,128)S(1)}, ...) custom-call(bf16[3,16,1024]{2,1,0:T(8,128)(2,1)S(1)} %collective-permute-done.refs_0_, ...), custom_call_target="tpu_custom_call" | custom-call | tf_op jit(solution)/shard_map/pallas_call | solution.py:37
  9.5 0.1 collective-permute-start.2
  9.6 2.1 %shard_map.62 = (f32[2176,128]{1,0:T(8,128)S(1)}, bf16[2176,128]{1,0:T(8,128)(2,1)S(1)}) custom-call(bf16[448,2304]{1,0:T(8,128)(2,1)S(1)} %get-tuple-element.39.refs_0_, bf16[128,2304]{1,0:T(8,128)(2,1)S(1)} %get-tuple-element.46.refs_1_, f32[448,128]{1,0:T(8,128)S(1)} %get-tuple-element.47.refs_2_, f32[128,128]{1,0:T(8,128)S(1)} %get-tuple-element.48.refs_3_, ...), custom_call_target="tpu_custom_call" | custom-call | flops 1000000000 | bytes 10000000 | tf_op jit(solution)/shard_map/pallas_call | solution.py:37
  11.7 0.6 %collective-permute-start.1 = (bf16[2176,128]{1,0:T(8,128)(2,1)S(1)}, bf16[2176,128]{1,0:T(8,128)(2,1)S(1)}, u32[]{:S(2)}, u32[]{:S(2)}) collective-permute-start(bf16[2176,128]{1,0:T(8,128)(2,1)S(1)} %get-tuple-element.53.refs_2_), channel_id=1, source_target_pairs={{0,2},{1,3},{2,0},{3,1},{4,6},{5,7},{6,4},{7,5},{8,10},{9,11},{10,... | collective-permute-start | bytes 1671176 | tf_op jit(solution)/shard_map/ppermute | solution.py:363
  12.3 0.0 collective-permute-done.2.refs_1_
  12.3 0.1 shard_map.63
  12.4 1.5 %collective-permute-start.4 = (bf16[1088,128]{1,0:T(8,128)(2,1)S(1)}, bf16[1088,128]{1,0:T(8,128)(2,1)S(1)}, u32[]{:S(2)}, u32[]{:S(2)}) collective-permute-start(bf16[1088,128]{1,0:T(8,128)(2,1)S(1)} %get-tuple-element.56.refs_2_), channel_id=1, source_target_pairs={{0,3},{1,11},{2,8},{3,0},{4,14},{5,6},{6,5},{7,13},{8,2},{9,10},{1... | collective-permute-start | bytes 835592 | tf_op jit(solution)/shard_map/ppermute | solution.py:370
  13.9 0.0 collective-permute-done.1.refs_1_
  13.9 0.1 shard_map.64
  14.0 1.8 %collective-permute-start.3 = (bf16[1088,128]{1,0:T(8,128)(2,1)S(1)}, bf16[1088,128]{1,0:T(8,128)(2,1)S(1)}, u32[]{:S(2)}, u32[]{:S(2)}) collective-permute-start(bf16[1088,128]{1,0:T(8,128)(2,1)S(1)} %get-tuple-element.58.refs_2_), channel_id=1, source_target_pairs={{0,6},{1,11},{2,8},{3,5},{4,14},{5,3},{6,0},{7,13},{8,2},{9,15},{1... | collective-permute-start | bytes 835592 | tf_op jit(solution)/shard_map/ppermute | solution.py:370
  15.8 2.6 %collective-permute-done.4.refs_1_ = bf16[1088,128]{1,0:T(8,128)(2,1)S(1)} collective-permute-done((bf16[1088,128]{1,0:T(8,128)(2,1)S(1)}, bf16[1088,128]{1,0:T(8,128)(2,1)S(1)}, u32[]{:S(2)}, u32[]{:S(2)}) %collective-permute-start.4) | collective-permute-done | bytes 278560 | tf_op jit(solution)/shard_map/ppermute | solution.py:370
  18.4 0.1 shard_map.65
  18.5 1.9 %collective-permute-start.6 = (bf16[544,128]{1,0:T(8,128)(2,1)S(1)}, bf16[544,128]{1,0:T(8,128)(2,1)S(1)}, u32[]{:S(2)}, u32[]{:S(2)}) collective-permute-start(bf16[544,128]{1,0:T(8,128)(2,1)S(1)} %get-tuple-element.60.refs_2_), channel_id=1, source_target_pairs={{0,6},{1,2},{2,1},{3,5},{4,7},{5,3},{6,0},{7,4},{8,11},{9,15},{10,... | collective-permute-start | bytes 417800 | tf_op jit(solution)/shard_map/ppermute | solution.py:370
  20.3 0.0 collective-permute-done.3.refs_1_
  20.3 0.1 shard_map.66
  20.4 1.9 %collective-permute-start.5 = (bf16[544,128]{1,0:T(8,128)(2,1)S(1)}, bf16[544,128]{1,0:T(8,128)(2,1)S(1)}, u32[]{:S(2)}, u32[]{:S(2)}) collective-permute-start(bf16[544,128]{1,0:T(8,128)(2,1)S(1)} %get-tuple-element.62.refs_2_), channel_id=1, source_target_pairs={{0,10},{1,2},{2,1},{3,9},{4,7},{5,15},{6,12},{7,4},{8,11},{9,3},{1... | collective-permute-start | bytes 417800 | tf_op jit(solution)/shard_map/ppermute | solution.py:370
  22.3 0.8 %collective-permute-done.6.refs_1_ = bf16[544,128]{1,0:T(8,128)(2,1)S(1)} collective-permute-done((bf16[544,128]{1,0:T(8,128)(2,1)S(1)}, bf16[544,128]{1,0:T(8,128)(2,1)S(1)}, u32[]{:S(2)}, u32[]{:S(2)}) %collective-permute-start.6) | collective-permute-done | bytes 139296 | tf_op jit(solution)/shard_map/ppermute | solution.py:370
  23.1 1.9 %collective-permute-start.8 = (bf16[272,128]{1,0:T(8,128)(2,1)S(1)}, bf16[272,128]{1,0:T(8,128)(2,1)S(1)}, u32[]{:S(2)}, u32[]{:S(2)}) collective-permute-start(bf16[272,128]{1,0:T(8,128)(2,1)S(1)} %get-tuple-element.64.refs_2_), channel_id=1, source_target_pairs={{0,10},{1,7},{2,4},{3,9},{4,2},{5,15},{6,12},{7,1},{8,14},{9,3},{1... | collective-permute-start | bytes 208904 | tf_op jit(solution)/shard_map/ppermute | solution.py:370
  25.0 0.1 collective-permute-done.5.refs_1_
  25.1 2.0 %collective-permute-start.7 = (bf16[272,128]{1,0:T(8,128)(2,1)S(1)}, bf16[272,128]{1,0:T(8,128)(2,1)S(1)}, u32[]{:S(2)}, u32[]{:S(2)}) collective-permute-start(bf16[272,128]{1,0:T(8,128)(2,1)S(1)} %get-tuple-element.66.refs_2_), channel_id=1, source_target_pairs={{0,3},{1,7},{2,4},{3,0},{4,2},{5,6},{6,5},{7,1},{8,14},{9,10},{10,... | collective-permute-start | bytes 208904 | tf_op jit(solution)/shard_map/ppermute | solution.py:370
  27.1 0.0 collective-permute-done.8.refs_1_
  27.1 2.7 %collective-permute-start.10 = (bf16[272,128]{1,0:T(8,128)(2,1)S(1)}, bf16[272,128]{1,0:T(8,128)(2,1)S(1)}, u32[]{:S(2)}, u32[]{:S(2)}) collective-permute-start(bf16[272,128]{1,0:T(8,128)(2,1)S(1)} %shard_map.69.refs_2_.refs_0_), channel_id=1, source_target_pairs={{0,18},{1,19},{2,16},{3,17},{4,22},{5,23},{6,20},{7,21},{8,26},{9,... | collective-permute-start | bytes 208904 | tf_op jit(solution)/shard_map/ppermute | solution.py:370
  29.8 0.0 collective-permute-done.7.refs_1_
  29.8 2.5 %collective-permute-start.9 = (bf16[272,128]{1,0:T(8,128)(2,1)S(1)}, bf16[272,128]{1,0:T(8,128)(2,1)S(1)}, u32[]{:S(2)}, u32[]{:S(2)}) collective-permute-start(bf16[272,128]{1,0:T(8,128)(2,1)S(1)} %shard_map.70.refs_2_.refs_0_), channel_id=1, source_target_pairs={{0,18},{1,19},{2,16},{3,17},{4,22},{5,23},{6,20},{7,21},{8,26},{9,... | collective-permute-start | bytes 208904 | tf_op jit(solution)/shard_map/ppermute | solution.py:370
  32.3 0.0 collective-permute-done.10.refs_1_
  32.3 1.8 %collective-permute-start.12 = (bf16[272,128]{1,0:T(8,128)(2,1)S(1)}, bf16[272,128]{1,0:T(8,128)(2,1)S(1)}, u32[]{:S(2)}, u32[]{:S(2)}) collective-permute-start(bf16[272,128]{1,0:T(8,128)(2,1)S(1)} %shard_map.71.refs_2_.refs_0_), channel_id=1, source_target_pairs={{0,10},{1,7},{2,4},{3,9},{4,2},{5,15},{6,12},{7,1},{8,14},{9,3},{1... | collective-permute-start | bytes 208904 | tf_op jit(solution)/shard_map/ppermute | solution.py:370
  34.2 2.9 %collective-permute-done.9.refs_1_ = bf16[272,128]{1,0:T(8,128)(2,1)S(1)} collective-permute-done((bf16[272,128]{1,0:T(8,128)(2,1)S(1)}, bf16[272,128]{1,0:T(8,128)(2,1)S(1)}, u32[]{:S(2)}, u32[]{:S(2)}) %collective-permute-start.9) | collective-permute-done | bytes 69664 | tf_op jit(solution)/shard_map/ppermute | solution.py:370
  37.1 1.4 %collective-permute-start.11 = (bf16[272,128]{1,0:T(8,128)(2,1)S(1)}, bf16[272,128]{1,0:T(8,128)(2,1)S(1)}, u32[]{:S(2)}, u32[]{:S(2)}) collective-permute-start(bf16[272,128]{1,0:T(8,128)(2,1)S(1)} %shard_map.72.refs_2_.refs_0_), channel_id=1, source_target_pairs={{0,3},{1,7},{2,4},{3,0},{4,2},{5,6},{6,5},{7,1},{8,14},{9,10},{10,... | collective-permute-start | bytes 208904 | tf_op jit(solution)/shard_map/ppermute | solution.py:370
  38.5 0.0 collective-permute-done.12.refs_1_
  38.5 0.6 %collective-permute-start.14 = (bf16[544,128]{1,0:T(8,128)(2,1)S(1)}, bf16[544,128]{1,0:T(8,128)(2,1)S(1)}, u32[]{:S(2)}, u32[]{:S(2)}) collective-permute-start(bf16[544,128]{1,0:T(8,128)(2,1)S(1)} %shard_map.73.refs_2_.refs_0_), channel_id=1, source_target_pairs={{0,6},{1,2},{2,1},{3,5},{4,7},{5,3},{6,0},{7,4},{8,11},{9,15},{10,... | collective-permute-start | bytes 417800 | tf_op jit(solution)/shard_map/ppermute | solution.py:370
  39.2 1.7 %collective-permute-done.11.refs_1_ = bf16[272,128]{1,0:T(8,128)(2,1)S(1)} collective-permute-done((bf16[272,128]{1,0:T(8,128)(2,1)S(1)}, bf16[272,128]{1,0:T(8,128)(2,1)S(1)}, u32[]{:S(2)}, u32[]{:S(2)}) %collective-permute-start.11) | collective-permute-done | bytes 69664 | tf_op jit(solution)/shard_map/ppermute | solution.py:370
  40.9 0.4 collective-permute-start.13
  41.3 1.8 %collective-permute-done.14.refs_1_ = bf16[544,128]{1,0:T(8,128)(2,1)S(1)} collective-permute-done((bf16[544,128]{1,0:T(8,128)(2,1)S(1)}, bf16[544,128]{1,0:T(8,128)(2,1)S(1)}, u32[]{:S(2)}, u32[]{:S(2)}) %collective-permute-start.14) | collective-permute-done | bytes 139296 | tf_op jit(solution)/shard_map/ppermute | solution.py:370
  43.1 1.3 %collective-permute-start.17 = (bf16[1088,128]{1,0:T(8,128)(2,1)S(1)}, bf16[1088,128]{1,0:T(8,128)(2,1)S(1)}, u32[]{:S(2)}, u32[]{:S(2)}) collective-permute-start(bf16[1088,128]{1,0:T(8,128)(2,1)S(1)} %shard_map.75.refs_2_.refs_0_), channel_id=1, source_target_pairs={{0,2},{1,3},{2,0},{3,1},{4,6},{5,7},{6,4},{7,5},{8,10},{9,11},{10,... | collective-permute-start | bytes 835592 | tf_op jit(solution)/shard_map/ppermute | solution.py:363
  44.5 1.4 %collective-permute-start.16 = (bf16[1088,128]{1,0:T(8,128)(2,1)S(1)}, bf16[1088,128]{1,0:T(8,128)(2,1)S(1)}, u32[]{:S(2)}, u32[]{:S(2)}) collective-permute-start(bf16[1088,128]{1,0:T(8,128)(2,1)S(1)} %shard_map.75.refs_2_.refs_0_), channel_id=1, source_target_pairs={{0,3},{1,11},{2,8},{3,0},{4,14},{5,6},{6,5},{7,13},{8,2},{9,10},{1... | collective-permute-start | bytes 835592 | tf_op jit(solution)/shard_map/ppermute | solution.py:370
  45.9 0.0 collective-permute-done.13.refs_1_
  45.9 0.1 collective-permute-start.18
  46.0 2.7 %collective-permute-start.15 = (bf16[1088,128]{1,0:T(8,128)(2,1)S(1)}, bf16[1088,128]{1,0:T(8,128)(2,1)S(1)}, u32[]{:S(2)}, u32[]{:S(2)}) collective-permute-start(bf16[1088,128]{1,0:T(8,128)(2,1)S(1)} %shard_map.76.refs_1_), channel_id=1, source_target_pairs={{0,6},{1,11},{2,8},{3,5},{4,14},{5,3},{6,0},{7,13},{8,2},{9,15},{1... | collective-permute-start | bytes 835592 | tf_op jit(solution)/shard_map/ppermute | solution.py:370
  48.7 0.0 collective-permute-done.17.refs_1_
  48.7 1.2 %shard_map.77 = (f32[1728,128]{1,0:T(8,128)}, f32[3456,256]{1,0:T(8,128)}, f32[8,128]{1,0:T(8,128)S(1)}) custom-call(bf16[1088,128]{1,0:T(8,128)(2,1)S(1)} %shard_map.75.refs_2_.refs_0_, bf16[1088,128]{1,0:T(8,128)(2,1)S(1)} %collective-permute-done.17.refs_1_), custom_call_target="tpu_custom_call" | custom-call | flops 4000000000 | bytes 80000000 | tf_op jit(solution)/shard_map/pallas_call | solution.py:491
  49.9 0.6 %collective-permute-done.16.refs_0_ = bf16[1088,128]{1,0:T(8,128)(2,1)S(1)} collective-permute-done((bf16[1088,128]{1,0:T(8,128)(2,1)S(1)}, bf16[1088,128]{1,0:T(8,128)(2,1)S(1)}, u32[]{:S(2)}, u32[]{:S(2)}) %collective-permute-start.16) | collective-permute-done | bytes 278560 | tf_op jit(solution)/shard_map/ppermute | solution.py:370
  50.4 0.4 collective-permute-start.20
  50.9 0.0 collective-permute-done.18.refs_2_
  50.9 1.4 %shard_map.79 = (f32[1728,128]{1,0:T(8,128)}, f32[3456,256]{1,0:T(8,128)}, f32[8,128]{1,0:T(8,128)S(1)}) custom-call(bf16[1088,128]{1,0:T(8,128)(2,1)S(1)} %shard_map.78.refs_0_.refs_1_, bf16[1088,128]{1,0:T(8,128)(2,1)S(1)} %shard_map.76.refs_1_, ...), custom_call_target="tpu_custom_call", output_to_operand_aliasing={{0}: (3, {}), {1}: (4, {})} | custom-call | flops 4000000000 | bytes 80000000 | tf_op jit(solution)/shard_map/pallas_call | solution.py:491
  52.3 0.6 %collective-permute-done.15.refs_0_ = bf16[1088,128]{1,0:T(8,128)(2,1)S(1)} collective-permute-done((bf16[1088,128]{1,0:T(8,128)(2,1)S(1)}, bf16[1088,128]{1,0:T(8,128)(2,1)S(1)}, u32[]{:S(2)}, u32[]{:S(2)}) %collective-permute-start.15) | collective-permute-done | bytes 278560 | tf_op jit(solution)/shard_map/ppermute | solution.py:370
  52.9 0.6 %collective-permute-start.19 = (bf16[1088,128]{1,0:T(8,128)(2,1)S(1)}, bf16[1088,128]{1,0:T(8,128)(2,1)S(1)}, u32[]{:S(2)}, u32[]{:S(2)}) collective-permute-start(bf16[1088,128]{1,0:T(8,128)(2,1)S(1)} %shard_map.80.refs_1_), channel_id=1, source_target_pairs={{0,2},{1,3},{2,0},{3,1},{4,6},{5,7},{6,4},{7,5},{8,10},{9,11},{10,... | collective-permute-start | bytes 835592 | tf_op jit(solution)/shard_map/ppermute | solution.py:363
  53.6 0.0 collective-permute-done.20.refs_0_
  53.6 1.1 %shard_map.81 = (f32[1728,128]{1,0:T(8,128)}, f32[3456,256]{1,0:T(8,128)}) custom-call(bf16[1088,128]{1,0:T(8,128)(2,1)S(1)} %collective-permute-done.20.refs_0_, bf16[1088,128]{1,0:T(8,128)(2,1)S(1)} %shard_map.80.refs_1_, f32[1728,128]{1,0:T(8,128)} %get-tuple-element.72.refs_2_, ...), custom_call_target="tpu_custom_call", output_to_operand_aliasing={{0}: (2, {}), {1}: (3, {})} | custom-call | flops 4000000000 | bytes 80000000 | tf_op jit(solution)/shard_map/pallas_call | solution.py:491
  54.7 0.0 collective-permute-done.19.refs_0_
  54.8 0.9 %shard_map.82 = (f32[1728,128]{1,0:T(8,128)}, f32[3456,256]{1,0:T(8,128)}) custom-call(bf16[1088,128]{1,0:T(8,128)(2,1)S(1)} %collective-permute-done.19.refs_0_, f32[1728,128]{1,0:T(8,128)} %get-tuple-element.74.refs_1_, f32[3456,256]{1,0:T(8,128)} %get-tuple-element.75.refs_2_), custom_call_target="tpu_custom_call", output_to_operand_aliasing={{0}: (1, {}), {1}: (2, {})} | custom-call | flops 4000000000 | bytes 80000000 | tf_op jit(solution)/shard_map/pallas_call | solution.py:491
  (12 shorter events, 0.2 us)
Async XLA Ops:
  2.0 5.8 %collective-permute-start = (bf16[3,16,1024]{2,1,0:T(8,128)(2,1)S(1)}, bf16[3,16,1024]{2,1,0:T(8,128)(2,1)S(1)}, u32[]{:S(2)}, u32[]{:S(2)}) collective-permute-start(bf16[3,16,1024]{2,1,0:T(8,128)(2,1)S(1)} %get-tuple-element.40), channel_id=1, source_target_pairs={{0,1},{1,0},{2,3},{3,2},{4,5},{5,4},{6,7},{7,6},{8,9},{9,8},{10,11... | collective-permute-start | bytes 294920 | tf_op jit(solution)/shard_map/ppermute | solution.py:397
  9.5 2.7 %collective-permute-start.2 = (bf16[2176,128]{1,0:T(8,128)(2,1)S(1)}, bf16[2176,128]{1,0:T(8,128)(2,1)S(1)}, u32[]{:S(2)}, u32[]{:S(2)}) collective-permute-start(bf16[2176,128]{1,0:T(8,128)(2,1)S(1)} %get-tuple-element.55), channel_id=1, source_target_pairs={{0,2},{1,3},{2,0},{3,1},{4,6},{5,7},{6,4},{7,5},{8,10},{9,11},{10,... | collective-permute-start | bytes 1671176 | tf_op jit(solution)/shard_map/ppermute | solution.py:363
  11.7 2.2 %collective-permute-start.1 = (bf16[2176,128]{1,0:T(8,128)(2,1)S(1)}, bf16[2176,128]{1,0:T(8,128)(2,1)S(1)}, u32[]{:S(2)}, u32[]{:S(2)}) collective-permute-start(bf16[2176,128]{1,0:T(8,128)(2,1)S(1)} %get-tuple-element.53.refs_2_), channel_id=1, source_target_pairs={{0,2},{1,3},{2,0},{3,1},{4,6},{5,7},{6,4},{7,5},{8,10},{9,11},{10,... | collective-permute-start | bytes 1671176 | tf_op jit(solution)/shard_map/ppermute | solution.py:363
  12.4 6.0 %collective-permute-start.4 = (bf16[1088,128]{1,0:T(8,128)(2,1)S(1)}, bf16[1088,128]{1,0:T(8,128)(2,1)S(1)}, u32[]{:S(2)}, u32[]{:S(2)}) collective-permute-start(bf16[1088,128]{1,0:T(8,128)(2,1)S(1)} %get-tuple-element.56.refs_2_), channel_id=1, source_target_pairs={{0,3},{1,11},{2,8},{3,0},{4,14},{5,6},{6,5},{7,13},{8,2},{9,10},{1... | collective-permute-start | bytes 835592 | tf_op jit(solution)/shard_map/ppermute | solution.py:370
  14.0 6.3 %collective-permute-start.3 = (bf16[1088,128]{1,0:T(8,128)(2,1)S(1)}, bf16[1088,128]{1,0:T(8,128)(2,1)S(1)}, u32[]{:S(2)}, u32[]{:S(2)}) collective-permute-start(bf16[1088,128]{1,0:T(8,128)(2,1)S(1)} %get-tuple-element.58.refs_2_), channel_id=1, source_target_pairs={{0,6},{1,11},{2,8},{3,5},{4,14},{5,3},{6,0},{7,13},{8,2},{9,15},{1... | collective-permute-start | bytes 835592 | tf_op jit(solution)/shard_map/ppermute | solution.py:370
  18.5 4.6 %collective-permute-start.6 = (bf16[544,128]{1,0:T(8,128)(2,1)S(1)}, bf16[544,128]{1,0:T(8,128)(2,1)S(1)}, u32[]{:S(2)}, u32[]{:S(2)}) collective-permute-start(bf16[544,128]{1,0:T(8,128)(2,1)S(1)} %get-tuple-element.60.refs_2_), channel_id=1, source_target_pairs={{0,6},{1,2},{2,1},{3,5},{4,7},{5,3},{6,0},{7,4},{8,11},{9,15},{10,... | collective-permute-start | bytes 417800 | tf_op jit(solution)/shard_map/ppermute | solution.py:370
  20.4 4.7 %collective-permute-start.5 = (bf16[544,128]{1,0:T(8,128)(2,1)S(1)}, bf16[544,128]{1,0:T(8,128)(2,1)S(1)}, u32[]{:S(2)}, u32[]{:S(2)}) collective-permute-start(bf16[544,128]{1,0:T(8,128)(2,1)S(1)} %get-tuple-element.62.refs_2_), channel_id=1, source_target_pairs={{0,10},{1,2},{2,1},{3,9},{4,7},{5,15},{6,12},{7,4},{8,11},{9,3},{1... | collective-permute-start | bytes 417800 | tf_op jit(solution)/shard_map/ppermute | solution.py:370
  23.1 4.0 %collective-permute-start.8 = (bf16[272,128]{1,0:T(8,128)(2,1)S(1)}, bf16[272,128]{1,0:T(8,128)(2,1)S(1)}, u32[]{:S(2)}, u32[]{:S(2)}) collective-permute-start(bf16[272,128]{1,0:T(8,128)(2,1)S(1)} %get-tuple-element.64.refs_2_), channel_id=1, source_target_pairs={{0,10},{1,7},{2,4},{3,9},{4,2},{5,15},{6,12},{7,1},{8,14},{9,3},{1... | collective-permute-start | bytes 208904 | tf_op jit(solution)/shard_map/ppermute | solution.py:370
  25.1 4.7 %collective-permute-start.7 = (bf16[272,128]{1,0:T(8,128)(2,1)S(1)}, bf16[272,128]{1,0:T(8,128)(2,1)S(1)}, u32[]{:S(2)}, u32[]{:S(2)}) collective-permute-start(bf16[272,128]{1,0:T(8,128)(2,1)S(1)} %get-tuple-element.66.refs_2_), channel_id=1, source_target_pairs={{0,3},{1,7},{2,4},{3,0},{4,2},{5,6},{6,5},{7,1},{8,14},{9,10},{10,... | collective-permute-start | bytes 208904 | tf_op jit(solution)/shard_map/ppermute | solution.py:370
  27.1 5.2 %collective-permute-start.10 = (bf16[272,128]{1,0:T(8,128)(2,1)S(1)}, bf16[272,128]{1,0:T(8,128)(2,1)S(1)}, u32[]{:S(2)}, u32[]{:S(2)}) collective-permute-start(bf16[272,128]{1,0:T(8,128)(2,1)S(1)} %shard_map.69.refs_2_.refs_0_), channel_id=1, source_target_pairs={{0,18},{1,19},{2,16},{3,17},{4,22},{5,23},{6,20},{7,21},{8,26},{9,... | collective-permute-start | bytes 208904 | tf_op jit(solution)/shard_map/ppermute | solution.py:370
  29.8 7.3 %collective-permute-start.9 = (bf16[272,128]{1,0:T(8,128)(2,1)S(1)}, bf16[272,128]{1,0:T(8,128)(2,1)S(1)}, u32[]{:S(2)}, u32[]{:S(2)}) collective-permute-start(bf16[272,128]{1,0:T(8,128)(2,1)S(1)} %shard_map.70.refs_2_.refs_0_), channel_id=1, source_target_pairs={{0,18},{1,19},{2,16},{3,17},{4,22},{5,23},{6,20},{7,21},{8,26},{9,... | collective-permute-start | bytes 208904 | tf_op jit(solution)/shard_map/ppermute | solution.py:370
  32.3 6.2 %collective-permute-start.12 = (bf16[272,128]{1,0:T(8,128)(2,1)S(1)}, bf16[272,128]{1,0:T(8,128)(2,1)S(1)}, u32[]{:S(2)}, u32[]{:S(2)}) collective-permute-start(bf16[272,128]{1,0:T(8,128)(2,1)S(1)} %shard_map.71.refs_2_.refs_0_), channel_id=1, source_target_pairs={{0,10},{1,7},{2,4},{3,9},{4,2},{5,15},{6,12},{7,1},{8,14},{9,3},{1... | collective-permute-start | bytes 208904 | tf_op jit(solution)/shard_map/ppermute | solution.py:370
  37.1 3.8 %collective-permute-start.11 = (bf16[272,128]{1,0:T(8,128)(2,1)S(1)}, bf16[272,128]{1,0:T(8,128)(2,1)S(1)}, u32[]{:S(2)}, u32[]{:S(2)}) collective-permute-start(bf16[272,128]{1,0:T(8,128)(2,1)S(1)} %shard_map.72.refs_2_.refs_0_), channel_id=1, source_target_pairs={{0,3},{1,7},{2,4},{3,0},{4,2},{5,6},{6,5},{7,1},{8,14},{9,10},{10,... | collective-permute-start | bytes 208904 | tf_op jit(solution)/shard_map/ppermute | solution.py:370
  38.5 4.5 %collective-permute-start.14 = (bf16[544,128]{1,0:T(8,128)(2,1)S(1)}, bf16[544,128]{1,0:T(8,128)(2,1)S(1)}, u32[]{:S(2)}, u32[]{:S(2)}) collective-permute-start(bf16[544,128]{1,0:T(8,128)(2,1)S(1)} %shard_map.73.refs_2_.refs_0_), channel_id=1, source_target_pairs={{0,6},{1,2},{2,1},{3,5},{4,7},{5,3},{6,0},{7,4},{8,11},{9,15},{10,... | collective-permute-start | bytes 417800 | tf_op jit(solution)/shard_map/ppermute | solution.py:370
  40.9 5.0 %collective-permute-start.13 = (bf16[544,128]{1,0:T(8,128)(2,1)S(1)}, bf16[544,128]{1,0:T(8,128)(2,1)S(1)}, u32[]{:S(2)}, u32[]{:S(2)}) collective-permute-start(bf16[544,128]{1,0:T(8,128)(2,1)S(1)} %shard_map.74.refs_2_.refs_0_), channel_id=1, source_target_pairs={{0,10},{1,2},{2,1},{3,9},{4,7},{5,15},{6,12},{7,4},{8,11},{9,3},{1... | collective-permute-start | bytes 417800 | tf_op jit(solution)/shard_map/ppermute | solution.py:370
  43.1 5.6 %collective-permute-start.17 = (bf16[1088,128]{1,0:T(8,128)(2,1)S(1)}, bf16[1088,128]{1,0:T(8,128)(2,1)S(1)}, u32[]{:S(2)}, u32[]{:S(2)}) collective-permute-start(bf16[1088,128]{1,0:T(8,128)(2,1)S(1)} %shard_map.75.refs_2_.refs_0_), channel_id=1, source_target_pairs={{0,2},{1,3},{2,0},{3,1},{4,6},{5,7},{6,4},{7,5},{8,10},{9,11},{10,... | collective-permute-start | bytes 835592 | tf_op jit(solution)/shard_map/ppermute | solution.py:363
  44.5 6.0 %collective-permute-start.16 = (bf16[1088,128]{1,0:T(8,128)(2,1)S(1)}, bf16[1088,128]{1,0:T(8,128)(2,1)S(1)}, u32[]{:S(2)}, u32[]{:S(2)}) collective-permute-start(bf16[1088,128]{1,0:T(8,128)(2,1)S(1)} %shard_map.75.refs_2_.refs_0_), channel_id=1, source_target_pairs={{0,3},{1,11},{2,8},{3,0},{4,14},{5,6},{6,5},{7,13},{8,2},{9,10},{1... | collective-permute-start | bytes 835592 | tf_op jit(solution)/shard_map/ppermute | solution.py:370
  45.9 5.0 %collective-permute-start.18 = (bf16[1088,128]{1,0:T(8,128)(2,1)S(1)}, bf16[1088,128]{1,0:T(8,128)(2,1)S(1)}, u32[]{:S(2)}, u32[]{:S(2)}) collective-permute-start(bf16[1088,128]{1,0:T(8,128)(2,1)S(1)} %shard_map.76.refs_1_), channel_id=1, source_target_pairs={{0,2},{1,3},{2,0},{3,1},{4,6},{5,7},{6,4},{7,5},{8,10},{9,11},{10,... | collective-permute-start | bytes 835592 | tf_op jit(solution)/shard_map/ppermute | solution.py:363
  46.0 6.9 %collective-permute-start.15 = (bf16[1088,128]{1,0:T(8,128)(2,1)S(1)}, bf16[1088,128]{1,0:T(8,128)(2,1)S(1)}, u32[]{:S(2)}, u32[]{:S(2)}) collective-permute-start(bf16[1088,128]{1,0:T(8,128)(2,1)S(1)} %shard_map.76.refs_1_), channel_id=1, source_target_pairs={{0,6},{1,11},{2,8},{3,5},{4,14},{5,3},{6,0},{7,13},{8,2},{9,15},{1... | collective-permute-start | bytes 835592 | tf_op jit(solution)/shard_map/ppermute | solution.py:370
  50.4 3.1 %collective-permute-start.20 = (bf16[1088,128]{1,0:T(8,128)(2,1)S(1)}, bf16[1088,128]{1,0:T(8,128)(2,1)S(1)}, u32[]{:S(2)}, u32[]{:S(2)}) collective-permute-start(bf16[1088,128]{1,0:T(8,128)(2,1)S(1)} %shard_map.78.refs_0_.refs_1_), channel_id=1, source_target_pairs={{0,2},{1,3},{2,0},{3,1},{4,6},{5,7},{6,4},{7,5},{8,10},{9,11},{10,... | collective-permute-start | bytes 835592 | tf_op jit(solution)/shard_map/ppermute | solution.py:363
  52.9 1.8 %collective-permute-start.19 = (bf16[1088,128]{1,0:T(8,128)(2,1)S(1)}, bf16[1088,128]{1,0:T(8,128)(2,1)S(1)}, u32[]{:S(2)}, u32[]{:S(2)}) collective-permute-start(bf16[1088,128]{1,0:T(8,128)(2,1)S(1)} %shard_map.80.refs_1_), channel_id=1, source_target_pairs={{0,2},{1,3},{2,0},{3,1},{4,6},{5,7},{6,4},{7,5},{8,10},{9,11},{10,... | collective-permute-start | bytes 835592 | tf_op jit(solution)/shard_map/ppermute | solution.py:363

commit v5 on v4

--- a/solution.py
+++ b/solution.py
@@ -12,7 +12,7 @@
 SECOND, FIRST = 3456, 864
 VMEM_BYTES = 32 * 1024 * 1024
 SPLIT = 17
-LANE_TURNS = (((0, 1, 2), (2, 0, 1)), ((1, 2, 0), (2, 0, 1)))
+LANE_TURNS = (((0, 1, 2), (1, 2, 0)), ((2, 0, 1), (1, 2, 0)))
 f32, bf16 = jnp.float32, jnp.bfloat16
 
 WRITES = (((0, 0), (0, 2)), ((0, 1), (1, 0), (1, 2)), ((0, 3), (1, 1)), ((1, 3),))
@@ -106,7 +106,7 @@
                         x1[rows, col + LANES : col + 2 * LANES] = right
 
 
-def load_kernel(vol_hbm, w1_hbm, face, low, x1, w1p, vol, w1, vpad, sems):
+def load_kernel(vol_hbm, w1_hbm, x1_mid, x1, w1p, vol, w1, vpad, sems):
     loads = [
         pltpu.make_async_copy(vol_hbm, vol, sems.at[0]),
         pltpu.make_async_copy(w1_hbm, w1, sems.at[1]),
@@ -115,8 +115,7 @@
         load.start()
     loads[0].wait()
     depth = vol.shape[0]
-    face[...] = vol[depth - 3 : depth]
-    low[...] = vol[0:2]
+    fill(vpad, x1_mid, [(e, vol[e - 3]) for e in (3, 4)], 1, 1)
     planes = [(e, vol[e - 3]) for e in range(4, depth + 3)]
     fill(vpad, x1, planes, 2, x1.shape[0] // 64)
     loads[1].wait()
@@ -131,16 +130,18 @@
     hidden = (first_pre * sig).astype(bf16)
     slope[...] = slope_of(first_pre, sig)
     select = selection()
-    for h in range(hidden.shape[0] // 64):
-        picked[h * 144 : (h + 1) * 144, :] = dot(
-            select, hidden[h * 64 : (h + 1) * 64]
-        ).astype(bf16)
-
-
-def upper_kernel(x1, w1p, w2_hbm, cot_hbm, slope, picked, w2, cot, cot_in, sems):
+    planes = hidden.shape[0] // 64
+    for h in range(0, planes, 2):
+        pair = [hidden[g * 64 : (g + 1) * 64] for g in range(h, min(h + 2, planes))]
+        cells = dot(select, jnp.concatenate(pair, 1)).astype(bf16)
+        for g in range(len(pair)):
+            at = (h + g) * 144
+            picked[at : at + 144, :] = cells[:, g * LANES : (g + 1) * LANES]
+
+
+def upper_kernel(x1, w1p, cot_hbm, slope, picked, cot, cot_in, sems):
     loads = [
         pltpu.make_async_copy(cot_hbm, cot_in, sems.at[0]),
-        pltpu.make_async_copy(w2_hbm, w2, sems.at[1]),
     ]
     for load in loads:
         load.start()
@@ -155,7 +156,6 @@
             part = dot(place, cot_in[o, :, k * 256 : (k + 1) * 256])
             cells = part if cells is None else cells + part
         cot[o * 16 : (o + 1) * 16, :] = cells
-    loads[1].wait()
 
 
 def second_taps(x2, own_first, keep, send, first_tap, last_tap):
@@ -178,13 +178,13 @@
 
 
 def lower_kernel(
-    bits, spatial_count, halo, low, w1p, picked_up, w2, cot,
+    bits, spatial_count, halo, x1_mid, w1p, picked_up, w2, cot,
     keep, send, x1, slope, x2, d2, own_first, vpad, picked,
 ):
     inside = jnp.where(lax.axis_index("spatial") > 0, 1.0, 0.0).astype(f32)
     planes = [(e, halo[e].astype(f32) * inside) for e in range(3)]
-    planes += [(e, low[e - 3]) for e in (3, 4)]
     fill(vpad, x1, planes, 0, 2)
+    x1[64:128, 768:] = x1_mid[:, 768:]
     hidden_of(x1, w1p, slope, picked)
     out_planes = x2.shape[0] // 16
     for o in range(out_planes):
@@ -226,16 +226,14 @@
         for a in range(h % 2, 3, 2):
             o = (h - a) // 2
             if 0 <= o < out_planes:
-                for piece in (coarse, fine):
-                    stack = jnp.concatenate(
-                        [
-                            piece[o * 16 : (o + 1) * 16, tap * LANES : (tap + 1) * LANES]
-                            for tap in range(a * 9, a * 9 + 9)
-                        ],
-                        0,
-                    )
-                    part = dot(select, stack, ((0,), (0,)))
-                    total = part if total is None else total + part
+                rows = slice(o * 16, (o + 1) * 16)
+                stack = []
+                for tap in range(a * 9, a * 9 + 9):
+                    columns = slice(tap * LANES, (tap + 1) * LANES)
+                    stack.append(jnp.concatenate([coarse[rows, columns], fine[rows, columns]], 1))
+                both = dot(select, jnp.concatenate(stack, 0), ((0,), (0,)))
+                part = both[:, :LANES] + both[:, LANES:]
+                total = part if total is None else total + part
         rounded = total.astype(bf16).astype(f32)
         if h < 2:
             slope = slope_low[h * 64 : (h + 1) * 64]
@@ -245,8 +243,8 @@
     d1_low, d1_up = jnp.concatenate(deltas[:2], 0), jnp.concatenate(deltas[2:], 0)
     for a in range(3):
         columns = slice(a * 768, (a + 1) * 768)
-        grad = dot(x1_up[:, columns], d1_up, ((0,), (0,)))
-        grad = grad + dot(x1_low[:, columns], d1_low, ((0,), (0,)))
+        grad = dot(d1_up, x1_up[:, columns], ((0,), (0,)))
+        grad = (grad + dot(d1_low, x1_low[:, columns], ((0,), (0,)))).T
         for b in range(3):
             at = (a * 3 + b) * 192
             g1[at : at + 192, :] = grad[b * 256 + 64 : (b + 1) * 256]
@@ -376,41 +374,42 @@
     slab_cot = cotangent[0]
     outside = pl.BlockSpec(memory_space=pl.ANY)
     far = pltpu.HBM
-    face, low, x1_up, w1p = call(
+    face = slab[-3:]
+    halo = lax.ppermute(
+        face, "spatial", [(i, (i + 1) % spatial_count) for i in range(spatial_count)]
+    )
+    w2 = w_second
+    x1_mid, x1_up, w1p = call(
         load_kernel,
         [
-            ((3, 16, 1024), bf16),
-            ((2, 16, 1024), bf16),
+            ((64, 9 * 256), bf16),
             ((up * 64, 9 * 256), bf16),
             ((9 * 256, 128), bf16),
         ],
         pltpu.with_memory_space_constraint(slab, far),
         pltpu.with_memory_space_constraint(w_first, far),
-        specs=[outside, outside],
+        specs=[outside] * 2,
         scratch=[
             pltpu.VMEM(slab.shape, bf16),
             pltpu.VMEM(w_first.shape, bf16),
             pltpu.VMEM((depth - 1, 8, 24, LANES), f32),
-            pltpu.SemaphoreType.DMA((2,)),
+            pltpu.SemaphoreType.DMA((3,)),
         ],
-    )
-    halo = lax.ppermute(
-        face, "spatial", [(i, (i + 1) % spatial_count) for i in range(spatial_count)]
+        after=(face,),
+        cost=STEP_COST,
     )
     cells = out_planes * 16
-    slope_up, picked_up, w2, cot = call(
+    slope_up, picked_up, cot = call(
         upper_kernel,
         [
             ((up * 64, LANES), f32),
             ((up * 144, LANES), bf16),
-            (w_second.shape, bf16),
             ((cells, 256), f32),
         ],
         x1_up,
         w1p,
-        pltpu.with_memory_space_constraint(w_second, far),
         pltpu.with_memory_space_constraint(slab_cot, far),
-        specs=[full(None), full(None), outside, outside],
+        specs=[full(None), full(None), outside],
         scratch=[pltpu.VMEM(slab_cot.shape, bf16), pltpu.SemaphoreType.DMA((2,))],
         cost=pl.CostEstimate(flops=4 * 10**8, bytes_accessed=10**7, transcendentals=0),
     )
@@ -427,12 +426,12 @@
             ((cells, 256), bf16),
         ],
         halo,
-        low,
+        x1_mid,
         w1p,
         picked_up,
         w2,
         cot,
-        scratch=[pltpu.VMEM((5, 8, 24, LANES), f32), pltpu.VMEM((288, LANES), bf16)],
+        scratch=[pltpu.VMEM((3, 8, 24, LANES), f32), pltpu.VMEM((288, LANES), bf16)],
     )
     recv0 = swap_core(send0)
     keep1, send1 = call(

time: 55.8 us -> 54.8 us (0.982)
  starting transfers between devices: 30.7 us -> 28.7 us
  Pallas kernels: 12.6 us -> 11.3 us
  waiting for transfers between devices: 11.6 us -> 12.8 us
  local copies, waits for them, and re-layouts: 0 us -> 0.99 us
    ppermute x14, starting transfers between devices: 24.5 us -> 22.6 us  [swap(): return lax.ppermute(array, BOTH, pairs)]
    ppermute x14, waiting for transfers between devices: 11 us -> 12.6 us  [swap(): return lax.ppermute(array, BOTH, pairs)]
    pallas_call x20, Pallas kernels: 7.98 us -> 6.73 us  [call(): pl.pallas_call(run, out_shape=shapes, in_specs=(specs or [full(a.shape) f...]
    slice x0 -> x1, local copies, waits for them, and re-layouts: none -> 0.9 us  [body(): face = slab[-3:]]
  transfers between devices with their start and end apart: 21 -> 21, of which waited for: 9 -> 10; matrix products, arithmetic and copies ran while one was open for 0% -> 0% of each run, Pallas kernels for 15% -> 16%
where the time goes in v5:
time: 54.8 us; the launch traced here: 54.6 us
  starting transfers between devices  28.7 us (52%)
  waiting for transfers between devices  12.8 us (23%)
  Pallas kernels  11.3 us (21%)
  local copies, waits for them, and re-layouts  0.99 us (2%)
  between operations  0.77 us (1%)
    ppermute x14, starting transfers between devices, swap(): return lax.ppermute(array, BOTH, pairs)  22.6 us
    ppermute x14, waiting for transfers between devices, swap(): return lax.ppermute(array, BOTH, pairs)  12.6 us
    pallas_call x20, Pallas kernels, call(): pl.pallas_call(run, out_shape=shapes, in_specs=(specs or [full(a.shape) f...  6.73 us
    pallas_call x4, Pallas kernels, write(): pl.pallas_call(functools.partial(final_kernel, bits, spatial_count, jobs,...  4.6 us
    ppermute x6, starting transfers between devices, swap_core(): lax.ppermute(array, BOTH, [(i, i ^ 1 << core_bit) for i in range(count)])  3.09 us
    ppermute x1, starting transfers between devices, body(): lax.ppermute(face, 'spatial', [(i, (i + 1) % spatial_count) for i in rang...  2.94 us
  transfers between devices with their start and end apart: 21, of which 10 were waited for; matrix products, arithmetic and copies ran while one was open for 0% of the time, Pallas kernels for 16%

profile of v5, /device:TPU:0, one launch (start us, length us, event | category | flops | bytes accessed | tf_op | source)
XLA Modules:
  0.0 54.6 jit_solution(17149542286854893215)
XLA Ops:
  0.6 0.9 %slice_bitcast_fusion.refs_2_ = bf16[3,16,1024]{2,1,0:T(8,128)(2,1)S(1)} fusion(bf16[1,16,16,1024]{3,2,1,0:T(8,128)(2,1)} %param.4), kind=kLoop, calls=%fused_computation | loop fusion | bytes 196608 | tf_op jit(solution)/shard_map/slice | solution.py:377
  1.5 2.9 %collective-permute-start = (bf16[3,16,1024]{2,1,0:T(8,128)(2,1)S(1)}, bf16[3,16,1024]{2,1,0:T(8,128)(2,1)S(1)}, u32[]{:S(2)}, u32[]{:S(2)}) collective-permute-start(bf16[3,16,1024]{2,1,0:T(8,128)(2,1)S(1)} %slice_bitcast_fusion.refs_2_), channel_id=1, source_target_pairs={{0,1},{1,0},{2,3},{3,2},{4,5},{5,4},{6,7},{7,6},{8,9},{9,8},{10,11... | collective-permute-start | bytes 294920 | tf_op jit(solution)/shard_map/ppermute | solution.py:378
  4.5 1.4 %shard_map.59 = (bf16[64,2304]{1,0:T(8,128)(2,1)S(1)}, bf16[448,2304]{1,0:T(8,128)(2,1)S(1)}, bf16[2304,128]{1,0:T(8,128)(2,1)S(1)}) custom-call(bf16[16,16,1024]{2,1,0:T(8,128)(2,1)} %bitcast.5, bf16[1728,128]{1,0:T(8,128)(2,1)} %refs_1_.1, bf16[3,16,1024]{2,1,0:T(8,128)(2,1)S(1)} %slice_bitcast_fusion.refs_2_), custom_call_target="tpu_custom_call" | custom-call | flops 4000000000 | bytes 80000000 | tf_op jit(solution)/shard_map/pallas_call | solution.py:37
  5.8 0.0 copy-start
  5.9 1.3 %shard_map.60 = (f32[448,128]{1,0:T(8,128)S(1)}, bf16[1008,128]{1,0:T(8,128)(2,1)S(1)}, f32[64,256]{1,0:T(8,128)S(1)}) custom-call(bf16[448,2304]{1,0:T(8,128)(2,1)S(1)} %get-tuple-element.37.refs_0_, bf16[2304,128]{1,0:T(8,128)(2,1)S(1)} %get-tuple-element.39.refs_1_.refs_2_, bf16[4,4,1024]{2,1,0:T(4,128)(2,1)} %bitcast.4), custom_call_target="tpu_custom_call" | custom-call | flops 400000000 | bytes 10000000 | tf_op jit(solution)/shard_map/pallas_call | solution.py:37
  7.1 0.1 collective-permute-done.refs_0_
  7.3 0.1 copy-done
  7.3 1.7 %shard_map.61 = (f32[2176,128]{1,0:T(8,128)S(1)}, bf16[2176,128]{1,0:T(8,128)(2,1)S(1)}, bf16[128,2304]{1,0:T(8,128)(2,1)S(1)}, f32[128,128]{1,0:T(8,128)S(1)}, ...) custom-call(bf16[3,16,1024]{2,1,0:T(8,128)(2,1)S(1)} %collective-permute-done.refs_0_, ...), custom_call_target="tpu_custom_call" | custom-call | tf_op jit(solution)/shard_map/pallas_call | solution.py:37
  9.1 0.1 collective-permute-start.2
  9.2 1.8 %shard_map.62 = (f32[2176,128]{1,0:T(8,128)S(1)}, bf16[2176,128]{1,0:T(8,128)(2,1)S(1)}) custom-call(bf16[448,2304]{1,0:T(8,128)(2,1)S(1)} %get-tuple-element.37.refs_0_, bf16[128,2304]{1,0:T(8,128)(2,1)S(1)} %get-tuple-element.42.refs_1_, f32[448,128]{1,0:T(8,128)S(1)} %get-tuple-element.43.refs_2_, f32[128,128]{1,0:T(8,128)S(1)} %get-tuple-element.44.refs_3_, ...), custom_call_target="tpu_custom_call" | custom-call | flops 1000000000 | bytes 10000000 | tf_op jit(solution)/shard_map/pallas_call | solution.py:37
  11.0 0.6 %collective-permute-start.1 = (bf16[2176,128]{1,0:T(8,128)(2,1)S(1)}, bf16[2176,128]{1,0:T(8,128)(2,1)S(1)}, u32[]{:S(2)}, u32[]{:S(2)}) collective-permute-start(bf16[2176,128]{1,0:T(8,128)(2,1)S(1)} %get-tuple-element.49.refs_2_), channel_id=1, source_target_pairs={{0,2},{1,3},{2,0},{3,1},{4,6},{5,7},{6,4},{7,5},{8,10},{9,11},{10,... | collective-permute-start | bytes 1671176 | tf_op jit(solution)/shard_map/ppermute | solution.py:361
  11.6 0.0 collective-permute-done.2.refs_1_
  11.6 0.1 shard_map.63
  11.7 1.5 %collective-permute-start.4 = (bf16[1088,128]{1,0:T(8,128)(2,1)S(1)}, bf16[1088,128]{1,0:T(8,128)(2,1)S(1)}, u32[]{:S(2)}, u32[]{:S(2)}) collective-permute-start(bf16[1088,128]{1,0:T(8,128)(2,1)S(1)} %get-tuple-element.52.refs_2_), channel_id=1, source_target_pairs={{0,3},{1,7},{2,4},{3,0},{4,2},{5,6},{6,5},{7,1},{8,14},{9,10},{10,... | collective-permute-start | bytes 835592 | tf_op jit(solution)/shard_map/ppermute | solution.py:368
  13.1 0.0 collective-permute-done.1.refs_1_
  13.2 0.1 shard_map.64
  13.2 1.9 %collective-permute-start.3 = (bf16[1088,128]{1,0:T(8,128)(2,1)S(1)}, bf16[1088,128]{1,0:T(8,128)(2,1)S(1)}, u32[]{:S(2)}, u32[]{:S(2)}) collective-permute-start(bf16[1088,128]{1,0:T(8,128)(2,1)S(1)} %get-tuple-element.54.refs_2_), channel_id=1, source_target_pairs={{0,10},{1,7},{2,4},{3,9},{4,2},{5,15},{6,12},{7,1},{8,14},{9,3},{1... | collective-permute-start | bytes 835592 | tf_op jit(solution)/shard_map/ppermute | solution.py:368
  15.1 2.6 %collective-permute-done.4.refs_1_ = bf16[1088,128]{1,0:T(8,128)(2,1)S(1)} collective-permute-done((bf16[1088,128]{1,0:T(8,128)(2,1)S(1)}, bf16[1088,128]{1,0:T(8,128)(2,1)S(1)}, u32[]{:S(2)}, u32[]{:S(2)}) %collective-permute-start.4) | collective-permute-done | bytes 278560 | tf_op jit(solution)/shard_map/ppermute | solution.py:368
  17.7 0.1 shard_map.65
  17.8 1.8 %collective-permute-start.6 = (bf16[544,128]{1,0:T(8,128)(2,1)S(1)}, bf16[544,128]{1,0:T(8,128)(2,1)S(1)}, u32[]{:S(2)}, u32[]{:S(2)}) collective-permute-start(bf16[544,128]{1,0:T(8,128)(2,1)S(1)} %get-tuple-element.56.refs_2_), channel_id=1, source_target_pairs={{0,6},{1,11},{2,8},{3,5},{4,14},{5,3},{6,0},{7,13},{8,2},{9,15},{1... | collective-permute-start | bytes 417800 | tf_op jit(solution)/shard_map/ppermute | solution.py:368
  19.6 0.0 collective-permute-done.3.refs_1_
  19.6 0.1 shard_map.66
  19.6 1.8 %collective-permute-start.5 = (bf16[544,128]{1,0:T(8,128)(2,1)S(1)}, bf16[544,128]{1,0:T(8,128)(2,1)S(1)}, u32[]{:S(2)}, u32[]{:S(2)}) collective-permute-start(bf16[544,128]{1,0:T(8,128)(2,1)S(1)} %get-tuple-element.58.refs_2_), channel_id=1, source_target_pairs={{0,3},{1,11},{2,8},{3,0},{4,14},{5,6},{6,5},{7,13},{8,2},{9,10},{1... | collective-permute-start | bytes 417800 | tf_op jit(solution)/shard_map/ppermute | solution.py:368
  21.4 1.1 %collective-permute-done.6.refs_1_ = bf16[544,128]{1,0:T(8,128)(2,1)S(1)} collective-permute-done((bf16[544,128]{1,0:T(8,128)(2,1)S(1)}, bf16[544,128]{1,0:T(8,128)(2,1)S(1)}, u32[]{:S(2)}, u32[]{:S(2)}) %collective-permute-start.6) | collective-permute-done | bytes 139296 | tf_op jit(solution)/shard_map/ppermute | solution.py:368
  22.5 1.7 %collective-permute-start.8 = (bf16[272,128]{1,0:T(8,128)(2,1)S(1)}, bf16[272,128]{1,0:T(8,128)(2,1)S(1)}, u32[]{:S(2)}, u32[]{:S(2)}) collective-permute-start(bf16[272,128]{1,0:T(8,128)(2,1)S(1)} %get-tuple-element.60.refs_2_), channel_id=1, source_target_pairs={{0,10},{1,2},{2,1},{3,9},{4,7},{5,15},{6,12},{7,4},{8,11},{9,3},{1... | collective-permute-start | bytes 208904 | tf_op jit(solution)/shard_map/ppermute | solution.py:368
  24.2 0.0 collective-permute-done.5.refs_1_
  24.2 2.1 %collective-permute-start.7 = (bf16[272,128]{1,0:T(8,128)(2,1)S(1)}, bf16[272,128]{1,0:T(8,128)(2,1)S(1)}, u32[]{:S(2)}, u32[]{:S(2)}) collective-permute-start(bf16[272,128]{1,0:T(8,128)(2,1)S(1)} %get-tuple-element.62.refs_2_), channel_id=1, source_target_pairs={{0,6},{1,2},{2,1},{3,5},{4,7},{5,3},{6,0},{7,4},{8,11},{9,15},{10,... | collective-permute-start | bytes 208904 | tf_op jit(solution)/shard_map/ppermute | solution.py:368
  26.3 0.5 collective-permute-done.8.refs_1_
  26.8 2.2 %collective-permute-start.10 = (bf16[272,128]{1,0:T(8,128)(2,1)S(1)}, bf16[272,128]{1,0:T(8,128)(2,1)S(1)}, u32[]{:S(2)}, u32[]{:S(2)}) collective-permute-start(bf16[272,128]{1,0:T(8,128)(2,1)S(1)} %shard_map.69.refs_2_.refs_0_), channel_id=1, source_target_pairs={{0,18},{1,19},{2,16},{3,17},{4,22},{5,23},{6,20},{7,21},{8,26},{9,... | collective-permute-start | bytes 208904 | tf_op jit(solution)/shard_map/ppermute | solution.py:368
  29.0 0.0 collective-permute-done.7.refs_1_
  29.1 2.5 %collective-permute-start.9 = (bf16[272,128]{1,0:T(8,128)(2,1)S(1)}, bf16[272,128]{1,0:T(8,128)(2,1)S(1)}, u32[]{:S(2)}, u32[]{:S(2)}) collective-permute-start(bf16[272,128]{1,0:T(8,128)(2,1)S(1)} %shard_map.70.refs_2_.refs_0_), channel_id=1, source_target_pairs={{0,18},{1,19},{2,16},{3,17},{4,22},{5,23},{6,20},{7,21},{8,26},{9,... | collective-permute-start | bytes 208904 | tf_op jit(solution)/shard_map/ppermute | solution.py:368
  31.5 0.0 collective-permute-done.10.refs_1_
  31.6 2.6 %collective-permute-start.12 = (bf16[272,128]{1,0:T(8,128)(2,1)S(1)}, bf16[272,128]{1,0:T(8,128)(2,1)S(1)}, u32[]{:S(2)}, u32[]{:S(2)}) collective-permute-start(bf16[272,128]{1,0:T(8,128)(2,1)S(1)} %shard_map.71.refs_2_.refs_0_), channel_id=1, source_target_pairs={{0,10},{1,2},{2,1},{3,9},{4,7},{5,15},{6,12},{7,4},{8,11},{9,3},{1... | collective-permute-start | bytes 208904 | tf_op jit(solution)/shard_map/ppermute | solution.py:368
  34.2 2.5 %collective-permute-done.9.refs_1_ = bf16[272,128]{1,0:T(8,128)(2,1)S(1)} collective-permute-done((bf16[272,128]{1,0:T(8,128)(2,1)S(1)}, bf16[272,128]{1,0:T(8,128)(2,1)S(1)}, u32[]{:S(2)}, u32[]{:S(2)}) %collective-permute-start.9) | collective-permute-done | bytes 69664 | tf_op jit(solution)/shard_map/ppermute | solution.py:368
  36.7 1.5 %collective-permute-start.11 = (bf16[272,128]{1,0:T(8,128)(2,1)S(1)}, bf16[272,128]{1,0:T(8,128)(2,1)S(1)}, u32[]{:S(2)}, u32[]{:S(2)}) collective-permute-start(bf16[272,128]{1,0:T(8,128)(2,1)S(1)} %shard_map.72.refs_2_.refs_0_), channel_id=1, source_target_pairs={{0,6},{1,2},{2,1},{3,5},{4,7},{5,3},{6,0},{7,4},{8,11},{9,15},{10,... | collective-permute-start | bytes 208904 | tf_op jit(solution)/shard_map/ppermute | solution.py:368
  38.2 0.0 collective-permute-done.12.refs_1_
  38.2 0.6 %collective-permute-start.14 = (bf16[544,128]{1,0:T(8,128)(2,1)S(1)}, bf16[544,128]{1,0:T(8,128)(2,1)S(1)}, u32[]{:S(2)}, u32[]{:S(2)}) collective-permute-start(bf16[544,128]{1,0:T(8,128)(2,1)S(1)} %shard_map.73.refs_2_.refs_0_), channel_id=1, source_target_pairs={{0,6},{1,11},{2,8},{3,5},{4,14},{5,3},{6,0},{7,13},{8,2},{9,15},{1... | collective-permute-start | bytes 417800 | tf_op jit(solution)/shard_map/ppermute | solution.py:368
  38.8 1.7 %collective-permute-done.11.refs_1_ = bf16[272,128]{1,0:T(8,128)(2,1)S(1)} collective-permute-done((bf16[272,128]{1,0:T(8,128)(2,1)S(1)}, bf16[272,128]{1,0:T(8,128)(2,1)S(1)}, u32[]{:S(2)}, u32[]{:S(2)}) %collective-permute-start.11) | collective-permute-done | bytes 69664 | tf_op jit(solution)/shard_map/ppermute | solution.py:368
  40.5 1.6 %collective-permute-start.13 = (bf16[544,128]{1,0:T(8,128)(2,1)S(1)}, bf16[544,128]{1,0:T(8,128)(2,1)S(1)}, u32[]{:S(2)}, u32[]{:S(2)}) collective-permute-start(bf16[544,128]{1,0:T(8,128)(2,1)S(1)} %shard_map.74.refs_2_.refs_0_), channel_id=1, source_target_pairs={{0,3},{1,11},{2,8},{3,0},{4,14},{5,6},{6,5},{7,13},{8,2},{9,10},{1... | collective-permute-start | bytes 417800 | tf_op jit(solution)/shard_map/ppermute | solution.py:368
  42.1 0.7 %collective-permute-done.14.refs_1_ = bf16[544,128]{1,0:T(8,128)(2,1)S(1)} collective-permute-done((bf16[544,128]{1,0:T(8,128)(2,1)S(1)}, bf16[544,128]{1,0:T(8,128)(2,1)S(1)}, u32[]{:S(2)}, u32[]{:S(2)}) %collective-permute-start.14) | collective-permute-done | bytes 139296 | tf_op jit(solution)/shard_map/ppermute | solution.py:368
  42.8 0.6 %collective-permute-start.17 = (bf16[1088,128]{1,0:T(8,128)(2,1)S(1)}, bf16[1088,128]{1,0:T(8,128)(2,1)S(1)}, u32[]{:S(2)}, u32[]{:S(2)}) collective-permute-start(bf16[1088,128]{1,0:T(8,128)(2,1)S(1)} %shard_map.75.refs_2_.refs_0_), channel_id=1, source_target_pairs={{0,2},{1,3},{2,0},{3,1},{4,6},{5,7},{6,4},{7,5},{8,10},{9,11},{10,... | collective-permute-start | bytes 835592 | tf_op jit(solution)/shard_map/ppermute | solution.py:361
  43.4 0.3 collective-permute-start.16
  43.6 1.4 %collective-permute-done.13.refs_1_ = bf16[544,128]{1,0:T(8,128)(2,1)S(1)} collective-permute-done((bf16[544,128]{1,0:T(8,128)(2,1)S(1)}, bf16[544,128]{1,0:T(8,128)(2,1)S(1)}, u32[]{:S(2)}, u32[]{:S(2)}) %collective-permute-start.13) | collective-permute-done | bytes 139296 | tf_op jit(solution)/shard_map/ppermute | solution.py:368
  45.1 0.4 collective-permute-start.18
  45.5 0.7 %collective-permute-start.15 = (bf16[1088,128]{1,0:T(8,128)(2,1)S(1)}, bf16[1088,128]{1,0:T(8,128)(2,1)S(1)}, u32[]{:S(2)}, u32[]{:S(2)}) collective-permute-start(bf16[1088,128]{1,0:T(8,128)(2,1)S(1)} %shard_map.76.refs_1_), channel_id=1, source_target_pairs={{0,10},{1,7},{2,4},{3,9},{4,2},{5,15},{6,12},{7,1},{8,14},{9,3},{1... | collective-permute-start | bytes 835592 | tf_op jit(solution)/shard_map/ppermute | solution.py:368
  46.2 0.0 collective-permute-done.17.refs_1_
  46.2 1.2 %shard_map.77 = (f32[1728,128]{1,0:T(8,128)}, f32[3456,256]{1,0:T(8,128)}, f32[8,128]{1,0:T(8,128)S(1)}) custom-call(bf16[1088,128]{1,0:T(8,128)(2,1)S(1)} %shard_map.75.refs_2_.refs_0_, bf16[1088,128]{1,0:T(8,128)(2,1)S(1)} %collective-permute-done.17.refs_1_), custom_call_target="tpu_custom_call" | custom-call | flops 4000000000 | bytes 80000000 | tf_op jit(solution)/shard_map/pallas_call | solution.py:490
  47.3 2.0 %collective-permute-done.16.refs_0_ = bf16[1088,128]{1,0:T(8,128)(2,1)S(1)} collective-permute-done((bf16[1088,128]{1,0:T(8,128)(2,1)S(1)}, bf16[1088,128]{1,0:T(8,128)(2,1)S(1)}, u32[]{:S(2)}, u32[]{:S(2)}) %collective-permute-start.16) | collective-permute-done | bytes 278560 | tf_op jit(solution)/shard_map/ppermute | solution.py:368
  49.4 0.4 collective-permute-start.20
  49.8 0.0 collective-permute-done.18.refs_2_
  49.8 1.4 %shard_map.79 = (f32[1728,128]{1,0:T(8,128)}, f32[3456,256]{1,0:T(8,128)}, f32[8,128]{1,0:T(8,128)S(1)}) custom-call(bf16[1088,128]{1,0:T(8,128)(2,1)S(1)} %shard_map.78.refs_0_.refs_1_, bf16[1088,128]{1,0:T(8,128)(2,1)S(1)} %shard_map.76.refs_1_, ...), custom_call_target="tpu_custom_call", output_to_operand_aliasing={{0}: (3, {}), {1}: (4, {})} | custom-call | flops 4000000000 | bytes 80000000 | tf_op jit(solution)/shard_map/pallas_call | solution.py:490
  51.2 0.3 collective-permute-done.15.refs_0_
  51.5 1.0 %collective-permute-start.19 = (bf16[1088,128]{1,0:T(8,128)(2,1)S(1)}, bf16[1088,128]{1,0:T(8,128)(2,1)S(1)}, u32[]{:S(2)}, u32[]{:S(2)}) collective-permute-start(bf16[1088,128]{1,0:T(8,128)(2,1)S(1)} %shard_map.80.refs_1_), channel_id=1, source_target_pairs={{0,2},{1,3},{2,0},{3,1},{4,6},{5,7},{6,4},{7,5},{8,10},{9,11},{10,... | collective-permute-start | bytes 835592 | tf_op jit(solution)/shard_map/ppermute | solution.py:361
  52.5 0.0 collective-permute-done.20.refs_0_
  52.5 1.1 %shard_map.81 = (f32[1728,128]{1,0:T(8,128)}, f32[3456,256]{1,0:T(8,128)}) custom-call(bf16[1088,128]{1,0:T(8,128)(2,1)S(1)} %collective-permute-done.20.refs_0_, bf16[1088,128]{1,0:T(8,128)(2,1)S(1)} %shard_map.80.refs_1_, f32[1728,128]{1,0:T(8,128)} %get-tuple-element.68.refs_2_, ...), custom_call_target="tpu_custom_call", output_to_operand_aliasing={{0}: (2, {}), {1}: (3, {})} | custom-call | flops 4000000000 | bytes 80000000 | tf_op jit(solution)/shard_map/pallas_call | solution.py:490
  53.7 0.0 collective-permute-done.19.refs_0_
  53.7 0.9 %shard_map.82 = (f32[1728,128]{1,0:T(8,128)}, f32[3456,256]{1,0:T(8,128)}) custom-call(bf16[1088,128]{1,0:T(8,128)(2,1)S(1)} %collective-permute-done.19.refs_0_, f32[1728,128]{1,0:T(8,128)} %get-tuple-element.70.refs_1_, f32[3456,256]{1,0:T(8,128)} %get-tuple-element.71.refs_2_), custom_call_target="tpu_custom_call", output_to_operand_aliasing={{0}: (1, {}), {1}: (2, {})} | custom-call | flops 4000000000 | bytes 80000000 | tf_op jit(solution)/shard_map/pallas_call | solution.py:490
  (12 shorter events, 0.2 us)
Async XLA Ops:
  1.5 5.7 %collective-permute-start = (bf16[3,16,1024]{2,1,0:T(8,128)(2,1)S(1)}, bf16[3,16,1024]{2,1,0:T(8,128)(2,1)S(1)}, u32[]{:S(2)}, u32[]{:S(2)}) collective-permute-start(bf16[3,16,1024]{2,1,0:T(8,128)(2,1)S(1)} %slice_bitcast_fusion.refs_2_), channel_id=1, source_target_pairs={{0,1},{1,0},{2,3},{3,2},{4,5},{5,4},{6,7},{7,6},{8,9},{9,8},{10,11... | collective-permute-start | bytes 294920 | tf_op jit(solution)/shard_map/ppermute | solution.py:378
  5.8 1.5 %copy-start = (bf16[3456,256]{1,0:T(8,128)(2,1)S(1)}, bf16[3456,256]{1,0:T(8,128)(2,1)}, u32[]{:S(2)}) copy-start(bf16[3456,256]{1,0:T(8,128)(2,1)} %refs_7_.1) | copy-start | bytes 5308420
  9.1 2.5 %collective-permute-start.2 = (bf16[2176,128]{1,0:T(8,128)(2,1)S(1)}, bf16[2176,128]{1,0:T(8,128)(2,1)S(1)}, u32[]{:S(2)}, u32[]{:S(2)}) collective-permute-start(bf16[2176,128]{1,0:T(8,128)(2,1)S(1)} %get-tuple-element.51), channel_id=1, source_target_pairs={{0,2},{1,3},{2,0},{3,1},{4,6},{5,7},{6,4},{7,5},{8,10},{9,11},{10,... | collective-permute-start | bytes 1671176 | tf_op jit(solution)/shard_map/ppermute | solution.py:361
  11.0 2.2 %collective-permute-start.1 = (bf16[2176,128]{1,0:T(8,128)(2,1)S(1)}, bf16[2176,128]{1,0:T(8,128)(2,1)S(1)}, u32[]{:S(2)}, u32[]{:S(2)}) collective-permute-start(bf16[2176,128]{1,0:T(8,128)(2,1)S(1)} %get-tuple-element.49.refs_2_), channel_id=1, source_target_pairs={{0,2},{1,3},{2,0},{3,1},{4,6},{5,7},{6,4},{7,5},{8,10},{9,11},{10,... | collective-permute-start | bytes 1671176 | tf_op jit(solution)/shard_map/ppermute | solution.py:361
  11.7 6.0 %collective-permute-start.4 = (bf16[1088,128]{1,0:T(8,128)(2,1)S(1)}, bf16[1088,128]{1,0:T(8,128)(2,1)S(1)}, u32[]{:S(2)}, u32[]{:S(2)}) collective-permute-start(bf16[1088,128]{1,0:T(8,128)(2,1)S(1)} %get-tuple-element.52.refs_2_), channel_id=1, source_target_pairs={{0,3},{1,7},{2,4},{3,0},{4,2},{5,6},{6,5},{7,1},{8,14},{9,10},{10,... | collective-permute-start | bytes 835592 | tf_op jit(solution)/shard_map/ppermute | solution.py:368
  13.2 6.3 %collective-permute-start.3 = (bf16[1088,128]{1,0:T(8,128)(2,1)S(1)}, bf16[1088,128]{1,0:T(8,128)(2,1)S(1)}, u32[]{:S(2)}, u32[]{:S(2)}) collective-permute-start(bf16[1088,128]{1,0:T(8,128)(2,1)S(1)} %get-tuple-element.54.refs_2_), channel_id=1, source_target_pairs={{0,10},{1,7},{2,4},{3,9},{4,2},{5,15},{6,12},{7,1},{8,14},{9,3},{1... | collective-permute-start | bytes 835592 | tf_op jit(solution)/shard_map/ppermute | solution.py:368
  17.8 4.7 %collective-permute-start.6 = (bf16[544,128]{1,0:T(8,128)(2,1)S(1)}, bf16[544,128]{1,0:T(8,128)(2,1)S(1)}, u32[]{:S(2)}, u32[]{:S(2)}) collective-permute-start(bf16[544,128]{1,0:T(8,128)(2,1)S(1)} %get-tuple-element.56.refs_2_), channel_id=1, source_target_pairs={{0,6},{1,11},{2,8},{3,5},{4,14},{5,3},{6,0},{7,13},{8,2},{9,15},{1... | collective-permute-start | bytes 417800 | tf_op jit(solution)/shard_map/ppermute | solution.py:368
  19.6 4.6 %collective-permute-start.5 = (bf16[544,128]{1,0:T(8,128)(2,1)S(1)}, bf16[544,128]{1,0:T(8,128)(2,1)S(1)}, u32[]{:S(2)}, u32[]{:S(2)}) collective-permute-start(bf16[544,128]{1,0:T(8,128)(2,1)S(1)} %get-tuple-element.58.refs_2_), channel_id=1, source_target_pairs={{0,3},{1,11},{2,8},{3,0},{4,14},{5,6},{6,5},{7,13},{8,2},{9,10},{1... | collective-permute-start | bytes 417800 | tf_op jit(solution)/shard_map/ppermute | solution.py:368
  22.5 4.2 %collective-permute-start.8 = (bf16[272,128]{1,0:T(8,128)(2,1)S(1)}, bf16[272,128]{1,0:T(8,128)(2,1)S(1)}, u32[]{:S(2)}, u32[]{:S(2)}) collective-permute-start(bf16[272,128]{1,0:T(8,128)(2,1)S(1)} %get-tuple-element.60.refs_2_), channel_id=1, source_target_pairs={{0,10},{1,2},{2,1},{3,9},{4,7},{5,15},{6,12},{7,4},{8,11},{9,3},{1... | collective-permute-start | bytes 208904 | tf_op jit(solution)/shard_map/ppermute | solution.py:368
  24.2 4.8 %collective-permute-start.7 = (bf16[272,128]{1,0:T(8,128)(2,1)S(1)}, bf16[272,128]{1,0:T(8,128)(2,1)S(1)}, u32[]{:S(2)}, u32[]{:S(2)}) collective-permute-start(bf16[272,128]{1,0:T(8,128)(2,1)S(1)} %get-tuple-element.62.refs_2_), channel_id=1, source_target_pairs={{0,6},{1,2},{2,1},{3,5},{4,7},{5,3},{6,0},{7,4},{8,11},{9,15},{10,... | collective-permute-start | bytes 208904 | tf_op jit(solution)/shard_map/ppermute | solution.py:368
  26.8 4.7 %collective-permute-start.10 = (bf16[272,128]{1,0:T(8,128)(2,1)S(1)}, bf16[272,128]{1,0:T(8,128)(2,1)S(1)}, u32[]{:S(2)}, u32[]{:S(2)}) collective-permute-start(bf16[272,128]{1,0:T(8,128)(2,1)S(1)} %shard_map.69.refs_2_.refs_0_), channel_id=1, source_target_pairs={{0,18},{1,19},{2,16},{3,17},{4,22},{5,23},{6,20},{7,21},{8,26},{9,... | collective-permute-start | bytes 208904 | tf_op jit(solution)/shard_map/ppermute | solution.py:368
  29.1 7.6 %collective-permute-start.9 = (bf16[272,128]{1,0:T(8,128)(2,1)S(1)}, bf16[272,128]{1,0:T(8,128)(2,1)S(1)}, u32[]{:S(2)}, u32[]{:S(2)}) collective-permute-start(bf16[272,128]{1,0:T(8,128)(2,1)S(1)} %shard_map.70.refs_2_.refs_0_), channel_id=1, source_target_pairs={{0,18},{1,19},{2,16},{3,17},{4,22},{5,23},{6,20},{7,21},{8,26},{9,... | collective-permute-start | bytes 208904 | tf_op jit(solution)/shard_map/ppermute | solution.py:368
  31.6 6.6 %collective-permute-start.12 = (bf16[272,128]{1,0:T(8,128)(2,1)S(1)}, bf16[272,128]{1,0:T(8,128)(2,1)S(1)}, u32[]{:S(2)}, u32[]{:S(2)}) collective-permute-start(bf16[272,128]{1,0:T(8,128)(2,1)S(1)} %shard_map.71.refs_2_.refs_0_), channel_id=1, source_target_pairs={{0,10},{1,2},{2,1},{3,9},{4,7},{5,15},{6,12},{7,4},{8,11},{9,3},{1... | collective-permute-start | bytes 208904 | tf_op jit(solution)/shard_map/ppermute | solution.py:368
  36.7 3.8 %collective-permute-start.11 = (bf16[272,128]{1,0:T(8,128)(2,1)S(1)}, bf16[272,128]{1,0:T(8,128)(2,1)S(1)}, u32[]{:S(2)}, u32[]{:S(2)}) collective-permute-start(bf16[272,128]{1,0:T(8,128)(2,1)S(1)} %shard_map.72.refs_2_.refs_0_), channel_id=1, source_target_pairs={{0,6},{1,2},{2,1},{3,5},{4,7},{5,3},{6,0},{7,4},{8,11},{9,15},{10,... | collective-permute-start | bytes 208904 | tf_op jit(solution)/shard_map/ppermute | solution.py:368
  38.2 4.5 %collective-permute-start.14 = (bf16[544,128]{1,0:T(8,128)(2,1)S(1)}, bf16[544,128]{1,0:T(8,128)(2,1)S(1)}, u32[]{:S(2)}, u32[]{:S(2)}) collective-permute-start(bf16[544,128]{1,0:T(8,128)(2,1)S(1)} %shard_map.73.refs_2_.refs_0_), channel_id=1, source_target_pairs={{0,6},{1,11},{2,8},{3,5},{4,14},{5,3},{6,0},{7,13},{8,2},{9,15},{1... | collective-permute-start | bytes 417800 | tf_op jit(solution)/shard_map/ppermute | solution.py:368
  40.5 4.5 %collective-permute-start.13 = (bf16[544,128]{1,0:T(8,128)(2,1)S(1)}, bf16[544,128]{1,0:T(8,128)(2,1)S(1)}, u32[]{:S(2)}, u32[]{:S(2)}) collective-permute-start(bf16[544,128]{1,0:T(8,128)(2,1)S(1)} %shard_map.74.refs_2_.refs_0_), channel_id=1, source_target_pairs={{0,3},{1,11},{2,8},{3,0},{4,14},{5,6},{6,5},{7,13},{8,2},{9,10},{1... | collective-permute-start | bytes 417800 | tf_op jit(solution)/shard_map/ppermute | solution.py:368
  42.8 3.4 %collective-permute-start.17 = (bf16[1088,128]{1,0:T(8,128)(2,1)S(1)}, bf16[1088,128]{1,0:T(8,128)(2,1)S(1)}, u32[]{:S(2)}, u32[]{:S(2)}) collective-permute-start(bf16[1088,128]{1,0:T(8,128)(2,1)S(1)} %shard_map.75.refs_2_.refs_0_), channel_id=1, source_target_pairs={{0,2},{1,3},{2,0},{3,1},{4,6},{5,7},{6,4},{7,5},{8,10},{9,11},{10,... | collective-permute-start | bytes 835592 | tf_op jit(solution)/shard_map/ppermute | solution.py:361
  43.4 6.0 %collective-permute-start.16 = (bf16[1088,128]{1,0:T(8,128)(2,1)S(1)}, bf16[1088,128]{1,0:T(8,128)(2,1)S(1)}, u32[]{:S(2)}, u32[]{:S(2)}) collective-permute-start(bf16[1088,128]{1,0:T(8,128)(2,1)S(1)} %shard_map.75.refs_2_.refs_0_), channel_id=1, source_target_pairs={{0,3},{1,7},{2,4},{3,0},{4,2},{5,6},{6,5},{7,1},{8,14},{9,10},{10,... | collective-permute-start | bytes 835592 | tf_op jit(solution)/shard_map/ppermute | solution.py:368
  45.1 4.7 %collective-permute-start.18 = (bf16[1088,128]{1,0:T(8,128)(2,1)S(1)}, bf16[1088,128]{1,0:T(8,128)(2,1)S(1)}, u32[]{:S(2)}, u32[]{:S(2)}) collective-permute-start(bf16[1088,128]{1,0:T(8,128)(2,1)S(1)} %shard_map.76.refs_1_), channel_id=1, source_target_pairs={{0,2},{1,3},{2,0},{3,1},{4,6},{5,7},{6,4},{7,5},{8,10},{9,11},{10,... | collective-permute-start | bytes 835592 | tf_op jit(solution)/shard_map/ppermute | solution.py:361
  45.5 6.0 %collective-permute-start.15 = (bf16[1088,128]{1,0:T(8,128)(2,1)S(1)}, bf16[1088,128]{1,0:T(8,128)(2,1)S(1)}, u32[]{:S(2)}, u32[]{:S(2)}) collective-permute-start(bf16[1088,128]{1,0:T(8,128)(2,1)S(1)} %shard_map.76.refs_1_), channel_id=1, source_target_pairs={{0,10},{1,7},{2,4},{3,9},{4,2},{5,15},{6,12},{7,1},{8,14},{9,3},{1... | collective-permute-start | bytes 835592 | tf_op jit(solution)/shard_map/ppermute | solution.py:368
  49.4 3.1 %collective-permute-start.20 = (bf16[1088,128]{1,0:T(8,128)(2,1)S(1)}, bf16[1088,128]{1,0:T(8,128)(2,1)S(1)}, u32[]{:S(2)}, u32[]{:S(2)}) collective-permute-start(bf16[1088,128]{1,0:T(8,128)(2,1)S(1)} %shard_map.78.refs_0_.refs_1_), channel_id=1, source_target_pairs={{0,2},{1,3},{2,0},{3,1},{4,6},{5,7},{6,4},{7,5},{8,10},{9,11},{10,... | collective-permute-start | bytes 835592 | tf_op jit(solution)/shard_map/ppermute | solution.py:361
  51.5 2.2 %collective-permute-start.19 = (bf16[1088,128]{1,0:T(8,128)(2,1)S(1)}, bf16[1088,128]{1,0:T(8,128)(2,1)S(1)}, u32[]{:S(2)}, u32[]{:S(2)}) collective-permute-start(bf16[1088,128]{1,0:T(8,128)(2,1)S(1)} %shard_map.80.refs_1_), channel_id=1, source_target_pairs={{0,2},{1,3},{2,0},{3,1},{4,6},{5,7},{6,4},{7,5},{8,10},{9,11},{10,... | collective-permute-start | bytes 835592 | tf_op jit(solution)/shard_map/ppermute | solution.py:361

commit v6 on v5

--- a/solution.py
+++ b/solution.py
@@ -15,7 +15,7 @@
 LANE_TURNS = (((0, 1, 2), (1, 2, 0)), ((2, 0, 1), (1, 2, 0)))
 f32, bf16 = jnp.float32, jnp.bfloat16
 
-WRITES = (((0, 0), (0, 2)), ((0, 1), (1, 0), (1, 2)), ((0, 3), (1, 1)), ((1, 3),))
+WRITES = (((0, 0), (1, 0)), ((0, 2), (1, 2), (0, 1)), ((0, 3), (1, 1)), ((1, 3),))
 STEP_COST = pl.CostEstimate(flops=4 * 10**9, bytes_accessed=8 * 10**7, transcendentals=0)
 
 
@@ -475,7 +475,7 @@
                 join_kernel, shape, keep[lane], recv[lane], after=(last,), cost=STEP_COST
             )[0]
             keep[lane], recv[lane] = last, swap(last, lane, step - 1)
-    held = [[keep[lane], None, swap_core(keep[lane]), None] for lane in range(lanes)]
+    held = [[keep[lane], None, None, None] for lane in range(lanes)]
     shapes = [jax.ShapeDtypeStruct((2 * FIRST, LANES), f32)]
     shapes += [jax.ShapeDtypeStruct((SECOND, 2 * LANES), f32)]
     token_shape = [jax.ShapeDtypeStruct((8, LANES), f32)]
@@ -499,10 +499,15 @@
             cost_estimate=STEP_COST,
         )(*parts, *grads)
 
+    def copied(array, after):
+        return call(copy_kernel, [(array.shape, bf16)], array, after=after, cost=STEP_COST)[0]
+
     for lane, group in enumerate(WRITES[:lanes]):
         *grads, token = write(group, grads, 1)
-        shape = [(recv[lane].shape, bf16)]
-        last = call(copy_kernel, shape, recv[lane], after=(last, token), cost=STEP_COST)[0]
+        if lane == 0:
+            for part in held:
+                part[2] = swap_core(copied(part[0], (token,)))
+        last = copied(recv[lane], (last, token))
         held[lane][1], held[lane][3] = last, swap_core(last)
     for group in WRITES[lanes:]:
         grads = write(group, grads, 0)

time: 54.8 us -> 54.7 us (level)
  waiting for transfers between devices: 12.8 us -> 11.5 us
  starting transfers between devices: 28.7 us -> 29.8 us
    ppermute x14, waiting for transfers between devices: 12.6 us -> 11 us  [swap(): return lax.ppermute(array, BOTH, pairs)]
    ppermute x6, starting transfers between devices: 3.09 us -> 3.96 us  [swap_core(): lax.ppermute(array, BOTH, [(i, i ^ 1 << core_bit) for i in range(count)])]
    pallas_call x20 -> x22, Pallas kernels: 6.73 us -> 6.77 us  [call(): pl.pallas_call(run, out_shape=shapes, in_specs=(specs or [full(a.shape) f...]
where the time goes in v6:
time: 54.7 us; the launch traced here: 54.5 us
  starting transfers between devices  29.8 us (54%)
  waiting for transfers between devices  11.5 us (21%)
  Pallas kernels  11.4 us (21%)
  local copies, waits for them, and re-layouts  0.99 us (2%)
  between operations  0.79 us (1%)
    ppermute x14, starting transfers between devices, swap(): return lax.ppermute(array, BOTH, pairs)  23 us
    ppermute x14, waiting for transfers between devices, swap(): return lax.ppermute(array, BOTH, pairs)  11 us
    pallas_call x22, Pallas kernels, call(): pl.pallas_call(run, out_shape=shapes, in_specs=(specs or [full(a.shape) f...  6.77 us
    pallas_call x4, Pallas kernels, write(): pl.pallas_call(functools.partial(final_kernel, bits, spatial_count, jobs,...  4.6 us
    ppermute x6, starting transfers between devices, swap_core(): lax.ppermute(array, BOTH, [(i, i ^ 1 << core_bit) for i in range(count)])  3.96 us
    ppermute x1, starting transfers between devices, body(): lax.ppermute(face, 'spatial', [(i, (i + 1) % spatial_count) for i in rang...  2.94 us
  transfers between devices with their start and end apart: 21, of which 10 were waited for; matrix products, arithmetic and copies ran while one was open for 0% of the time, Pallas kernels for 16%

profile of v6, /device:TPU:0, one launch (start us, length us, event | category | flops | bytes accessed | tf_op | source)
XLA Modules:
  0.0 54.5 jit_solution(8845402277901546259)
XLA Ops:
  0.6 0.9 %slice_bitcast_fusion.refs_2_ = bf16[3,16,1024]{2,1,0:T(8,128)(2,1)S(1)} fusion(bf16[1,16,16,1024]{3,2,1,0:T(8,128)(2,1)} %param.4), kind=kLoop, calls=%fused_computation | loop fusion | bytes 196608 | tf_op jit(solution)/shard_map/slice | solution.py:377
  1.5 2.9 %collective-permute-start = (bf16[3,16,1024]{2,1,0:T(8,128)(2,1)S(1)}, bf16[3,16,1024]{2,1,0:T(8,128)(2,1)S(1)}, u32[]{:S(2)}, u32[]{:S(2)}) collective-permute-start(bf16[3,16,1024]{2,1,0:T(8,128)(2,1)S(1)} %slice_bitcast_fusion.refs_2_), channel_id=1, source_target_pairs={{0,1},{1,0},{2,3},{3,2},{4,5},{5,4},{6,7},{7,6},{8,9},{9,8},{10,11... | collective-permute-start | bytes 294920 | tf_op jit(solution)/shard_map/ppermute | solution.py:378
  4.5 1.4 %shard_map.59 = (bf16[64,2304]{1,0:T(8,128)(2,1)S(1)}, bf16[448,2304]{1,0:T(8,128)(2,1)S(1)}, bf16[2304,128]{1,0:T(8,128)(2,1)S(1)}) custom-call(bf16[16,16,1024]{2,1,0:T(8,128)(2,1)} %bitcast.5, bf16[1728,128]{1,0:T(8,128)(2,1)} %refs_1_.1, bf16[3,16,1024]{2,1,0:T(8,128)(2,1)S(1)} %slice_bitcast_fusion.refs_2_), custom_call_target="tpu_custom_call" | custom-call | flops 4000000000 | bytes 80000000 | tf_op jit(solution)/shard_map/pallas_call | solution.py:37
  5.8 0.0 copy-start
  5.9 1.3 %shard_map.60 = (f32[448,128]{1,0:T(8,128)S(1)}, bf16[1008,128]{1,0:T(8,128)(2,1)S(1)}, f32[64,256]{1,0:T(8,128)S(1)}) custom-call(bf16[448,2304]{1,0:T(8,128)(2,1)S(1)} %get-tuple-element.37.refs_0_, bf16[2304,128]{1,0:T(8,128)(2,1)S(1)} %get-tuple-element.39.refs_1_.refs_2_, bf16[4,4,1024]{2,1,0:T(4,128)(2,1)} %bitcast.4), custom_call_target="tpu_custom_call" | custom-call | flops 400000000 | bytes 10000000 | tf_op jit(solution)/shard_map/pallas_call | solution.py:37
  7.1 0.1 collective-permute-done.refs_0_
  7.3 0.1 copy-done
  7.3 1.7 %shard_map.61 = (f32[2176,128]{1,0:T(8,128)S(1)}, bf16[2176,128]{1,0:T(8,128)(2,1)S(1)}, bf16[128,2304]{1,0:T(8,128)(2,1)S(1)}, f32[128,128]{1,0:T(8,128)S(1)}, ...) custom-call(bf16[3,16,1024]{2,1,0:T(8,128)(2,1)S(1)} %collective-permute-done.refs_0_, ...), custom_call_target="tpu_custom_call" | custom-call | tf_op jit(solution)/shard_map/pallas_call | solution.py:37
  9.1 0.1 collective-permute-start.2
  9.2 1.8 %shard_map.62 = (f32[2176,128]{1,0:T(8,128)S(1)}, bf16[2176,128]{1,0:T(8,128)(2,1)S(1)}) custom-call(bf16[448,2304]{1,0:T(8,128)(2,1)S(1)} %get-tuple-element.37.refs_0_, bf16[128,2304]{1,0:T(8,128)(2,1)S(1)} %get-tuple-element.42.refs_1_, f32[448,128]{1,0:T(8,128)S(1)} %get-tuple-element.43.refs_2_, f32[128,128]{1,0:T(8,128)S(1)} %get-tuple-element.44.refs_3_, ...), custom_call_target="tpu_custom_call" | custom-call | flops 1000000000 | bytes 10000000 | tf_op jit(solution)/shard_map/pallas_call | solution.py:37
  11.0 0.6 %collective-permute-start.1 = (bf16[2176,128]{1,0:T(8,128)(2,1)S(1)}, bf16[2176,128]{1,0:T(8,128)(2,1)S(1)}, u32[]{:S(2)}, u32[]{:S(2)}) collective-permute-start(bf16[2176,128]{1,0:T(8,128)(2,1)S(1)} %get-tuple-element.49.refs_2_), channel_id=1, source_target_pairs={{0,2},{1,3},{2,0},{3,1},{4,6},{5,7},{6,4},{7,5},{8,10},{9,11},{10,... | collective-permute-start | bytes 1671176 | tf_op jit(solution)/shard_map/ppermute | solution.py:361
  11.6 0.0 collective-permute-done.2.refs_1_
  11.6 0.1 shard_map.63
  11.7 1.5 %collective-permute-start.4 = (bf16[1088,128]{1,0:T(8,128)(2,1)S(1)}, bf16[1088,128]{1,0:T(8,128)(2,1)S(1)}, u32[]{:S(2)}, u32[]{:S(2)}) collective-permute-start(bf16[1088,128]{1,0:T(8,128)(2,1)S(1)} %get-tuple-element.52.refs_2_), channel_id=1, source_target_pairs={{0,3},{1,7},{2,4},{3,0},{4,2},{5,6},{6,5},{7,1},{8,14},{9,10},{10,... | collective-permute-start | bytes 835592 | tf_op jit(solution)/shard_map/ppermute | solution.py:368
  13.1 0.0 collective-permute-done.1.refs_1_
  13.2 0.1 shard_map.64
  13.2 1.9 %collective-permute-start.3 = (bf16[1088,128]{1,0:T(8,128)(2,1)S(1)}, bf16[1088,128]{1,0:T(8,128)(2,1)S(1)}, u32[]{:S(2)}, u32[]{:S(2)}) collective-permute-start(bf16[1088,128]{1,0:T(8,128)(2,1)S(1)} %get-tuple-element.54.refs_2_), channel_id=1, source_target_pairs={{0,10},{1,7},{2,4},{3,9},{4,2},{5,15},{6,12},{7,1},{8,14},{9,3},{1... | collective-permute-start | bytes 835592 | tf_op jit(solution)/shard_map/ppermute | solution.py:368
  15.1 2.6 %collective-permute-done.4.refs_1_ = bf16[1088,128]{1,0:T(8,128)(2,1)S(1)} collective-permute-done((bf16[1088,128]{1,0:T(8,128)(2,1)S(1)}, bf16[1088,128]{1,0:T(8,128)(2,1)S(1)}, u32[]{:S(2)}, u32[]{:S(2)}) %collective-permute-start.4) | collective-permute-done | bytes 278560 | tf_op jit(solution)/shard_map/ppermute | solution.py:368
  17.7 0.1 shard_map.65
  17.8 1.8 %collective-permute-start.6 = (bf16[544,128]{1,0:T(8,128)(2,1)S(1)}, bf16[544,128]{1,0:T(8,128)(2,1)S(1)}, u32[]{:S(2)}, u32[]{:S(2)}) collective-permute-start(bf16[544,128]{1,0:T(8,128)(2,1)S(1)} %get-tuple-element.56.refs_2_), channel_id=1, source_target_pairs={{0,6},{1,11},{2,8},{3,5},{4,14},{5,3},{6,0},{7,13},{8,2},{9,15},{1... | collective-permute-start | bytes 417800 | tf_op jit(solution)/shard_map/ppermute | solution.py:368
  19.6 0.0 collective-permute-done.3.refs_1_
  19.6 0.1 shard_map.66
  19.6 1.8 %collective-permute-start.5 = (bf16[544,128]{1,0:T(8,128)(2,1)S(1)}, bf16[544,128]{1,0:T(8,128)(2,1)S(1)}, u32[]{:S(2)}, u32[]{:S(2)}) collective-permute-start(bf16[544,128]{1,0:T(8,128)(2,1)S(1)} %get-tuple-element.58.refs_2_), channel_id=1, source_target_pairs={{0,3},{1,11},{2,8},{3,0},{4,14},{5,6},{6,5},{7,13},{8,2},{9,10},{1... | collective-permute-start | bytes 417800 | tf_op jit(solution)/shard_map/ppermute | solution.py:368
  21.4 1.1 %collective-permute-done.6.refs_1_ = bf16[544,128]{1,0:T(8,128)(2,1)S(1)} collective-permute-done((bf16[544,128]{1,0:T(8,128)(2,1)S(1)}, bf16[544,128]{1,0:T(8,128)(2,1)S(1)}, u32[]{:S(2)}, u32[]{:S(2)}) %collective-permute-start.6) | collective-permute-done | bytes 139296 | tf_op jit(solution)/shard_map/ppermute | solution.py:368
  22.5 1.7 %collective-permute-start.8 = (bf16[272,128]{1,0:T(8,128)(2,1)S(1)}, bf16[272,128]{1,0:T(8,128)(2,1)S(1)}, u32[]{:S(2)}, u32[]{:S(2)}) collective-permute-start(bf16[272,128]{1,0:T(8,128)(2,1)S(1)} %get-tuple-element.60.refs_2_), channel_id=1, source_target_pairs={{0,10},{1,2},{2,1},{3,9},{4,7},{5,15},{6,12},{7,4},{8,11},{9,3},{1... | collective-permute-start | bytes 208904 | tf_op jit(solution)/shard_map/ppermute | solution.py:368
  24.2 0.0 collective-permute-done.5.refs_1_
  24.2 2.1 %collective-permute-start.7 = (bf16[272,128]{1,0:T(8,128)(2,1)S(1)}, bf16[272,128]{1,0:T(8,128)(2,1)S(1)}, u32[]{:S(2)}, u32[]{:S(2)}) collective-permute-start(bf16[272,128]{1,0:T(8,128)(2,1)S(1)} %get-tuple-element.62.refs_2_), channel_id=1, source_target_pairs={{0,6},{1,2},{2,1},{3,5},{4,7},{5,3},{6,0},{7,4},{8,11},{9,15},{10,... | collective-permute-start | bytes 208904 | tf_op jit(solution)/shard_map/ppermute | solution.py:368
  26.3 0.5 collective-permute-done.8.refs_1_
  26.8 2.2 %collective-permute-start.10 = (bf16[272,128]{1,0:T(8,128)(2,1)S(1)}, bf16[272,128]{1,0:T(8,128)(2,1)S(1)}, u32[]{:S(2)}, u32[]{:S(2)}) collective-permute-start(bf16[272,128]{1,0:T(8,128)(2,1)S(1)} %shard_map.69.refs_2_.refs_0_), channel_id=1, source_target_pairs={{0,18},{1,19},{2,16},{3,17},{4,22},{5,23},{6,20},{7,21},{8,26},{9,... | collective-permute-start | bytes 208904 | tf_op jit(solution)/shard_map/ppermute | solution.py:368
  29.0 0.0 collective-permute-done.7.refs_1_
  29.1 2.5 %collective-permute-start.9 = (bf16[272,128]{1,0:T(8,128)(2,1)S(1)}, bf16[272,128]{1,0:T(8,128)(2,1)S(1)}, u32[]{:S(2)}, u32[]{:S(2)}) collective-permute-start(bf16[272,128]{1,0:T(8,128)(2,1)S(1)} %shard_map.70.refs_2_.refs_0_), channel_id=1, source_target_pairs={{0,18},{1,19},{2,16},{3,17},{4,22},{5,23},{6,20},{7,21},{8,26},{9,... | collective-permute-start | bytes 208904 | tf_op jit(solution)/shard_map/ppermute | solution.py:368
  31.5 0.0 collective-permute-done.10.refs_1_
  31.6 2.6 %collective-permute-start.12 = (bf16[272,128]{1,0:T(8,128)(2,1)S(1)}, bf16[272,128]{1,0:T(8,128)(2,1)S(1)}, u32[]{:S(2)}, u32[]{:S(2)}) collective-permute-start(bf16[272,128]{1,0:T(8,128)(2,1)S(1)} %shard_map.71.refs_2_.refs_0_), channel_id=1, source_target_pairs={{0,10},{1,2},{2,1},{3,9},{4,7},{5,15},{6,12},{7,4},{8,11},{9,3},{1... | collective-permute-start | bytes 208904 | tf_op jit(solution)/shard_map/ppermute | solution.py:368
  34.2 2.5 %collective-permute-done.9.refs_1_ = bf16[272,128]{1,0:T(8,128)(2,1)S(1)} collective-permute-done((bf16[272,128]{1,0:T(8,128)(2,1)S(1)}, bf16[272,128]{1,0:T(8,128)(2,1)S(1)}, u32[]{:S(2)}, u32[]{:S(2)}) %collective-permute-start.9) | collective-permute-done | bytes 69664 | tf_op jit(solution)/shard_map/ppermute | solution.py:368
  36.7 1.5 %collective-permute-start.11 = (bf16[272,128]{1,0:T(8,128)(2,1)S(1)}, bf16[272,128]{1,0:T(8,128)(2,1)S(1)}, u32[]{:S(2)}, u32[]{:S(2)}) collective-permute-start(bf16[272,128]{1,0:T(8,128)(2,1)S(1)} %shard_map.72.refs_2_.refs_0_), channel_id=1, source_target_pairs={{0,6},{1,2},{2,1},{3,5},{4,7},{5,3},{6,0},{7,4},{8,11},{9,15},{10,... | collective-permute-start | bytes 208904 | tf_op jit(solution)/shard_map/ppermute | solution.py:368
  38.2 0.0 collective-permute-done.12.refs_1_
  38.2 0.6 %collective-permute-start.14 = (bf16[544,128]{1,0:T(8,128)(2,1)S(1)}, bf16[544,128]{1,0:T(8,128)(2,1)S(1)}, u32[]{:S(2)}, u32[]{:S(2)}) collective-permute-start(bf16[544,128]{1,0:T(8,128)(2,1)S(1)} %shard_map.73.refs_2_.refs_0_), channel_id=1, source_target_pairs={{0,6},{1,11},{2,8},{3,5},{4,14},{5,3},{6,0},{7,13},{8,2},{9,15},{1... | collective-permute-start | bytes 417800 | tf_op jit(solution)/shard_map/ppermute | solution.py:368
  38.8 1.7 %collective-permute-done.11.refs_1_ = bf16[272,128]{1,0:T(8,128)(2,1)S(1)} collective-permute-done((bf16[272,128]{1,0:T(8,128)(2,1)S(1)}, bf16[272,128]{1,0:T(8,128)(2,1)S(1)}, u32[]{:S(2)}, u32[]{:S(2)}) %collective-permute-start.11) | collective-permute-done | bytes 69664 | tf_op jit(solution)/shard_map/ppermute | solution.py:368
  40.5 1.6 %collective-permute-start.13 = (bf16[544,128]{1,0:T(8,128)(2,1)S(1)}, bf16[544,128]{1,0:T(8,128)(2,1)S(1)}, u32[]{:S(2)}, u32[]{:S(2)}) collective-permute-start(bf16[544,128]{1,0:T(8,128)(2,1)S(1)} %shard_map.74.refs_2_.refs_0_), channel_id=1, source_target_pairs={{0,3},{1,11},{2,8},{3,0},{4,14},{5,6},{6,5},{7,13},{8,2},{9,10},{1... | collective-permute-start | bytes 417800 | tf_op jit(solution)/shard_map/ppermute | solution.py:368
  42.1 0.7 %collective-permute-done.14.refs_1_ = bf16[544,128]{1,0:T(8,128)(2,1)S(1)} collective-permute-done((bf16[544,128]{1,0:T(8,128)(2,1)S(1)}, bf16[544,128]{1,0:T(8,128)(2,1)S(1)}, u32[]{:S(2)}, u32[]{:S(2)}) %collective-permute-start.14) | collective-permute-done | bytes 139296 | tf_op jit(solution)/shard_map/ppermute | solution.py:368
  42.8 0.5 collective-permute-start.16
  43.3 1.8 %collective-permute-done.13.refs_1_ = bf16[544,128]{1,0:T(8,128)(2,1)S(1)} collective-permute-done((bf16[544,128]{1,0:T(8,128)(2,1)S(1)}, bf16[544,128]{1,0:T(8,128)(2,1)S(1)}, u32[]{:S(2)}, u32[]{:S(2)}) %collective-permute-start.13) | collective-permute-done | bytes 139296 | tf_op jit(solution)/shard_map/ppermute | solution.py:368
  45.1 0.7 %collective-permute-start.15 = (bf16[1088,128]{1,0:T(8,128)(2,1)S(1)}, bf16[1088,128]{1,0:T(8,128)(2,1)S(1)}, u32[]{:S(2)}, u32[]{:S(2)}) collective-permute-start(bf16[1088,128]{1,0:T(8,128)(2,1)S(1)} %shard_map.76.refs_1_.refs_0_), channel_id=1, source_target_pairs={{0,10},{1,7},{2,4},{3,9},{4,2},{5,15},{6,12},{7,1},{8,14},{9,3},{1... | collective-permute-start | bytes 835592 | tf_op jit(solution)/shard_map/ppermute | solution.py:368
  45.8 1.1 %shard_map.77 = (f32[1728,128]{1,0:T(8,128)}, f32[3456,256]{1,0:T(8,128)}, f32[8,128]{1,0:T(8,128)S(1)}) custom-call(bf16[1088,128]{1,0:T(8,128)(2,1)S(1)} %shard_map.75.refs_2_.refs_0_, bf16[1088,128]{1,0:T(8,128)(2,1)S(1)} %shard_map.76.refs_1_.refs_0_), custom_call_target="tpu_custom_call" | custom-call | flops 4000000000 | bytes 80000000 | tf_op jit(solution)/shard_map/pallas_call | solution.py:490
  47.0 1.5 %collective-permute-start.17 = (bf16[1088,128]{1,0:T(8,128)(2,1)S(1)}, bf16[1088,128]{1,0:T(8,128)(2,1)S(1)}, u32[]{:S(2)}, u32[]{:S(2)}) collective-permute-start(bf16[1088,128]{1,0:T(8,128)(2,1)S(1)} %shard_map.79), channel_id=1, source_target_pairs={{0,2},{1,3},{2,0},{3,1},{4,6},{5,7},{6,4},{7,5},{8,10},{9,11},{10,... | collective-permute-start | bytes 835592 | tf_op jit(solution)/shard_map/ppermute | solution.py:361
  48.5 0.1 collective-permute-start.18
  48.5 0.3 collective-permute-done.16.refs_0_
  48.8 0.9 %collective-permute-start.20 = (bf16[1088,128]{1,0:T(8,128)(2,1)S(1)}, bf16[1088,128]{1,0:T(8,128)(2,1)S(1)}, u32[]{:S(2)}, u32[]{:S(2)}) collective-permute-start(bf16[1088,128]{1,0:T(8,128)(2,1)S(1)} %shard_map.78.refs_2_.refs_1_), channel_id=1, source_target_pairs={{0,2},{1,3},{2,0},{3,1},{4,6},{5,7},{6,4},{7,5},{8,10},{9,11},{10,... | collective-permute-start | bytes 835592 | tf_op jit(solution)/shard_map/ppermute | solution.py:361
  49.7 0.0 collective-permute-done.17.refs_0_
  49.7 0.4 collective-permute-done.18.refs_1_
  50.1 1.4 %shard_map.81 = (f32[1728,128]{1,0:T(8,128)}, f32[3456,256]{1,0:T(8,128)}, f32[8,128]{1,0:T(8,128)S(1)}) custom-call(bf16[1088,128]{1,0:T(8,128)(2,1)S(1)} %collective-permute-done.17.refs_0_, bf16[1088,128]{1,0:T(8,128)(2,1)S(1)} %collective-permute-done.18.refs_1_, ...), custom_call_target="tpu_custom_call", output_to_operand_aliasing={{0}: (3, {}), {1}: (4, {})} | custom-call | flops 4000000000 | bytes 80000000 | tf_op jit(solution)/shard_map/pallas_call | solution.py:490
  51.5 0.0 collective-permute-done.15.refs_0_
  51.5 0.9 %collective-permute-start.19 = (bf16[1088,128]{1,0:T(8,128)(2,1)S(1)}, bf16[1088,128]{1,0:T(8,128)(2,1)S(1)}, u32[]{:S(2)}, u32[]{:S(2)}) collective-permute-start(bf16[1088,128]{1,0:T(8,128)(2,1)S(1)} %shard_map.82.refs_1_), channel_id=1, source_target_pairs={{0,2},{1,3},{2,0},{3,1},{4,6},{5,7},{6,4},{7,5},{8,10},{9,11},{10,... | collective-permute-start | bytes 835592 | tf_op jit(solution)/shard_map/ppermute | solution.py:361
  52.4 0.0 collective-permute-done.20.refs_0_
  52.4 1.1 %shard_map.83 = (f32[1728,128]{1,0:T(8,128)}, f32[3456,256]{1,0:T(8,128)}) custom-call(bf16[1088,128]{1,0:T(8,128)(2,1)S(1)} %collective-permute-done.20.refs_0_, bf16[1088,128]{1,0:T(8,128)(2,1)S(1)} %shard_map.82.refs_1_, f32[1728,128]{1,0:T(8,128)} %get-tuple-element.68.refs_2_, ...), custom_call_target="tpu_custom_call", output_to_operand_aliasing={{0}: (2, {}), {1}: (3, {})} | custom-call | flops 4000000000 | bytes 80000000 | tf_op jit(solution)/shard_map/pallas_call | solution.py:490
  53.6 0.0 collective-permute-done.19.refs_0_
  53.6 0.9 %shard_map.84 = (f32[1728,128]{1,0:T(8,128)}, f32[3456,256]{1,0:T(8,128)}) custom-call(bf16[1088,128]{1,0:T(8,128)(2,1)S(1)} %collective-permute-done.19.refs_0_, f32[1728,128]{1,0:T(8,128)} %get-tuple-element.70.refs_1_, f32[3456,256]{1,0:T(8,128)} %get-tuple-element.71.refs_2_), custom_call_target="tpu_custom_call", output_to_operand_aliasing={{0}: (1, {}), {1}: (2, {})} | custom-call | flops 4000000000 | bytes 80000000 | tf_op jit(solution)/shard_map/pallas_call | solution.py:490
  (14 shorter events, 0.3 us)
Async XLA Ops:
  1.5 5.7 %collective-permute-start = (bf16[3,16,1024]{2,1,0:T(8,128)(2,1)S(1)}, bf16[3,16,1024]{2,1,0:T(8,128)(2,1)S(1)}, u32[]{:S(2)}, u32[]{:S(2)}) collective-permute-start(bf16[3,16,1024]{2,1,0:T(8,128)(2,1)S(1)} %slice_bitcast_fusion.refs_2_), channel_id=1, source_target_pairs={{0,1},{1,0},{2,3},{3,2},{4,5},{5,4},{6,7},{7,6},{8,9},{9,8},{10,11... | collective-permute-start | bytes 294920 | tf_op jit(solution)/shard_map/ppermute | solution.py:378
  5.8 1.5 %copy-start = (bf16[3456,256]{1,0:T(8,128)(2,1)S(1)}, bf16[3456,256]{1,0:T(8,128)(2,1)}, u32[]{:S(2)}) copy-start(bf16[3456,256]{1,0:T(8,128)(2,1)} %refs_7_.1) | copy-start | bytes 5308420
  9.1 2.5 %collective-permute-start.2 = (bf16[2176,128]{1,0:T(8,128)(2,1)S(1)}, bf16[2176,128]{1,0:T(8,128)(2,1)S(1)}, u32[]{:S(2)}, u32[]{:S(2)}) collective-permute-start(bf16[2176,128]{1,0:T(8,128)(2,1)S(1)} %get-tuple-element.51), channel_id=1, source_target_pairs={{0,2},{1,3},{2,0},{3,1},{4,6},{5,7},{6,4},{7,5},{8,10},{9,11},{10,... | collective-permute-start | bytes 1671176 | tf_op jit(solution)/shard_map/ppermute | solution.py:361
  11.0 2.2 %collective-permute-start.1 = (bf16[2176,128]{1,0:T(8,128)(2,1)S(1)}, bf16[2176,128]{1,0:T(8,128)(2,1)S(1)}, u32[]{:S(2)}, u32[]{:S(2)}) collective-permute-start(bf16[2176,128]{1,0:T(8,128)(2,1)S(1)} %get-tuple-element.49.refs_2_), channel_id=1, source_target_pairs={{0,2},{1,3},{2,0},{3,1},{4,6},{5,7},{6,4},{7,5},{8,10},{9,11},{10,... | collective-permute-start | bytes 1671176 | tf_op jit(solution)/shard_map/ppermute | solution.py:361
  11.7 6.0 %collective-permute-start.4 = (bf16[1088,128]{1,0:T(8,128)(2,1)S(1)}, bf16[1088,128]{1,0:T(8,128)(2,1)S(1)}, u32[]{:S(2)}, u32[]{:S(2)}) collective-permute-start(bf16[1088,128]{1,0:T(8,128)(2,1)S(1)} %get-tuple-element.52.refs_2_), channel_id=1, source_target_pairs={{0,3},{1,7},{2,4},{3,0},{4,2},{5,6},{6,5},{7,1},{8,14},{9,10},{10,... | collective-permute-start | bytes 835592 | tf_op jit(solution)/shard_map/ppermute | solution.py:368
  13.2 6.3 %collective-permute-start.3 = (bf16[1088,128]{1,0:T(8,128)(2,1)S(1)}, bf16[1088,128]{1,0:T(8,128)(2,1)S(1)}, u32[]{:S(2)}, u32[]{:S(2)}) collective-permute-start(bf16[1088,128]{1,0:T(8,128)(2,1)S(1)} %get-tuple-element.54.refs_2_), channel_id=1, source_target_pairs={{0,10},{1,7},{2,4},{3,9},{4,2},{5,15},{6,12},{7,1},{8,14},{9,3},{1... | collective-permute-start | bytes 835592 | tf_op jit(solution)/shard_map/ppermute | solution.py:368
  17.8 4.7 %collective-permute-start.6 = (bf16[544,128]{1,0:T(8,128)(2,1)S(1)}, bf16[544,128]{1,0:T(8,128)(2,1)S(1)}, u32[]{:S(2)}, u32[]{:S(2)}) collective-permute-start(bf16[544,128]{1,0:T(8,128)(2,1)S(1)} %get-tuple-element.56.refs_2_), channel_id=1, source_target_pairs={{0,6},{1,11},{2,8},{3,5},{4,14},{5,3},{6,0},{7,13},{8,2},{9,15},{1... | collective-permute-start | bytes 417800 | tf_op jit(solution)/shard_map/ppermute | solution.py:368
  19.6 4.6 %collective-permute-start.5 = (bf16[544,128]{1,0:T(8,128)(2,1)S(1)}, bf16[544,128]{1,0:T(8,128)(2,1)S(1)}, u32[]{:S(2)}, u32[]{:S(2)}) collective-permute-start(bf16[544,128]{1,0:T(8,128)(2,1)S(1)} %get-tuple-element.58.refs_2_), channel_id=1, source_target_pairs={{0,3},{1,11},{2,8},{3,0},{4,14},{5,6},{6,5},{7,13},{8,2},{9,10},{1... | collective-permute-start | bytes 417800 | tf_op jit(solution)/shard_map/ppermute | solution.py:368
  22.5 4.2 %collective-permute-start.8 = (bf16[272,128]{1,0:T(8,128)(2,1)S(1)}, bf16[272,128]{1,0:T(8,128)(2,1)S(1)}, u32[]{:S(2)}, u32[]{:S(2)}) collective-permute-start(bf16[272,128]{1,0:T(8,128)(2,1)S(1)} %get-tuple-element.60.refs_2_), channel_id=1, source_target_pairs={{0,10},{1,2},{2,1},{3,9},{4,7},{5,15},{6,12},{7,4},{8,11},{9,3},{1... | collective-permute-start | bytes 208904 | tf_op jit(solution)/shard_map/ppermute | solution.py:368
  24.2 4.8 %collective-permute-start.7 = (bf16[272,128]{1,0:T(8,128)(2,1)S(1)}, bf16[272,128]{1,0:T(8,128)(2,1)S(1)}, u32[]{:S(2)}, u32[]{:S(2)}) collective-permute-start(bf16[272,128]{1,0:T(8,128)(2,1)S(1)} %get-tuple-element.62.refs_2_), channel_id=1, source_target_pairs={{0,6},{1,2},{2,1},{3,5},{4,7},{5,3},{6,0},{7,4},{8,11},{9,15},{10,... | collective-permute-start | bytes 208904 | tf_op jit(solution)/shard_map/ppermute | solution.py:368
  26.8 4.7 %collective-permute-start.10 = (bf16[272,128]{1,0:T(8,128)(2,1)S(1)}, bf16[272,128]{1,0:T(8,128)(2,1)S(1)}, u32[]{:S(2)}, u32[]{:S(2)}) collective-permute-start(bf16[272,128]{1,0:T(8,128)(2,1)S(1)} %shard_map.69.refs_2_.refs_0_), channel_id=1, source_target_pairs={{0,18},{1,19},{2,16},{3,17},{4,22},{5,23},{6,20},{7,21},{8,26},{9,... | collective-permute-start | bytes 208904 | tf_op jit(solution)/shard_map/ppermute | solution.py:368
  29.1 7.6 %collective-permute-start.9 = (bf16[272,128]{1,0:T(8,128)(2,1)S(1)}, bf16[272,128]{1,0:T(8,128)(2,1)S(1)}, u32[]{:S(2)}, u32[]{:S(2)}) collective-permute-start(bf16[272,128]{1,0:T(8,128)(2,1)S(1)} %shard_map.70.refs_2_.refs_0_), channel_id=1, source_target_pairs={{0,18},{1,19},{2,16},{3,17},{4,22},{5,23},{6,20},{7,21},{8,26},{9,... | collective-permute-start | bytes 208904 | tf_op jit(solution)/shard_map/ppermute | solution.py:368
  31.6 6.6 %collective-permute-start.12 = (bf16[272,128]{1,0:T(8,128)(2,1)S(1)}, bf16[272,128]{1,0:T(8,128)(2,1)S(1)}, u32[]{:S(2)}, u32[]{:S(2)}) collective-permute-start(bf16[272,128]{1,0:T(8,128)(2,1)S(1)} %shard_map.71.refs_2_.refs_0_), channel_id=1, source_target_pairs={{0,10},{1,2},{2,1},{3,9},{4,7},{5,15},{6,12},{7,4},{8,11},{9,3},{1... | collective-permute-start | bytes 208904 | tf_op jit(solution)/shard_map/ppermute | solution.py:368
  36.7 3.8 %collective-permute-start.11 = (bf16[272,128]{1,0:T(8,128)(2,1)S(1)}, bf16[272,128]{1,0:T(8,128)(2,1)S(1)}, u32[]{:S(2)}, u32[]{:S(2)}) collective-permute-start(bf16[272,128]{1,0:T(8,128)(2,1)S(1)} %shard_map.72.refs_2_.refs_0_), channel_id=1, source_target_pairs={{0,6},{1,2},{2,1},{3,5},{4,7},{5,3},{6,0},{7,4},{8,11},{9,15},{10,... | collective-permute-start | bytes 208904 | tf_op jit(solution)/shard_map/ppermute | solution.py:368
  38.2 4.5 %collective-permute-start.14 = (bf16[544,128]{1,0:T(8,128)(2,1)S(1)}, bf16[544,128]{1,0:T(8,128)(2,1)S(1)}, u32[]{:S(2)}, u32[]{:S(2)}) collective-permute-start(bf16[544,128]{1,0:T(8,128)(2,1)S(1)} %shard_map.73.refs_2_.refs_0_), channel_id=1, source_target_pairs={{0,6},{1,11},{2,8},{3,5},{4,14},{5,3},{6,0},{7,13},{8,2},{9,15},{1... | collective-permute-start | bytes 417800 | tf_op jit(solution)/shard_map/ppermute | solution.py:368
  40.5 4.5 %collective-permute-start.13 = (bf16[544,128]{1,0:T(8,128)(2,1)S(1)}, bf16[544,128]{1,0:T(8,128)(2,1)S(1)}, u32[]{:S(2)}, u32[]{:S(2)}) collective-permute-start(bf16[544,128]{1,0:T(8,128)(2,1)S(1)} %shard_map.74.refs_2_.refs_0_), channel_id=1, source_target_pairs={{0,3},{1,11},{2,8},{3,0},{4,14},{5,6},{6,5},{7,13},{8,2},{9,10},{1... | collective-permute-start | bytes 417800 | tf_op jit(solution)/shard_map/ppermute | solution.py:368
  42.8 6.0 %collective-permute-start.16 = (bf16[1088,128]{1,0:T(8,128)(2,1)S(1)}, bf16[1088,128]{1,0:T(8,128)(2,1)S(1)}, u32[]{:S(2)}, u32[]{:S(2)}) collective-permute-start(bf16[1088,128]{1,0:T(8,128)(2,1)S(1)} %shard_map.75.refs_2_.refs_0_), channel_id=1, source_target_pairs={{0,3},{1,7},{2,4},{3,0},{4,2},{5,6},{6,5},{7,1},{8,14},{9,10},{10,... | collective-permute-start | bytes 835592 | tf_op jit(solution)/shard_map/ppermute | solution.py:368
  45.1 6.4 %collective-permute-start.15 = (bf16[1088,128]{1,0:T(8,128)(2,1)S(1)}, bf16[1088,128]{1,0:T(8,128)(2,1)S(1)}, u32[]{:S(2)}, u32[]{:S(2)}) collective-permute-start(bf16[1088,128]{1,0:T(8,128)(2,1)S(1)} %shard_map.76.refs_1_.refs_0_), channel_id=1, source_target_pairs={{0,10},{1,7},{2,4},{3,9},{4,2},{5,15},{6,12},{7,1},{8,14},{9,3},{1... | collective-permute-start | bytes 835592 | tf_op jit(solution)/shard_map/ppermute | solution.py:368
  47.0 2.8 %collective-permute-start.17 = (bf16[1088,128]{1,0:T(8,128)(2,1)S(1)}, bf16[1088,128]{1,0:T(8,128)(2,1)S(1)}, u32[]{:S(2)}, u32[]{:S(2)}) collective-permute-start(bf16[1088,128]{1,0:T(8,128)(2,1)S(1)} %shard_map.79), channel_id=1, source_target_pairs={{0,2},{1,3},{2,0},{3,1},{4,6},{5,7},{6,4},{7,5},{8,10},{9,11},{10,... | collective-permute-start | bytes 835592 | tf_op jit(solution)/shard_map/ppermute | solution.py:361
  48.5 1.6 %collective-permute-start.18 = (bf16[1088,128]{1,0:T(8,128)(2,1)S(1)}, bf16[1088,128]{1,0:T(8,128)(2,1)S(1)}, u32[]{:S(2)}, u32[]{:S(2)}) collective-permute-start(bf16[1088,128]{1,0:T(8,128)(2,1)S(1)} %shard_map.80), channel_id=1, source_target_pairs={{0,2},{1,3},{2,0},{3,1},{4,6},{5,7},{6,4},{7,5},{8,10},{9,11},{10,... | collective-permute-start | bytes 835592 | tf_op jit(solution)/shard_map/ppermute | solution.py:361
  48.8 3.6 %collective-permute-start.20 = (bf16[1088,128]{1,0:T(8,128)(2,1)S(1)}, bf16[1088,128]{1,0:T(8,128)(2,1)S(1)}, u32[]{:S(2)}, u32[]{:S(2)}) collective-permute-start(bf16[1088,128]{1,0:T(8,128)(2,1)S(1)} %shard_map.78.refs_2_.refs_1_), channel_id=1, source_target_pairs={{0,2},{1,3},{2,0},{3,1},{4,6},{5,7},{6,4},{7,5},{8,10},{9,11},{10,... | collective-permute-start | bytes 835592 | tf_op jit(solution)/shard_map/ppermute | solution.py:361
  51.5 2.1 %collective-permute-start.19 = (bf16[1088,128]{1,0:T(8,128)(2,1)S(1)}, bf16[1088,128]{1,0:T(8,128)(2,1)S(1)}, u32[]{:S(2)}, u32[]{:S(2)}) collective-permute-start(bf16[1088,128]{1,0:T(8,128)(2,1)S(1)} %shard_map.82.refs_1_), channel_id=1, source_target_pairs={{0,2},{1,3},{2,0},{3,1},{4,6},{5,7},{6,4},{7,5},{8,10},{9,11},{10,... | collective-permute-start | bytes 835592 | tf_op jit(solution)/shard_map/ppermute | solution.py:361

commit v7 on v6

--- a/solution.py
+++ b/solution.py
@@ -392,7 +392,7 @@
         scratch=[
             pltpu.VMEM(slab.shape, bf16),
             pltpu.VMEM(w_first.shape, bf16),
-            pltpu.VMEM((depth - 1, 8, 24, LANES), f32),
+            pltpu.VMEM((depth - 1, 8, 32, LANES), f32),
             pltpu.SemaphoreType.DMA((3,)),
         ],
         after=(face,),
@@ -431,7 +431,7 @@
         picked_up,
         w2,
         cot,
-        scratch=[pltpu.VMEM((3, 8, 24, LANES), f32), pltpu.VMEM((288, LANES), bf16)],
+        scratch=[pltpu.VMEM((3, 8, 32, LANES), f32), pltpu.VMEM((288, LANES), bf16)],
     )
     recv0 = swap_core(send0)
     keep1, send1 = call(

time: 54.7 us -> 54.7 us (level)
  transfers between devices with their start and end apart: 21 -> 21, of which waited for: 10 -> 11; matrix products, arithmetic and copies ran while one was open for 0% -> 0% of each run, Pallas kernels for 16% -> 16%
where the time goes in v7:
time: 54.7 us; the launch traced here: 54.5 us
  starting transfers between devices  29.7 us (54%)
  waiting for transfers between devices  11.5 us (21%)
  Pallas kernels  11.4 us (21%)
  local copies, waits for them, and re-layouts  1.03 us (2%)
  between operations  0.79 us (1%)
    ppermute x14, starting transfers between devices, swap(): return lax.ppermute(array, BOTH, pairs)  22.8 us
    ppermute x14, waiting for transfers between devices, swap(): return lax.ppermute(array, BOTH, pairs)  11 us
    pallas_call x22, Pallas kernels, call(): pl.pallas_call(run, out_shape=shapes, in_specs=(specs or [full(a.shape) f...  6.83 us
    pallas_call x4, Pallas kernels, write(): pl.pallas_call(functools.partial(final_kernel, bits, spatial_count, jobs,...  4.6 us
    ppermute x6, starting transfers between devices, swap_core(): lax.ppermute(array, BOTH, [(i, i ^ 1 << core_bit) for i in range(count)])  3.96 us
    ppermute x1, starting transfers between devices, body(): lax.ppermute(face, 'spatial', [(i, (i + 1) % spatial_count) for i in rang...  2.94 us
  transfers between devices with their start and end apart: 21, of which 11 were waited for; matrix products, arithmetic and copies ran while one was open for 0% of the time, Pallas kernels for 16%

profile of v7, /device:TPU:0, one launch (start us, length us, event | category | flops | bytes accessed | tf_op | source)
XLA Modules:
  0.0 54.5 jit_solution(4319901118474603918)
XLA Ops:
  0.6 0.9 %slice_bitcast_fusion.refs_2_ = bf16[3,16,1024]{2,1,0:T(8,128)(2,1)S(1)} fusion(bf16[1,16,16,1024]{3,2,1,0:T(8,128)(2,1)} %param.4), kind=kLoop, calls=%fused_computation | loop fusion | bytes 196608 | tf_op jit(solution)/shard_map/slice | solution.py:377
  1.5 2.9 %collective-permute-start = (bf16[3,16,1024]{2,1,0:T(8,128)(2,1)S(1)}, bf16[3,16,1024]{2,1,0:T(8,128)(2,1)S(1)}, u32[]{:S(2)}, u32[]{:S(2)}) collective-permute-start(bf16[3,16,1024]{2,1,0:T(8,128)(2,1)S(1)} %slice_bitcast_fusion.refs_2_), channel_id=1, source_target_pairs={{0,1},{1,0},{2,3},{3,2},{4,5},{5,4},{6,7},{7,6},{8,9},{9,8},{10,11... | collective-permute-start | bytes 294920 | tf_op jit(solution)/shard_map/ppermute | solution.py:378
  4.5 1.4 %shard_map.59 = (bf16[64,2304]{1,0:T(8,128)(2,1)S(1)}, bf16[448,2304]{1,0:T(8,128)(2,1)S(1)}, bf16[2304,128]{1,0:T(8,128)(2,1)S(1)}) custom-call(bf16[16,16,1024]{2,1,0:T(8,128)(2,1)} %bitcast.5, bf16[1728,128]{1,0:T(8,128)(2,1)} %refs_1_.1, bf16[3,16,1024]{2,1,0:T(8,128)(2,1)S(1)} %slice_bitcast_fusion.refs_2_), custom_call_target="tpu_custom_call" | custom-call | flops 4000000000 | bytes 80000000 | tf_op jit(solution)/shard_map/pallas_call | solution.py:37
  5.9 0.0 copy-start
  5.9 1.3 %shard_map.60 = (f32[448,128]{1,0:T(8,128)S(1)}, bf16[1008,128]{1,0:T(8,128)(2,1)S(1)}, f32[64,256]{1,0:T(8,128)S(1)}) custom-call(bf16[448,2304]{1,0:T(8,128)(2,1)S(1)} %get-tuple-element.37.refs_0_, bf16[2304,128]{1,0:T(8,128)(2,1)S(1)} %get-tuple-element.39.refs_1_.refs_2_, bf16[4,4,1024]{2,1,0:T(4,128)(2,1)} %bitcast.4), custom_call_target="tpu_custom_call" | custom-call | flops 400000000 | bytes 10000000 | tf_op jit(solution)/shard_map/pallas_call | solution.py:37
  7.2 0.1 collective-permute-done.refs_0_
  7.3 0.1 copy-done
  7.4 1.8 %shard_map.61 = (f32[2176,128]{1,0:T(8,128)S(1)}, bf16[2176,128]{1,0:T(8,128)(2,1)S(1)}, bf16[128,2304]{1,0:T(8,128)(2,1)S(1)}, f32[128,128]{1,0:T(8,128)S(1)}, ...) custom-call(bf16[3,16,1024]{2,1,0:T(8,128)(2,1)S(1)} %collective-permute-done.refs_0_, ...), custom_call_target="tpu_custom_call" | custom-call | tf_op jit(solution)/shard_map/pallas_call | solution.py:37
  9.1 0.1 collective-permute-start.2
  9.2 1.8 %shard_map.62 = (f32[2176,128]{1,0:T(8,128)S(1)}, bf16[2176,128]{1,0:T(8,128)(2,1)S(1)}) custom-call(bf16[448,2304]{1,0:T(8,128)(2,1)S(1)} %get-tuple-element.37.refs_0_, bf16[128,2304]{1,0:T(8,128)(2,1)S(1)} %get-tuple-element.42.refs_1_, f32[448,128]{1,0:T(8,128)S(1)} %get-tuple-element.43.refs_2_, f32[128,128]{1,0:T(8,128)S(1)} %get-tuple-element.44.refs_3_, ...), custom_call_target="tpu_custom_call" | custom-call | flops 1000000000 | bytes 10000000 | tf_op jit(solution)/shard_map/pallas_call | solution.py:37
  11.0 0.6 %collective-permute-start.1 = (bf16[2176,128]{1,0:T(8,128)(2,1)S(1)}, bf16[2176,128]{1,0:T(8,128)(2,1)S(1)}, u32[]{:S(2)}, u32[]{:S(2)}) collective-permute-start(bf16[2176,128]{1,0:T(8,128)(2,1)S(1)} %get-tuple-element.49.refs_2_), channel_id=1, source_target_pairs={{0,2},{1,3},{2,0},{3,1},{4,6},{5,7},{6,4},{7,5},{8,10},{9,11},{10,... | collective-permute-start | bytes 1671176 | tf_op jit(solution)/shard_map/ppermute | solution.py:361
  11.6 0.0 collective-permute-done.2.refs_1_
  11.6 0.1 shard_map.63
  11.7 1.4 %collective-permute-start.4 = (bf16[1088,128]{1,0:T(8,128)(2,1)S(1)}, bf16[1088,128]{1,0:T(8,128)(2,1)S(1)}, u32[]{:S(2)}, u32[]{:S(2)}) collective-permute-start(bf16[1088,128]{1,0:T(8,128)(2,1)S(1)} %get-tuple-element.52.refs_2_), channel_id=1, source_target_pairs={{0,3},{1,7},{2,4},{3,0},{4,2},{5,6},{6,5},{7,1},{8,14},{9,10},{10,... | collective-permute-start | bytes 835592 | tf_op jit(solution)/shard_map/ppermute | solution.py:368
  13.1 0.1 collective-permute-done.1.refs_1_
  13.2 0.1 shard_map.64
  13.3 1.8 %collective-permute-start.3 = (bf16[1088,128]{1,0:T(8,128)(2,1)S(1)}, bf16[1088,128]{1,0:T(8,128)(2,1)S(1)}, u32[]{:S(2)}, u32[]{:S(2)}) collective-permute-start(bf16[1088,128]{1,0:T(8,128)(2,1)S(1)} %get-tuple-element.54.refs_2_), channel_id=1, source_target_pairs={{0,10},{1,7},{2,4},{3,9},{4,2},{5,15},{6,12},{7,1},{8,14},{9,3},{1... | collective-permute-start | bytes 835592 | tf_op jit(solution)/shard_map/ppermute | solution.py:368
  15.1 2.6 %collective-permute-done.4.refs_1_ = bf16[1088,128]{1,0:T(8,128)(2,1)S(1)} collective-permute-done((bf16[1088,128]{1,0:T(8,128)(2,1)S(1)}, bf16[1088,128]{1,0:T(8,128)(2,1)S(1)}, u32[]{:S(2)}, u32[]{:S(2)}) %collective-permute-start.4) | collective-permute-done | bytes 278560 | tf_op jit(solution)/shard_map/ppermute | solution.py:368
  17.8 0.1 shard_map.65
  17.8 1.8 %collective-permute-start.6 = (bf16[544,128]{1,0:T(8,128)(2,1)S(1)}, bf16[544,128]{1,0:T(8,128)(2,1)S(1)}, u32[]{:S(2)}, u32[]{:S(2)}) collective-permute-start(bf16[544,128]{1,0:T(8,128)(2,1)S(1)} %get-tuple-element.56.refs_2_), channel_id=1, source_target_pairs={{0,6},{1,11},{2,8},{3,5},{4,14},{5,3},{6,0},{7,13},{8,2},{9,15},{1... | collective-permute-start | bytes 417800 | tf_op jit(solution)/shard_map/ppermute | solution.py:368
  19.6 0.0 collective-permute-done.3.refs_1_
  19.6 0.1 shard_map.66
  19.6 1.8 %collective-permute-start.5 = (bf16[544,128]{1,0:T(8,128)(2,1)S(1)}, bf16[544,128]{1,0:T(8,128)(2,1)S(1)}, u32[]{:S(2)}, u32[]{:S(2)}) collective-permute-start(bf16[544,128]{1,0:T(8,128)(2,1)S(1)} %get-tuple-element.58.refs_2_), channel_id=1, source_target_pairs={{0,3},{1,11},{2,8},{3,0},{4,14},{5,6},{6,5},{7,13},{8,2},{9,10},{1... | collective-permute-start | bytes 417800 | tf_op jit(solution)/shard_map/ppermute | solution.py:368
  21.4 1.1 %collective-permute-done.6.refs_1_ = bf16[544,128]{1,0:T(8,128)(2,1)S(1)} collective-permute-done((bf16[544,128]{1,0:T(8,128)(2,1)S(1)}, bf16[544,128]{1,0:T(8,128)(2,1)S(1)}, u32[]{:S(2)}, u32[]{:S(2)}) %collective-permute-start.6) | collective-permute-done | bytes 139296 | tf_op jit(solution)/shard_map/ppermute | solution.py:368
  22.5 1.7 %collective-permute-start.8 = (bf16[272,128]{1,0:T(8,128)(2,1)S(1)}, bf16[272,128]{1,0:T(8,128)(2,1)S(1)}, u32[]{:S(2)}, u32[]{:S(2)}) collective-permute-start(bf16[272,128]{1,0:T(8,128)(2,1)S(1)} %get-tuple-element.60.refs_2_), channel_id=1, source_target_pairs={{0,10},{1,2},{2,1},{3,9},{4,7},{5,15},{6,12},{7,4},{8,11},{9,3},{1... | collective-permute-start | bytes 208904 | tf_op jit(solution)/shard_map/ppermute | solution.py:368
  24.2 0.0 collective-permute-done.5.refs_1_
  24.2 2.1 %collective-permute-start.7 = (bf16[272,128]{1,0:T(8,128)(2,1)S(1)}, bf16[272,128]{1,0:T(8,128)(2,1)S(1)}, u32[]{:S(2)}, u32[]{:S(2)}) collective-permute-start(bf16[272,128]{1,0:T(8,128)(2,1)S(1)} %get-tuple-element.62.refs_2_), channel_id=1, source_target_pairs={{0,6},{1,2},{2,1},{3,5},{4,7},{5,3},{6,0},{7,4},{8,11},{9,15},{10,... | collective-permute-start | bytes 208904 | tf_op jit(solution)/shard_map/ppermute | solution.py:368
  26.3 0.4 collective-permute-done.8.refs_1_
  26.8 2.3 %collective-permute-start.10 = (bf16[272,128]{1,0:T(8,128)(2,1)S(1)}, bf16[272,128]{1,0:T(8,128)(2,1)S(1)}, u32[]{:S(2)}, u32[]{:S(2)}) collective-permute-start(bf16[272,128]{1,0:T(8,128)(2,1)S(1)} %shard_map.69.refs_2_.refs_0_), channel_id=1, source_target_pairs={{0,18},{1,19},{2,16},{3,17},{4,22},{5,23},{6,20},{7,21},{8,26},{9,... | collective-permute-start | bytes 208904 | tf_op jit(solution)/shard_map/ppermute | solution.py:368
  29.0 0.0 collective-permute-done.7.refs_1_
  29.1 2.5 %collective-permute-start.9 = (bf16[272,128]{1,0:T(8,128)(2,1)S(1)}, bf16[272,128]{1,0:T(8,128)(2,1)S(1)}, u32[]{:S(2)}, u32[]{:S(2)}) collective-permute-start(bf16[272,128]{1,0:T(8,128)(2,1)S(1)} %shard_map.70.refs_2_.refs_0_), channel_id=1, source_target_pairs={{0,18},{1,19},{2,16},{3,17},{4,22},{5,23},{6,20},{7,21},{8,26},{9,... | collective-permute-start | bytes 208904 | tf_op jit(solution)/shard_map/ppermute | solution.py:368
  31.5 0.0 collective-permute-done.10.refs_1_
  31.5 2.6 %collective-permute-start.12 = (bf16[272,128]{1,0:T(8,128)(2,1)S(1)}, bf16[272,128]{1,0:T(8,128)(2,1)S(1)}, u32[]{:S(2)}, u32[]{:S(2)}) collective-permute-start(bf16[272,128]{1,0:T(8,128)(2,1)S(1)} %shard_map.71.refs_2_.refs_0_), channel_id=1, source_target_pairs={{0,10},{1,2},{2,1},{3,9},{4,7},{5,15},{6,12},{7,4},{8,11},{9,3},{1... | collective-permute-start | bytes 208904 | tf_op jit(solution)/shard_map/ppermute | solution.py:368
  34.2 2.5 %collective-permute-done.9.refs_1_ = bf16[272,128]{1,0:T(8,128)(2,1)S(1)} collective-permute-done((bf16[272,128]{1,0:T(8,128)(2,1)S(1)}, bf16[272,128]{1,0:T(8,128)(2,1)S(1)}, u32[]{:S(2)}, u32[]{:S(2)}) %collective-permute-start.9) | collective-permute-done | bytes 69664 | tf_op jit(solution)/shard_map/ppermute | solution.py:368
  36.7 1.5 %collective-permute-start.11 = (bf16[272,128]{1,0:T(8,128)(2,1)S(1)}, bf16[272,128]{1,0:T(8,128)(2,1)S(1)}, u32[]{:S(2)}, u32[]{:S(2)}) collective-permute-start(bf16[272,128]{1,0:T(8,128)(2,1)S(1)} %shard_map.72.refs_2_.refs_0_), channel_id=1, source_target_pairs={{0,6},{1,2},{2,1},{3,5},{4,7},{5,3},{6,0},{7,4},{8,11},{9,15},{10,... | collective-permute-start | bytes 208904 | tf_op jit(solution)/shard_map/ppermute | solution.py:368
  38.2 0.0 collective-permute-done.12.refs_1_
  38.2 0.6 %collective-permute-start.14 = (bf16[544,128]{1,0:T(8,128)(2,1)S(1)}, bf16[544,128]{1,0:T(8,128)(2,1)S(1)}, u32[]{:S(2)}, u32[]{:S(2)}) collective-permute-start(bf16[544,128]{1,0:T(8,128)(2,1)S(1)} %shard_map.73.refs_2_.refs_0_), channel_id=1, source_target_pairs={{0,6},{1,11},{2,8},{3,5},{4,14},{5,3},{6,0},{7,13},{8,2},{9,15},{1... | collective-permute-start | bytes 417800 | tf_op jit(solution)/shard_map/ppermute | solution.py:368
  38.8 1.7 %collective-permute-done.11.refs_1_ = bf16[272,128]{1,0:T(8,128)(2,1)S(1)} collective-permute-done((bf16[272,128]{1,0:T(8,128)(2,1)S(1)}, bf16[272,128]{1,0:T(8,128)(2,1)S(1)}, u32[]{:S(2)}, u32[]{:S(2)}) %collective-permute-start.11) | collective-permute-done | bytes 69664 | tf_op jit(solution)/shard_map/ppermute | solution.py:368
  40.5 1.6 %collective-permute-start.13 = (bf16[544,128]{1,0:T(8,128)(2,1)S(1)}, bf16[544,128]{1,0:T(8,128)(2,1)S(1)}, u32[]{:S(2)}, u32[]{:S(2)}) collective-permute-start(bf16[544,128]{1,0:T(8,128)(2,1)S(1)} %shard_map.74.refs_2_.refs_0_), channel_id=1, source_target_pairs={{0,3},{1,11},{2,8},{3,0},{4,14},{5,6},{6,5},{7,13},{8,2},{9,10},{1... | collective-permute-start | bytes 417800 | tf_op jit(solution)/shard_map/ppermute | solution.py:368
  42.1 0.7 %collective-permute-done.14.refs_1_ = bf16[544,128]{1,0:T(8,128)(2,1)S(1)} collective-permute-done((bf16[544,128]{1,0:T(8,128)(2,1)S(1)}, bf16[544,128]{1,0:T(8,128)(2,1)S(1)}, u32[]{:S(2)}, u32[]{:S(2)}) %collective-permute-start.14) | collective-permute-done | bytes 139296 | tf_op jit(solution)/shard_map/ppermute | solution.py:368
  42.8 0.5 collective-permute-start.16
  43.3 1.8 %collective-permute-done.13.refs_1_ = bf16[544,128]{1,0:T(8,128)(2,1)S(1)} collective-permute-done((bf16[544,128]{1,0:T(8,128)(2,1)S(1)}, bf16[544,128]{1,0:T(8,128)(2,1)S(1)}, u32[]{:S(2)}, u32[]{:S(2)}) %collective-permute-start.13) | collective-permute-done | bytes 139296 | tf_op jit(solution)/shard_map/ppermute | solution.py:368
  45.1 0.7 %collective-permute-start.15 = (bf16[1088,128]{1,0:T(8,128)(2,1)S(1)}, bf16[1088,128]{1,0:T(8,128)(2,1)S(1)}, u32[]{:S(2)}, u32[]{:S(2)}) collective-permute-start(bf16[1088,128]{1,0:T(8,128)(2,1)S(1)} %shard_map.76.refs_1_.refs_0_), channel_id=1, source_target_pairs={{0,10},{1,7},{2,4},{3,9},{4,2},{5,15},{6,12},{7,1},{8,14},{9,3},{1... | collective-permute-start | bytes 835592 | tf_op jit(solution)/shard_map/ppermute | solution.py:368
  45.8 1.1 %shard_map.77 = (f32[1728,128]{1,0:T(8,128)}, f32[3456,256]{1,0:T(8,128)}, f32[8,128]{1,0:T(8,128)S(1)}) custom-call(bf16[1088,128]{1,0:T(8,128)(2,1)S(1)} %shard_map.75.refs_2_.refs_0_, bf16[1088,128]{1,0:T(8,128)(2,1)S(1)} %shard_map.76.refs_1_.refs_0_), custom_call_target="tpu_custom_call" | custom-call | flops 4000000000 | bytes 80000000 | tf_op jit(solution)/shard_map/pallas_call | solution.py:490
  47.0 1.5 %collective-permute-start.17 = (bf16[1088,128]{1,0:T(8,128)(2,1)S(1)}, bf16[1088,128]{1,0:T(8,128)(2,1)S(1)}, u32[]{:S(2)}, u32[]{:S(2)}) collective-permute-start(bf16[1088,128]{1,0:T(8,128)(2,1)S(1)} %shard_map.79), channel_id=1, source_target_pairs={{0,2},{1,3},{2,0},{3,1},{4,6},{5,7},{6,4},{7,5},{8,10},{9,11},{10,... | collective-permute-start | bytes 835592 | tf_op jit(solution)/shard_map/ppermute | solution.py:361
  48.5 0.1 collective-permute-start.18
  48.5 0.3 collective-permute-done.16.refs_0_
  48.8 0.9 %collective-permute-start.20 = (bf16[1088,128]{1,0:T(8,128)(2,1)S(1)}, bf16[1088,128]{1,0:T(8,128)(2,1)S(1)}, u32[]{:S(2)}, u32[]{:S(2)}) collective-permute-start(bf16[1088,128]{1,0:T(8,128)(2,1)S(1)} %shard_map.78.refs_2_.refs_1_), channel_id=1, source_target_pairs={{0,2},{1,3},{2,0},{3,1},{4,6},{5,7},{6,4},{7,5},{8,10},{9,11},{10,... | collective-permute-start | bytes 835592 | tf_op jit(solution)/shard_map/ppermute | solution.py:361
  49.7 0.0 collective-permute-done.17.refs_0_
  49.7 0.4 collective-permute-done.18.refs_1_
  50.1 1.4 %shard_map.81 = (f32[1728,128]{1,0:T(8,128)}, f32[3456,256]{1,0:T(8,128)}, f32[8,128]{1,0:T(8,128)S(1)}) custom-call(bf16[1088,128]{1,0:T(8,128)(2,1)S(1)} %collective-permute-done.17.refs_0_, bf16[1088,128]{1,0:T(8,128)(2,1)S(1)} %collective-permute-done.18.refs_1_, ...), custom_call_target="tpu_custom_call", output_to_operand_aliasing={{0}: (3, {}), {1}: (4, {})} | custom-call | flops 4000000000 | bytes 80000000 | tf_op jit(solution)/shard_map/pallas_call | solution.py:490
  51.5 0.0 collective-permute-done.15.refs_0_
  51.5 0.9 %collective-permute-start.19 = (bf16[1088,128]{1,0:T(8,128)(2,1)S(1)}, bf16[1088,128]{1,0:T(8,128)(2,1)S(1)}, u32[]{:S(2)}, u32[]{:S(2)}) collective-permute-start(bf16[1088,128]{1,0:T(8,128)(2,1)S(1)} %shard_map.82.refs_1_), channel_id=1, source_target_pairs={{0,2},{1,3},{2,0},{3,1},{4,6},{5,7},{6,4},{7,5},{8,10},{9,11},{10,... | collective-permute-start | bytes 835592 | tf_op jit(solution)/shard_map/ppermute | solution.py:361
  52.4 0.0 collective-permute-done.20.refs_0_
  52.4 1.1 %shard_map.83 = (f32[1728,128]{1,0:T(8,128)}, f32[3456,256]{1,0:T(8,128)}) custom-call(bf16[1088,128]{1,0:T(8,128)(2,1)S(1)} %collective-permute-done.20.refs_0_, bf16[1088,128]{1,0:T(8,128)(2,1)S(1)} %shard_map.82.refs_1_, f32[1728,128]{1,0:T(8,128)} %get-tuple-element.68.refs_2_, ...), custom_call_target="tpu_custom_call", output_to_operand_aliasing={{0}: (2, {}), {1}: (3, {})} | custom-call | flops 4000000000 | bytes 80000000 | tf_op jit(solution)/shard_map/pallas_call | solution.py:490
  53.6 0.0 collective-permute-done.19.refs_0_
  53.6 0.9 %shard_map.84 = (f32[1728,128]{1,0:T(8,128)}, f32[3456,256]{1,0:T(8,128)}) custom-call(bf16[1088,128]{1,0:T(8,128)(2,1)S(1)} %collective-permute-done.19.refs_0_, f32[1728,128]{1,0:T(8,128)} %get-tuple-element.70.refs_1_, f32[3456,256]{1,0:T(8,128)} %get-tuple-element.71.refs_2_), custom_call_target="tpu_custom_call", output_to_operand_aliasing={{0}: (1, {}), {1}: (2, {})} | custom-call | flops 4000000000 | bytes 80000000 | tf_op jit(solution)/shard_map/pallas_call | solution.py:490
  (14 shorter events, 0.3 us)
Async XLA Ops:
  1.5 5.7 %collective-permute-start = (bf16[3,16,1024]{2,1,0:T(8,128)(2,1)S(1)}, bf16[3,16,1024]{2,1,0:T(8,128)(2,1)S(1)}, u32[]{:S(2)}, u32[]{:S(2)}) collective-permute-start(bf16[3,16,1024]{2,1,0:T(8,128)(2,1)S(1)} %slice_bitcast_fusion.refs_2_), channel_id=1, source_target_pairs={{0,1},{1,0},{2,3},{3,2},{4,5},{5,4},{6,7},{7,6},{8,9},{9,8},{10,11... | collective-permute-start | bytes 294920 | tf_op jit(solution)/shard_map/ppermute | solution.py:378
  5.9 1.5 %copy-start = (bf16[3456,256]{1,0:T(8,128)(2,1)S(1)}, bf16[3456,256]{1,0:T(8,128)(2,1)}, u32[]{:S(2)}) copy-start(bf16[3456,256]{1,0:T(8,128)(2,1)} %refs_7_.1) | copy-start | bytes 5308420
  9.1 2.5 %collective-permute-start.2 = (bf16[2176,128]{1,0:T(8,128)(2,1)S(1)}, bf16[2176,128]{1,0:T(8,128)(2,1)S(1)}, u32[]{:S(2)}, u32[]{:S(2)}) collective-permute-start(bf16[2176,128]{1,0:T(8,128)(2,1)S(1)} %get-tuple-element.51), channel_id=1, source_target_pairs={{0,2},{1,3},{2,0},{3,1},{4,6},{5,7},{6,4},{7,5},{8,10},{9,11},{10,... | collective-permute-start | bytes 1671176 | tf_op jit(solution)/shard_map/ppermute | solution.py:361
  11.0 2.2 %collective-permute-start.1 = (bf16[2176,128]{1,0:T(8,128)(2,1)S(1)}, bf16[2176,128]{1,0:T(8,128)(2,1)S(1)}, u32[]{:S(2)}, u32[]{:S(2)}) collective-permute-start(bf16[2176,128]{1,0:T(8,128)(2,1)S(1)} %get-tuple-element.49.refs_2_), channel_id=1, source_target_pairs={{0,2},{1,3},{2,0},{3,1},{4,6},{5,7},{6,4},{7,5},{8,10},{9,11},{10,... | collective-permute-start | bytes 1671176 | tf_op jit(solution)/shard_map/ppermute | solution.py:361
  11.7 6.0 %collective-permute-start.4 = (bf16[1088,128]{1,0:T(8,128)(2,1)S(1)}, bf16[1088,128]{1,0:T(8,128)(2,1)S(1)}, u32[]{:S(2)}, u32[]{:S(2)}) collective-permute-start(bf16[1088,128]{1,0:T(8,128)(2,1)S(1)} %get-tuple-element.52.refs_2_), channel_id=1, source_target_pairs={{0,3},{1,7},{2,4},{3,0},{4,2},{5,6},{6,5},{7,1},{8,14},{9,10},{10,... | collective-permute-start | bytes 835592 | tf_op jit(solution)/shard_map/ppermute | solution.py:368
  13.3 6.3 %collective-permute-start.3 = (bf16[1088,128]{1,0:T(8,128)(2,1)S(1)}, bf16[1088,128]{1,0:T(8,128)(2,1)S(1)}, u32[]{:S(2)}, u32[]{:S(2)}) collective-permute-start(bf16[1088,128]{1,0:T(8,128)(2,1)S(1)} %get-tuple-element.54.refs_2_), channel_id=1, source_target_pairs={{0,10},{1,7},{2,4},{3,9},{4,2},{5,15},{6,12},{7,1},{8,14},{9,3},{1... | collective-permute-start | bytes 835592 | tf_op jit(solution)/shard_map/ppermute | solution.py:368
  17.8 4.7 %collective-permute-start.6 = (bf16[544,128]{1,0:T(8,128)(2,1)S(1)}, bf16[544,128]{1,0:T(8,128)(2,1)S(1)}, u32[]{:S(2)}, u32[]{:S(2)}) collective-permute-start(bf16[544,128]{1,0:T(8,128)(2,1)S(1)} %get-tuple-element.56.refs_2_), channel_id=1, source_target_pairs={{0,6},{1,11},{2,8},{3,5},{4,14},{5,3},{6,0},{7,13},{8,2},{9,15},{1... | collective-permute-start | bytes 417800 | tf_op jit(solution)/shard_map/ppermute | solution.py:368
  19.6 4.6 %collective-permute-start.5 = (bf16[544,128]{1,0:T(8,128)(2,1)S(1)}, bf16[544,128]{1,0:T(8,128)(2,1)S(1)}, u32[]{:S(2)}, u32[]{:S(2)}) collective-permute-start(bf16[544,128]{1,0:T(8,128)(2,1)S(1)} %get-tuple-element.58.refs_2_), channel_id=1, source_target_pairs={{0,3},{1,11},{2,8},{3,0},{4,14},{5,6},{6,5},{7,13},{8,2},{9,10},{1... | collective-permute-start | bytes 417800 | tf_op jit(solution)/shard_map/ppermute | solution.py:368
  22.5 4.2 %collective-permute-start.8 = (bf16[272,128]{1,0:T(8,128)(2,1)S(1)}, bf16[272,128]{1,0:T(8,128)(2,1)S(1)}, u32[]{:S(2)}, u32[]{:S(2)}) collective-permute-start(bf16[272,128]{1,0:T(8,128)(2,1)S(1)} %get-tuple-element.60.refs_2_), channel_id=1, source_target_pairs={{0,10},{1,2},{2,1},{3,9},{4,7},{5,15},{6,12},{7,4},{8,11},{9,3},{1... | collective-permute-start | bytes 208904 | tf_op jit(solution)/shard_map/ppermute | solution.py:368
  24.2 4.8 %collective-permute-start.7 = (bf16[272,128]{1,0:T(8,128)(2,1)S(1)}, bf16[272,128]{1,0:T(8,128)(2,1)S(1)}, u32[]{:S(2)}, u32[]{:S(2)}) collective-permute-start(bf16[272,128]{1,0:T(8,128)(2,1)S(1)} %get-tuple-element.62.refs_2_), channel_id=1, source_target_pairs={{0,6},{1,2},{2,1},{3,5},{4,7},{5,3},{6,0},{7,4},{8,11},{9,15},{10,... | collective-permute-start | bytes 208904 | tf_op jit(solution)/shard_map/ppermute | solution.py:368
  26.8 4.7 %collective-permute-start.10 = (bf16[272,128]{1,0:T(8,128)(2,1)S(1)}, bf16[272,128]{1,0:T(8,128)(2,1)S(1)}, u32[]{:S(2)}, u32[]{:S(2)}) collective-permute-start(bf16[272,128]{1,0:T(8,128)(2,1)S(1)} %shard_map.69.refs_2_.refs_0_), channel_id=1, source_target_pairs={{0,18},{1,19},{2,16},{3,17},{4,22},{5,23},{6,20},{7,21},{8,26},{9,... | collective-permute-start | bytes 208904 | tf_op jit(solution)/shard_map/ppermute | solution.py:368
  29.1 7.6 %collective-permute-start.9 = (bf16[272,128]{1,0:T(8,128)(2,1)S(1)}, bf16[272,128]{1,0:T(8,128)(2,1)S(1)}, u32[]{:S(2)}, u32[]{:S(2)}) collective-permute-start(bf16[272,128]{1,0:T(8,128)(2,1)S(1)} %shard_map.70.refs_2_.refs_0_), channel_id=1, source_target_pairs={{0,18},{1,19},{2,16},{3,17},{4,22},{5,23},{6,20},{7,21},{8,26},{9,... | collective-permute-start | bytes 208904 | tf_op jit(solution)/shard_map/ppermute | solution.py:368
  31.5 6.6 %collective-permute-start.12 = (bf16[272,128]{1,0:T(8,128)(2,1)S(1)}, bf16[272,128]{1,0:T(8,128)(2,1)S(1)}, u32[]{:S(2)}, u32[]{:S(2)}) collective-permute-start(bf16[272,128]{1,0:T(8,128)(2,1)S(1)} %shard_map.71.refs_2_.refs_0_), channel_id=1, source_target_pairs={{0,10},{1,2},{2,1},{3,9},{4,7},{5,15},{6,12},{7,4},{8,11},{9,3},{1... | collective-permute-start | bytes 208904 | tf_op jit(solution)/shard_map/ppermute | solution.py:368
  36.7 3.8 %collective-permute-start.11 = (bf16[272,128]{1,0:T(8,128)(2,1)S(1)}, bf16[272,128]{1,0:T(8,128)(2,1)S(1)}, u32[]{:S(2)}, u32[]{:S(2)}) collective-permute-start(bf16[272,128]{1,0:T(8,128)(2,1)S(1)} %shard_map.72.refs_2_.refs_0_), channel_id=1, source_target_pairs={{0,6},{1,2},{2,1},{3,5},{4,7},{5,3},{6,0},{7,4},{8,11},{9,15},{10,... | collective-permute-start | bytes 208904 | tf_op jit(solution)/shard_map/ppermute | solution.py:368
  38.2 4.5 %collective-permute-start.14 = (bf16[544,128]{1,0:T(8,128)(2,1)S(1)}, bf16[544,128]{1,0:T(8,128)(2,1)S(1)}, u32[]{:S(2)}, u32[]{:S(2)}) collective-permute-start(bf16[544,128]{1,0:T(8,128)(2,1)S(1)} %shard_map.73.refs_2_.refs_0_), channel_id=1, source_target_pairs={{0,6},{1,11},{2,8},{3,5},{4,14},{5,3},{6,0},{7,13},{8,2},{9,15},{1... | collective-permute-start | bytes 417800 | tf_op jit(solution)/shard_map/ppermute | solution.py:368
  40.5 4.5 %collective-permute-start.13 = (bf16[544,128]{1,0:T(8,128)(2,1)S(1)}, bf16[544,128]{1,0:T(8,128)(2,1)S(1)}, u32[]{:S(2)}, u32[]{:S(2)}) collective-permute-start(bf16[544,128]{1,0:T(8,128)(2,1)S(1)} %shard_map.74.refs_2_.refs_0_), channel_id=1, source_target_pairs={{0,3},{1,11},{2,8},{3,0},{4,14},{5,6},{6,5},{7,13},{8,2},{9,10},{1... | collective-permute-start | bytes 417800 | tf_op jit(solution)/shard_map/ppermute | solution.py:368
  42.8 6.0 %collective-permute-start.16 = (bf16[1088,128]{1,0:T(8,128)(2,1)S(1)}, bf16[1088,128]{1,0:T(8,128)(2,1)S(1)}, u32[]{:S(2)}, u32[]{:S(2)}) collective-permute-start(bf16[1088,128]{1,0:T(8,128)(2,1)S(1)} %shard_map.75.refs_2_.refs_0_), channel_id=1, source_target_pairs={{0,3},{1,7},{2,4},{3,0},{4,2},{5,6},{6,5},{7,1},{8,14},{9,10},{10,... | collective-permute-start | bytes 835592 | tf_op jit(solution)/shard_map/ppermute | solution.py:368
  45.1 6.4 %collective-permute-start.15 = (bf16[1088,128]{1,0:T(8,128)(2,1)S(1)}, bf16[1088,128]{1,0:T(8,128)(2,1)S(1)}, u32[]{:S(2)}, u32[]{:S(2)}) collective-permute-start(bf16[1088,128]{1,0:T(8,128)(2,1)S(1)} %shard_map.76.refs_1_.refs_0_), channel_id=1, source_target_pairs={{0,10},{1,7},{2,4},{3,9},{4,2},{5,15},{6,12},{7,1},{8,14},{9,3},{1... | collective-permute-start | bytes 835592 | tf_op jit(solution)/shard_map/ppermute | solution.py:368
  47.0 2.8 %collective-permute-start.17 = (bf16[1088,128]{1,0:T(8,128)(2,1)S(1)}, bf16[1088,128]{1,0:T(8,128)(2,1)S(1)}, u32[]{:S(2)}, u32[]{:S(2)}) collective-permute-start(bf16[1088,128]{1,0:T(8,128)(2,1)S(1)} %shard_map.79), channel_id=1, source_target_pairs={{0,2},{1,3},{2,0},{3,1},{4,6},{5,7},{6,4},{7,5},{8,10},{9,11},{10,... | collective-permute-start | bytes 835592 | tf_op jit(solution)/shard_map/ppermute | solution.py:361
  48.5 1.6 %collective-permute-start.18 = (bf16[1088,128]{1,0:T(8,128)(2,1)S(1)}, bf16[1088,128]{1,0:T(8,128)(2,1)S(1)}, u32[]{:S(2)}, u32[]{:S(2)}) collective-permute-start(bf16[1088,128]{1,0:T(8,128)(2,1)S(1)} %shard_map.80), channel_id=1, source_target_pairs={{0,2},{1,3},{2,0},{3,1},{4,6},{5,7},{6,4},{7,5},{8,10},{9,11},{10,... | collective-permute-start | bytes 835592 | tf_op jit(solution)/shard_map/ppermute | solution.py:361
  48.8 3.6 %collective-permute-start.20 = (bf16[1088,128]{1,0:T(8,128)(2,1)S(1)}, bf16[1088,128]{1,0:T(8,128)(2,1)S(1)}, u32[]{:S(2)}, u32[]{:S(2)}) collective-permute-start(bf16[1088,128]{1,0:T(8,128)(2,1)S(1)} %shard_map.78.refs_2_.refs_1_), channel_id=1, source_target_pairs={{0,2},{1,3},{2,0},{3,1},{4,6},{5,7},{6,4},{7,5},{8,10},{9,11},{10,... | collective-permute-start | bytes 835592 | tf_op jit(solution)/shard_map/ppermute | solution.py:361
  51.5 2.1 %collective-permute-start.19 = (bf16[1088,128]{1,0:T(8,128)(2,1)S(1)}, bf16[1088,128]{1,0:T(8,128)(2,1)S(1)}, u32[]{:S(2)}, u32[]{:S(2)}) collective-permute-start(bf16[1088,128]{1,0:T(8,128)(2,1)S(1)} %shard_map.82.refs_1_), channel_id=1, source_target_pairs={{0,2},{1,3},{2,0},{3,1},{4,6},{5,7},{6,4},{7,5},{8,10},{9,11},{10,... | collective-permute-start | bytes 835592 | tf_op jit(solution)/shard_map/ppermute | solution.py:361

commit v8 on v7

--- a/solution.py
+++ b/solution.py
@@ -196,7 +196,9 @@
                 at = (h - 2) * 144 + pair * 16
                 cells = picked_up[at : at + 16, :]
             x2[o * 16 : (o + 1) * 16, tap * LANES : (tap + 1) * LANES] = cells
-    second_pre = dot(x2[...], w2[...])
+    second_pre = jnp.concatenate(
+        [dot(x2[...], w2[:, :LANES]), dot(x2[...], w2[:, LANES:])], 1
+    )
     sig = sigmoid(second_pre)
     delta = cot[...] * slope_of(second_pre, sig)
     d2[...] = delta.astype(bf16)

time: 54.7 us -> 54.3 us (level)
  no operation moved by 1% of the time
where the time goes in v8:
time: 54.3 us; the launch traced here: 54.1 us
  starting transfers between devices  29.7 us (55%)
  waiting for transfers between devices  11.5 us (21%)
  Pallas kernels  11 us (20%)
  local copies, waits for them, and re-layouts  1.03 us (2%)
  between operations  0.79 us (1%)
    ppermute x14, starting transfers between devices, swap(): return lax.ppermute(array, BOTH, pairs)  22.8 us
    ppermute x14, waiting for transfers between devices, swap(): return lax.ppermute(array, BOTH, pairs)  11 us
    pallas_call x22, Pallas kernels, call(): pl.pallas_call(run, out_shape=shapes, in_specs=(specs or [full(a.shape) f...  6.42 us
    pallas_call x4, Pallas kernels, write(): pl.pallas_call(functools.partial(final_kernel, bits, spatial_count, jobs,...  4.6 us
    ppermute x6, starting transfers between devices, swap_core(): lax.ppermute(array, BOTH, [(i, i ^ 1 << core_bit) for i in range(count)])  3.96 us
    ppermute x1, starting transfers between devices, body(): lax.ppermute(face, 'spatial', [(i, (i + 1) % spatial_count) for i in rang...  2.94 us
  transfers between devices with their start and end apart: 21, of which 11 were waited for; matrix products, arithmetic and copies ran while one was open for 0% of the time, Pallas kernels for 16%

profile of v8, /device:TPU:0, one launch (start us, length us, event | category | flops | bytes accessed | tf_op | source)
XLA Modules:
  0.0 54.1 jit_solution(2310043078289376769)
XLA Ops:
  0.6 0.9 %slice_bitcast_fusion.refs_2_ = bf16[3,16,1024]{2,1,0:T(8,128)(2,1)S(1)} fusion(bf16[1,16,16,1024]{3,2,1,0:T(8,128)(2,1)} %param.4), kind=kLoop, calls=%fused_computation | loop fusion | bytes 196608 | tf_op jit(solution)/shard_map/slice | solution.py:379
  1.5 2.9 %collective-permute-start = (bf16[3,16,1024]{2,1,0:T(8,128)(2,1)S(1)}, bf16[3,16,1024]{2,1,0:T(8,128)(2,1)S(1)}, u32[]{:S(2)}, u32[]{:S(2)}) collective-permute-start(bf16[3,16,1024]{2,1,0:T(8,128)(2,1)S(1)} %slice_bitcast_fusion.refs_2_), channel_id=1, source_target_pairs={{0,1},{1,0},{2,3},{3,2},{4,5},{5,4},{6,7},{7,6},{8,9},{9,8},{10,11... | collective-permute-start | bytes 294920 | tf_op jit(solution)/shard_map/ppermute | solution.py:380
  4.5 1.4 %shard_map.59 = (bf16[64,2304]{1,0:T(8,128)(2,1)S(1)}, bf16[448,2304]{1,0:T(8,128)(2,1)S(1)}, bf16[2304,128]{1,0:T(8,128)(2,1)S(1)}) custom-call(bf16[16,16,1024]{2,1,0:T(8,128)(2,1)} %bitcast.5, bf16[1728,128]{1,0:T(8,128)(2,1)} %refs_1_.1, bf16[3,16,1024]{2,1,0:T(8,128)(2,1)S(1)} %slice_bitcast_fusion.refs_2_), custom_call_target="tpu_custom_call" | custom-call | flops 4000000000 | bytes 80000000 | tf_op jit(solution)/shard_map/pallas_call | solution.py:37
  5.9 0.0 copy-start
  5.9 1.3 %shard_map.60 = (f32[448,128]{1,0:T(8,128)S(1)}, bf16[1008,128]{1,0:T(8,128)(2,1)S(1)}, f32[64,256]{1,0:T(8,128)S(1)}) custom-call(bf16[448,2304]{1,0:T(8,128)(2,1)S(1)} %get-tuple-element.37.refs_0_, bf16[2304,128]{1,0:T(8,128)(2,1)S(1)} %get-tuple-element.39.refs_1_.refs_2_, bf16[4,4,1024]{2,1,0:T(4,128)(2,1)} %bitcast.4), custom_call_target="tpu_custom_call" | custom-call | flops 400000000 | bytes 10000000 | tf_op jit(solution)/shard_map/pallas_call | solution.py:37
  7.2 0.1 collective-permute-done.refs_0_
  7.3 0.1 copy-done
  7.4 1.3 %shard_map.61 = (f32[2176,128]{1,0:T(8,128)S(1)}, bf16[2176,128]{1,0:T(8,128)(2,1)S(1)}, bf16[128,2304]{1,0:T(8,128)(2,1)S(1)}, f32[128,128]{1,0:T(8,128)S(1)}, ...) custom-call(bf16[3,16,1024]{2,1,0:T(8,128)(2,1)S(1)} %collective-permute-done.refs_0_, ...), custom_call_target="tpu_custom_call" | custom-call | tf_op jit(solution)/shard_map/pallas_call | solution.py:37
  8.7 0.1 collective-permute-start.2
  8.8 1.8 %shard_map.62 = (f32[2176,128]{1,0:T(8,128)S(1)}, bf16[2176,128]{1,0:T(8,128)(2,1)S(1)}) custom-call(bf16[448,2304]{1,0:T(8,128)(2,1)S(1)} %get-tuple-element.37.refs_0_, bf16[128,2304]{1,0:T(8,128)(2,1)S(1)} %get-tuple-element.42.refs_1_, f32[448,128]{1,0:T(8,128)S(1)} %get-tuple-element.43.refs_2_, f32[128,128]{1,0:T(8,128)S(1)} %get-tuple-element.44.refs_3_, ...), custom_call_target="tpu_custom_call" | custom-call | flops 1000000000 | bytes 10000000 | tf_op jit(solution)/shard_map/pallas_call | solution.py:37
  10.6 0.6 %collective-permute-start.1 = (bf16[2176,128]{1,0:T(8,128)(2,1)S(1)}, bf16[2176,128]{1,0:T(8,128)(2,1)S(1)}, u32[]{:S(2)}, u32[]{:S(2)}) collective-permute-start(bf16[2176,128]{1,0:T(8,128)(2,1)S(1)} %get-tuple-element.49.refs_2_), channel_id=1, source_target_pairs={{0,2},{1,3},{2,0},{3,1},{4,6},{5,7},{6,4},{7,5},{8,10},{9,11},{10,... | collective-permute-start | bytes 1671176 | tf_op jit(solution)/shard_map/ppermute | solution.py:363
  11.2 0.0 collective-permute-done.2.refs_1_
  11.2 0.1 shard_map.63
  11.3 1.4 %collective-permute-start.4 = (bf16[1088,128]{1,0:T(8,128)(2,1)S(1)}, bf16[1088,128]{1,0:T(8,128)(2,1)S(1)}, u32[]{:S(2)}, u32[]{:S(2)}) collective-permute-start(bf16[1088,128]{1,0:T(8,128)(2,1)S(1)} %get-tuple-element.52.refs_2_), channel_id=1, source_target_pairs={{0,3},{1,7},{2,4},{3,0},{4,2},{5,6},{6,5},{7,1},{8,14},{9,10},{10,... | collective-permute-start | bytes 835592 | tf_op jit(solution)/shard_map/ppermute | solution.py:370
  12.7 0.1 collective-permute-done.1.refs_1_
  12.8 0.1 shard_map.64
  12.9 1.8 %collective-permute-start.3 = (bf16[1088,128]{1,0:T(8,128)(2,1)S(1)}, bf16[1088,128]{1,0:T(8,128)(2,1)S(1)}, u32[]{:S(2)}, u32[]{:S(2)}) collective-permute-start(bf16[1088,128]{1,0:T(8,128)(2,1)S(1)} %get-tuple-element.54.refs_2_), channel_id=1, source_target_pairs={{0,10},{1,7},{2,4},{3,9},{4,2},{5,15},{6,12},{7,1},{8,14},{9,3},{1... | collective-permute-start | bytes 835592 | tf_op jit(solution)/shard_map/ppermute | solution.py:370
  14.7 2.6 %collective-permute-done.4.refs_1_ = bf16[1088,128]{1,0:T(8,128)(2,1)S(1)} collective-permute-done((bf16[1088,128]{1,0:T(8,128)(2,1)S(1)}, bf16[1088,128]{1,0:T(8,128)(2,1)S(1)}, u32[]{:S(2)}, u32[]{:S(2)}) %collective-permute-start.4) | collective-permute-done | bytes 278560 | tf_op jit(solution)/shard_map/ppermute | solution.py:370
  17.4 0.1 shard_map.65
  17.4 1.8 %collective-permute-start.6 = (bf16[544,128]{1,0:T(8,128)(2,1)S(1)}, bf16[544,128]{1,0:T(8,128)(2,1)S(1)}, u32[]{:S(2)}, u32[]{:S(2)}) collective-permute-start(bf16[544,128]{1,0:T(8,128)(2,1)S(1)} %get-tuple-element.56.refs_2_), channel_id=1, source_target_pairs={{0,6},{1,11},{2,8},{3,5},{4,14},{5,3},{6,0},{7,13},{8,2},{9,15},{1... | collective-permute-start | bytes 417800 | tf_op jit(solution)/shard_map/ppermute | solution.py:370
  19.2 0.0 collective-permute-done.3.refs_1_
  19.2 0.1 shard_map.66
  19.2 1.8 %collective-permute-start.5 = (bf16[544,128]{1,0:T(8,128)(2,1)S(1)}, bf16[544,128]{1,0:T(8,128)(2,1)S(1)}, u32[]{:S(2)}, u32[]{:S(2)}) collective-permute-start(bf16[544,128]{1,0:T(8,128)(2,1)S(1)} %get-tuple-element.58.refs_2_), channel_id=1, source_target_pairs={{0,3},{1,11},{2,8},{3,0},{4,14},{5,6},{6,5},{7,13},{8,2},{9,10},{1... | collective-permute-start | bytes 417800 | tf_op jit(solution)/shard_map/ppermute | solution.py:370
  21.0 1.1 %collective-permute-done.6.refs_1_ = bf16[544,128]{1,0:T(8,128)(2,1)S(1)} collective-permute-done((bf16[544,128]{1,0:T(8,128)(2,1)S(1)}, bf16[544,128]{1,0:T(8,128)(2,1)S(1)}, u32[]{:S(2)}, u32[]{:S(2)}) %collective-permute-start.6) | collective-permute-done | bytes 139296 | tf_op jit(solution)/shard_map/ppermute | solution.py:370
  22.1 1.6 %collective-permute-start.8 = (bf16[272,128]{1,0:T(8,128)(2,1)S(1)}, bf16[272,128]{1,0:T(8,128)(2,1)S(1)}, u32[]{:S(2)}, u32[]{:S(2)}) collective-permute-start(bf16[272,128]{1,0:T(8,128)(2,1)S(1)} %get-tuple-element.60.refs_2_), channel_id=1, source_target_pairs={{0,10},{1,2},{2,1},{3,9},{4,7},{5,15},{6,12},{7,4},{8,11},{9,3},{1... | collective-permute-start | bytes 208904 | tf_op jit(solution)/shard_map/ppermute | solution.py:370
  23.8 0.0 collective-permute-done.5.refs_1_
  23.8 2.1 %collective-permute-start.7 = (bf16[272,128]{1,0:T(8,128)(2,1)S(1)}, bf16[272,128]{1,0:T(8,128)(2,1)S(1)}, u32[]{:S(2)}, u32[]{:S(2)}) collective-permute-start(bf16[272,128]{1,0:T(8,128)(2,1)S(1)} %get-tuple-element.62.refs_2_), channel_id=1, source_target_pairs={{0,6},{1,2},{2,1},{3,5},{4,7},{5,3},{6,0},{7,4},{8,11},{9,15},{10,... | collective-permute-start | bytes 208904 | tf_op jit(solution)/shard_map/ppermute | solution.py:370
  25.9 0.4 collective-permute-done.8.refs_1_
  26.4 2.3 %collective-permute-start.10 = (bf16[272,128]{1,0:T(8,128)(2,1)S(1)}, bf16[272,128]{1,0:T(8,128)(2,1)S(1)}, u32[]{:S(2)}, u32[]{:S(2)}) collective-permute-start(bf16[272,128]{1,0:T(8,128)(2,1)S(1)} %shard_map.69.refs_2_.refs_0_), channel_id=1, source_target_pairs={{0,18},{1,19},{2,16},{3,17},{4,22},{5,23},{6,20},{7,21},{8,26},{9,... | collective-permute-start | bytes 208904 | tf_op jit(solution)/shard_map/ppermute | solution.py:370
  28.6 0.0 collective-permute-done.7.refs_1_
  28.7 2.5 %collective-permute-start.9 = (bf16[272,128]{1,0:T(8,128)(2,1)S(1)}, bf16[272,128]{1,0:T(8,128)(2,1)S(1)}, u32[]{:S(2)}, u32[]{:S(2)}) collective-permute-start(bf16[272,128]{1,0:T(8,128)(2,1)S(1)} %shard_map.70.refs_2_.refs_0_), channel_id=1, source_target_pairs={{0,18},{1,19},{2,16},{3,17},{4,22},{5,23},{6,20},{7,21},{8,26},{9,... | collective-permute-start | bytes 208904 | tf_op jit(solution)/shard_map/ppermute | solution.py:370
  31.1 0.0 collective-permute-done.10.refs_1_
  31.1 2.6 %collective-permute-start.12 = (bf16[272,128]{1,0:T(8,128)(2,1)S(1)}, bf16[272,128]{1,0:T(8,128)(2,1)S(1)}, u32[]{:S(2)}, u32[]{:S(2)}) collective-permute-start(bf16[272,128]{1,0:T(8,128)(2,1)S(1)} %shard_map.71.refs_2_.refs_0_), channel_id=1, source_target_pairs={{0,10},{1,2},{2,1},{3,9},{4,7},{5,15},{6,12},{7,4},{8,11},{9,3},{1... | collective-permute-start | bytes 208904 | tf_op jit(solution)/shard_map/ppermute | solution.py:370
  33.8 2.5 %collective-permute-done.9.refs_1_ = bf16[272,128]{1,0:T(8,128)(2,1)S(1)} collective-permute-done((bf16[272,128]{1,0:T(8,128)(2,1)S(1)}, bf16[272,128]{1,0:T(8,128)(2,1)S(1)}, u32[]{:S(2)}, u32[]{:S(2)}) %collective-permute-start.9) | collective-permute-done | bytes 69664 | tf_op jit(solution)/shard_map/ppermute | solution.py:370
  36.3 1.5 %collective-permute-start.11 = (bf16[272,128]{1,0:T(8,128)(2,1)S(1)}, bf16[272,128]{1,0:T(8,128)(2,1)S(1)}, u32[]{:S(2)}, u32[]{:S(2)}) collective-permute-start(bf16[272,128]{1,0:T(8,128)(2,1)S(1)} %shard_map.72.refs_2_.refs_0_), channel_id=1, source_target_pairs={{0,6},{1,2},{2,1},{3,5},{4,7},{5,3},{6,0},{7,4},{8,11},{9,15},{10,... | collective-permute-start | bytes 208904 | tf_op jit(solution)/shard_map/ppermute | solution.py:370
  37.8 0.0 collective-permute-done.12.refs_1_
  37.8 0.6 %collective-permute-start.14 = (bf16[544,128]{1,0:T(8,128)(2,1)S(1)}, bf16[544,128]{1,0:T(8,128)(2,1)S(1)}, u32[]{:S(2)}, u32[]{:S(2)}) collective-permute-start(bf16[544,128]{1,0:T(8,128)(2,1)S(1)} %shard_map.73.refs_2_.refs_0_), channel_id=1, source_target_pairs={{0,6},{1,11},{2,8},{3,5},{4,14},{5,3},{6,0},{7,13},{8,2},{9,15},{1... | collective-permute-start | bytes 417800 | tf_op jit(solution)/shard_map/ppermute | solution.py:370
  38.4 1.7 %collective-permute-done.11.refs_1_ = bf16[272,128]{1,0:T(8,128)(2,1)S(1)} collective-permute-done((bf16[272,128]{1,0:T(8,128)(2,1)S(1)}, bf16[272,128]{1,0:T(8,128)(2,1)S(1)}, u32[]{:S(2)}, u32[]{:S(2)}) %collective-permute-start.11) | collective-permute-done | bytes 69664 | tf_op jit(solution)/shard_map/ppermute | solution.py:370
  40.1 1.6 %collective-permute-start.13 = (bf16[544,128]{1,0:T(8,128)(2,1)S(1)}, bf16[544,128]{1,0:T(8,128)(2,1)S(1)}, u32[]{:S(2)}, u32[]{:S(2)}) collective-permute-start(bf16[544,128]{1,0:T(8,128)(2,1)S(1)} %shard_map.74.refs_2_.refs_0_), channel_id=1, source_target_pairs={{0,3},{1,11},{2,8},{3,0},{4,14},{5,6},{6,5},{7,13},{8,2},{9,10},{1... | collective-permute-start | bytes 417800 | tf_op jit(solution)/shard_map/ppermute | solution.py:370
  41.7 0.7 %collective-permute-done.14.refs_1_ = bf16[544,128]{1,0:T(8,128)(2,1)S(1)} collective-permute-done((bf16[544,128]{1,0:T(8,128)(2,1)S(1)}, bf16[544,128]{1,0:T(8,128)(2,1)S(1)}, u32[]{:S(2)}, u32[]{:S(2)}) %collective-permute-start.14) | collective-permute-done | bytes 139296 | tf_op jit(solution)/shard_map/ppermute | solution.py:370
  42.4 0.5 collective-permute-start.16
  42.9 1.8 %collective-permute-done.13.refs_1_ = bf16[544,128]{1,0:T(8,128)(2,1)S(1)} collective-permute-done((bf16[544,128]{1,0:T(8,128)(2,1)S(1)}, bf16[544,128]{1,0:T(8,128)(2,1)S(1)}, u32[]{:S(2)}, u32[]{:S(2)}) %collective-permute-start.13) | collective-permute-done | bytes 139296 | tf_op jit(solution)/shard_map/ppermute | solution.py:370
  44.7 0.7 %collective-permute-start.15 = (bf16[1088,128]{1,0:T(8,128)(2,1)S(1)}, bf16[1088,128]{1,0:T(8,128)(2,1)S(1)}, u32[]{:S(2)}, u32[]{:S(2)}) collective-permute-start(bf16[1088,128]{1,0:T(8,128)(2,1)S(1)} %shard_map.76.refs_1_.refs_0_), channel_id=1, source_target_pairs={{0,10},{1,7},{2,4},{3,9},{4,2},{5,15},{6,12},{7,1},{8,14},{9,3},{1... | collective-permute-start | bytes 835592 | tf_op jit(solution)/shard_map/ppermute | solution.py:370
  45.4 1.1 %shard_map.77 = (f32[1728,128]{1,0:T(8,128)}, f32[3456,256]{1,0:T(8,128)}, f32[8,128]{1,0:T(8,128)S(1)}) custom-call(bf16[1088,128]{1,0:T(8,128)(2,1)S(1)} %shard_map.75.refs_2_.refs_0_, bf16[1088,128]{1,0:T(8,128)(2,1)S(1)} %shard_map.76.refs_1_.refs_0_), custom_call_target="tpu_custom_call" | custom-call | flops 4000000000 | bytes 80000000 | tf_op jit(solution)/shard_map/pallas_call | solution.py:492
  46.5 1.5 %collective-permute-start.17 = (bf16[1088,128]{1,0:T(8,128)(2,1)S(1)}, bf16[1088,128]{1,0:T(8,128)(2,1)S(1)}, u32[]{:S(2)}, u32[]{:S(2)}) collective-permute-start(bf16[1088,128]{1,0:T(8,128)(2,1)S(1)} %shard_map.79), channel_id=1, source_target_pairs={{0,2},{1,3},{2,0},{3,1},{4,6},{5,7},{6,4},{7,5},{8,10},{9,11},{10,... | collective-permute-start | bytes 835592 | tf_op jit(solution)/shard_map/ppermute | solution.py:363
  48.0 0.1 collective-permute-start.18
  48.1 0.3 collective-permute-done.16.refs_0_
  48.4 0.9 %collective-permute-start.20 = (bf16[1088,128]{1,0:T(8,128)(2,1)S(1)}, bf16[1088,128]{1,0:T(8,128)(2,1)S(1)}, u32[]{:S(2)}, u32[]{:S(2)}) collective-permute-start(bf16[1088,128]{1,0:T(8,128)(2,1)S(1)} %shard_map.78.refs_2_.refs_1_), channel_id=1, source_target_pairs={{0,2},{1,3},{2,0},{3,1},{4,6},{5,7},{6,4},{7,5},{8,10},{9,11},{10,... | collective-permute-start | bytes 835592 | tf_op jit(solution)/shard_map/ppermute | solution.py:363
  49.3 0.0 collective-permute-done.17.refs_0_
  49.3 0.4 collective-permute-done.18.refs_1_
  49.7 1.4 %shard_map.81 = (f32[1728,128]{1,0:T(8,128)}, f32[3456,256]{1,0:T(8,128)}, f32[8,128]{1,0:T(8,128)S(1)}) custom-call(bf16[1088,128]{1,0:T(8,128)(2,1)S(1)} %collective-permute-done.17.refs_0_, bf16[1088,128]{1,0:T(8,128)(2,1)S(1)} %collective-permute-done.18.refs_1_, ...), custom_call_target="tpu_custom_call", output_to_operand_aliasing={{0}: (3, {}), {1}: (4, {})} | custom-call | flops 4000000000 | bytes 80000000 | tf_op jit(solution)/shard_map/pallas_call | solution.py:492
  51.1 0.0 collective-permute-done.15.refs_0_
  51.1 0.9 %collective-permute-start.19 = (bf16[1088,128]{1,0:T(8,128)(2,1)S(1)}, bf16[1088,128]{1,0:T(8,128)(2,1)S(1)}, u32[]{:S(2)}, u32[]{:S(2)}) collective-permute-start(bf16[1088,128]{1,0:T(8,128)(2,1)S(1)} %shard_map.82.refs_1_), channel_id=1, source_target_pairs={{0,2},{1,3},{2,0},{3,1},{4,6},{5,7},{6,4},{7,5},{8,10},{9,11},{10,... | collective-permute-start | bytes 835592 | tf_op jit(solution)/shard_map/ppermute | solution.py:363
  52.0 0.0 collective-permute-done.20.refs_0_
  52.0 1.1 %shard_map.83 = (f32[1728,128]{1,0:T(8,128)}, f32[3456,256]{1,0:T(8,128)}) custom-call(bf16[1088,128]{1,0:T(8,128)(2,1)S(1)} %collective-permute-done.20.refs_0_, bf16[1088,128]{1,0:T(8,128)(2,1)S(1)} %shard_map.82.refs_1_, f32[1728,128]{1,0:T(8,128)} %get-tuple-element.68.refs_2_, ...), custom_call_target="tpu_custom_call", output_to_operand_aliasing={{0}: (2, {}), {1}: (3, {})} | custom-call | flops 4000000000 | bytes 80000000 | tf_op jit(solution)/shard_map/pallas_call | solution.py:492
  53.2 0.0 collective-permute-done.19.refs_0_
  53.2 0.9 %shard_map.84 = (f32[1728,128]{1,0:T(8,128)}, f32[3456,256]{1,0:T(8,128)}) custom-call(bf16[1088,128]{1,0:T(8,128)(2,1)S(1)} %collective-permute-done.19.refs_0_, f32[1728,128]{1,0:T(8,128)} %get-tuple-element.70.refs_1_, f32[3456,256]{1,0:T(8,128)} %get-tuple-element.71.refs_2_), custom_call_target="tpu_custom_call", output_to_operand_aliasing={{0}: (1, {}), {1}: (2, {})} | custom-call | flops 4000000000 | bytes 80000000 | tf_op jit(solution)/shard_map/pallas_call | solution.py:492
  (14 shorter events, 0.3 us)
Async XLA Ops:
  1.5 5.7 %collective-permute-start = (bf16[3,16,1024]{2,1,0:T(8,128)(2,1)S(1)}, bf16[3,16,1024]{2,1,0:T(8,128)(2,1)S(1)}, u32[]{:S(2)}, u32[]{:S(2)}) collective-permute-start(bf16[3,16,1024]{2,1,0:T(8,128)(2,1)S(1)} %slice_bitcast_fusion.refs_2_), channel_id=1, source_target_pairs={{0,1},{1,0},{2,3},{3,2},{4,5},{5,4},{6,7},{7,6},{8,9},{9,8},{10,11... | collective-permute-start | bytes 294920 | tf_op jit(solution)/shard_map/ppermute | solution.py:380
  5.9 1.5 %copy-start = (bf16[3456,256]{1,0:T(8,128)(2,1)S(1)}, bf16[3456,256]{1,0:T(8,128)(2,1)}, u32[]{:S(2)}) copy-start(bf16[3456,256]{1,0:T(8,128)(2,1)} %refs_7_.1) | copy-start | bytes 5308420
  8.7 2.5 %collective-permute-start.2 = (bf16[2176,128]{1,0:T(8,128)(2,1)S(1)}, bf16[2176,128]{1,0:T(8,128)(2,1)S(1)}, u32[]{:S(2)}, u32[]{:S(2)}) collective-permute-start(bf16[2176,128]{1,0:T(8,128)(2,1)S(1)} %get-tuple-element.51), channel_id=1, source_target_pairs={{0,2},{1,3},{2,0},{3,1},{4,6},{5,7},{6,4},{7,5},{8,10},{9,11},{10,... | collective-permute-start | bytes 1671176 | tf_op jit(solution)/shard_map/ppermute | solution.py:363
  10.6 2.2 %collective-permute-start.1 = (bf16[2176,128]{1,0:T(8,128)(2,1)S(1)}, bf16[2176,128]{1,0:T(8,128)(2,1)S(1)}, u32[]{:S(2)}, u32[]{:S(2)}) collective-permute-start(bf16[2176,128]{1,0:T(8,128)(2,1)S(1)} %get-tuple-element.49.refs_2_), channel_id=1, source_target_pairs={{0,2},{1,3},{2,0},{3,1},{4,6},{5,7},{6,4},{7,5},{8,10},{9,11},{10,... | collective-permute-start | bytes 1671176 | tf_op jit(solution)/shard_map/ppermute | solution.py:363
  11.3 6.0 %collective-permute-start.4 = (bf16[1088,128]{1,0:T(8,128)(2,1)S(1)}, bf16[1088,128]{1,0:T(8,128)(2,1)S(1)}, u32[]{:S(2)}, u32[]{:S(2)}) collective-permute-start(bf16[1088,128]{1,0:T(8,128)(2,1)S(1)} %get-tuple-element.52.refs_2_), channel_id=1, source_target_pairs={{0,3},{1,7},{2,4},{3,0},{4,2},{5,6},{6,5},{7,1},{8,14},{9,10},{10,... | collective-permute-start | bytes 835592 | tf_op jit(solution)/shard_map/ppermute | solution.py:370
  12.9 6.3 %collective-permute-start.3 = (bf16[1088,128]{1,0:T(8,128)(2,1)S(1)}, bf16[1088,128]{1,0:T(8,128)(2,1)S(1)}, u32[]{:S(2)}, u32[]{:S(2)}) collective-permute-start(bf16[1088,128]{1,0:T(8,128)(2,1)S(1)} %get-tuple-element.54.refs_2_), channel_id=1, source_target_pairs={{0,10},{1,7},{2,4},{3,9},{4,2},{5,15},{6,12},{7,1},{8,14},{9,3},{1... | collective-permute-start | bytes 835592 | tf_op jit(solution)/shard_map/ppermute | solution.py:370
  17.4 4.7 %collective-permute-start.6 = (bf16[544,128]{1,0:T(8,128)(2,1)S(1)}, bf16[544,128]{1,0:T(8,128)(2,1)S(1)}, u32[]{:S(2)}, u32[]{:S(2)}) collective-permute-start(bf16[544,128]{1,0:T(8,128)(2,1)S(1)} %get-tuple-element.56.refs_2_), channel_id=1, source_target_pairs={{0,6},{1,11},{2,8},{3,5},{4,14},{5,3},{6,0},{7,13},{8,2},{9,15},{1... | collective-permute-start | bytes 417800 | tf_op jit(solution)/shard_map/ppermute | solution.py:370
  19.2 4.6 %collective-permute-start.5 = (bf16[544,128]{1,0:T(8,128)(2,1)S(1)}, bf16[544,128]{1,0:T(8,128)(2,1)S(1)}, u32[]{:S(2)}, u32[]{:S(2)}) collective-permute-start(bf16[544,128]{1,0:T(8,128)(2,1)S(1)} %get-tuple-element.58.refs_2_), channel_id=1, source_target_pairs={{0,3},{1,11},{2,8},{3,0},{4,14},{5,6},{6,5},{7,13},{8,2},{9,10},{1... | collective-permute-start | bytes 417800 | tf_op jit(solution)/shard_map/ppermute | solution.py:370
  22.1 4.2 %collective-permute-start.8 = (bf16[272,128]{1,0:T(8,128)(2,1)S(1)}, bf16[272,128]{1,0:T(8,128)(2,1)S(1)}, u32[]{:S(2)}, u32[]{:S(2)}) collective-permute-start(bf16[272,128]{1,0:T(8,128)(2,1)S(1)} %get-tuple-element.60.refs_2_), channel_id=1, source_target_pairs={{0,10},{1,2},{2,1},{3,9},{4,7},{5,15},{6,12},{7,4},{8,11},{9,3},{1... | collective-permute-start | bytes 208904 | tf_op jit(solution)/shard_map/ppermute | solution.py:370
  23.8 4.8 %collective-permute-start.7 = (bf16[272,128]{1,0:T(8,128)(2,1)S(1)}, bf16[272,128]{1,0:T(8,128)(2,1)S(1)}, u32[]{:S(2)}, u32[]{:S(2)}) collective-permute-start(bf16[272,128]{1,0:T(8,128)(2,1)S(1)} %get-tuple-element.62.refs_2_), channel_id=1, source_target_pairs={{0,6},{1,2},{2,1},{3,5},{4,7},{5,3},{6,0},{7,4},{8,11},{9,15},{10,... | collective-permute-start | bytes 208904 | tf_op jit(solution)/shard_map/ppermute | solution.py:370
  26.4 4.7 %collective-permute-start.10 = (bf16[272,128]{1,0:T(8,128)(2,1)S(1)}, bf16[272,128]{1,0:T(8,128)(2,1)S(1)}, u32[]{:S(2)}, u32[]{:S(2)}) collective-permute-start(bf16[272,128]{1,0:T(8,128)(2,1)S(1)} %shard_map.69.refs_2_.refs_0_), channel_id=1, source_target_pairs={{0,18},{1,19},{2,16},{3,17},{4,22},{5,23},{6,20},{7,21},{8,26},{9,... | collective-permute-start | bytes 208904 | tf_op jit(solution)/shard_map/ppermute | solution.py:370
  28.7 7.6 %collective-permute-start.9 = (bf16[272,128]{1,0:T(8,128)(2,1)S(1)}, bf16[272,128]{1,0:T(8,128)(2,1)S(1)}, u32[]{:S(2)}, u32[]{:S(2)}) collective-permute-start(bf16[272,128]{1,0:T(8,128)(2,1)S(1)} %shard_map.70.refs_2_.refs_0_), channel_id=1, source_target_pairs={{0,18},{1,19},{2,16},{3,17},{4,22},{5,23},{6,20},{7,21},{8,26},{9,... | collective-permute-start | bytes 208904 | tf_op jit(solution)/shard_map/ppermute | solution.py:370
  31.1 6.6 %collective-permute-start.12 = (bf16[272,128]{1,0:T(8,128)(2,1)S(1)}, bf16[272,128]{1,0:T(8,128)(2,1)S(1)}, u32[]{:S(2)}, u32[]{:S(2)}) collective-permute-start(bf16[272,128]{1,0:T(8,128)(2,1)S(1)} %shard_map.71.refs_2_.refs_0_), channel_id=1, source_target_pairs={{0,10},{1,2},{2,1},{3,9},{4,7},{5,15},{6,12},{7,4},{8,11},{9,3},{1... | collective-permute-start | bytes 208904 | tf_op jit(solution)/shard_map/ppermute | solution.py:370
  36.3 3.8 %collective-permute-start.11 = (bf16[272,128]{1,0:T(8,128)(2,1)S(1)}, bf16[272,128]{1,0:T(8,128)(2,1)S(1)}, u32[]{:S(2)}, u32[]{:S(2)}) collective-permute-start(bf16[272,128]{1,0:T(8,128)(2,1)S(1)} %shard_map.72.refs_2_.refs_0_), channel_id=1, source_target_pairs={{0,6},{1,2},{2,1},{3,5},{4,7},{5,3},{6,0},{7,4},{8,11},{9,15},{10,... | collective-permute-start | bytes 208904 | tf_op jit(solution)/shard_map/ppermute | solution.py:370
  37.8 4.5 %collective-permute-start.14 = (bf16[544,128]{1,0:T(8,128)(2,1)S(1)}, bf16[544,128]{1,0:T(8,128)(2,1)S(1)}, u32[]{:S(2)}, u32[]{:S(2)}) collective-permute-start(bf16[544,128]{1,0:T(8,128)(2,1)S(1)} %shard_map.73.refs_2_.refs_0_), channel_id=1, source_target_pairs={{0,6},{1,11},{2,8},{3,5},{4,14},{5,3},{6,0},{7,13},{8,2},{9,15},{1... | collective-permute-start | bytes 417800 | tf_op jit(solution)/shard_map/ppermute | solution.py:370
  40.1 4.5 %collective-permute-start.13 = (bf16[544,128]{1,0:T(8,128)(2,1)S(1)}, bf16[544,128]{1,0:T(8,128)(2,1)S(1)}, u32[]{:S(2)}, u32[]{:S(2)}) collective-permute-start(bf16[544,128]{1,0:T(8,128)(2,1)S(1)} %shard_map.74.refs_2_.refs_0_), channel_id=1, source_target_pairs={{0,3},{1,11},{2,8},{3,0},{4,14},{5,6},{6,5},{7,13},{8,2},{9,10},{1... | collective-permute-start | bytes 417800 | tf_op jit(solution)/shard_map/ppermute | solution.py:370
  42.4 6.0 %collective-permute-start.16 = (bf16[1088,128]{1,0:T(8,128)(2,1)S(1)}, bf16[1088,128]{1,0:T(8,128)(2,1)S(1)}, u32[]{:S(2)}, u32[]{:S(2)}) collective-permute-start(bf16[1088,128]{1,0:T(8,128)(2,1)S(1)} %shard_map.75.refs_2_.refs_0_), channel_id=1, source_target_pairs={{0,3},{1,7},{2,4},{3,0},{4,2},{5,6},{6,5},{7,1},{8,14},{9,10},{10,... | collective-permute-start | bytes 835592 | tf_op jit(solution)/shard_map/ppermute | solution.py:370
  44.7 6.4 %collective-permute-start.15 = (bf16[1088,128]{1,0:T(8,128)(2,1)S(1)}, bf16[1088,128]{1,0:T(8,128)(2,1)S(1)}, u32[]{:S(2)}, u32[]{:S(2)}) collective-permute-start(bf16[1088,128]{1,0:T(8,128)(2,1)S(1)} %shard_map.76.refs_1_.refs_0_), channel_id=1, source_target_pairs={{0,10},{1,7},{2,4},{3,9},{4,2},{5,15},{6,12},{7,1},{8,14},{9,3},{1... | collective-permute-start | bytes 835592 | tf_op jit(solution)/shard_map/ppermute | solution.py:370
  46.5 2.8 %collective-permute-start.17 = (bf16[1088,128]{1,0:T(8,128)(2,1)S(1)}, bf16[1088,128]{1,0:T(8,128)(2,1)S(1)}, u32[]{:S(2)}, u32[]{:S(2)}) collective-permute-start(bf16[1088,128]{1,0:T(8,128)(2,1)S(1)} %shard_map.79), channel_id=1, source_target_pairs={{0,2},{1,3},{2,0},{3,1},{4,6},{5,7},{6,4},{7,5},{8,10},{9,11},{10,... | collective-permute-start | bytes 835592 | tf_op jit(solution)/shard_map/ppermute | solution.py:363
  48.0 1.6 %collective-permute-start.18 = (bf16[1088,128]{1,0:T(8,128)(2,1)S(1)}, bf16[1088,128]{1,0:T(8,128)(2,1)S(1)}, u32[]{:S(2)}, u32[]{:S(2)}) collective-permute-start(bf16[1088,128]{1,0:T(8,128)(2,1)S(1)} %shard_map.80), channel_id=1, source_target_pairs={{0,2},{1,3},{2,0},{3,1},{4,6},{5,7},{6,4},{7,5},{8,10},{9,11},{10,... | collective-permute-start | bytes 835592 | tf_op jit(solution)/shard_map/ppermute | solution.py:363
  48.4 3.6 %collective-permute-start.20 = (bf16[1088,128]{1,0:T(8,128)(2,1)S(1)}, bf16[1088,128]{1,0:T(8,128)(2,1)S(1)}, u32[]{:S(2)}, u32[]{:S(2)}) collective-permute-start(bf16[1088,128]{1,0:T(8,128)(2,1)S(1)} %shard_map.78.refs_2_.refs_1_), channel_id=1, source_target_pairs={{0,2},{1,3},{2,0},{3,1},{4,6},{5,7},{6,4},{7,5},{8,10},{9,11},{10,... | collective-permute-start | bytes 835592 | tf_op jit(solution)/shard_map/ppermute | solution.py:363
  51.1 2.1 %collective-permute-start.19 = (bf16[1088,128]{1,0:T(8,128)(2,1)S(1)}, bf16[1088,128]{1,0:T(8,128)(2,1)S(1)}, u32[]{:S(2)}, u32[]{:S(2)}) collective-permute-start(bf16[1088,128]{1,0:T(8,128)(2,1)S(1)} %shard_map.82.refs_1_), channel_id=1, source_target_pairs={{0,2},{1,3},{2,0},{3,1},{4,6},{5,7},{6,4},{7,5},{8,10},{9,11},{10,... | collective-permute-start | bytes 835592 | tf_op jit(solution)/shard_map/ppermute | solution.py:363

commit v9 on v8

--- a/solution.py
+++ b/solution.py
@@ -125,7 +125,10 @@
 
 
 def hidden_of(x1, w1p, slope, picked):
-    first_pre = dot(x1[...], w1p[...])
+    rows = x1.shape[0]
+    middle = rows // 128 * 64
+    cuts = [(0, middle), (middle, rows)] if middle else [(0, rows)]
+    first_pre = jnp.concatenate([dot(x1[low:high, :], w1p[...]) for low, high in cuts], 0)
     sig = sigmoid(first_pre)
     hidden = (first_pre * sig).astype(bf16)
     slope[...] = slope_of(first_pre, sig)
@@ -244,12 +247,11 @@
         deltas.append((rounded * slope).astype(bf16))
     d1_low, d1_up = jnp.concatenate(deltas[:2], 0), jnp.concatenate(deltas[2:], 0)
     for a in range(3):
-        columns = slice(a * 768, (a + 1) * 768)
-        grad = dot(d1_up, x1_up[:, columns], ((0,), (0,)))
-        grad = (grad + dot(d1_low, x1_low[:, columns], ((0,), (0,)))).T
         for b in range(3):
-            at = (a * 3 + b) * 192
-            g1[at : at + 192, :] = grad[b * 256 + 64 : (b + 1) * 256]
+            at, block = (a * 3 + b) * 192, slice(a * 768 + b * 256, a * 768 + (b + 1) * 256)
+            grad = dot(d1_up, x1_up[:, block], ((0,), (0,)))
+            grad = (grad + dot(d1_low, x1_low[:, block], ((0,), (0,)))).T
+            g1[at : at + 192, :] = grad[64:256]
     core = half_of(flat_index(spatial_count), bits)
     start, quarter = (27 - SPLIT) * LANES // 2, FIRST // 2
     for v in range(2):

time: 54.3 us -> 54.3 us (level)
  no operation moved by 1% of the time
where the time goes in v9:
time: 54.3 us; the launch traced here: 54.1 us
  starting transfers between devices  29.7 us (55%)
  waiting for transfers between devices  11.7 us (22%)
  Pallas kernels  10.9 us (20%)
  local copies, waits for them, and re-layouts  1.03 us (2%)
  between operations  0.79 us (1%)
    ppermute x14, starting transfers between devices, swap(): return lax.ppermute(array, BOTH, pairs)  22.8 us
    ppermute x14, waiting for transfers between devices, swap(): return lax.ppermute(array, BOTH, pairs)  11 us
    pallas_call x22, Pallas kernels, call(): pl.pallas_call(run, out_shape=shapes, in_specs=(specs or [full(a.shape) f...  6.31 us
    pallas_call x4, Pallas kernels, write(): pl.pallas_call(functools.partial(final_kernel, bits, spatial_count, jobs,...  4.6 us
    ppermute x6, starting transfers between devices, swap_core(): lax.ppermute(array, BOTH, [(i, i ^ 1 << core_bit) for i in range(count)])  3.96 us
    ppermute x1, starting transfers between devices, body(): lax.ppermute(face, 'spatial', [(i, (i + 1) % spatial_count) for i in rang...  2.94 us
  transfers between devices with their start and end apart: 21, of which 11 were waited for; matrix products, arithmetic and copies ran while one was open for 0% of the time, Pallas kernels for 16%

profile of v9, /device:TPU:0, one launch (start us, length us, event | category | flops | bytes accessed | tf_op | source)
XLA Modules:
  0.0 54.1 jit_solution(13527583353952471862)
XLA Ops:
  0.6 0.9 %slice_bitcast_fusion.refs_2_ = bf16[3,16,1024]{2,1,0:T(8,128)(2,1)S(1)} fusion(bf16[1,16,16,1024]{3,2,1,0:T(8,128)(2,1)} %param.4), kind=kLoop, calls=%fused_computation | loop fusion | bytes 196608 | tf_op jit(solution)/shard_map/slice | solution.py:381
  1.5 2.9 %collective-permute-start = (bf16[3,16,1024]{2,1,0:T(8,128)(2,1)S(1)}, bf16[3,16,1024]{2,1,0:T(8,128)(2,1)S(1)}, u32[]{:S(2)}, u32[]{:S(2)}) collective-permute-start(bf16[3,16,1024]{2,1,0:T(8,128)(2,1)S(1)} %slice_bitcast_fusion.refs_2_), channel_id=1, source_target_pairs={{0,1},{1,0},{2,3},{3,2},{4,5},{5,4},{6,7},{7,6},{8,9},{9,8},{10,11... | collective-permute-start | bytes 294920 | tf_op jit(solution)/shard_map/ppermute | solution.py:382
  4.5 1.4 %shard_map.59 = (bf16[64,2304]{1,0:T(8,128)(2,1)S(1)}, bf16[448,2304]{1,0:T(8,128)(2,1)S(1)}, bf16[2304,128]{1,0:T(8,128)(2,1)S(1)}) custom-call(bf16[16,16,1024]{2,1,0:T(8,128)(2,1)} %bitcast.5, bf16[1728,128]{1,0:T(8,128)(2,1)} %refs_1_.1, bf16[3,16,1024]{2,1,0:T(8,128)(2,1)S(1)} %slice_bitcast_fusion.refs_2_), custom_call_target="tpu_custom_call" | custom-call | flops 4000000000 | bytes 80000000 | tf_op jit(solution)/shard_map/pallas_call | solution.py:37
  5.9 0.0 copy-start
  5.9 1.1 %shard_map.60 = (f32[448,128]{1,0:T(8,128)S(1)}, bf16[1008,128]{1,0:T(8,128)(2,1)S(1)}, f32[64,256]{1,0:T(8,128)S(1)}) custom-call(bf16[448,2304]{1,0:T(8,128)(2,1)S(1)} %get-tuple-element.37.refs_0_, bf16[2304,128]{1,0:T(8,128)(2,1)S(1)} %get-tuple-element.39.refs_1_.refs_2_, bf16[4,4,1024]{2,1,0:T(4,128)(2,1)} %bitcast.4), custom_call_target="tpu_custom_call" | custom-call | flops 400000000 | bytes 10000000 | tf_op jit(solution)/shard_map/pallas_call | solution.py:37
  7.0 0.2 collective-permute-done.refs_0_
  7.3 0.1 copy-done
  7.4 1.3 %shard_map.61 = (f32[2176,128]{1,0:T(8,128)S(1)}, bf16[2176,128]{1,0:T(8,128)(2,1)S(1)}, bf16[128,2304]{1,0:T(8,128)(2,1)S(1)}, f32[128,128]{1,0:T(8,128)S(1)}, ...) custom-call(bf16[3,16,1024]{2,1,0:T(8,128)(2,1)S(1)} %collective-permute-done.refs_0_, ...), custom_call_target="tpu_custom_call" | custom-call | tf_op jit(solution)/shard_map/pallas_call | solution.py:37
  8.7 0.1 collective-permute-start.2
  8.8 1.9 %shard_map.62 = (f32[2176,128]{1,0:T(8,128)S(1)}, bf16[2176,128]{1,0:T(8,128)(2,1)S(1)}) custom-call(bf16[448,2304]{1,0:T(8,128)(2,1)S(1)} %get-tuple-element.37.refs_0_, bf16[128,2304]{1,0:T(8,128)(2,1)S(1)} %get-tuple-element.42.refs_1_, f32[448,128]{1,0:T(8,128)S(1)} %get-tuple-element.43.refs_2_, f32[128,128]{1,0:T(8,128)S(1)} %get-tuple-element.44.refs_3_, ...), custom_call_target="tpu_custom_call" | custom-call | flops 1000000000 | bytes 10000000 | tf_op jit(solution)/shard_map/pallas_call | solution.py:37
  10.7 0.6 %collective-permute-start.1 = (bf16[2176,128]{1,0:T(8,128)(2,1)S(1)}, bf16[2176,128]{1,0:T(8,128)(2,1)S(1)}, u32[]{:S(2)}, u32[]{:S(2)}) collective-permute-start(bf16[2176,128]{1,0:T(8,128)(2,1)S(1)} %get-tuple-element.49.refs_2_), channel_id=1, source_target_pairs={{0,2},{1,3},{2,0},{3,1},{4,6},{5,7},{6,4},{7,5},{8,10},{9,11},{10,... | collective-permute-start | bytes 1671176 | tf_op jit(solution)/shard_map/ppermute | solution.py:365
  11.2 0.0 collective-permute-done.2.refs_1_
  11.2 0.1 shard_map.63
  11.3 1.4 %collective-permute-start.4 = (bf16[1088,128]{1,0:T(8,128)(2,1)S(1)}, bf16[1088,128]{1,0:T(8,128)(2,1)S(1)}, u32[]{:S(2)}, u32[]{:S(2)}) collective-permute-start(bf16[1088,128]{1,0:T(8,128)(2,1)S(1)} %get-tuple-element.52.refs_2_), channel_id=1, source_target_pairs={{0,3},{1,7},{2,4},{3,0},{4,2},{5,6},{6,5},{7,1},{8,14},{9,10},{10,... | collective-permute-start | bytes 835592 | tf_op jit(solution)/shard_map/ppermute | solution.py:372
  12.8 0.1 collective-permute-done.1.refs_1_
  12.8 0.1 shard_map.64
  12.9 1.8 %collective-permute-start.3 = (bf16[1088,128]{1,0:T(8,128)(2,1)S(1)}, bf16[1088,128]{1,0:T(8,128)(2,1)S(1)}, u32[]{:S(2)}, u32[]{:S(2)}) collective-permute-start(bf16[1088,128]{1,0:T(8,128)(2,1)S(1)} %get-tuple-element.54.refs_2_), channel_id=1, source_target_pairs={{0,10},{1,7},{2,4},{3,9},{4,2},{5,15},{6,12},{7,1},{8,14},{9,3},{1... | collective-permute-start | bytes 835592 | tf_op jit(solution)/shard_map/ppermute | solution.py:372
  14.8 2.6 %collective-permute-done.4.refs_1_ = bf16[1088,128]{1,0:T(8,128)(2,1)S(1)} collective-permute-done((bf16[1088,128]{1,0:T(8,128)(2,1)S(1)}, bf16[1088,128]{1,0:T(8,128)(2,1)S(1)}, u32[]{:S(2)}, u32[]{:S(2)}) %collective-permute-start.4) | collective-permute-done | bytes 278560 | tf_op jit(solution)/shard_map/ppermute | solution.py:372
  17.4 0.1 shard_map.65
  17.4 1.8 %collective-permute-start.6 = (bf16[544,128]{1,0:T(8,128)(2,1)S(1)}, bf16[544,128]{1,0:T(8,128)(2,1)S(1)}, u32[]{:S(2)}, u32[]{:S(2)}) collective-permute-start(bf16[544,128]{1,0:T(8,128)(2,1)S(1)} %get-tuple-element.56.refs_2_), channel_id=1, source_target_pairs={{0,6},{1,11},{2,8},{3,5},{4,14},{5,3},{6,0},{7,13},{8,2},{9,15},{1... | collective-permute-start | bytes 417800 | tf_op jit(solution)/shard_map/ppermute | solution.py:372
  19.2 0.0 collective-permute-done.3.refs_1_
  19.2 0.1 shard_map.66
  19.3 1.8 %collective-permute-start.5 = (bf16[544,128]{1,0:T(8,128)(2,1)S(1)}, bf16[544,128]{1,0:T(8,128)(2,1)S(1)}, u32[]{:S(2)}, u32[]{:S(2)}) collective-permute-start(bf16[544,128]{1,0:T(8,128)(2,1)S(1)} %get-tuple-element.58.refs_2_), channel_id=1, source_target_pairs={{0,3},{1,11},{2,8},{3,0},{4,14},{5,6},{6,5},{7,13},{8,2},{9,10},{1... | collective-permute-start | bytes 417800 | tf_op jit(solution)/shard_map/ppermute | solution.py:372
  21.1 1.1 %collective-permute-done.6.refs_1_ = bf16[544,128]{1,0:T(8,128)(2,1)S(1)} collective-permute-done((bf16[544,128]{1,0:T(8,128)(2,1)S(1)}, bf16[544,128]{1,0:T(8,128)(2,1)S(1)}, u32[]{:S(2)}, u32[]{:S(2)}) %collective-permute-start.6) | collective-permute-done | bytes 139296 | tf_op jit(solution)/shard_map/ppermute | solution.py:372
  22.2 1.7 %collective-permute-start.8 = (bf16[272,128]{1,0:T(8,128)(2,1)S(1)}, bf16[272,128]{1,0:T(8,128)(2,1)S(1)}, u32[]{:S(2)}, u32[]{:S(2)}) collective-permute-start(bf16[272,128]{1,0:T(8,128)(2,1)S(1)} %get-tuple-element.60.refs_2_), channel_id=1, source_target_pairs={{0,10},{1,2},{2,1},{3,9},{4,7},{5,15},{6,12},{7,4},{8,11},{9,3},{1... | collective-permute-start | bytes 208904 | tf_op jit(solution)/shard_map/ppermute | solution.py:372
  23.8 0.0 collective-permute-done.5.refs_1_
  23.9 2.1 %collective-permute-start.7 = (bf16[272,128]{1,0:T(8,128)(2,1)S(1)}, bf16[272,128]{1,0:T(8,128)(2,1)S(1)}, u32[]{:S(2)}, u32[]{:S(2)}) collective-permute-start(bf16[272,128]{1,0:T(8,128)(2,1)S(1)} %get-tuple-element.62.refs_2_), channel_id=1, source_target_pairs={{0,6},{1,2},{2,1},{3,5},{4,7},{5,3},{6,0},{7,4},{8,11},{9,15},{10,... | collective-permute-start | bytes 208904 | tf_op jit(solution)/shard_map/ppermute | solution.py:372
  26.0 0.4 collective-permute-done.8.refs_1_
  26.4 2.3 %collective-permute-start.10 = (bf16[272,128]{1,0:T(8,128)(2,1)S(1)}, bf16[272,128]{1,0:T(8,128)(2,1)S(1)}, u32[]{:S(2)}, u32[]{:S(2)}) collective-permute-start(bf16[272,128]{1,0:T(8,128)(2,1)S(1)} %shard_map.69.refs_2_.refs_0_), channel_id=1, source_target_pairs={{0,18},{1,19},{2,16},{3,17},{4,22},{5,23},{6,20},{7,21},{8,26},{9,... | collective-permute-start | bytes 208904 | tf_op jit(solution)/shard_map/ppermute | solution.py:372
  28.7 0.0 collective-permute-done.7.refs_1_
  28.7 2.5 %collective-permute-start.9 = (bf16[272,128]{1,0:T(8,128)(2,1)S(1)}, bf16[272,128]{1,0:T(8,128)(2,1)S(1)}, u32[]{:S(2)}, u32[]{:S(2)}) collective-permute-start(bf16[272,128]{1,0:T(8,128)(2,1)S(1)} %shard_map.70.refs_2_.refs_0_), channel_id=1, source_target_pairs={{0,18},{1,19},{2,16},{3,17},{4,22},{5,23},{6,20},{7,21},{8,26},{9,... | collective-permute-start | bytes 208904 | tf_op jit(solution)/shard_map/ppermute | solution.py:372
  31.1 0.0 collective-permute-done.10.refs_1_
  31.2 2.6 %collective-permute-start.12 = (bf16[272,128]{1,0:T(8,128)(2,1)S(1)}, bf16[272,128]{1,0:T(8,128)(2,1)S(1)}, u32[]{:S(2)}, u32[]{:S(2)}) collective-permute-start(bf16[272,128]{1,0:T(8,128)(2,1)S(1)} %shard_map.71.refs_2_.refs_0_), channel_id=1, source_target_pairs={{0,10},{1,2},{2,1},{3,9},{4,7},{5,15},{6,12},{7,4},{8,11},{9,3},{1... | collective-permute-start | bytes 208904 | tf_op jit(solution)/shard_map/ppermute | solution.py:372
  33.8 2.5 %collective-permute-done.9.refs_1_ = bf16[272,128]{1,0:T(8,128)(2,1)S(1)} collective-permute-done((bf16[272,128]{1,0:T(8,128)(2,1)S(1)}, bf16[272,128]{1,0:T(8,128)(2,1)S(1)}, u32[]{:S(2)}, u32[]{:S(2)}) %collective-permute-start.9) | collective-permute-done | bytes 69664 | tf_op jit(solution)/shard_map/ppermute | solution.py:372
  36.3 1.5 %collective-permute-start.11 = (bf16[272,128]{1,0:T(8,128)(2,1)S(1)}, bf16[272,128]{1,0:T(8,128)(2,1)S(1)}, u32[]{:S(2)}, u32[]{:S(2)}) collective-permute-start(bf16[272,128]{1,0:T(8,128)(2,1)S(1)} %shard_map.72.refs_2_.refs_0_), channel_id=1, source_target_pairs={{0,6},{1,2},{2,1},{3,5},{4,7},{5,3},{6,0},{7,4},{8,11},{9,15},{10,... | collective-permute-start | bytes 208904 | tf_op jit(solution)/shard_map/ppermute | solution.py:372
  37.8 0.0 collective-permute-done.12.refs_1_
  37.8 0.6 %collective-permute-start.14 = (bf16[544,128]{1,0:T(8,128)(2,1)S(1)}, bf16[544,128]{1,0:T(8,128)(2,1)S(1)}, u32[]{:S(2)}, u32[]{:S(2)}) collective-permute-start(bf16[544,128]{1,0:T(8,128)(2,1)S(1)} %shard_map.73.refs_2_.refs_0_), channel_id=1, source_target_pairs={{0,6},{1,11},{2,8},{3,5},{4,14},{5,3},{6,0},{7,13},{8,2},{9,15},{1... | collective-permute-start | bytes 417800 | tf_op jit(solution)/shard_map/ppermute | solution.py:372
  38.5 1.7 %collective-permute-done.11.refs_1_ = bf16[272,128]{1,0:T(8,128)(2,1)S(1)} collective-permute-done((bf16[272,128]{1,0:T(8,128)(2,1)S(1)}, bf16[272,128]{1,0:T(8,128)(2,1)S(1)}, u32[]{:S(2)}, u32[]{:S(2)}) %collective-permute-start.11) | collective-permute-done | bytes 69664 | tf_op jit(solution)/shard_map/ppermute | solution.py:372
  40.1 1.6 %collective-permute-start.13 = (bf16[544,128]{1,0:T(8,128)(2,1)S(1)}, bf16[544,128]{1,0:T(8,128)(2,1)S(1)}, u32[]{:S(2)}, u32[]{:S(2)}) collective-permute-start(bf16[544,128]{1,0:T(8,128)(2,1)S(1)} %shard_map.74.refs_2_.refs_0_), channel_id=1, source_target_pairs={{0,3},{1,11},{2,8},{3,0},{4,14},{5,6},{6,5},{7,13},{8,2},{9,10},{1... | collective-permute-start | bytes 417800 | tf_op jit(solution)/shard_map/ppermute | solution.py:372
  41.7 0.7 %collective-permute-done.14.refs_1_ = bf16[544,128]{1,0:T(8,128)(2,1)S(1)} collective-permute-done((bf16[544,128]{1,0:T(8,128)(2,1)S(1)}, bf16[544,128]{1,0:T(8,128)(2,1)S(1)}, u32[]{:S(2)}, u32[]{:S(2)}) %collective-permute-start.14) | collective-permute-done | bytes 139296 | tf_op jit(solution)/shard_map/ppermute | solution.py:372
  42.4 0.5 collective-permute-start.16
  42.9 1.8 %collective-permute-done.13.refs_1_ = bf16[544,128]{1,0:T(8,128)(2,1)S(1)} collective-permute-done((bf16[544,128]{1,0:T(8,128)(2,1)S(1)}, bf16[544,128]{1,0:T(8,128)(2,1)S(1)}, u32[]{:S(2)}, u32[]{:S(2)}) %collective-permute-start.13) | collective-permute-done | bytes 139296 | tf_op jit(solution)/shard_map/ppermute | solution.py:372
  44.7 0.7 %collective-permute-start.15 = (bf16[1088,128]{1,0:T(8,128)(2,1)S(1)}, bf16[1088,128]{1,0:T(8,128)(2,1)S(1)}, u32[]{:S(2)}, u32[]{:S(2)}) collective-permute-start(bf16[1088,128]{1,0:T(8,128)(2,1)S(1)} %shard_map.76.refs_1_.refs_0_), channel_id=1, source_target_pairs={{0,10},{1,7},{2,4},{3,9},{4,2},{5,15},{6,12},{7,1},{8,14},{9,3},{1... | collective-permute-start | bytes 835592 | tf_op jit(solution)/shard_map/ppermute | solution.py:372
  45.4 1.1 %shard_map.77 = (f32[1728,128]{1,0:T(8,128)}, f32[3456,256]{1,0:T(8,128)}, f32[8,128]{1,0:T(8,128)S(1)}) custom-call(bf16[1088,128]{1,0:T(8,128)(2,1)S(1)} %shard_map.75.refs_2_.refs_0_, bf16[1088,128]{1,0:T(8,128)(2,1)S(1)} %shard_map.76.refs_1_.refs_0_), custom_call_target="tpu_custom_call" | custom-call | flops 4000000000 | bytes 80000000 | tf_op jit(solution)/shard_map/pallas_call | solution.py:494
  46.6 1.5 %collective-permute-start.17 = (bf16[1088,128]{1,0:T(8,128)(2,1)S(1)}, bf16[1088,128]{1,0:T(8,128)(2,1)S(1)}, u32[]{:S(2)}, u32[]{:S(2)}) collective-permute-start(bf16[1088,128]{1,0:T(8,128)(2,1)S(1)} %shard_map.79), channel_id=1, source_target_pairs={{0,2},{1,3},{2,0},{3,1},{4,6},{5,7},{6,4},{7,5},{8,10},{9,11},{10,... | collective-permute-start | bytes 835592 | tf_op jit(solution)/shard_map/ppermute | solution.py:365
  48.1 0.1 collective-permute-start.18
  48.2 0.3 collective-permute-done.16.refs_0_
  48.5 0.9 %collective-permute-start.20 = (bf16[1088,128]{1,0:T(8,128)(2,1)S(1)}, bf16[1088,128]{1,0:T(8,128)(2,1)S(1)}, u32[]{:S(2)}, u32[]{:S(2)}) collective-permute-start(bf16[1088,128]{1,0:T(8,128)(2,1)S(1)} %shard_map.78.refs_2_.refs_1_), channel_id=1, source_target_pairs={{0,2},{1,3},{2,0},{3,1},{4,6},{5,7},{6,4},{7,5},{8,10},{9,11},{10,... | collective-permute-start | bytes 835592 | tf_op jit(solution)/shard_map/ppermute | solution.py:365
  49.4 0.0 collective-permute-done.17.refs_0_
  49.4 0.4 collective-permute-done.18.refs_1_
  49.7 1.4 %shard_map.81 = (f32[1728,128]{1,0:T(8,128)}, f32[3456,256]{1,0:T(8,128)}, f32[8,128]{1,0:T(8,128)S(1)}) custom-call(bf16[1088,128]{1,0:T(8,128)(2,1)S(1)} %collective-permute-done.17.refs_0_, bf16[1088,128]{1,0:T(8,128)(2,1)S(1)} %collective-permute-done.18.refs_1_, ...), custom_call_target="tpu_custom_call", output_to_operand_aliasing={{0}: (3, {}), {1}: (4, {})} | custom-call | flops 4000000000 | bytes 80000000 | tf_op jit(solution)/shard_map/pallas_call | solution.py:494
  51.1 0.0 collective-permute-done.15.refs_0_
  51.2 0.9 %collective-permute-start.19 = (bf16[1088,128]{1,0:T(8,128)(2,1)S(1)}, bf16[1088,128]{1,0:T(8,128)(2,1)S(1)}, u32[]{:S(2)}, u32[]{:S(2)}) collective-permute-start(bf16[1088,128]{1,0:T(8,128)(2,1)S(1)} %shard_map.82.refs_1_), channel_id=1, source_target_pairs={{0,2},{1,3},{2,0},{3,1},{4,6},{5,7},{6,4},{7,5},{8,10},{9,11},{10,... | collective-permute-start | bytes 835592 | tf_op jit(solution)/shard_map/ppermute | solution.py:365
  52.0 0.0 collective-permute-done.20.refs_0_
  52.0 1.1 %shard_map.83 = (f32[1728,128]{1,0:T(8,128)}, f32[3456,256]{1,0:T(8,128)}) custom-call(bf16[1088,128]{1,0:T(8,128)(2,1)S(1)} %collective-permute-done.20.refs_0_, bf16[1088,128]{1,0:T(8,128)(2,1)S(1)} %shard_map.82.refs_1_, f32[1728,128]{1,0:T(8,128)} %get-tuple-element.68.refs_2_, ...), custom_call_target="tpu_custom_call", output_to_operand_aliasing={{0}: (2, {}), {1}: (3, {})} | custom-call | flops 4000000000 | bytes 80000000 | tf_op jit(solution)/shard_map/pallas_call | solution.py:494
  53.2 0.0 collective-permute-done.19.refs_0_
  53.2 0.9 %shard_map.84 = (f32[1728,128]{1,0:T(8,128)}, f32[3456,256]{1,0:T(8,128)}) custom-call(bf16[1088,128]{1,0:T(8,128)(2,1)S(1)} %collective-permute-done.19.refs_0_, f32[1728,128]{1,0:T(8,128)} %get-tuple-element.70.refs_1_, f32[3456,256]{1,0:T(8,128)} %get-tuple-element.71.refs_2_), custom_call_target="tpu_custom_call", output_to_operand_aliasing={{0}: (1, {}), {1}: (2, {})} | custom-call | flops 4000000000 | bytes 80000000 | tf_op jit(solution)/shard_map/pallas_call | solution.py:494
  (14 shorter events, 0.3 us)
Async XLA Ops:
  1.5 5.7 %collective-permute-start = (bf16[3,16,1024]{2,1,0:T(8,128)(2,1)S(1)}, bf16[3,16,1024]{2,1,0:T(8,128)(2,1)S(1)}, u32[]{:S(2)}, u32[]{:S(2)}) collective-permute-start(bf16[3,16,1024]{2,1,0:T(8,128)(2,1)S(1)} %slice_bitcast_fusion.refs_2_), channel_id=1, source_target_pairs={{0,1},{1,0},{2,3},{3,2},{4,5},{5,4},{6,7},{7,6},{8,9},{9,8},{10,11... | collective-permute-start | bytes 294920 | tf_op jit(solution)/shard_map/ppermute | solution.py:382
  5.9 1.5 %copy-start = (bf16[3456,256]{1,0:T(8,128)(2,1)S(1)}, bf16[3456,256]{1,0:T(8,128)(2,1)}, u32[]{:S(2)}) copy-start(bf16[3456,256]{1,0:T(8,128)(2,1)} %refs_7_.1) | copy-start | bytes 5308420
  8.7 2.5 %collective-permute-start.2 = (bf16[2176,128]{1,0:T(8,128)(2,1)S(1)}, bf16[2176,128]{1,0:T(8,128)(2,1)S(1)}, u32[]{:S(2)}, u32[]{:S(2)}) collective-permute-start(bf16[2176,128]{1,0:T(8,128)(2,1)S(1)} %get-tuple-element.51), channel_id=1, source_target_pairs={{0,2},{1,3},{2,0},{3,1},{4,6},{5,7},{6,4},{7,5},{8,10},{9,11},{10,... | collective-permute-start | bytes 1671176 | tf_op jit(solution)/shard_map/ppermute | solution.py:365
  10.7 2.2 %collective-permute-start.1 = (bf16[2176,128]{1,0:T(8,128)(2,1)S(1)}, bf16[2176,128]{1,0:T(8,128)(2,1)S(1)}, u32[]{:S(2)}, u32[]{:S(2)}) collective-permute-start(bf16[2176,128]{1,0:T(8,128)(2,1)S(1)} %get-tuple-element.49.refs_2_), channel_id=1, source_target_pairs={{0,2},{1,3},{2,0},{3,1},{4,6},{5,7},{6,4},{7,5},{8,10},{9,11},{10,... | collective-permute-start | bytes 1671176 | tf_op jit(solution)/shard_map/ppermute | solution.py:365
  11.3 6.0 %collective-permute-start.4 = (bf16[1088,128]{1,0:T(8,128)(2,1)S(1)}, bf16[1088,128]{1,0:T(8,128)(2,1)S(1)}, u32[]{:S(2)}, u32[]{:S(2)}) collective-permute-start(bf16[1088,128]{1,0:T(8,128)(2,1)S(1)} %get-tuple-element.52.refs_2_), channel_id=1, source_target_pairs={{0,3},{1,7},{2,4},{3,0},{4,2},{5,6},{6,5},{7,1},{8,14},{9,10},{10,... | collective-permute-start | bytes 835592 | tf_op jit(solution)/shard_map/ppermute | solution.py:372
  12.9 6.3 %collective-permute-start.3 = (bf16[1088,128]{1,0:T(8,128)(2,1)S(1)}, bf16[1088,128]{1,0:T(8,128)(2,1)S(1)}, u32[]{:S(2)}, u32[]{:S(2)}) collective-permute-start(bf16[1088,128]{1,0:T(8,128)(2,1)S(1)} %get-tuple-element.54.refs_2_), channel_id=1, source_target_pairs={{0,10},{1,7},{2,4},{3,9},{4,2},{5,15},{6,12},{7,1},{8,14},{9,3},{1... | collective-permute-start | bytes 835592 | tf_op jit(solution)/shard_map/ppermute | solution.py:372
  17.4 4.7 %collective-permute-start.6 = (bf16[544,128]{1,0:T(8,128)(2,1)S(1)}, bf16[544,128]{1,0:T(8,128)(2,1)S(1)}, u32[]{:S(2)}, u32[]{:S(2)}) collective-permute-start(bf16[544,128]{1,0:T(8,128)(2,1)S(1)} %get-tuple-element.56.refs_2_), channel_id=1, source_target_pairs={{0,6},{1,11},{2,8},{3,5},{4,14},{5,3},{6,0},{7,13},{8,2},{9,15},{1... | collective-permute-start | bytes 417800 | tf_op jit(solution)/shard_map/ppermute | solution.py:372
  19.3 4.6 %collective-permute-start.5 = (bf16[544,128]{1,0:T(8,128)(2,1)S(1)}, bf16[544,128]{1,0:T(8,128)(2,1)S(1)}, u32[]{:S(2)}, u32[]{:S(2)}) collective-permute-start(bf16[544,128]{1,0:T(8,128)(2,1)S(1)} %get-tuple-element.58.refs_2_), channel_id=1, source_target_pairs={{0,3},{1,11},{2,8},{3,0},{4,14},{5,6},{6,5},{7,13},{8,2},{9,10},{1... | collective-permute-start | bytes 417800 | tf_op jit(solution)/shard_map/ppermute | solution.py:372
  22.2 4.2 %collective-permute-start.8 = (bf16[272,128]{1,0:T(8,128)(2,1)S(1)}, bf16[272,128]{1,0:T(8,128)(2,1)S(1)}, u32[]{:S(2)}, u32[]{:S(2)}) collective-permute-start(bf16[272,128]{1,0:T(8,128)(2,1)S(1)} %get-tuple-element.60.refs_2_), channel_id=1, source_target_pairs={{0,10},{1,2},{2,1},{3,9},{4,7},{5,15},{6,12},{7,4},{8,11},{9,3},{1... | collective-permute-start | bytes 208904 | tf_op jit(solution)/shard_map/ppermute | solution.py:372
  23.9 4.8 %collective-permute-start.7 = (bf16[272,128]{1,0:T(8,128)(2,1)S(1)}, bf16[272,128]{1,0:T(8,128)(2,1)S(1)}, u32[]{:S(2)}, u32[]{:S(2)}) collective-permute-start(bf16[272,128]{1,0:T(8,128)(2,1)S(1)} %get-tuple-element.62.refs_2_), channel_id=1, source_target_pairs={{0,6},{1,2},{2,1},{3,5},{4,7},{5,3},{6,0},{7,4},{8,11},{9,15},{10,... | collective-permute-start | bytes 208904 | tf_op jit(solution)/shard_map/ppermute | solution.py:372
  26.4 4.7 %collective-permute-start.10 = (bf16[272,128]{1,0:T(8,128)(2,1)S(1)}, bf16[272,128]{1,0:T(8,128)(2,1)S(1)}, u32[]{:S(2)}, u32[]{:S(2)}) collective-permute-start(bf16[272,128]{1,0:T(8,128)(2,1)S(1)} %shard_map.69.refs_2_.refs_0_), channel_id=1, source_target_pairs={{0,18},{1,19},{2,16},{3,17},{4,22},{5,23},{6,20},{7,21},{8,26},{9,... | collective-permute-start | bytes 208904 | tf_op jit(solution)/shard_map/ppermute | solution.py:372
  28.7 7.6 %collective-permute-start.9 = (bf16[272,128]{1,0:T(8,128)(2,1)S(1)}, bf16[272,128]{1,0:T(8,128)(2,1)S(1)}, u32[]{:S(2)}, u32[]{:S(2)}) collective-permute-start(bf16[272,128]{1,0:T(8,128)(2,1)S(1)} %shard_map.70.refs_2_.refs_0_), channel_id=1, source_target_pairs={{0,18},{1,19},{2,16},{3,17},{4,22},{5,23},{6,20},{7,21},{8,26},{9,... | collective-permute-start | bytes 208904 | tf_op jit(solution)/shard_map/ppermute | solution.py:372
  31.2 6.6 %collective-permute-start.12 = (bf16[272,128]{1,0:T(8,128)(2,1)S(1)}, bf16[272,128]{1,0:T(8,128)(2,1)S(1)}, u32[]{:S(2)}, u32[]{:S(2)}) collective-permute-start(bf16[272,128]{1,0:T(8,128)(2,1)S(1)} %shard_map.71.refs_2_.refs_0_), channel_id=1, source_target_pairs={{0,10},{1,2},{2,1},{3,9},{4,7},{5,15},{6,12},{7,4},{8,11},{9,3},{1... | collective-permute-start | bytes 208904 | tf_op jit(solution)/shard_map/ppermute | solution.py:372
  36.3 3.8 %collective-permute-start.11 = (bf16[272,128]{1,0:T(8,128)(2,1)S(1)}, bf16[272,128]{1,0:T(8,128)(2,1)S(1)}, u32[]{:S(2)}, u32[]{:S(2)}) collective-permute-start(bf16[272,128]{1,0:T(8,128)(2,1)S(1)} %shard_map.72.refs_2_.refs_0_), channel_id=1, source_target_pairs={{0,6},{1,2},{2,1},{3,5},{4,7},{5,3},{6,0},{7,4},{8,11},{9,15},{10,... | collective-permute-start | bytes 208904 | tf_op jit(solution)/shard_map/ppermute | solution.py:372
  37.8 4.5 %collective-permute-start.14 = (bf16[544,128]{1,0:T(8,128)(2,1)S(1)}, bf16[544,128]{1,0:T(8,128)(2,1)S(1)}, u32[]{:S(2)}, u32[]{:S(2)}) collective-permute-start(bf16[544,128]{1,0:T(8,128)(2,1)S(1)} %shard_map.73.refs_2_.refs_0_), channel_id=1, source_target_pairs={{0,6},{1,11},{2,8},{3,5},{4,14},{5,3},{6,0},{7,13},{8,2},{9,15},{1... | collective-permute-start | bytes 417800 | tf_op jit(solution)/shard_map/ppermute | solution.py:372
  40.1 4.5 %collective-permute-start.13 = (bf16[544,128]{1,0:T(8,128)(2,1)S(1)}, bf16[544,128]{1,0:T(8,128)(2,1)S(1)}, u32[]{:S(2)}, u32[]{:S(2)}) collective-permute-start(bf16[544,128]{1,0:T(8,128)(2,1)S(1)} %shard_map.74.refs_2_.refs_0_), channel_id=1, source_target_pairs={{0,3},{1,11},{2,8},{3,0},{4,14},{5,6},{6,5},{7,13},{8,2},{9,10},{1... | collective-permute-start | bytes 417800 | tf_op jit(solution)/shard_map/ppermute | solution.py:372
  42.4 6.0 %collective-permute-start.16 = (bf16[1088,128]{1,0:T(8,128)(2,1)S(1)}, bf16[1088,128]{1,0:T(8,128)(2,1)S(1)}, u32[]{:S(2)}, u32[]{:S(2)}) collective-permute-start(bf16[1088,128]{1,0:T(8,128)(2,1)S(1)} %shard_map.75.refs_2_.refs_0_), channel_id=1, source_target_pairs={{0,3},{1,7},{2,4},{3,0},{4,2},{5,6},{6,5},{7,1},{8,14},{9,10},{10,... | collective-permute-start | bytes 835592 | tf_op jit(solution)/shard_map/ppermute | solution.py:372
  44.7 6.4 %collective-permute-start.15 = (bf16[1088,128]{1,0:T(8,128)(2,1)S(1)}, bf16[1088,128]{1,0:T(8,128)(2,1)S(1)}, u32[]{:S(2)}, u32[]{:S(2)}) collective-permute-start(bf16[1088,128]{1,0:T(8,128)(2,1)S(1)} %shard_map.76.refs_1_.refs_0_), channel_id=1, source_target_pairs={{0,10},{1,7},{2,4},{3,9},{4,2},{5,15},{6,12},{7,1},{8,14},{9,3},{1... | collective-permute-start | bytes 835592 | tf_op jit(solution)/shard_map/ppermute | solution.py:372
  46.6 2.8 %collective-permute-start.17 = (bf16[1088,128]{1,0:T(8,128)(2,1)S(1)}, bf16[1088,128]{1,0:T(8,128)(2,1)S(1)}, u32[]{:S(2)}, u32[]{:S(2)}) collective-permute-start(bf16[1088,128]{1,0:T(8,128)(2,1)S(1)} %shard_map.79), channel_id=1, source_target_pairs={{0,2},{1,3},{2,0},{3,1},{4,6},{5,7},{6,4},{7,5},{8,10},{9,11},{10,... | collective-permute-start | bytes 835592 | tf_op jit(solution)/shard_map/ppermute | solution.py:365
  48.1 1.6 %collective-permute-start.18 = (bf16[1088,128]{1,0:T(8,128)(2,1)S(1)}, bf16[1088,128]{1,0:T(8,128)(2,1)S(1)}, u32[]{:S(2)}, u32[]{:S(2)}) collective-permute-start(bf16[1088,128]{1,0:T(8,128)(2,1)S(1)} %shard_map.80), channel_id=1, source_target_pairs={{0,2},{1,3},{2,0},{3,1},{4,6},{5,7},{6,4},{7,5},{8,10},{9,11},{10,... | collective-permute-start | bytes 835592 | tf_op jit(solution)/shard_map/ppermute | solution.py:365
  48.5 3.6 %collective-permute-start.20 = (bf16[1088,128]{1,0:T(8,128)(2,1)S(1)}, bf16[1088,128]{1,0:T(8,128)(2,1)S(1)}, u32[]{:S(2)}, u32[]{:S(2)}) collective-permute-start(bf16[1088,128]{1,0:T(8,128)(2,1)S(1)} %shard_map.78.refs_2_.refs_1_), channel_id=1, source_target_pairs={{0,2},{1,3},{2,0},{3,1},{4,6},{5,7},{6,4},{7,5},{8,10},{9,11},{10,... | collective-permute-start | bytes 835592 | tf_op jit(solution)/shard_map/ppermute | solution.py:365
  51.2 2.1 %collective-permute-start.19 = (bf16[1088,128]{1,0:T(8,128)(2,1)S(1)}, bf16[1088,128]{1,0:T(8,128)(2,1)S(1)}, u32[]{:S(2)}, u32[]{:S(2)}) collective-permute-start(bf16[1088,128]{1,0:T(8,128)(2,1)S(1)} %shard_map.82.refs_1_), channel_id=1, source_target_pairs={{0,2},{1,3},{2,0},{3,1},{4,6},{5,7},{6,4},{7,5},{8,10},{9,11},{10,... | collective-permute-start | bytes 835592 | tf_op jit(solution)/shard_map/ppermute | solution.py:365
